TPU v7x, 32 devices: a whole 2x2x4 slice. The times are simulated.
32 devices in a mesh: fsdp: 4 (over y, core), ctx: 8 (over z, x).
Axes of the slice: x: 2, y: 2, z: 4, core: 2. Of those that a mesh axis runs over, the one named last changes fastest.
Arguments:
- hidden: bfloat16 [4, 1024, 2048], P('fsdp', 'ctx'), may hold values from -6 to 6
- queries: bfloat16 [4, 1024, 1024], P('fsdp', 'ctx'), may hold values from -6 to 6
- attn_out: bfloat16 [4, 1024, 1024], P('fsdp', 'ctx'), may hold values from -6 to 6
- grad_out: bfloat16 [4, 1024, 1024], P('fsdp', 'ctx'), may hold values from -6 to 6
- log_sums: float32 [4, 16, 1024], P('fsdp', None, 'ctx'), may hold values from 6 to 9
- block_order: int32 [4, 8], P('fsdp'), may hold values from 0 to 7, each once within a row
- w_kv: bfloat16 [2048, 512], P('fsdp'), may hold values from -0.125 to 0.125
Outputs:
- query_grads: bfloat16 [4, 1024, 1024], P('fsdp', 'ctx')
- input_grads: bfloat16 [4, 1024, 2048], P('fsdp', 'ctx')
- weight_grads: float32 [2048, 512], P(('fsdp', 'ctx'))
Inputs may be any that keep to these rules, and one draw needn't show every extreme that they name: Each row of block_order is a permutation of the 8 block numbers.
All inputs are finite; a program needn't handle non-finite values.
Results may differ from a plain program's by a relative error of at most 0.013.
The roundings to bfloat16 on the way count: a program that leaves them out, or rounds other values in their place, can miss the bound.
Values may be sent and summed in bfloat16 or wider, within the bound.
No kernel may reach another device: no remote copies, remote signals or barrier semaphores. Data moves between devices by JAX's collectives and lax.ppermute only.
A program may use at most 128 MiB of HBM per device.

v0:
```python
import functools

import jax
import jax.numpy as jnp
from jax import lax
from jax.experimental import pallas as pl
from jax.experimental.pallas import tpu as pltpu
from jax.sharding import PartitionSpec as P

Q_HEADS = 16
KV_HEADS = 4
HEAD_DIM = 64
GROUPS = Q_HEADS // KV_HEADS
KEY_WIDTH = KV_HEADS * HEAD_DIM
PAIR = 2 * HEAD_DIM
TEAM = 2 * KV_HEADS
GROUP = GROUPS * HEAD_DIM
SCALE = HEAD_DIM ** -0.5
LOWER = HEAD_DIM

NT = (((1,), (1,)), ((), ()))
TN = (((0,), (0,)), ((), ()))
VMEM = pl.BlockSpec(memory_space=pltpu.VMEM)
SMEM = pl.BlockSpec(memory_space=pltpu.SMEM)
ANY = pl.BlockSpec(memory_space=pl.ANY)
HBM = pl.BlockSpec(memory_space=pltpu.HBM)
PARAMS = pltpu.CompilerParams(vmem_limit_bytes=40 * 1024 * 1024)
WHOLE = pltpu.CompilerParams(vmem_limit_bytes=60 * 1024 * 1024)


def matmul(left, right, dims=(((1,), (0,)), ((), ()))):
    return lax.dot_general(left, right, dims, preferred_element_type=jnp.float32)


def swapped(array, axis, bits):
    size = lax.axis_size(axis)
    return lax.ppermute(array, axis, [(i, i ^ bits) for i in range(size)])


def call(kernel, out_shape, scratch, args, smem=0, hbm=0, after=()):
    given = len(args)
    params = WHOLE if hbm == given else PARAMS

    def body(*refs):
        kernel(*refs[:given], *refs[given + len(after):])

    specs = [SMEM] * smem + [HBM] * hbm + [VMEM] * (given - smem - hbm) + [ANY] * len(after)
    return pl.pallas_call(
        body,
        out_shape=out_shape,
        in_specs=specs,
        out_specs=[VMEM] * len(out_shape),
        scratch_shapes=scratch,
        compiler_params=params,
    )(*args, *after)


def held(array, after):
    def body(*refs):
        pass

    return pl.pallas_call(
        body,
        out_shape=sds(array.shape, array.dtype),
        in_specs=[ANY] * (1 + len(after)),
        out_specs=ANY,
        input_output_aliases={0: 0},
        compiler_params=PARAMS,
    )(array, *after)


def sds(shape, dtype=jnp.bfloat16):
    return jax.ShapeDtypeStruct(shape, dtype)


def head_side():
    me = lax.rem(lax.axis_index("ctx"), TEAM)
    return me // 2, lax.rem(me, 2)


def split(exact):
    first = exact.astype(jnp.bfloat16).astype(jnp.float32)
    second = (exact - first).astype(jnp.bfloat16).astype(jnp.float32)
    return first, second, exact - first - second


def pieces_kernel(q_ref, go_ref, ao_ref, lse_ref, *rest):
    out_refs, (grad, output, lse, stat, sems) = rest[:KV_HEADS], rest[KV_HEADS:]
    rows, width = q_ref.shape
    head, _ = head_side()
    loads = [pltpu.make_async_copy(ref, to, sems.at[i])
             for i, (ref, to) in enumerate(((go_ref, grad), (ao_ref, output), (lse_ref, lse)))]
    moves = []
    for m in range(KV_HEADS):
        columns = pl.ds(pl.multiple_of(jnp.bitwise_xor(head, m) * GROUP, GROUP), GROUP)
        for i, ref in enumerate((q_ref, go_ref)):
            moves.append(pltpu.make_async_copy(
                ref.at[:, columns], out_refs[m].at[0:rows, i * GROUP:(i + 1) * GROUP], sems.at[3 + 2 * m + i]))
    for copy in loads + moves:
        copy.start()
    for copy in loads:
        copy.wait()
    product = grad[...].astype(jnp.float32) * output[...].astype(jnp.float32)
    high = product.astype(jnp.bfloat16)
    low = (product - high.astype(jnp.float32)).astype(jnp.bfloat16)
    head_of = lax.broadcasted_iota(jnp.int32, (Q_HEADS, width), 1) // HEAD_DIM
    ones = (head_of == lax.broadcasted_iota(jnp.int32, (Q_HEADS, width), 0)).astype(jnp.bfloat16)
    delta = matmul(ones, high, NT) + matmul(ones, low, NT)
    for g in range(KV_HEADS):
        part = slice(g * GROUPS, (g + 1) * GROUPS)
        stat[g] = jnp.concatenate([lse[part, :], delta[part, :]], axis=0)
    zero = jnp.zeros((2 * GROUPS, rows), jnp.float32)
    for m in range(KV_HEADS):
        lines = [*split(stat[jnp.bitwise_xor(head, m)]), zero]
        for i, one in enumerate(lines):
            full = jnp.concatenate([one, zero], axis=0).astype(jnp.bfloat16)
            out_refs[m][rows:, i * rows:(i + 1) * rows] = full
    for copy in moves:
        copy.wait()


def hidden_moves(hid_ref, near_refs, far_ref, sems):
    mine = lax.axis_index("fsdp")
    near = len(near_refs)
    span = far_ref.shape[2]
    copies = []
    for m in range(near + far_ref.shape[0]):
        columns = pl.ds(pl.multiple_of(jnp.bitwise_xor(mine, m) * span, span), span)
        to = near_refs[m] if m < near else far_ref.at[m - near]
        copies.append(pltpu.make_async_copy(hid_ref.at[:, columns], to, sems.at[m]))
    for copy in copies:
        copy.start()
    return copies


def hidden_kernel(hid_ref, *rest):
    for copy in hidden_moves(hid_ref, rest[:-2], *rest[-2:]):
        copy.wait()


def project_kernel(fsdp, hid_ref, *rest):
    w_refs, out_refs, (parts,) = rest[:fsdp], rest[fsdp:fsdp + KV_HEADS], rest[fsdp + KV_HEADS:]
    mine = lax.axis_index("fsdp")
    head, _ = head_side()
    span = w_refs[0].shape[0]
    total = None
    for m in range(fsdp):
        start = pl.multiple_of(jnp.bitwise_xor(mine, m) * span, span)
        term = matmul(hid_ref[:, pl.ds(start, span)], w_refs[m][...])
        total = term if total is None else total + term
    low = total.astype(jnp.bfloat16)
    for g in range(KV_HEADS):
        key = low[:, g * HEAD_DIM:(g + 1) * HEAD_DIM]
        value = low[:, KEY_WIDTH + g * HEAD_DIM:KEY_WIDTH + (g + 1) * HEAD_DIM]
        parts[g] = jnp.concatenate([key, value], axis=1)
    for m in range(KV_HEADS):
        out_refs[m][...] = parts[jnp.bitwise_xor(head, m)]


def lower_half(shape):
    return lax.broadcasted_iota(jnp.int32, shape, len(shape) - 1) < LOWER


def stacked(key_value):
    wide = key_value.astype(jnp.float32)
    turned = pltpu.roll(wide, LOWER, 1)
    lower = lower_half(wide.shape)
    zero = jnp.zeros_like(wide)
    keys = jnp.concatenate([jnp.where(lower, wide, zero), jnp.where(lower, zero, turned)], axis=0) * SCALE
    values = jnp.concatenate([jnp.where(lower, turned, zero), jnp.where(lower, zero, wide)], axis=0)
    return keys.astype(jnp.bfloat16), values.astype(jnp.bfloat16)


def tile(keys, values, query, grad, stats, mask):
    size = keys.shape[0] // 2
    lse, delta = stats[:2], stats[2:]
    scores = matmul(keys, query, NT)
    prob_grad = matmul(values, grad, NT)
    lows, grads = [], []
    for head in range(2):
        part = slice(head * size, (head + 1) * size)
        probs = jnp.exp(scores[part] - lse[head])
        edge = mask.shape[1]
        seen = jnp.where(mask, probs[:, :edge], 0.0)
        probs = seen if edge == probs.shape[1] else jnp.concatenate([seen, probs[:, edge:]], axis=1)
        lows.append(probs.astype(jnp.bfloat16))
        grads.append((probs * (prob_grad[part] - delta[head])).astype(jnp.bfloat16))
    low, score_grad = jnp.concatenate(lows, axis=0), jnp.concatenate(grads, axis=0)
    return matmul(score_grad, query), matmul(low, grad), matmul(score_grad, keys, TN)


def folded(key_sum, value_sum):
    size = key_sum.shape[0] // 2
    lower = lower_half((size, PAIR))
    straight = jnp.where(lower, key_sum[:size], value_sum[size:])
    crossed = jnp.where(lower, value_sum[:size], key_sum[size:])
    return (straight + pltpu.roll(crossed, LOWER, 1)) * jnp.where(lower, SCALE, 1.0)


def unpacked(part, rows):
    exact = part[rows:, 0:3 * rows].astype(jnp.float32)[0:2 * GROUPS]
    return exact[:, 0:rows] + exact[:, rows:2 * rows] + exact[:, 2 * rows:]


def pair_stats(stat, pair):
    first = 2 * pair
    return [stat[first:first + 1], stat[first + 1:first + 2],
            stat[GROUPS + first:GROUPS + first + 1], stat[GROUPS + first + 1:GROUPS + first + 2]]


def sequence_kernel(near_parts, order_ref, hid_ref, *rest):
    qd_refs, kv_refs, rest = rest[:TEAM], rest[TEAM:TEAM + KV_HEADS], rest[TEAM + KV_HEADS:]
    dkv_refs, keep_ref, send_ref, rest = rest[:KV_HEADS], rest[KV_HEADS], rest[KV_HEADS + 1], rest[KV_HEADS + 2:]
    near_refs, far_ref, rest = rest[:near_parts], rest[near_parts], rest[near_parts + 1:]
    q_all, go_all, stat_all, key_all, value_all, dq_all, dkv_all, sems = rest
    moves = hidden_moves(hid_ref, near_refs, far_ref, sems)
    rows = kv_refs[0].shape[0]
    head, side = head_side()
    near = [order_ref[0, 2 * jnp.bitwise_xor(head, m) + side] for m in range(KV_HEADS)]
    far = [order_ref[0, 2 * jnp.bitwise_xor(head, m) + 1 - side] for m in range(KV_HEADS)]
    for place, ref in zip(near + far, qd_refs):
        q_all[place] = ref[0:rows, 0:GROUP]
        go_all[place] = ref[0:rows, GROUP:]
        stat_all[place] = unpacked(ref, rows)
    for place, ref in zip(near, kv_refs):
        key_all[place], value_all[place] = stacked(ref[...])
    dq_all[...] = jnp.zeros_like(dq_all)
    for block in range(TEAM):
        mine = functools.reduce(jnp.logical_or, [place == block for place in near])

        @pl.when(mine)
        def _():
            count = TEAM - block
            shape = (rows, rows)
            mask = lax.broadcasted_iota(jnp.int32, shape, 0) <= lax.broadcasted_iota(jnp.int32, shape, 1)
            stats = jnp.concatenate([stat_all[i] for i in range(block, TEAM)], axis=1)
            key_sum = value_sum = None
            for pair in range(GROUPS // 2):
                columns = slice(pair * PAIR, (pair + 1) * PAIR)
                query = q_all[block:, :, columns].reshape(count * rows, PAIR)
                grad = go_all[block:, :, columns].reshape(count * rows, PAIR)
                key_part, value_part, query_part = tile(
                    key_all[block], value_all[block], query, grad, pair_stats(stats, pair), mask)
                key_sum = key_part if key_sum is None else key_sum + key_part
                value_sum = value_part if value_sum is None else value_sum + value_part
                dq_all[block:, :, columns] += query_part.reshape(count, rows, PAIR)
            dkv_all[block] = folded(key_sum, value_sum)

    for m in range(KV_HEADS):
        dkv_refs[m][...] = dkv_all[near[m]].astype(jnp.bfloat16)
        keep_ref[m] = dq_all[near[m]]
        send_ref[m] = dq_all[far[m]].astype(jnp.bfloat16)
    for copy in moves:
        copy.wait()


def teams_kernel(order_ref, qd_ref, kv_ref, dkv_ref, keep_ref, send_ref, dq_all):
    rows = kv_ref.shape[1]
    head, side = head_side()
    base = lax.axis_index("ctx") // TEAM * TEAM
    dq_all[...] = jnp.zeros_like(dq_all)

    @pl.loop(0, kv_ref.shape[0])
    def _(block):
        keys, values = stacked(kv_ref[block])
        dkv_ref[block] = jnp.zeros((rows, PAIR), jnp.float32)
        stored = block // KV_HEADS * TEAM + 2 * jnp.bitwise_xor(head, lax.rem(block, KV_HEADS)) + side
        place = order_ref[0, stored]

        @pl.loop(0, TEAM)
        def _(at):
            turned = jnp.where(at < KV_HEADS, side, 1 - side)
            own = order_ref[0, base + 2 * jnp.bitwise_xor(head, lax.rem(at, KV_HEADS)) + turned]

            @pl.when(place <= own)
            def _():
                shape = (rows, rows)
                mask = (place * rows + lax.broadcasted_iota(jnp.int32, shape, 0)
                        <= own * rows + lax.broadcasted_iota(jnp.int32, shape, 1))
                one = qd_ref.at[at]
                stats = unpacked(one, rows)
                for pair in range(GROUPS // 2):
                    first = pair * PAIR
                    key_part, value_part, query_part = tile(
                        keys, values, one[0:rows, first:first + PAIR], one[0:rows, GROUP + first:GROUP + first + PAIR],
                        pair_stats(stats, pair), mask)
                    dq_all[at, :, first:first + PAIR] += query_part
                    dkv_ref[block] += folded(key_part, value_part)

    keep_ref[...] = dq_all[0:KV_HEADS]
    send_ref[...] = dq_all[KV_HEADS:].astype(jnp.bfloat16)


def owner_kernel(*rest):
    dkv_refs, out_ref, parts = rest[:KV_HEADS], rest[KV_HEADS], rest[KV_HEADS + 1]
    head, _ = head_side()
    for m in range(KV_HEADS):
        parts[jnp.bitwise_xor(head, m)] = dkv_refs[m][...]
    keys = [parts[g, :, :HEAD_DIM] for g in range(KV_HEADS)]
    values = [parts[g, :, HEAD_DIM:] for g in range(KV_HEADS)]
    out_ref[...] = jnp.concatenate(keys + values, axis=1)


def pair_kernel(keep_ref, got_ref, *out_refs):
    for m in range(KV_HEADS):
        out_refs[m][...] = (keep_ref[m] + got_ref[m].astype(jnp.float32)).astype(out_refs[m].dtype)


def query_kernel(*rest):
    dq_refs, out_ref = rest[:KV_HEADS], rest[KV_HEADS]
    head, _ = head_side()
    for m in range(KV_HEADS):
        columns = pl.ds(pl.multiple_of(jnp.bitwise_xor(head, m) * GROUP, GROUP), GROUP)
        out_ref[:, columns] = dq_refs[m][...]


def input_kernel(fsdp, grad_ref, *rest):
    w_refs, out_ref = rest[:fsdp], rest[fsdp]
    mine = lax.axis_index("fsdp")
    span = w_refs[0].shape[0]
    for m in range(fsdp):
        start = pl.multiple_of(jnp.bitwise_xor(mine, m) * span, span)
        out_ref[:, pl.ds(start, span)] = matmul(grad_ref[...], w_refs[m][...], NT).astype(jnp.bfloat16)


def weight_sums(fsdp, refs):
    hid = jnp.concatenate([ref[...] for ref in refs[:fsdp]], axis=0)
    grad = jnp.concatenate([ref[...] for ref in refs[fsdp:2 * fsdp]], axis=0)
    return matmul(hid, grad, TN)


def weight_kernel(fsdp, *rest):
    rest[2 * fsdp][...] = weight_sums(fsdp, rest).astype(jnp.bfloat16)


def sides_kernel(fsdp, *rest):
    keep_ref, send_ref, parts = rest[2 * fsdp:]
    head, side = head_side()
    parts[...] = weight_sums(fsdp, rest).reshape(parts.shape)
    for m in range(KV_HEADS):
        to = 2 * jnp.bitwise_xor(head, m)
        keep_ref[m] = parts[to + side]
        send_ref[m] = parts[to + 1 - side].astype(jnp.bfloat16)


def own_total_kernel(own_ref, *rest):
    total = own_ref[...]
    for ref in rest[:-1]:
        total = total + ref[...].astype(jnp.float32)
    rest[-1][...] = total


def total_kernel(part_ref, out_ref):
    total = part_ref[0].astype(jnp.float32)
    for i in range(1, part_ref.shape[0]):
        total = total + part_ref[i].astype(jnp.float32)
    out_ref[...] = total


def over_fsdp(own, bits):
    got = list(own)
    while bits:
        for m in range(len(own)):
            if m & bits:
                got[m] = swapped(got[m], "fsdp", bits)
        bits //= 2
    return got


def shards(hidden, queries, attn_out, grad_out, log_sums, block_order, w_kv):
    rows, model = hidden.shape[1:]
    fsdp, devices = lax.axis_size("fsdp"), lax.axis_size("ctx")
    teams = devices // TEAM
    f32 = jnp.float32
    span = model // fsdp
    inputs = hidden[0]
    columns = 2 * KEY_WIDTH
    block, wide = (rows, PAIR), (rows, GROUP)

    def along_heads(arrays):
        return [arrays[0]] + [swapped(arrays[m], "ctx", 2 * m) for m in range(1, KV_HEADS)]

    far = fsdp // 2
    qd = call(
        pieces_kernel, [sds((rows + 16, 2 * GROUP))] * KV_HEADS,
        [pltpu.VMEM((rows, Q_HEADS * HEAD_DIM), jnp.bfloat16)] * 2
        + [pltpu.VMEM((Q_HEADS, rows), f32), pltpu.VMEM((KV_HEADS, 2 * GROUPS, rows), f32),
           pltpu.SemaphoreType.DMA((3 + 2 * KV_HEADS,))],
        (queries[0], grad_out[0], attn_out[0], log_sums[0]), hbm=4)
    qd = along_heads(qd)
    turned = [swapped(one, "ctx", 1) for one in qd[:2]]
    w_far = held(swapped(w_kv, "fsdp", far), (*qd[1:KV_HEADS - 1], *turned))
    w_parts = over_fsdp([w_kv] * far + [w_far] * (fsdp - far), far // 2)

    kv = call(
        functools.partial(project_kernel, fsdp), [sds(block)] * KV_HEADS,
        [pltpu.VMEM((KV_HEADS,) + block, jnp.bfloat16)], (inputs, *w_parts))
    own_kv, kv = kv[:1], along_heads(kv)
    late = [held(qd[2], own_kv), held(qd[3], kv[1:])]
    qd = qd[:2] + late + turned + [swapped(one, "ctx", 1) for one in late]

    half = (KV_HEADS,) + wide
    cut = [sds((rows, span))] * far + [sds((fsdp - far, rows, span))]
    cut_sems = pltpu.SemaphoreType.DMA((fsdp,))
    if teams == 1:
        outs = call(
            functools.partial(sequence_kernel, far), [sds(block)] * KV_HEADS + [sds(half, f32), sds(half)] + cut,
            [pltpu.VMEM((TEAM,) + wide, jnp.bfloat16)] * 2 + [pltpu.VMEM((TEAM, 2 * GROUPS, rows), f32)]
            + [pltpu.VMEM((TEAM, 2 * rows, PAIR), jnp.bfloat16)] * 2
            + [pltpu.VMEM((TEAM,) + wide, f32), pltpu.VMEM((TEAM,) + block, f32), cut_sems],
            (block_order, inputs, *qd, *kv), smem=1, hbm=1)
        dkv, (keep, give, *hid, hid_far) = outs[:KV_HEADS], outs[KV_HEADS:]
    else:
        alike = [[t * TEAM + i for t in range(teams)] for i in range(TEAM)]
        kv = lax.all_gather(jnp.stack(kv), "ctx", axis_index_groups=alike, axis=0, tiled=True)
        dkv, keep, give = call(
            teams_kernel, [sds((teams * KV_HEADS,) + block, f32), sds(half, f32), sds(half)],
            [pltpu.VMEM((TEAM,) + wide, f32)], (block_order, jnp.stack(qd), kv), smem=1)
        dkv = lax.psum_scatter(dkv, "ctx", axis_index_groups=alike, scatter_dimension=0, tiled=True)
        dkv = [dkv[m].astype(jnp.bfloat16) for m in range(KV_HEADS)]
        *hid, hid_far = call(hidden_kernel, cut, [cut_sems], (inputs,), hbm=1)

    hid_far = swapped(hid_far, "fsdp", far)
    hid = over_fsdp(hid + [hid_far[m] for m in range(fsdp - far)], far // 2)
    dkv = along_heads(dkv)
    give = swapped(give, "ctx", 1)
    (kv_grad,) = call(
        owner_kernel, [sds((rows, columns))], [pltpu.VMEM((KV_HEADS,) + block, jnp.bfloat16)],
        dkv, after=(give,))
    grads = over_fsdp([kv_grad] * fsdp, far)
    if teams == 1:
        share = (span // devices, columns)
        own_sums, send_sums = call(
            functools.partial(sides_kernel, fsdp), [sds((KV_HEADS,) + share, f32), sds((KV_HEADS,) + share)],
            [pltpu.VMEM((devices,) + share, f32)], (*hid, *grads))
        formed = (own_sums,)
        dq = along_heads(call(pair_kernel, [sds(wide)] * KV_HEADS, [], (keep, give), after=formed))
        sums = call(
            pair_kernel, [sds(share, f32)] + [sds(share)] * (KV_HEADS - 1), [],
            (own_sums, swapped(send_sums, "ctx", 1)), after=dq[2:3])
        (weight_grads,) = call(own_total_kernel, [sds(share, f32)], [], along_heads(sums))
    else:
        formed = call(functools.partial(weight_kernel, fsdp), [sds((span, columns))], [], (*hid, *grads))
        dq = along_heads(call(pair_kernel, [sds(wide)] * KV_HEADS, [], (keep, give), after=formed))
        sums = lax.all_to_all(formed[0].reshape(devices, span // devices, columns), "ctx", 0, 0, tiled=True)
        (weight_grads,) = call(total_kernel, [sds((span // devices, columns), f32)], [], (sums,))
    (query_grads,) = call(query_kernel, [sds((rows, Q_HEADS * HEAD_DIM))], [], dq, after=formed)
    (input_grads,) = call(
        functools.partial(input_kernel, fsdp), [sds((rows, model))], [], (kv_grad, *w_parts), after=formed)
    return query_grads[None], input_grads[None], weight_grads


def solution(mesh):
    return jax.shard_map(
        shards,
        mesh=mesh,
        in_specs=(
            P("fsdp", "ctx", None),
            P("fsdp", "ctx", None),
            P("fsdp", "ctx", None),
            P("fsdp", "ctx", None),
            P("fsdp", None, "ctx"),
            P("fsdp", None),
            P("fsdp", None),
        ),
        out_specs=(P("fsdp", "ctx", None), P("fsdp", "ctx", None), P(("fsdp", "ctx"), None)),
        check_vma=False,
    )
```

profile of v0, /device:TPU:0, one launch (start us, length us, event | category | flops | bytes accessed | tf_op | source)
XLA Modules:
  0.0 77.3 jit_solution(4069431589584383077)
XLA Ops:
  0.6 3.0 %collective-permute-start.3 = (bf16[512,512]{1,0:T(8,128)(2,1)}, bf16[512,512]{1,0:T(8,128)(2,1)S(1)}, u32[]{:S(2)}, u32[]{:S(2)}) collective-permute-start(bf16[512,512]{1,0:T(8,128)(2,1)} %refs_1_.3), channel_id=1, source_target_pairs={{0,16},{8,24},{16,0},{24,8},{1,17},{9,25},{17,1},{25,9},{2,18},{10... | collective-permute-start | bytes 1572872 | tf_op jit(solution)/shard_map/ppermute | solution.py:37
  3.7 2.2 %shard_map.94 = (bf16[144,512]{1,0:T(8,128)(2,1)}, bf16[144,512]{1,0:T(8,128)(2,1)}, bf16[144,512]{1,0:T(8,128)(2,1)}, bf16[144,512]{1,0:T(8,128)(2,1)}) custom-call(bf16[128,1024]{1,0:T(8,128)(2,1)} %bitcast.14, bf16[128,1024]{1,0:T(8,128)(2,1)} %bitcast.15, bf16[128,1024]{1,0:T(8,128)(2,1)} %bitcast.16, f32[16,128]{1,0:T(8,128)} %bitcast.18), custom_call_target="tpu_custom_call" | custom-call | tf_op jit(solution)/shard_map/pallas_call | solution.py:48
  5.9 1.6 %collective-permute-start = (bf16[144,512]{1,0:T(8,128)(2,1)}, bf16[144,512]{1,0:T(8,128)(2,1)S(1)}, u32[]{:S(2)}, u32[]{:S(2)}) collective-permute-start(bf16[144,512]{1,0:T(8,128)(2,1)} %get-tuple-element.31), channel_id=1, source_target_pairs={{0,2},{1,3},{2,0},{3,1},{4,6},{5,7},{6,4},{7,5},{8,10},{9,11},{10,... | collective-permute-start | bytes 442376 | tf_op jit(solution)/shard_map/ppermute | solution.py:37
  7.5 2.6 %collective-permute-start.1 = (bf16[144,512]{1,0:T(8,128)(2,1)}, bf16[144,512]{1,0:T(8,128)(2,1)S(1)}, u32[]{:S(2)}, u32[]{:S(2)}) collective-permute-start(bf16[144,512]{1,0:T(8,128)(2,1)} %get-tuple-element.32), channel_id=1, source_target_pairs={{0,4},{1,5},{2,6},{3,7},{4,0},{5,1},{6,2},{7,3},{8,12},{9,13},{10,... | collective-permute-start | bytes 442376 | tf_op jit(solution)/shard_map/ppermute | solution.py:37
  10.1 1.5 %collective-permute-start.4 = (bf16[144,512]{1,0:T(8,128)(2,1)}, bf16[144,512]{1,0:T(8,128)(2,1)S(1)}, u32[]{:S(2)}, u32[]{:S(2)}) collective-permute-start(bf16[144,512]{1,0:T(8,128)(2,1)} %get-tuple-element.30.refs_2_), channel_id=1, source_target_pairs={{0,1},{1,0},{2,3},{3,2},{4,5},{5,4},{6,7},{7,6},{8,9},{9,8},{10,11... | collective-permute-start | bytes 442376 | tf_op jit(solution)/shard_map/ppermute | solution.py:37
  11.6 2.2 %collective-permute-done.refs_1_.refs_3_ = bf16[144,512]{1,0:T(8,128)(2,1)S(1)} collective-permute-done((bf16[144,512]{1,0:T(8,128)(2,1)}, bf16[144,512]{1,0:T(8,128)(2,1)S(1)}, u32[]{:S(2)}, u32[]{:S(2)}) %collective-permute-start) | collective-permute-done | bytes 147488 | tf_op jit(solution)/shard_map/ppermute | solution.py:37
  13.9 1.5 %collective-permute-start.5 = (bf16[144,512]{1,0:T(8,128)(2,1)S(1)}, bf16[144,512]{1,0:T(8,128)(2,1)S(1)}, u32[]{:S(2)}, u32[]{:S(2)}) collective-permute-start(bf16[144,512]{1,0:T(8,128)(2,1)S(1)} %collective-permute-done.refs_1_.refs_3_), channel_id=1, source_target_pairs={{0,1},{1,0},{2,3},{3,2},{4,5},{5,4},{6,7},{7,6},{8,9},{9,8},{10,11... | collective-permute-start | bytes 442376 | tf_op jit(solution)/shard_map/ppermute | solution.py:37
  15.4 1.5 %collective-permute-done.1.refs_2_.refs_0_ = bf16[144,512]{1,0:T(8,128)(2,1)S(1)} collective-permute-done((bf16[144,512]{1,0:T(8,128)(2,1)}, bf16[144,512]{1,0:T(8,128)(2,1)S(1)}, u32[]{:S(2)}, u32[]{:S(2)}) %collective-permute-start.1) | collective-permute-done | bytes 147488 | tf_op jit(solution)/shard_map/ppermute | solution.py:37
  16.9 2.1 %collective-permute-done.5.refs_4_.refs_7_ = bf16[144,512]{1,0:T(8,128)(2,1)S(1)} collective-permute-done((bf16[144,512]{1,0:T(8,128)(2,1)S(1)}, bf16[144,512]{1,0:T(8,128)(2,1)S(1)}, u32[]{:S(2)}, u32[]{:S(2)}) %collective-permute-start.5) | collective-permute-done | bytes 147488 | tf_op jit(solution)/shard_map/ppermute | solution.py:37
  19.0 3.1 %collective-permute-start.7 = (bf16[144,512]{1,0:T(8,128)(2,1)S(1)}, bf16[144,512]{1,0:T(8,128)(2,1)S(1)}, u32[]{:S(2)}, u32[]{:S(2)}) collective-permute-start(bf16[144,512]{1,0:T(8,128)(2,1)S(1)} %copy-done.4), channel_id=1, source_target_pairs={{0,6},{1,7},{2,4},{3,5},{4,2},{5,3},{6,0},{7,1},{8,14},{9,15},{10,... | collective-permute-start | bytes 442376 | tf_op jit(solution)/shard_map/ppermute | solution.py:37
  22.8 2.4 %collective-permute-start.9 = (bf16[128,128]{1,0:T(8,128)(2,1)S(1)}, bf16[128,128]{1,0:T(8,128)(2,1)S(1)}, u32[]{:S(2)}, u32[]{:S(2)}) collective-permute-start(bf16[128,128]{1,0:T(8,128)(2,1)S(1)} %get-tuple-element.36), channel_id=1, source_target_pairs={{0,4},{1,5},{2,6},{3,7},{4,0},{5,1},{6,2},{7,3},{8,12},{9,13},{10,... | collective-permute-start | bytes 98312 | tf_op jit(solution)/shard_map/ppermute | solution.py:37
  25.2 2.0 %collective-permute-start.10 = (bf16[128,128]{1,0:T(8,128)(2,1)S(1)}, bf16[128,128]{1,0:T(8,128)(2,1)S(1)}, u32[]{:S(2)}, u32[]{:S(2)}) collective-permute-start(bf16[128,128]{1,0:T(8,128)(2,1)S(1)} %get-tuple-element.37), channel_id=1, source_target_pairs={{0,6},{1,7},{2,4},{3,5},{4,2},{5,3},{6,0},{7,1},{8,14},{9,15},{10,... | collective-permute-start | bytes 98312 | tf_op jit(solution)/shard_map/ppermute | solution.py:37
  27.2 1.5 %collective-permute-start.11 = (bf16[144,512]{1,0:T(8,128)(2,1)S(1)}, bf16[144,512]{1,0:T(8,128)(2,1)S(1)}, u32[]{:S(2)}, u32[]{:S(2)}) collective-permute-start(bf16[144,512]{1,0:T(8,128)(2,1)S(1)} %shard_map.97.refs_4_), channel_id=1, source_target_pairs={{0,1},{1,0},{2,3},{3,2},{4,5},{5,4},{6,7},{7,6},{8,9},{9,8},{10,11... | collective-permute-start | bytes 442376 | tf_op jit(solution)/shard_map/ppermute | solution.py:37
  28.7 1.7 %collective-permute-done.9.refs_2_.refs_12_ = bf16[128,128]{1,0:T(8,128)(2,1)S(1)} collective-permute-done((bf16[128,128]{1,0:T(8,128)(2,1)S(1)}, bf16[128,128]{1,0:T(8,128)(2,1)S(1)}, u32[]{:S(2)}, u32[]{:S(2)}) %collective-permute-start.9) | collective-permute-done | bytes 32800 | tf_op jit(solution)/shard_map/ppermute | solution.py:37
  31.0 1.5 %collective-permute-start.12 = (bf16[144,512]{1,0:T(8,128)(2,1)S(1)}, bf16[144,512]{1,0:T(8,128)(2,1)S(1)}, u32[]{:S(2)}, u32[]{:S(2)}) collective-permute-start(bf16[144,512]{1,0:T(8,128)(2,1)S(1)} %shard_map.98.refs_5_), channel_id=1, source_target_pairs={{0,1},{1,0},{2,3},{3,2},{4,5},{5,4},{6,7},{7,6},{8,9},{9,8},{10,11... | collective-permute-start | bytes 442376 | tf_op jit(solution)/shard_map/ppermute | solution.py:37
  32.5 3.6 %collective-permute-done.12.refs_9_ = bf16[144,512]{1,0:T(8,128)(2,1)S(1)} collective-permute-done((bf16[144,512]{1,0:T(8,128)(2,1)S(1)}, bf16[144,512]{1,0:T(8,128)(2,1)S(1)}, u32[]{:S(2)}, u32[]{:S(2)}) %collective-permute-start.12) | collective-permute-done | bytes 147488 | tf_op jit(solution)/shard_map/ppermute | solution.py:37
  36.1 5.5 %shard_map.99 = (bf16[128,128]{1,0:T(8,128)(2,1)S(1)}, bf16[128,128]{1,0:T(8,128)(2,1)S(1)}, bf16[128,128]{1,0:T(8,128)(2,1)S(1)}, bf16[128,128]{1,0:T(8,128)(2,...) custom-call(s32[1,8]{1,0:T(1,128)S(1)} %copy-done.3, ...), custom_call_target="tpu_custom_call" | custom-call | tf_op jit(solution)/shard_map/pallas_call | solution.py:48
  41.7 2.5 %collective-permute-start.13 = (bf16[4,128,256]{2,1,0:T(8,128)(2,1)S(1)}, bf16[4,128,256]{2,1,0:T(8,128)(2,1)S(1)}, u32[]{:S(2)}, u32[]{:S(2)}) collective-permute-start(bf16[4,128,256]{2,1,0:T(8,128)(2,1)S(1)} %get-tuple-element.39), channel_id=1, source_target_pairs={{0,1},{1,0},{2,3},{3,2},{4,5},{5,4},{6,7},{7,6},{8,9},{9,8},{10,11... | collective-permute-start | bytes 786440 | tf_op jit(solution)/shard_map/ppermute | solution.py:37
  45.1 2.2 %collective-permute-start.18 = (bf16[128,128]{1,0:T(8,128)(2,1)S(1)}, bf16[128,128]{1,0:T(8,128)(2,1)S(1)}, u32[]{:S(2)}, u32[]{:S(2)}) collective-permute-start(bf16[128,128]{1,0:T(8,128)(2,1)S(1)} %get-tuple-element.45), channel_id=1, source_target_pairs={{0,4},{1,5},{2,6},{3,7},{4,0},{5,1},{6,2},{7,3},{8,12},{9,13},{10,... | collective-permute-start | bytes 98312 | tf_op jit(solution)/shard_map/ppermute | solution.py:37
  47.2 1.3 %collective-permute-start.19 = (bf16[128,128]{1,0:T(8,128)(2,1)S(1)}, bf16[128,128]{1,0:T(8,128)(2,1)S(1)}, u32[]{:S(2)}, u32[]{:S(2)}) collective-permute-start(bf16[128,128]{1,0:T(8,128)(2,1)S(1)} %get-tuple-element.46), channel_id=1, source_target_pairs={{0,6},{1,7},{2,4},{3,5},{4,2},{5,3},{6,0},{7,1},{8,14},{9,15},{10,... | collective-permute-start | bytes 98312 | tf_op jit(solution)/shard_map/ppermute | solution.py:37
  48.6 1.3 %collective-permute-done.18.refs_2_ = bf16[128,128]{1,0:T(8,128)(2,1)S(1)} collective-permute-done((bf16[128,128]{1,0:T(8,128)(2,1)S(1)}, bf16[128,128]{1,0:T(8,128)(2,1)S(1)}, u32[]{:S(2)}, u32[]{:S(2)}) %collective-permute-start.18) | collective-permute-done | bytes 32800 | tf_op jit(solution)/shard_map/ppermute | solution.py:37
  49.9 3.1 %collective-permute-done.19.refs_3_ = bf16[128,128]{1,0:T(8,128)(2,1)S(1)} collective-permute-done((bf16[128,128]{1,0:T(8,128)(2,1)S(1)}, bf16[128,128]{1,0:T(8,128)(2,1)S(1)}, u32[]{:S(2)}, u32[]{:S(2)}) %collective-permute-start.19) | collective-permute-done | bytes 32800 | tf_op jit(solution)/shard_map/ppermute | solution.py:37
  53.1 2.1 %collective-permute-start.21 = (bf16[128,512]{1,0:T(8,128)(2,1)S(1)}, bf16[128,512]{1,0:T(8,128)(2,1)S(1)}, u32[]{:S(2)}, u32[]{:S(2)}) collective-permute-start(bf16[128,512]{1,0:T(8,128)(2,1)S(1)} %shard_map.100.refs_4_.refs_0_), channel_id=1, source_target_pairs={{0,16},{8,24},{16,0},{24,8},{1,17},{9,25},{17,1},{25,9},{2,18},{10... | collective-permute-start | bytes 393224 | tf_op jit(solution)/shard_map/ppermute | solution.py:37
  55.8 2.3 %collective-permute-done.21.refs_6_ = bf16[128,512]{1,0:T(8,128)(2,1)S(1)} collective-permute-done((bf16[128,512]{1,0:T(8,128)(2,1)S(1)}, bf16[128,512]{1,0:T(8,128)(2,1)S(1)}, u32[]{:S(2)}, u32[]{:S(2)}) %collective-permute-start.21) | collective-permute-done | bytes 131104 | tf_op jit(solution)/shard_map/ppermute | solution.py:37
  58.1 1.3 %collective-permute-done.22.refs_7_ = bf16[128,512]{1,0:T(8,128)(2,1)S(1)} collective-permute-done((bf16[128,512]{1,0:T(8,128)(2,1)S(1)}, bf16[128,512]{1,0:T(8,128)(2,1)S(1)}, u32[]{:S(2)}, u32[]{:S(2)}) %collective-permute-start.22) | collective-permute-done | bytes 131104 | tf_op jit(solution)/shard_map/ppermute | solution.py:37
  60.0 1.3 %collective-permute-start.26 = (bf16[4,64,512]{2,1,0:T(8,128)(2,1)S(1)}, bf16[4,64,512]{2,1,0:T(8,128)(2,1)S(1)}, u32[]{:S(2)}, u32[]{:S(2)}) collective-permute-start(bf16[4,64,512]{2,1,0:T(8,128)(2,1)S(1)} %get-tuple-element.52), channel_id=1, source_target_pairs={{0,1},{1,0},{2,3},{3,2},{4,5},{5,4},{6,7},{7,6},{8,9},{9,8},{10,11... | collective-permute-start | bytes 786440 | tf_op jit(solution)/shard_map/ppermute | solution.py:37
  61.5 1.9 %collective-permute-start.23 = (bf16[128,256]{1,0:T(8,128)(2,1)S(1)}, bf16[128,256]{1,0:T(8,128)(2,1)S(1)}, u32[]{:S(2)}, u32[]{:S(2)}) collective-permute-start(bf16[128,256]{1,0:T(8,128)(2,1)S(1)} %get-tuple-element.49), channel_id=1, source_target_pairs={{0,2},{1,3},{2,0},{3,1},{4,6},{5,7},{6,4},{7,5},{8,10},{9,11},{10,... | collective-permute-start | bytes 196616 | tf_op jit(solution)/shard_map/ppermute | solution.py:37
  63.4 2.5 %collective-permute-start.25 = (bf16[128,256]{1,0:T(8,128)(2,1)S(1)}, bf16[128,256]{1,0:T(8,128)(2,1)S(1)}, u32[]{:S(2)}, u32[]{:S(2)}) collective-permute-start(bf16[128,256]{1,0:T(8,128)(2,1)S(1)} %get-tuple-element.51), channel_id=1, source_target_pairs={{0,6},{1,7},{2,4},{3,5},{4,2},{5,3},{6,0},{7,1},{8,14},{9,15},{10,... | collective-permute-start | bytes 196616 | tf_op jit(solution)/shard_map/ppermute | solution.py:37
  65.9 2.0 %collective-permute-done.24.refs_2_ = bf16[128,256]{1,0:T(8,128)(2,1)S(1)} collective-permute-done((bf16[128,256]{1,0:T(8,128)(2,1)S(1)}, bf16[128,256]{1,0:T(8,128)(2,1)S(1)}, u32[]{:S(2)}, u32[]{:S(2)}) %collective-permute-start.24) | collective-permute-done | bytes 65568 | tf_op jit(solution)/shard_map/ppermute | solution.py:37
  68.5 1.9 %collective-permute-start.28 = (bf16[64,512]{1,0:T(8,128)(2,1)S(1)}, bf16[64,512]{1,0:T(8,128)(2,1)S(1)}, u32[]{:S(2)}, u32[]{:S(2)}) collective-permute-start(bf16[64,512]{1,0:T(8,128)(2,1)S(1)} %get-tuple-element.55), channel_id=1, source_target_pairs={{0,4},{1,5},{2,6},{3,7},{4,0},{5,1},{6,2},{7,3},{8,12},{9,13},{10,... | collective-permute-start | bytes 196616 | tf_op jit(solution)/shard_map/ppermute | solution.py:37
  70.4 2.5 %collective-permute-start.29 = (bf16[64,512]{1,0:T(8,128)(2,1)S(1)}, bf16[64,512]{1,0:T(8,128)(2,1)S(1)}, u32[]{:S(2)}, u32[]{:S(2)}) collective-permute-start(bf16[64,512]{1,0:T(8,128)(2,1)S(1)} %get-tuple-element.56), channel_id=1, source_target_pairs={{0,6},{1,7},{2,4},{3,5},{4,2},{5,3},{6,0},{7,1},{8,14},{9,15},{10,... | collective-permute-start | bytes 196616 | tf_op jit(solution)/shard_map/ppermute | solution.py:37
  72.9 1.6 %shard_map.104 = bf16[128,2048]{1,0:T(8,128)(2,1)} custom-call(bf16[128,512]{1,0:T(8,128)(2,1)S(1)} %shard_map.100.refs_4_.refs_0_, bf16[512,512]{1,0:T(8,128)(2,1)S(1)} %copy-done, bf16[512,512]{1,0:T(8,128)(2,1)S(1)} %collective-permute-done.2.refs_2_, bf16[512,512]{1,0:T(8,128)(2,1)S(1)} %shard_map.95.refs_3_, ...), custom_call_target="tpu_custom_call" | custom-call | tf_op jit(solution)/shard_map/pallas_call | solution.py:48
  (52 shorter events, 7.0 us)
Async XLA Ops:
  0.6 14.7 %copy-start = (bf16[512,512]{1,0:T(8,128)(2,1)S(1)}, bf16[512,512]{1,0:T(8,128)(2,1)}, u32[]{:S(2)}) copy-start(bf16[512,512]{1,0:T(8,128)(2,1)} %refs_1_.3) | copy-start | bytes 1572868
  0.6 18.4 %collective-permute-start.3 = (bf16[512,512]{1,0:T(8,128)(2,1)}, bf16[512,512]{1,0:T(8,128)(2,1)S(1)}, u32[]{:S(2)}, u32[]{:S(2)}) collective-permute-start(bf16[512,512]{1,0:T(8,128)(2,1)} %refs_1_.3), channel_id=1, source_target_pairs={{0,16},{8,24},{16,0},{24,8},{1,17},{9,25},{17,1},{25,9},{2,18},{10... | collective-permute-start | bytes 1572872 | tf_op jit(solution)/shard_map/ppermute | solution.py:37
  5.9 8.0 %collective-permute-start = (bf16[144,512]{1,0:T(8,128)(2,1)}, bf16[144,512]{1,0:T(8,128)(2,1)S(1)}, u32[]{:S(2)}, u32[]{:S(2)}) collective-permute-start(bf16[144,512]{1,0:T(8,128)(2,1)} %get-tuple-element.31), channel_id=1, source_target_pairs={{0,2},{1,3},{2,0},{3,1},{4,6},{5,7},{6,4},{7,5},{8,10},{9,11},{10,... | collective-permute-start | bytes 442376 | tf_op jit(solution)/shard_map/ppermute | solution.py:37
  7.5 9.3 %collective-permute-start.1 = (bf16[144,512]{1,0:T(8,128)(2,1)}, bf16[144,512]{1,0:T(8,128)(2,1)S(1)}, u32[]{:S(2)}, u32[]{:S(2)}) collective-permute-start(bf16[144,512]{1,0:T(8,128)(2,1)} %get-tuple-element.32), channel_id=1, source_target_pairs={{0,4},{1,5},{2,6},{3,7},{4,0},{5,1},{6,2},{7,3},{8,12},{9,13},{10,... | collective-permute-start | bytes 442376 | tf_op jit(solution)/shard_map/ppermute | solution.py:37
  10.1 12.0 %copy-start.1 = (bf16[1,128,2048]{2,1,0:T(8,128)(2,1)S(1)}, bf16[1,128,2048]{2,1,0:T(8,128)(2,1)}, u32[]{:S(2)}) copy-start(bf16[1,128,2048]{2,1,0:T(8,128)(2,1)} %param.7) | copy-start | bytes 1572868
  10.1 6.8 %collective-permute-start.4 = (bf16[144,512]{1,0:T(8,128)(2,1)}, bf16[144,512]{1,0:T(8,128)(2,1)S(1)}, u32[]{:S(2)}, u32[]{:S(2)}) collective-permute-start(bf16[144,512]{1,0:T(8,128)(2,1)} %get-tuple-element.30.refs_2_), channel_id=1, source_target_pairs={{0,1},{1,0},{2,3},{3,2},{4,5},{5,4},{6,7},{7,6},{8,9},{9,8},{10,11... | collective-permute-start | bytes 442376 | tf_op jit(solution)/shard_map/ppermute | solution.py:37
  13.9 5.1 %collective-permute-start.5 = (bf16[144,512]{1,0:T(8,128)(2,1)S(1)}, bf16[144,512]{1,0:T(8,128)(2,1)S(1)}, u32[]{:S(2)}, u32[]{:S(2)}) collective-permute-start(bf16[144,512]{1,0:T(8,128)(2,1)S(1)} %collective-permute-done.refs_1_.refs_3_), channel_id=1, source_target_pairs={{0,1},{1,0},{2,3},{3,2},{4,5},{5,4},{6,7},{7,6},{8,9},{9,8},{10,11... | collective-permute-start | bytes 442376 | tf_op jit(solution)/shard_map/ppermute | solution.py:37
  15.4 6.8 %collective-permute-start.2 = (bf16[512,512]{1,0:T(8,128)(2,1)S(1)}, bf16[512,512]{1,0:T(8,128)(2,1)S(1)}, u32[]{:S(2)}, u32[]{:S(2)}) collective-permute-start(bf16[512,512]{1,0:T(8,128)(2,1)S(1)} %copy-done), channel_id=1, source_target_pairs={{0,8},{8,0},{16,24},{24,16},{1,9},{9,1},{17,25},{25,17},{2,10},{10... | collective-permute-start | bytes 1572872 | tf_op jit(solution)/shard_map/ppermute | solution.py:37
  19.0 3.1 %collective-permute-start.6 = (bf16[512,512]{1,0:T(8,128)(2,1)S(1)}, bf16[512,512]{1,0:T(8,128)(2,1)S(1)}, u32[]{:S(2)}, u32[]{:S(2)}) collective-permute-start(bf16[512,512]{1,0:T(8,128)(2,1)S(1)} %shard_map.95.refs_3_), channel_id=1, source_target_pairs={{0,8},{8,0},{16,24},{24,16},{1,9},{9,1},{17,25},{25,17},{2,10},{10... | collective-permute-start | bytes 1572872 | tf_op jit(solution)/shard_map/ppermute | solution.py:37
  19.0 9.6 %collective-permute-start.7 = (bf16[144,512]{1,0:T(8,128)(2,1)S(1)}, bf16[144,512]{1,0:T(8,128)(2,1)S(1)}, u32[]{:S(2)}, u32[]{:S(2)}) collective-permute-start(bf16[144,512]{1,0:T(8,128)(2,1)S(1)} %copy-done.4), channel_id=1, source_target_pairs={{0,6},{1,7},{2,4},{3,5},{4,2},{5,3},{6,0},{7,1},{8,14},{9,15},{10,... | collective-permute-start | bytes 442376 | tf_op jit(solution)/shard_map/ppermute | solution.py:37
  22.7 6.0 %collective-permute-start.8 = (bf16[128,128]{1,0:T(8,128)(2,1)S(1)}, bf16[128,128]{1,0:T(8,128)(2,1)S(1)}, u32[]{:S(2)}, u32[]{:S(2)}) collective-permute-start(bf16[128,128]{1,0:T(8,128)(2,1)S(1)} %get-tuple-element.35), channel_id=1, source_target_pairs={{0,2},{1,3},{2,0},{3,1},{4,6},{5,7},{6,4},{7,5},{8,10},{9,11},{10,... | collective-permute-start | bytes 98312 | tf_op jit(solution)/shard_map/ppermute | solution.py:37
  22.8 7.6 %collective-permute-start.9 = (bf16[128,128]{1,0:T(8,128)(2,1)S(1)}, bf16[128,128]{1,0:T(8,128)(2,1)S(1)}, u32[]{:S(2)}, u32[]{:S(2)}) collective-permute-start(bf16[128,128]{1,0:T(8,128)(2,1)S(1)} %get-tuple-element.36), channel_id=1, source_target_pairs={{0,4},{1,5},{2,6},{3,7},{4,0},{5,1},{6,2},{7,3},{8,12},{9,13},{10,... | collective-permute-start | bytes 98312 | tf_op jit(solution)/shard_map/ppermute | solution.py:37
  25.2 5.8 %collective-permute-start.10 = (bf16[128,128]{1,0:T(8,128)(2,1)S(1)}, bf16[128,128]{1,0:T(8,128)(2,1)S(1)}, u32[]{:S(2)}, u32[]{:S(2)}) collective-permute-start(bf16[128,128]{1,0:T(8,128)(2,1)S(1)} %get-tuple-element.37), channel_id=1, source_target_pairs={{0,6},{1,7},{2,4},{3,5},{4,2},{5,3},{6,0},{7,1},{8,14},{9,15},{10,... | collective-permute-start | bytes 98312 | tf_op jit(solution)/shard_map/ppermute | solution.py:37
  27.2 5.3 %collective-permute-start.11 = (bf16[144,512]{1,0:T(8,128)(2,1)S(1)}, bf16[144,512]{1,0:T(8,128)(2,1)S(1)}, u32[]{:S(2)}, u32[]{:S(2)}) collective-permute-start(bf16[144,512]{1,0:T(8,128)(2,1)S(1)} %shard_map.97.refs_4_), channel_id=1, source_target_pairs={{0,1},{1,0},{2,3},{3,2},{4,5},{5,4},{6,7},{7,6},{8,9},{9,8},{10,11... | collective-permute-start | bytes 442376 | tf_op jit(solution)/shard_map/ppermute | solution.py:37
  31.0 5.1 %collective-permute-start.12 = (bf16[144,512]{1,0:T(8,128)(2,1)S(1)}, bf16[144,512]{1,0:T(8,128)(2,1)S(1)}, u32[]{:S(2)}, u32[]{:S(2)}) collective-permute-start(bf16[144,512]{1,0:T(8,128)(2,1)S(1)} %shard_map.98.refs_5_), channel_id=1, source_target_pairs={{0,1},{1,0},{2,3},{3,2},{4,5},{5,4},{6,7},{7,6},{8,9},{9,8},{10,11... | collective-permute-start | bytes 442376 | tf_op jit(solution)/shard_map/ppermute | solution.py:37
  41.7 11.3 %collective-permute-start.13 = (bf16[4,128,256]{2,1,0:T(8,128)(2,1)S(1)}, bf16[4,128,256]{2,1,0:T(8,128)(2,1)S(1)}, u32[]{:S(2)}, u32[]{:S(2)}) collective-permute-start(bf16[4,128,256]{2,1,0:T(8,128)(2,1)S(1)} %get-tuple-element.39), channel_id=1, source_target_pairs={{0,1},{1,0},{2,3},{3,2},{4,5},{5,4},{6,7},{7,6},{8,9},{9,8},{10,11... | collective-permute-start | bytes 786440 | tf_op jit(solution)/shard_map/ppermute | solution.py:37
  44.2 11.0 %collective-permute-start.15 = (bf16[2,128,512]{2,1,0:T(8,128)(2,1)S(1)}, bf16[2,128,512]{2,1,0:T(8,128)(2,1)S(1)}, u32[]{:S(2)}, u32[]{:S(2)}) collective-permute-start(bf16[2,128,512]{2,1,0:T(8,128)(2,1)S(1)} %get-tuple-element.42), channel_id=1, source_target_pairs={{0,16},{8,24},{16,0},{24,8},{1,17},{9,25},{17,1},{25,9},{2,18},{10... | collective-permute-start | bytes 786440 | tf_op jit(solution)/shard_map/ppermute | solution.py:37
  44.2 4.4 %collective-permute-start.17 = (bf16[128,128]{1,0:T(8,128)(2,1)S(1)}, bf16[128,128]{1,0:T(8,128)(2,1)S(1)}, u32[]{:S(2)}, u32[]{:S(2)}) collective-permute-start(bf16[128,128]{1,0:T(8,128)(2,1)S(1)} %get-tuple-element.44), channel_id=1, source_target_pairs={{0,2},{1,3},{2,0},{3,1},{4,6},{5,7},{6,4},{7,5},{8,10},{9,11},{10,... | collective-permute-start | bytes 98312 | tf_op jit(solution)/shard_map/ppermute | solution.py:37
  45.1 4.8 %collective-permute-start.18 = (bf16[128,128]{1,0:T(8,128)(2,1)S(1)}, bf16[128,128]{1,0:T(8,128)(2,1)S(1)}, u32[]{:S(2)}, u32[]{:S(2)}) collective-permute-start(bf16[128,128]{1,0:T(8,128)(2,1)S(1)} %get-tuple-element.45), channel_id=1, source_target_pairs={{0,4},{1,5},{2,6},{3,7},{4,0},{5,1},{6,2},{7,3},{8,12},{9,13},{10,... | collective-permute-start | bytes 98312 | tf_op jit(solution)/shard_map/ppermute | solution.py:37
  47.2 5.7 %collective-permute-start.19 = (bf16[128,128]{1,0:T(8,128)(2,1)S(1)}, bf16[128,128]{1,0:T(8,128)(2,1)S(1)}, u32[]{:S(2)}, u32[]{:S(2)}) collective-permute-start(bf16[128,128]{1,0:T(8,128)(2,1)S(1)} %get-tuple-element.46), channel_id=1, source_target_pairs={{0,6},{1,7},{2,4},{3,5},{4,2},{5,3},{6,0},{7,1},{8,14},{9,15},{10,... | collective-permute-start | bytes 98312 | tf_op jit(solution)/shard_map/ppermute | solution.py:37
  48.6 9.6 %collective-permute-start.14 = (bf16[128,512]{1,0:T(8,128)(2,1)S(1)}, bf16[128,512]{1,0:T(8,128)(2,1)S(1)}, u32[]{:S(2)}, u32[]{:S(2)}) collective-permute-start(bf16[128,512]{1,0:T(8,128)(2,1)S(1)} %get-tuple-element.41), channel_id=1, source_target_pairs={{0,8},{8,0},{16,24},{24,16},{1,9},{9,1},{17,25},{25,17},{2,10},{10... | collective-permute-start | bytes 393224 | tf_op jit(solution)/shard_map/ppermute | solution.py:37
  53.1 5.0 %collective-permute-start.21 = (bf16[128,512]{1,0:T(8,128)(2,1)S(1)}, bf16[128,512]{1,0:T(8,128)(2,1)S(1)}, u32[]{:S(2)}, u32[]{:S(2)}) collective-permute-start(bf16[128,512]{1,0:T(8,128)(2,1)S(1)} %shard_map.100.refs_4_.refs_0_), channel_id=1, source_target_pairs={{0,16},{8,24},{16,0},{24,8},{1,17},{9,25},{17,1},{25,9},{2,18},{10... | collective-permute-start | bytes 393224 | tf_op jit(solution)/shard_map/ppermute | solution.py:37
  55.2 3.0 %collective-permute-start.20 = (bf16[128,512]{1,0:T(8,128)(2,1)S(1)}, bf16[128,512]{1,0:T(8,128)(2,1)S(1)}, u32[]{:S(2)}, u32[]{:S(2)}) collective-permute-start(bf16[128,512]{1,0:T(8,128)(2,1)S(1)} %shard_map.100.refs_4_.refs_0_), channel_id=1, source_target_pairs={{0,8},{8,0},{16,24},{24,16},{1,9},{9,1},{17,25},{25,17},{2,10},{10... | collective-permute-start | bytes 393224 | tf_op jit(solution)/shard_map/ppermute | solution.py:37
  55.2 2.9 %collective-permute-start.16 = (bf16[128,512]{1,0:T(8,128)(2,1)S(1)}, bf16[128,512]{1,0:T(8,128)(2,1)S(1)}, u32[]{:S(2)}, u32[]{:S(2)}) collective-permute-start(bf16[128,512]{1,0:T(8,128)(2,1)S(1)} %get-tuple-element.57), channel_id=1, source_target_pairs={{0,8},{8,0},{16,24},{24,16},{1,9},{9,1},{17,25},{25,17},{2,10},{10... | collective-permute-start | bytes 393224 | tf_op jit(solution)/shard_map/ppermute | solution.py:37
  58.1 1.3 %collective-permute-start.22 = (bf16[128,512]{1,0:T(8,128)(2,1)S(1)}, bf16[128,512]{1,0:T(8,128)(2,1)S(1)}, u32[]{:S(2)}, u32[]{:S(2)}) collective-permute-start(bf16[128,512]{1,0:T(8,128)(2,1)S(1)} %collective-permute-done.21.refs_6_), channel_id=1, source_target_pairs={{0,8},{8,0},{16,24},{24,16},{1,9},{9,1},{17,25},{25,17},{2,10},{10... | collective-permute-start | bytes 393224 | tf_op jit(solution)/shard_map/ppermute | solution.py:37
  60.0 8.4 %collective-permute-start.26 = (bf16[4,64,512]{2,1,0:T(8,128)(2,1)S(1)}, bf16[4,64,512]{2,1,0:T(8,128)(2,1)S(1)}, u32[]{:S(2)}, u32[]{:S(2)}) collective-permute-start(bf16[4,64,512]{2,1,0:T(8,128)(2,1)S(1)} %get-tuple-element.52), channel_id=1, source_target_pairs={{0,1},{1,0},{2,3},{3,2},{4,5},{5,4},{6,7},{7,6},{8,9},{9,8},{10,11... | collective-permute-start | bytes 786440 | tf_op jit(solution)/shard_map/ppermute | solution.py:37
  61.4 6.4 %collective-permute-start.24 = (bf16[128,256]{1,0:T(8,128)(2,1)S(1)}, bf16[128,256]{1,0:T(8,128)(2,1)S(1)}, u32[]{:S(2)}, u32[]{:S(2)}) collective-permute-start(bf16[128,256]{1,0:T(8,128)(2,1)S(1)} %get-tuple-element.50), channel_id=1, source_target_pairs={{0,4},{1,5},{2,6},{3,7},{4,0},{5,1},{6,2},{7,3},{8,12},{9,13},{10,... | collective-permute-start | bytes 196616 | tf_op jit(solution)/shard_map/ppermute | solution.py:37
  61.5 13.0 %collective-permute-start.23 = (bf16[128,256]{1,0:T(8,128)(2,1)S(1)}, bf16[128,256]{1,0:T(8,128)(2,1)S(1)}, u32[]{:S(2)}, u32[]{:S(2)}) collective-permute-start(bf16[128,256]{1,0:T(8,128)(2,1)S(1)} %get-tuple-element.49), channel_id=1, source_target_pairs={{0,2},{1,3},{2,0},{3,1},{4,6},{5,7},{6,4},{7,5},{8,10},{9,11},{10,... | collective-permute-start | bytes 196616 | tf_op jit(solution)/shard_map/ppermute | solution.py:37
  63.4 11.2 %collective-permute-start.25 = (bf16[128,256]{1,0:T(8,128)(2,1)S(1)}, bf16[128,256]{1,0:T(8,128)(2,1)S(1)}, u32[]{:S(2)}, u32[]{:S(2)}) collective-permute-start(bf16[128,256]{1,0:T(8,128)(2,1)S(1)} %get-tuple-element.51), channel_id=1, source_target_pairs={{0,6},{1,7},{2,4},{3,5},{4,2},{5,3},{6,0},{7,1},{8,14},{9,15},{10,... | collective-permute-start | bytes 196616 | tf_op jit(solution)/shard_map/ppermute | solution.py:37
  68.5 6.8 %collective-permute-start.27 = (bf16[64,512]{1,0:T(8,128)(2,1)S(1)}, bf16[64,512]{1,0:T(8,128)(2,1)S(1)}, u32[]{:S(2)}, u32[]{:S(2)}) collective-permute-start(bf16[64,512]{1,0:T(8,128)(2,1)S(1)} %get-tuple-element.54), channel_id=1, source_target_pairs={{0,2},{1,3},{2,0},{3,1},{4,6},{5,7},{6,4},{7,5},{8,10},{9,11},{10,... | collective-permute-start | bytes 196616 | tf_op jit(solution)/shard_map/ppermute | solution.py:37
  68.5 7.1 %collective-permute-start.28 = (bf16[64,512]{1,0:T(8,128)(2,1)S(1)}, bf16[64,512]{1,0:T(8,128)(2,1)S(1)}, u32[]{:S(2)}, u32[]{:S(2)}) collective-permute-start(bf16[64,512]{1,0:T(8,128)(2,1)S(1)} %get-tuple-element.55), channel_id=1, source_target_pairs={{0,4},{1,5},{2,6},{3,7},{4,0},{5,1},{6,2},{7,3},{8,12},{9,13},{10,... | collective-permute-start | bytes 196616 | tf_op jit(solution)/shard_map/ppermute | solution.py:37
  70.4 6.2 %collective-permute-start.29 = (bf16[64,512]{1,0:T(8,128)(2,1)S(1)}, bf16[64,512]{1,0:T(8,128)(2,1)S(1)}, u32[]{:S(2)}, u32[]{:S(2)}) collective-permute-start(bf16[64,512]{1,0:T(8,128)(2,1)S(1)} %get-tuple-element.56), channel_id=1, source_target_pairs={{0,6},{1,7},{2,4},{3,5},{4,2},{5,3},{6,0},{7,1},{8,14},{9,15},{10,... | collective-permute-start | bytes 196616 | tf_op jit(solution)/shard_map/ppermute | solution.py:37
  (3 other events, 26.8 us)
where the time goes:
time: 77.3 us
  starting transfers between devices  40.6 us (53%)
  waiting for transfers between devices  23.8 us (31%)
  Pallas kernels  12.1 us (16%)
    ppermute x30, starting transfers between devices, swapped(): return lax.ppermute(array, axis, [(i, i ^ bits) for i in range(size)])  40.6 us
    ppermute x30, waiting for transfers between devices, swapped(): return lax.ppermute(array, axis, [(i, i ^ bits) for i in range(size)])  23.8 us
    pallas_call x10, Pallas kernels, call(): pl.pallas_call(body, out_shape=out_shape, in_specs=specs, out_specs=[VMEM...  12.1 us
  transfers between devices with their start and end apart: 30, of which 14 were waited for; matrix products, arithmetic and copies ran while one was open for 0% of the time, Pallas kernels for 7%

commit v1 on v0

--- a/solution.py
+++ b/solution.py
@@ -14,6 +14,7 @@
 KEY_WIDTH = KV_HEADS * HEAD_DIM
 PAIR = 2 * HEAD_DIM
 TEAM = 2 * KV_HEADS
+PAIRS = GROUPS // 2
 GROUP = GROUPS * HEAD_DIM
 SCALE = HEAD_DIM ** -0.5
 LOWER = HEAD_DIM
@@ -172,19 +173,25 @@
 
 
 def tile(keys, values, query, grad, stats, mask):
-    size = keys.shape[0] // 2
-    lse, delta = stats[:2], stats[2:]
+    size, edge = keys.shape[0] // 2, mask.shape[1]
+    pairs = len(stats)
+    width = query.shape[0] // pairs
     scores = matmul(keys, query, NT)
     prob_grad = matmul(values, grad, NT)
     lows, grads = [], []
     for head in range(2):
         part = slice(head * size, (head + 1) * size)
-        probs = jnp.exp(scores[part] - lse[head])
-        edge = mask.shape[1]
-        seen = jnp.where(mask, probs[:, :edge], 0.0)
-        probs = seen if edge == probs.shape[1] else jnp.concatenate([seen, probs[:, edge:]], axis=1)
+        lse = jnp.concatenate([lines[head] for lines in stats], axis=1)
+        delta = jnp.concatenate([lines[2 + head] for lines in stats], axis=1)
+        probs = jnp.exp(scores[part] - lse)
+        pieces = []
+        for first in range(0, pairs * width, width):
+            pieces.append(jnp.where(mask, probs[:, first:first + edge], 0.0))
+            if edge < width:
+                pieces.append(probs[:, first + edge:first + width])
+        probs = jnp.concatenate(pieces, axis=1)
         lows.append(probs.astype(jnp.bfloat16))
-        grads.append((probs * (prob_grad[part] - delta[head])).astype(jnp.bfloat16))
+        grads.append((probs * (prob_grad[part] - delta)).astype(jnp.bfloat16))
     low, score_grad = jnp.concatenate(lows, axis=0), jnp.concatenate(grads, axis=0)
     return matmul(score_grad, query), matmul(low, grad), matmul(score_grad, keys, TN)
 
@@ -219,8 +226,9 @@
     near = [order_ref[0, 2 * jnp.bitwise_xor(head, m) + side] for m in range(KV_HEADS)]
     far = [order_ref[0, 2 * jnp.bitwise_xor(head, m) + 1 - side] for m in range(KV_HEADS)]
     for place, ref in zip(near + far, qd_refs):
-        q_all[place] = ref[0:rows, 0:GROUP]
-        go_all[place] = ref[0:rows, GROUP:]
+        for pair in range(PAIRS):
+            q_all[pair, place] = ref[0:rows, pair * PAIR:(pair + 1) * PAIR]
+            go_all[pair, place] = ref[0:rows, GROUP + pair * PAIR:GROUP + (pair + 1) * PAIR]
         stat_all[place] = unpacked(ref, rows)
     for place, ref in zip(near, kv_refs):
         key_all[place], value_all[place] = stacked(ref[...])
@@ -234,22 +242,19 @@
             shape = (rows, rows)
             mask = lax.broadcasted_iota(jnp.int32, shape, 0) <= lax.broadcasted_iota(jnp.int32, shape, 1)
             stats = jnp.concatenate([stat_all[i] for i in range(block, TEAM)], axis=1)
-            key_sum = value_sum = None
-            for pair in range(GROUPS // 2):
-                columns = slice(pair * PAIR, (pair + 1) * PAIR)
-                query = q_all[block:, :, columns].reshape(count * rows, PAIR)
-                grad = go_all[block:, :, columns].reshape(count * rows, PAIR)
-                key_part, value_part, query_part = tile(
-                    key_all[block], value_all[block], query, grad, pair_stats(stats, pair), mask)
-                key_sum = key_part if key_sum is None else key_sum + key_part
-                value_sum = value_part if value_sum is None else value_sum + value_part
-                dq_all[block:, :, columns] += query_part.reshape(count, rows, PAIR)
+            query = q_all[:, block:].reshape(PAIRS * count * rows, PAIR)
+            grad = go_all[:, block:].reshape(PAIRS * count * rows, PAIR)
+            key_sum, value_sum, query_part = tile(
+                key_all[block], value_all[block], query, grad, [pair_stats(stats, pair) for pair in range(PAIRS)], mask)
+            dq_all[:, block:] += query_part.reshape(PAIRS, count, rows, PAIR)
             dkv_all[block] = folded(key_sum, value_sum)
 
     for m in range(KV_HEADS):
         dkv_refs[m][...] = dkv_all[near[m]].astype(jnp.bfloat16)
-        keep_ref[m] = dq_all[near[m]]
-        send_ref[m] = dq_all[far[m]].astype(jnp.bfloat16)
+        for pair in range(PAIRS):
+            columns = slice(pair * PAIR, (pair + 1) * PAIR)
+            keep_ref[m, :, columns] = dq_all[pair, near[m]]
+            send_ref[m, :, columns] = dq_all[pair, far[m]].astype(jnp.bfloat16)
     for copy in moves:
         copy.wait()
 
@@ -279,11 +284,11 @@
                         <= own * rows + lax.broadcasted_iota(jnp.int32, shape, 1))
                 one = qd_ref.at[at]
                 stats = unpacked(one, rows)
-                for pair in range(GROUPS // 2):
+                for pair in range(PAIRS):
                     first = pair * PAIR
                     key_part, value_part, query_part = tile(
                         keys, values, one[0:rows, first:first + PAIR], one[0:rows, GROUP + first:GROUP + first + PAIR],
-                        pair_stats(stats, pair), mask)
+                        [pair_stats(stats, pair)], mask)
                     dq_all[at, :, first:first + PAIR] += query_part
                     dkv_ref[block] += folded(key_part, value_part)
 
@@ -389,15 +394,14 @@
         (queries[0], grad_out[0], attn_out[0], log_sums[0]), hbm=4)
     qd = along_heads(qd)
     turned = [swapped(one, "ctx", 1) for one in qd[:2]]
-    w_far = held(swapped(w_kv, "fsdp", far), (*qd[1:KV_HEADS - 1], *turned))
+    w_far = held(swapped(w_kv, "fsdp", far), (*qd[1:], *turned))
     w_parts = over_fsdp([w_kv] * far + [w_far] * (fsdp - far), far // 2)
 
     kv = call(
         functools.partial(project_kernel, fsdp), [sds(block)] * KV_HEADS,
         [pltpu.VMEM((KV_HEADS,) + block, jnp.bfloat16)], (inputs, *w_parts))
-    own_kv, kv = kv[:1], along_heads(kv)
-    late = [held(qd[2], own_kv), held(qd[3], kv[1:])]
-    qd = qd[:2] + late + turned + [swapped(one, "ctx", 1) for one in late]
+    kv = along_heads(kv)
+    qd = qd + turned + [swapped(one, "ctx", 1) for one in qd[2:]]
 
     half = (KV_HEADS,) + wide
     cut = [sds((rows, span))] * far + [sds((fsdp - far, rows, span))]
@@ -405,9 +409,9 @@
     if teams == 1:
         outs = call(
             functools.partial(sequence_kernel, far), [sds(block)] * KV_HEADS + [sds(half, f32), sds(half)] + cut,
-            [pltpu.VMEM((TEAM,) + wide, jnp.bfloat16)] * 2 + [pltpu.VMEM((TEAM, 2 * GROUPS, rows), f32)]
+            [pltpu.VMEM((PAIRS, TEAM) + block, jnp.bfloat16)] * 2 + [pltpu.VMEM((TEAM, 2 * GROUPS, rows), f32)]
             + [pltpu.VMEM((TEAM, 2 * rows, PAIR), jnp.bfloat16)] * 2
-            + [pltpu.VMEM((TEAM,) + wide, f32), pltpu.VMEM((TEAM,) + block, f32), cut_sems],
+            + [pltpu.VMEM((PAIRS, TEAM) + block, f32), pltpu.VMEM((TEAM,) + block, f32), cut_sems],
             (block_order, inputs, *qd, *kv), smem=1, hbm=1)
         dkv, (keep, give, *hid, hid_far) = outs[:KV_HEADS], outs[KV_HEADS:]
     else:

time: 77.3 us -> 74.1 us (0.959)
  starting transfers between devices: 40.6 us -> 34.6 us
  waiting for transfers between devices: 23.8 us -> 25.7 us
  Pallas kernels: 12.1 us -> 13.2 us
    ppermute x30, starting transfers between devices: 40.6 us -> 34.6 us  [swapped(): return lax.ppermute(array, axis, [(i, i ^ bits) for i in range(size)])]
    ppermute x30, waiting for transfers between devices: 23.8 us -> 25.7 us  [swapped(): return lax.ppermute(array, axis, [(i, i ^ bits) for i in range(size)])]
    pallas_call x10, Pallas kernels: 12.1 us -> 13.2 us  [call(): pl.pallas_call(body, out_shape=out_shape, in_specs=specs, out_specs=[VMEM...]
  transfers between devices with their start and end apart: 30 -> 30, of which waited for: 14 -> 13; matrix products, arithmetic and copies ran while one was open for 0% -> 0% of each run, Pallas kernels for 7% -> 7%
where the time goes in v1:
time: 74.1 us; the launch traced here: 74.3 us
  starting transfers between devices  34.6 us (47%)
  waiting for transfers between devices  25.7 us (35%)
  Pallas kernels  13.2 us (18%)
  between operations  0.79 us (1%)
    ppermute x30, starting transfers between devices, swapped(): return lax.ppermute(array, axis, [(i, i ^ bits) for i in range(size)])  34.6 us
    ppermute x30, waiting for transfers between devices, swapped(): return lax.ppermute(array, axis, [(i, i ^ bits) for i in range(size)])  25.7 us
    pallas_call x10, Pallas kernels, call(): pl.pallas_call(body, out_shape=out_shape, in_specs=specs, out_specs=[VMEM...  13.2 us
  transfers between devices with their start and end apart: 30, of which 13 were waited for; matrix products, arithmetic and copies ran while one was open for 0% of the time, Pallas kernels for 7%

profile of v1, /device:TPU:0, one launch (start us, length us, event | category | flops | bytes accessed | tf_op | source)
XLA Modules:
  0.0 74.3 jit_solution(12787845134144006647)
XLA Ops:
  0.6 3.0 %collective-permute-start.8 = (bf16[512,512]{1,0:T(8,128)(2,1)}, bf16[512,512]{1,0:T(8,128)(2,1)S(1)}, u32[]{:S(2)}, u32[]{:S(2)}) collective-permute-start(bf16[512,512]{1,0:T(8,128)(2,1)} %refs_1_.3), channel_id=1, source_target_pairs={{0,16},{8,24},{16,0},{24,8},{1,17},{9,25},{17,1},{25,9},{2,18},{10... | collective-permute-start | bytes 1572872 | tf_op jit(solution)/shard_map/ppermute | solution.py:38
  3.7 2.2 %shard_map.94 = (bf16[144,512]{1,0:T(8,128)(2,1)}, bf16[144,512]{1,0:T(8,128)(2,1)}, bf16[144,512]{1,0:T(8,128)(2,1)}, bf16[144,512]{1,0:T(8,128)(2,1)}) custom-call(bf16[128,1024]{1,0:T(8,128)(2,1)} %bitcast.14, bf16[128,1024]{1,0:T(8,128)(2,1)} %bitcast.15, bf16[128,1024]{1,0:T(8,128)(2,1)} %bitcast.16, f32[16,128]{1,0:T(8,128)} %bitcast.18), custom_call_target="tpu_custom_call" | custom-call | tf_op jit(solution)/shard_map/pallas_call | solution.py:49
  5.9 1.6 %collective-permute-start = (bf16[144,512]{1,0:T(8,128)(2,1)}, bf16[144,512]{1,0:T(8,128)(2,1)S(1)}, u32[]{:S(2)}, u32[]{:S(2)}) collective-permute-start(bf16[144,512]{1,0:T(8,128)(2,1)} %get-tuple-element.31), channel_id=1, source_target_pairs={{0,2},{1,3},{2,0},{3,1},{4,6},{5,7},{6,4},{7,5},{8,10},{9,11},{10,... | collective-permute-start | bytes 442376 | tf_op jit(solution)/shard_map/ppermute | solution.py:38
  7.5 2.6 %collective-permute-start.1 = (bf16[144,512]{1,0:T(8,128)(2,1)}, bf16[144,512]{1,0:T(8,128)(2,1)S(1)}, u32[]{:S(2)}, u32[]{:S(2)}) collective-permute-start(bf16[144,512]{1,0:T(8,128)(2,1)} %get-tuple-element.32), channel_id=1, source_target_pairs={{0,4},{1,5},{2,6},{3,7},{4,0},{5,1},{6,2},{7,3},{8,12},{9,13},{10,... | collective-permute-start | bytes 442376 | tf_op jit(solution)/shard_map/ppermute | solution.py:38
  10.4 1.5 %collective-permute-start.3 = (bf16[144,512]{1,0:T(8,128)(2,1)}, bf16[144,512]{1,0:T(8,128)(2,1)S(1)}, u32[]{:S(2)}, u32[]{:S(2)}) collective-permute-start(bf16[144,512]{1,0:T(8,128)(2,1)} %get-tuple-element.30.refs_2_), channel_id=1, source_target_pairs={{0,1},{1,0},{2,3},{3,2},{4,5},{5,4},{6,7},{7,6},{8,9},{9,8},{10,11... | collective-permute-start | bytes 442376 | tf_op jit(solution)/shard_map/ppermute | solution.py:38
  11.9 1.5 %collective-permute-done.refs_1_.refs_3_ = bf16[144,512]{1,0:T(8,128)(2,1)S(1)} collective-permute-done((bf16[144,512]{1,0:T(8,128)(2,1)}, bf16[144,512]{1,0:T(8,128)(2,1)S(1)}, u32[]{:S(2)}, u32[]{:S(2)}) %collective-permute-start) | collective-permute-done | bytes 147488 | tf_op jit(solution)/shard_map/ppermute | solution.py:38
  13.3 1.5 %collective-permute-start.4 = (bf16[144,512]{1,0:T(8,128)(2,1)S(1)}, bf16[144,512]{1,0:T(8,128)(2,1)S(1)}, u32[]{:S(2)}, u32[]{:S(2)}) collective-permute-start(bf16[144,512]{1,0:T(8,128)(2,1)S(1)} %collective-permute-done.refs_1_.refs_3_), channel_id=1, source_target_pairs={{0,1},{1,0},{2,3},{3,2},{4,5},{5,4},{6,7},{7,6},{8,9},{9,8},{10,11... | collective-permute-start | bytes 442376 | tf_op jit(solution)/shard_map/ppermute | solution.py:38
  14.8 6.8 %collective-permute-done.1.refs_2_.refs_4_ = bf16[144,512]{1,0:T(8,128)(2,1)S(1)} collective-permute-done((bf16[144,512]{1,0:T(8,128)(2,1)}, bf16[144,512]{1,0:T(8,128)(2,1)S(1)}, u32[]{:S(2)}, u32[]{:S(2)}) %collective-permute-start.1) | collective-permute-done | bytes 147488 | tf_op jit(solution)/shard_map/ppermute | solution.py:38
  22.2 1.5 %collective-permute-start.5 = (bf16[144,512]{1,0:T(8,128)(2,1)S(1)}, bf16[144,512]{1,0:T(8,128)(2,1)S(1)}, u32[]{:S(2)}, u32[]{:S(2)}) collective-permute-start(bf16[144,512]{1,0:T(8,128)(2,1)S(1)} %collective-permute-done.1.refs_2_.refs_4_), channel_id=1, source_target_pairs={{0,1},{1,0},{2,3},{3,2},{4,5},{5,4},{6,7},{7,6},{8,9},{9,8},{10,11... | collective-permute-start | bytes 442376 | tf_op jit(solution)/shard_map/ppermute | solution.py:38
  24.8 1.8 %collective-permute-start.10 = (bf16[128,128]{1,0:T(8,128)(2,1)S(1)}, bf16[128,128]{1,0:T(8,128)(2,1)S(1)}, u32[]{:S(2)}, u32[]{:S(2)}) collective-permute-start(bf16[128,128]{1,0:T(8,128)(2,1)S(1)} %get-tuple-element.35), channel_id=1, source_target_pairs={{0,2},{1,3},{2,0},{3,1},{4,6},{5,7},{6,4},{7,5},{8,10},{9,11},{10,... | collective-permute-start | bytes 98312 | tf_op jit(solution)/shard_map/ppermute | solution.py:38
  26.6 1.1 %collective-permute-start.11 = (bf16[128,128]{1,0:T(8,128)(2,1)S(1)}, bf16[128,128]{1,0:T(8,128)(2,1)S(1)}, u32[]{:S(2)}, u32[]{:S(2)}) collective-permute-start(bf16[128,128]{1,0:T(8,128)(2,1)S(1)} %get-tuple-element.36), channel_id=1, source_target_pairs={{0,4},{1,5},{2,6},{3,7},{4,0},{5,1},{6,2},{7,3},{8,12},{9,13},{10,... | collective-permute-start | bytes 98312 | tf_op jit(solution)/shard_map/ppermute | solution.py:38
  27.7 1.6 %collective-permute-start.12 = (bf16[128,128]{1,0:T(8,128)(2,1)S(1)}, bf16[128,128]{1,0:T(8,128)(2,1)S(1)}, u32[]{:S(2)}, u32[]{:S(2)}) collective-permute-start(bf16[128,128]{1,0:T(8,128)(2,1)S(1)} %get-tuple-element.37), channel_id=1, source_target_pairs={{0,6},{1,7},{2,4},{3,5},{4,2},{5,3},{6,0},{7,1},{8,14},{9,15},{10,... | collective-permute-start | bytes 98312 | tf_op jit(solution)/shard_map/ppermute | solution.py:38
  29.3 1.9 %collective-permute-done.6.refs_9_ = bf16[144,512]{1,0:T(8,128)(2,1)S(1)} collective-permute-done((bf16[144,512]{1,0:T(8,128)(2,1)S(1)}, bf16[144,512]{1,0:T(8,128)(2,1)S(1)}, u32[]{:S(2)}, u32[]{:S(2)}) %collective-permute-start.6) | collective-permute-done | bytes 147488 | tf_op jit(solution)/shard_map/ppermute | solution.py:38
  31.2 1.1 %collective-permute-done.11.refs_12_ = bf16[128,128]{1,0:T(8,128)(2,1)S(1)} collective-permute-done((bf16[128,128]{1,0:T(8,128)(2,1)S(1)}, bf16[128,128]{1,0:T(8,128)(2,1)S(1)}, u32[]{:S(2)}, u32[]{:S(2)}) %collective-permute-start.11) | collective-permute-done | bytes 32800 | tf_op jit(solution)/shard_map/ppermute | solution.py:38
  32.4 1.1 %collective-permute-done.12.refs_13_ = bf16[128,128]{1,0:T(8,128)(2,1)S(1)} collective-permute-done((bf16[128,128]{1,0:T(8,128)(2,1)S(1)}, bf16[128,128]{1,0:T(8,128)(2,1)S(1)}, u32[]{:S(2)}, u32[]{:S(2)}) %collective-permute-start.12) | collective-permute-done | bytes 32800 | tf_op jit(solution)/shard_map/ppermute | solution.py:38
  33.5 6.7 %shard_map.97 = (bf16[128,128]{1,0:T(8,128)(2,1)S(1)}, bf16[128,128]{1,0:T(8,128)(2,1)S(1)}, bf16[128,128]{1,0:T(8,128)(2,1)S(1)}, bf16[128,128]{1,0:T(8,128)(2,...) custom-call(s32[1,8]{1,0:T(1,128)S(1)} %copy-done.3, ...), custom_call_target="tpu_custom_call" | custom-call | tf_op jit(solution)/shard_map/pallas_call | solution.py:49
  40.3 1.1 %collective-permute-start.15 = (bf16[2,128,512]{2,1,0:T(8,128)(2,1)S(1)}, bf16[2,128,512]{2,1,0:T(8,128)(2,1)S(1)}, u32[]{:S(2)}, u32[]{:S(2)}) collective-permute-start(bf16[2,128,512]{2,1,0:T(8,128)(2,1)S(1)} %get-tuple-element.42), channel_id=1, source_target_pairs={{0,16},{8,24},{16,0},{24,8},{1,17},{9,25},{17,1},{25,9},{2,18},{10... | collective-permute-start | bytes 786440 | tf_op jit(solution)/shard_map/ppermute | solution.py:38
  41.5 2.0 %collective-permute-start.18 = (bf16[128,128]{1,0:T(8,128)(2,1)S(1)}, bf16[128,128]{1,0:T(8,128)(2,1)S(1)}, u32[]{:S(2)}, u32[]{:S(2)}) collective-permute-start(bf16[128,128]{1,0:T(8,128)(2,1)S(1)} %get-tuple-element.45), channel_id=1, source_target_pairs={{0,4},{1,5},{2,6},{3,7},{4,0},{5,1},{6,2},{7,3},{8,12},{9,13},{10,... | collective-permute-start | bytes 98312 | tf_op jit(solution)/shard_map/ppermute | solution.py:38
  43.5 2.2 %collective-permute-start.19 = (bf16[128,128]{1,0:T(8,128)(2,1)S(1)}, bf16[128,128]{1,0:T(8,128)(2,1)S(1)}, u32[]{:S(2)}, u32[]{:S(2)}) collective-permute-start(bf16[128,128]{1,0:T(8,128)(2,1)S(1)} %get-tuple-element.46), channel_id=1, source_target_pairs={{0,6},{1,7},{2,4},{3,5},{4,2},{5,3},{6,0},{7,1},{8,14},{9,15},{10,... | collective-permute-start | bytes 98312 | tf_op jit(solution)/shard_map/ppermute | solution.py:38
  46.3 2.9 %collective-permute-done.19.refs_3_ = bf16[128,128]{1,0:T(8,128)(2,1)S(1)} collective-permute-done((bf16[128,128]{1,0:T(8,128)(2,1)S(1)}, bf16[128,128]{1,0:T(8,128)(2,1)S(1)}, u32[]{:S(2)}, u32[]{:S(2)}) %collective-permute-start.19) | collective-permute-done | bytes 32800 | tf_op jit(solution)/shard_map/ppermute | solution.py:38
  49.3 1.1 %collective-permute-start.21 = (bf16[128,512]{1,0:T(8,128)(2,1)S(1)}, bf16[128,512]{1,0:T(8,128)(2,1)S(1)}, u32[]{:S(2)}, u32[]{:S(2)}) collective-permute-start(bf16[128,512]{1,0:T(8,128)(2,1)S(1)} %shard_map.98.refs_4_.refs_0_), channel_id=1, source_target_pairs={{0,16},{8,24},{16,0},{24,8},{1,17},{9,25},{17,1},{25,9},{2,18},{10... | collective-permute-start | bytes 393224 | tf_op jit(solution)/shard_map/ppermute | solution.py:38
  51.0 3.4 %collective-permute-done.21.refs_6_ = bf16[128,512]{1,0:T(8,128)(2,1)S(1)} collective-permute-done((bf16[128,512]{1,0:T(8,128)(2,1)S(1)}, bf16[128,512]{1,0:T(8,128)(2,1)S(1)}, u32[]{:S(2)}, u32[]{:S(2)}) %collective-permute-start.21) | collective-permute-done | bytes 131104 | tf_op jit(solution)/shard_map/ppermute | solution.py:38
  54.4 1.3 %collective-permute-done.22.refs_7_ = bf16[128,512]{1,0:T(8,128)(2,1)S(1)} collective-permute-done((bf16[128,512]{1,0:T(8,128)(2,1)S(1)}, bf16[128,512]{1,0:T(8,128)(2,1)S(1)}, u32[]{:S(2)}, u32[]{:S(2)}) %collective-permute-start.22) | collective-permute-done | bytes 131104 | tf_op jit(solution)/shard_map/ppermute | solution.py:38
  56.2 1.0 %collective-permute-start.26 = (bf16[4,64,512]{2,1,0:T(8,128)(2,1)S(1)}, bf16[4,64,512]{2,1,0:T(8,128)(2,1)S(1)}, u32[]{:S(2)}, u32[]{:S(2)}) collective-permute-start(bf16[4,64,512]{2,1,0:T(8,128)(2,1)S(1)} %get-tuple-element.52), channel_id=1, source_target_pairs={{0,1},{1,0},{2,3},{3,2},{4,5},{5,4},{6,7},{7,6},{8,9},{9,8},{10,11... | collective-permute-start | bytes 786440 | tf_op jit(solution)/shard_map/ppermute | solution.py:38
  57.4 2.8 %collective-permute-start.23 = (bf16[128,256]{1,0:T(8,128)(2,1)S(1)}, bf16[128,256]{1,0:T(8,128)(2,1)S(1)}, u32[]{:S(2)}, u32[]{:S(2)}) collective-permute-start(bf16[128,256]{1,0:T(8,128)(2,1)S(1)} %get-tuple-element.49), channel_id=1, source_target_pairs={{0,2},{1,3},{2,0},{3,1},{4,6},{5,7},{6,4},{7,5},{8,10},{9,11},{10,... | collective-permute-start | bytes 196616 | tf_op jit(solution)/shard_map/ppermute | solution.py:38
  60.2 1.6 %collective-permute-start.25 = (bf16[128,256]{1,0:T(8,128)(2,1)S(1)}, bf16[128,256]{1,0:T(8,128)(2,1)S(1)}, u32[]{:S(2)}, u32[]{:S(2)}) collective-permute-start(bf16[128,256]{1,0:T(8,128)(2,1)S(1)} %get-tuple-element.51), channel_id=1, source_target_pairs={{0,6},{1,7},{2,4},{3,5},{4,2},{5,3},{6,0},{7,1},{8,14},{9,15},{10,... | collective-permute-start | bytes 196616 | tf_op jit(solution)/shard_map/ppermute | solution.py:38
  61.7 1.6 %collective-permute-done.24.refs_2_ = bf16[128,256]{1,0:T(8,128)(2,1)S(1)} collective-permute-done((bf16[128,256]{1,0:T(8,128)(2,1)S(1)}, bf16[128,256]{1,0:T(8,128)(2,1)S(1)}, u32[]{:S(2)}, u32[]{:S(2)}) %collective-permute-start.24) | collective-permute-done | bytes 65568 | tf_op jit(solution)/shard_map/ppermute | solution.py:38
  63.3 1.4 %collective-permute-done.26.refs_1_ = bf16[4,64,512]{2,1,0:T(8,128)(2,1)S(1)} collective-permute-done((bf16[4,64,512]{2,1,0:T(8,128)(2,1)S(1)}, bf16[4,64,512]{2,1,0:T(8,128)(2,1)S(1)}, u32[]{:S(2)}, u32[]{:S(2)}) %collective-permute-start.26) | collective-permute-done | bytes 262176 | tf_op jit(solution)/shard_map/ppermute | solution.py:38
  64.8 2.8 %collective-permute-start.28 = (bf16[64,512]{1,0:T(8,128)(2,1)S(1)}, bf16[64,512]{1,0:T(8,128)(2,1)S(1)}, u32[]{:S(2)}, u32[]{:S(2)}) collective-permute-start(bf16[64,512]{1,0:T(8,128)(2,1)S(1)} %get-tuple-element.55), channel_id=1, source_target_pairs={{0,4},{1,5},{2,6},{3,7},{4,0},{5,1},{6,2},{7,3},{8,12},{9,13},{10,... | collective-permute-start | bytes 196616 | tf_op jit(solution)/shard_map/ppermute | solution.py:38
  67.6 1.6 %collective-permute-start.29 = (bf16[64,512]{1,0:T(8,128)(2,1)S(1)}, bf16[64,512]{1,0:T(8,128)(2,1)S(1)}, u32[]{:S(2)}, u32[]{:S(2)}) collective-permute-start(bf16[64,512]{1,0:T(8,128)(2,1)S(1)} %get-tuple-element.56), channel_id=1, source_target_pairs={{0,6},{1,7},{2,4},{3,5},{4,2},{5,3},{6,0},{7,1},{8,14},{9,15},{10,... | collective-permute-start | bytes 196616 | tf_op jit(solution)/shard_map/ppermute | solution.py:38
  69.2 1.6 %shard_map.102 = bf16[128,2048]{1,0:T(8,128)(2,1)} custom-call(bf16[128,512]{1,0:T(8,128)(2,1)S(1)} %shard_map.98.refs_4_.refs_0_, bf16[512,512]{1,0:T(8,128)(2,1)S(1)} %copy-done, bf16[512,512]{1,0:T(8,128)(2,1)S(1)} %collective-permute-done.7.refs_2_, bf16[512,512]{1,0:T(8,128)(2,1)S(1)} %shard_map.95.refs_3_, ...), custom_call_target="tpu_custom_call" | custom-call | tf_op jit(solution)/shard_map/pallas_call | solution.py:49
  72.2 1.4 %collective-permute-done.29.refs_3_ = bf16[64,512]{1,0:T(8,128)(2,1)S(1)} collective-permute-done((bf16[64,512]{1,0:T(8,128)(2,1)S(1)}, bf16[64,512]{1,0:T(8,128)(2,1)S(1)}, u32[]{:S(2)}, u32[]{:S(2)}) %collective-permute-start.29) | collective-permute-done | bytes 65568 | tf_op jit(solution)/shard_map/ppermute | solution.py:38
  (48 shorter events, 6.3 us)
Async XLA Ops:
  0.6 21.0 %copy-start = (bf16[512,512]{1,0:T(8,128)(2,1)S(1)}, bf16[512,512]{1,0:T(8,128)(2,1)}, u32[]{:S(2)}) copy-start(bf16[512,512]{1,0:T(8,128)(2,1)} %refs_1_.3) | copy-start | bytes 1572868
  0.6 21.0 %collective-permute-start.8 = (bf16[512,512]{1,0:T(8,128)(2,1)}, bf16[512,512]{1,0:T(8,128)(2,1)S(1)}, u32[]{:S(2)}, u32[]{:S(2)}) collective-permute-start(bf16[512,512]{1,0:T(8,128)(2,1)} %refs_1_.3), channel_id=1, source_target_pairs={{0,16},{8,24},{16,0},{24,8},{1,17},{9,25},{17,1},{25,9},{2,18},{10... | collective-permute-start | bytes 1572872 | tf_op jit(solution)/shard_map/ppermute | solution.py:38
  5.9 7.4 %collective-permute-start = (bf16[144,512]{1,0:T(8,128)(2,1)}, bf16[144,512]{1,0:T(8,128)(2,1)S(1)}, u32[]{:S(2)}, u32[]{:S(2)}) collective-permute-start(bf16[144,512]{1,0:T(8,128)(2,1)} %get-tuple-element.31), channel_id=1, source_target_pairs={{0,2},{1,3},{2,0},{3,1},{4,6},{5,7},{6,4},{7,5},{8,10},{9,11},{10,... | collective-permute-start | bytes 442376 | tf_op jit(solution)/shard_map/ppermute | solution.py:38
  7.5 14.1 %collective-permute-start.1 = (bf16[144,512]{1,0:T(8,128)(2,1)}, bf16[144,512]{1,0:T(8,128)(2,1)S(1)}, u32[]{:S(2)}, u32[]{:S(2)}) collective-permute-start(bf16[144,512]{1,0:T(8,128)(2,1)} %get-tuple-element.32), channel_id=1, source_target_pairs={{0,4},{1,5},{2,6},{3,7},{4,0},{5,1},{6,2},{7,3},{8,12},{9,13},{10,... | collective-permute-start | bytes 442376 | tf_op jit(solution)/shard_map/ppermute | solution.py:38
  10.1 11.5 %collective-permute-start.2 = (bf16[144,512]{1,0:T(8,128)(2,1)}, bf16[144,512]{1,0:T(8,128)(2,1)S(1)}, u32[]{:S(2)}, u32[]{:S(2)}) collective-permute-start(bf16[144,512]{1,0:T(8,128)(2,1)} %get-tuple-element.33), channel_id=1, source_target_pairs={{0,6},{1,7},{2,4},{3,5},{4,2},{5,3},{6,0},{7,1},{8,14},{9,15},{10,... | collective-permute-start | bytes 442376 | tf_op jit(solution)/shard_map/ppermute | solution.py:38
  10.4 13.9 %copy-start.1 = (bf16[1,128,2048]{2,1,0:T(8,128)(2,1)S(1)}, bf16[1,128,2048]{2,1,0:T(8,128)(2,1)}, u32[]{:S(2)}) copy-start(bf16[1,128,2048]{2,1,0:T(8,128)(2,1)} %param.7) | copy-start | bytes 1572868
  10.4 11.3 %collective-permute-start.3 = (bf16[144,512]{1,0:T(8,128)(2,1)}, bf16[144,512]{1,0:T(8,128)(2,1)S(1)}, u32[]{:S(2)}, u32[]{:S(2)}) collective-permute-start(bf16[144,512]{1,0:T(8,128)(2,1)} %get-tuple-element.30.refs_2_), channel_id=1, source_target_pairs={{0,1},{1,0},{2,3},{3,2},{4,5},{5,4},{6,7},{7,6},{8,9},{9,8},{10,11... | collective-permute-start | bytes 442376 | tf_op jit(solution)/shard_map/ppermute | solution.py:38
  13.3 8.3 %collective-permute-start.4 = (bf16[144,512]{1,0:T(8,128)(2,1)S(1)}, bf16[144,512]{1,0:T(8,128)(2,1)S(1)}, u32[]{:S(2)}, u32[]{:S(2)}) collective-permute-start(bf16[144,512]{1,0:T(8,128)(2,1)S(1)} %collective-permute-done.refs_1_.refs_3_), channel_id=1, source_target_pairs={{0,1},{1,0},{2,3},{3,2},{4,5},{5,4},{6,7},{7,6},{8,9},{9,8},{10,11... | collective-permute-start | bytes 442376 | tf_op jit(solution)/shard_map/ppermute | solution.py:38
  21.6 2.6 %collective-permute-start.7 = (bf16[512,512]{1,0:T(8,128)(2,1)S(1)}, bf16[512,512]{1,0:T(8,128)(2,1)S(1)}, u32[]{:S(2)}, u32[]{:S(2)}) collective-permute-start(bf16[512,512]{1,0:T(8,128)(2,1)S(1)} %copy-done), channel_id=1, source_target_pairs={{0,8},{8,0},{16,24},{24,16},{1,9},{9,1},{17,25},{25,17},{2,10},{10... | collective-permute-start | bytes 1572872 | tf_op jit(solution)/shard_map/ppermute | solution.py:38
  21.7 2.6 %collective-permute-start.9 = (bf16[512,512]{1,0:T(8,128)(2,1)S(1)}, bf16[512,512]{1,0:T(8,128)(2,1)S(1)}, u32[]{:S(2)}, u32[]{:S(2)}) collective-permute-start(bf16[512,512]{1,0:T(8,128)(2,1)S(1)} %shard_map.95.refs_3_), channel_id=1, source_target_pairs={{0,8},{8,0},{16,24},{24,16},{1,9},{9,1},{17,25},{25,17},{2,10},{10... | collective-permute-start | bytes 1572872 | tf_op jit(solution)/shard_map/ppermute | solution.py:38
  22.2 7.1 %collective-permute-start.5 = (bf16[144,512]{1,0:T(8,128)(2,1)S(1)}, bf16[144,512]{1,0:T(8,128)(2,1)S(1)}, u32[]{:S(2)}, u32[]{:S(2)}) collective-permute-start(bf16[144,512]{1,0:T(8,128)(2,1)S(1)} %collective-permute-done.1.refs_2_.refs_4_), channel_id=1, source_target_pairs={{0,1},{1,0},{2,3},{3,2},{4,5},{5,4},{6,7},{7,6},{8,9},{9,8},{10,11... | collective-permute-start | bytes 442376 | tf_op jit(solution)/shard_map/ppermute | solution.py:38
  23.7 7.5 %collective-permute-start.6 = (bf16[144,512]{1,0:T(8,128)(2,1)S(1)}, bf16[144,512]{1,0:T(8,128)(2,1)S(1)}, u32[]{:S(2)}, u32[]{:S(2)}) collective-permute-start(bf16[144,512]{1,0:T(8,128)(2,1)S(1)} %collective-permute-done.2.refs_3_.refs_5_), channel_id=1, source_target_pairs={{0,1},{1,0},{2,3},{3,2},{4,5},{5,4},{6,7},{7,6},{8,9},{9,8},{10,11... | collective-permute-start | bytes 442376 | tf_op jit(solution)/shard_map/ppermute | solution.py:38
  24.8 6.4 %collective-permute-start.10 = (bf16[128,128]{1,0:T(8,128)(2,1)S(1)}, bf16[128,128]{1,0:T(8,128)(2,1)S(1)}, u32[]{:S(2)}, u32[]{:S(2)}) collective-permute-start(bf16[128,128]{1,0:T(8,128)(2,1)S(1)} %get-tuple-element.35), channel_id=1, source_target_pairs={{0,2},{1,3},{2,0},{3,1},{4,6},{5,7},{6,4},{7,5},{8,10},{9,11},{10,... | collective-permute-start | bytes 98312 | tf_op jit(solution)/shard_map/ppermute | solution.py:38
  26.6 5.8 %collective-permute-start.11 = (bf16[128,128]{1,0:T(8,128)(2,1)S(1)}, bf16[128,128]{1,0:T(8,128)(2,1)S(1)}, u32[]{:S(2)}, u32[]{:S(2)}) collective-permute-start(bf16[128,128]{1,0:T(8,128)(2,1)S(1)} %get-tuple-element.36), channel_id=1, source_target_pairs={{0,4},{1,5},{2,6},{3,7},{4,0},{5,1},{6,2},{7,3},{8,12},{9,13},{10,... | collective-permute-start | bytes 98312 | tf_op jit(solution)/shard_map/ppermute | solution.py:38
  27.7 5.7 %collective-permute-start.12 = (bf16[128,128]{1,0:T(8,128)(2,1)S(1)}, bf16[128,128]{1,0:T(8,128)(2,1)S(1)}, u32[]{:S(2)}, u32[]{:S(2)}) collective-permute-start(bf16[128,128]{1,0:T(8,128)(2,1)S(1)} %get-tuple-element.37), channel_id=1, source_target_pairs={{0,6},{1,7},{2,4},{3,5},{4,2},{5,3},{6,0},{7,1},{8,14},{9,15},{10,... | collective-permute-start | bytes 98312 | tf_op jit(solution)/shard_map/ppermute | solution.py:38
  40.2 9.0 %collective-permute-start.13 = (bf16[4,128,256]{2,1,0:T(8,128)(2,1)S(1)}, bf16[4,128,256]{2,1,0:T(8,128)(2,1)S(1)}, u32[]{:S(2)}, u32[]{:S(2)}) collective-permute-start(bf16[4,128,256]{2,1,0:T(8,128)(2,1)S(1)} %get-tuple-element.39), channel_id=1, source_target_pairs={{0,1},{1,0},{2,3},{3,2},{4,5},{5,4},{6,7},{7,6},{8,9},{9,8},{10,11... | collective-permute-start | bytes 786440 | tf_op jit(solution)/shard_map/ppermute | solution.py:38
  40.3 10.1 %collective-permute-start.15 = (bf16[2,128,512]{2,1,0:T(8,128)(2,1)S(1)}, bf16[2,128,512]{2,1,0:T(8,128)(2,1)S(1)}, u32[]{:S(2)}, u32[]{:S(2)}) collective-permute-start(bf16[2,128,512]{2,1,0:T(8,128)(2,1)S(1)} %get-tuple-element.42), channel_id=1, source_target_pairs={{0,16},{8,24},{16,0},{24,8},{1,17},{9,25},{17,1},{25,9},{2,18},{10... | collective-permute-start | bytes 786440 | tf_op jit(solution)/shard_map/ppermute | solution.py:38
  41.3 4.4 %collective-permute-start.17 = (bf16[128,128]{1,0:T(8,128)(2,1)S(1)}, bf16[128,128]{1,0:T(8,128)(2,1)S(1)}, u32[]{:S(2)}, u32[]{:S(2)}) collective-permute-start(bf16[128,128]{1,0:T(8,128)(2,1)S(1)} %get-tuple-element.44), channel_id=1, source_target_pairs={{0,2},{1,3},{2,0},{3,1},{4,6},{5,7},{6,4},{7,5},{8,10},{9,11},{10,... | collective-permute-start | bytes 98312 | tf_op jit(solution)/shard_map/ppermute | solution.py:38
  41.5 4.8 %collective-permute-start.18 = (bf16[128,128]{1,0:T(8,128)(2,1)S(1)}, bf16[128,128]{1,0:T(8,128)(2,1)S(1)}, u32[]{:S(2)}, u32[]{:S(2)}) collective-permute-start(bf16[128,128]{1,0:T(8,128)(2,1)S(1)} %get-tuple-element.45), channel_id=1, source_target_pairs={{0,4},{1,5},{2,6},{3,7},{4,0},{5,1},{6,2},{7,3},{8,12},{9,13},{10,... | collective-permute-start | bytes 98312 | tf_op jit(solution)/shard_map/ppermute | solution.py:38
  43.5 5.7 %collective-permute-start.19 = (bf16[128,128]{1,0:T(8,128)(2,1)S(1)}, bf16[128,128]{1,0:T(8,128)(2,1)S(1)}, u32[]{:S(2)}, u32[]{:S(2)}) collective-permute-start(bf16[128,128]{1,0:T(8,128)(2,1)S(1)} %get-tuple-element.46), channel_id=1, source_target_pairs={{0,6},{1,7},{2,4},{3,5},{4,2},{5,3},{6,0},{7,1},{8,14},{9,15},{10,... | collective-permute-start | bytes 98312 | tf_op jit(solution)/shard_map/ppermute | solution.py:38
  45.7 8.6 %collective-permute-start.14 = (bf16[128,512]{1,0:T(8,128)(2,1)S(1)}, bf16[128,512]{1,0:T(8,128)(2,1)S(1)}, u32[]{:S(2)}, u32[]{:S(2)}) collective-permute-start(bf16[128,512]{1,0:T(8,128)(2,1)S(1)} %get-tuple-element.41), channel_id=1, source_target_pairs={{0,8},{8,0},{16,24},{24,16},{1,9},{9,1},{17,25},{25,17},{2,10},{10... | collective-permute-start | bytes 393224 | tf_op jit(solution)/shard_map/ppermute | solution.py:38
  49.3 5.0 %collective-permute-start.21 = (bf16[128,512]{1,0:T(8,128)(2,1)S(1)}, bf16[128,512]{1,0:T(8,128)(2,1)S(1)}, u32[]{:S(2)}, u32[]{:S(2)}) collective-permute-start(bf16[128,512]{1,0:T(8,128)(2,1)S(1)} %shard_map.98.refs_4_.refs_0_), channel_id=1, source_target_pairs={{0,16},{8,24},{16,0},{24,8},{1,17},{9,25},{17,1},{25,9},{2,18},{10... | collective-permute-start | bytes 393224 | tf_op jit(solution)/shard_map/ppermute | solution.py:38
  50.4 4.0 %collective-permute-start.20 = (bf16[128,512]{1,0:T(8,128)(2,1)S(1)}, bf16[128,512]{1,0:T(8,128)(2,1)S(1)}, u32[]{:S(2)}, u32[]{:S(2)}) collective-permute-start(bf16[128,512]{1,0:T(8,128)(2,1)S(1)} %shard_map.98.refs_4_.refs_0_), channel_id=1, source_target_pairs={{0,8},{8,0},{16,24},{24,16},{1,9},{9,1},{17,25},{25,17},{2,10},{10... | collective-permute-start | bytes 393224 | tf_op jit(solution)/shard_map/ppermute | solution.py:38
  50.4 4.0 %collective-permute-start.16 = (bf16[128,512]{1,0:T(8,128)(2,1)S(1)}, bf16[128,512]{1,0:T(8,128)(2,1)S(1)}, u32[]{:S(2)}, u32[]{:S(2)}) collective-permute-start(bf16[128,512]{1,0:T(8,128)(2,1)S(1)} %get-tuple-element.57), channel_id=1, source_target_pairs={{0,8},{8,0},{16,24},{24,16},{1,9},{9,1},{17,25},{25,17},{2,10},{10... | collective-permute-start | bytes 393224 | tf_op jit(solution)/shard_map/ppermute | solution.py:38
  54.3 1.3 %collective-permute-start.22 = (bf16[128,512]{1,0:T(8,128)(2,1)S(1)}, bf16[128,512]{1,0:T(8,128)(2,1)S(1)}, u32[]{:S(2)}, u32[]{:S(2)}) collective-permute-start(bf16[128,512]{1,0:T(8,128)(2,1)S(1)} %collective-permute-done.21.refs_6_), channel_id=1, source_target_pairs={{0,8},{8,0},{16,24},{24,16},{1,9},{9,1},{17,25},{25,17},{2,10},{10... | collective-permute-start | bytes 393224 | tf_op jit(solution)/shard_map/ppermute | solution.py:38
  56.2 8.4 %collective-permute-start.26 = (bf16[4,64,512]{2,1,0:T(8,128)(2,1)S(1)}, bf16[4,64,512]{2,1,0:T(8,128)(2,1)S(1)}, u32[]{:S(2)}, u32[]{:S(2)}) collective-permute-start(bf16[4,64,512]{2,1,0:T(8,128)(2,1)S(1)} %get-tuple-element.52), channel_id=1, source_target_pairs={{0,1},{1,0},{2,3},{3,2},{4,5},{5,4},{6,7},{7,6},{8,9},{9,8},{10,11... | collective-permute-start | bytes 786440 | tf_op jit(solution)/shard_map/ppermute | solution.py:38
  57.3 6.0 %collective-permute-start.24 = (bf16[128,256]{1,0:T(8,128)(2,1)S(1)}, bf16[128,256]{1,0:T(8,128)(2,1)S(1)}, u32[]{:S(2)}, u32[]{:S(2)}) collective-permute-start(bf16[128,256]{1,0:T(8,128)(2,1)S(1)} %get-tuple-element.50), channel_id=1, source_target_pairs={{0,4},{1,5},{2,6},{3,7},{4,0},{5,1},{6,2},{7,3},{8,12},{9,13},{10,... | collective-permute-start | bytes 196616 | tf_op jit(solution)/shard_map/ppermute | solution.py:38
  57.4 13.4 %collective-permute-start.23 = (bf16[128,256]{1,0:T(8,128)(2,1)S(1)}, bf16[128,256]{1,0:T(8,128)(2,1)S(1)}, u32[]{:S(2)}, u32[]{:S(2)}) collective-permute-start(bf16[128,256]{1,0:T(8,128)(2,1)S(1)} %get-tuple-element.49), channel_id=1, source_target_pairs={{0,2},{1,3},{2,0},{3,1},{4,6},{5,7},{6,4},{7,5},{8,10},{9,11},{10,... | collective-permute-start | bytes 196616 | tf_op jit(solution)/shard_map/ppermute | solution.py:38
  60.2 10.6 %collective-permute-start.25 = (bf16[128,256]{1,0:T(8,128)(2,1)S(1)}, bf16[128,256]{1,0:T(8,128)(2,1)S(1)}, u32[]{:S(2)}, u32[]{:S(2)}) collective-permute-start(bf16[128,256]{1,0:T(8,128)(2,1)S(1)} %get-tuple-element.51), channel_id=1, source_target_pairs={{0,6},{1,7},{2,4},{3,5},{4,2},{5,3},{6,0},{7,1},{8,14},{9,15},{10,... | collective-permute-start | bytes 196616 | tf_op jit(solution)/shard_map/ppermute | solution.py:38
  64.7 6.8 %collective-permute-start.27 = (bf16[64,512]{1,0:T(8,128)(2,1)S(1)}, bf16[64,512]{1,0:T(8,128)(2,1)S(1)}, u32[]{:S(2)}, u32[]{:S(2)}) collective-permute-start(bf16[64,512]{1,0:T(8,128)(2,1)S(1)} %get-tuple-element.54), channel_id=1, source_target_pairs={{0,2},{1,3},{2,0},{3,1},{4,6},{5,7},{6,4},{7,5},{8,10},{9,11},{10,... | collective-permute-start | bytes 196616 | tf_op jit(solution)/shard_map/ppermute | solution.py:38
  64.8 7.5 %collective-permute-start.28 = (bf16[64,512]{1,0:T(8,128)(2,1)S(1)}, bf16[64,512]{1,0:T(8,128)(2,1)S(1)}, u32[]{:S(2)}, u32[]{:S(2)}) collective-permute-start(bf16[64,512]{1,0:T(8,128)(2,1)S(1)} %get-tuple-element.55), channel_id=1, source_target_pairs={{0,4},{1,5},{2,6},{3,7},{4,0},{5,1},{6,2},{7,3},{8,12},{9,13},{10,... | collective-permute-start | bytes 196616 | tf_op jit(solution)/shard_map/ppermute | solution.py:38
  67.6 6.1 %collective-permute-start.29 = (bf16[64,512]{1,0:T(8,128)(2,1)S(1)}, bf16[64,512]{1,0:T(8,128)(2,1)S(1)}, u32[]{:S(2)}, u32[]{:S(2)}) collective-permute-start(bf16[64,512]{1,0:T(8,128)(2,1)S(1)} %get-tuple-element.56), channel_id=1, source_target_pairs={{0,6},{1,7},{2,4},{3,5},{4,2},{5,3},{6,0},{7,1},{8,14},{9,15},{10,... | collective-permute-start | bytes 196616 | tf_op jit(solution)/shard_map/ppermute | solution.py:38
  (2 other events, 14.9 us)

commit v2 on v1

--- a/solution.py
+++ b/solution.py
@@ -77,6 +77,14 @@
 def head_side():
     me = lax.rem(lax.axis_index("ctx"), TEAM)
     return me // 2, lax.rem(me, 2)
+
+
+def far_first(arrays):
+    return [arrays[m] for m in (0, 2, 3, 1)]
+
+
+def by_head(refs):
+    return [refs[i] for i in (0, 3, 1, 2)]
 
 
 def split(exact):
@@ -230,7 +238,7 @@
             q_all[pair, place] = ref[0:rows, pair * PAIR:(pair + 1) * PAIR]
             go_all[pair, place] = ref[0:rows, GROUP + pair * PAIR:GROUP + (pair + 1) * PAIR]
         stat_all[place] = unpacked(ref, rows)
-    for place, ref in zip(near, kv_refs):
+    for place, ref in zip(near, by_head(kv_refs)):
         key_all[place], value_all[place] = stacked(ref[...])
     dq_all[...] = jnp.zeros_like(dq_all)
     for block in range(TEAM):
@@ -299,8 +307,8 @@
 def owner_kernel(*rest):
     dkv_refs, out_ref, parts = rest[:KV_HEADS], rest[KV_HEADS], rest[KV_HEADS + 1]
     head, _ = head_side()
-    for m in range(KV_HEADS):
-        parts[jnp.bitwise_xor(head, m)] = dkv_refs[m][...]
+    for m, ref in enumerate(by_head(dkv_refs)):
+        parts[jnp.bitwise_xor(head, m)] = ref[...]
     keys = [parts[g, :, :HEAD_DIM] for g in range(KV_HEADS)]
     values = [parts[g, :, HEAD_DIM:] for g in range(KV_HEADS)]
     out_ref[...] = jnp.concatenate(keys + values, axis=1)
@@ -314,9 +322,9 @@
 def query_kernel(*rest):
     dq_refs, out_ref = rest[:KV_HEADS], rest[KV_HEADS]
     head, _ = head_side()
-    for m in range(KV_HEADS):
+    for m, ref in enumerate(by_head(dq_refs)):
         columns = pl.ds(pl.multiple_of(jnp.bitwise_xor(head, m) * GROUP, GROUP), GROUP)
-        out_ref[:, columns] = dq_refs[m][...]
+        out_ref[:, columns] = ref[...]
 
 
 def input_kernel(fsdp, grad_ref, *rest):
@@ -394,7 +402,7 @@
         (queries[0], grad_out[0], attn_out[0], log_sums[0]), hbm=4)
     qd = along_heads(qd)
     turned = [swapped(one, "ctx", 1) for one in qd[:2]]
-    w_far = held(swapped(w_kv, "fsdp", far), (*qd[1:], *turned))
+    w_far = held(swapped(w_kv, "fsdp", far), (*far_first(qd[:KV_HEADS])[1:], *turned))
     w_parts = over_fsdp([w_kv] * far + [w_far] * (fsdp - far), far // 2)
 
     kv = call(
@@ -412,7 +420,7 @@
             [pltpu.VMEM((PAIRS, TEAM) + block, jnp.bfloat16)] * 2 + [pltpu.VMEM((TEAM, 2 * GROUPS, rows), f32)]
             + [pltpu.VMEM((TEAM, 2 * rows, PAIR), jnp.bfloat16)] * 2
             + [pltpu.VMEM((PAIRS, TEAM) + block, f32), pltpu.VMEM((TEAM,) + block, f32), cut_sems],
-            (block_order, inputs, *qd, *kv), smem=1, hbm=1)
+            (block_order, inputs, *qd, *far_first(kv)), smem=1, hbm=1)
         dkv, (keep, give, *hid, hid_far) = outs[:KV_HEADS], outs[KV_HEADS:]
     else:
         alike = [[t * TEAM + i for t in range(teams)] for i in range(TEAM)]
@@ -430,7 +438,7 @@
     give = swapped(give, "ctx", 1)
     (kv_grad,) = call(
         owner_kernel, [sds((rows, columns))], [pltpu.VMEM((KV_HEADS,) + block, jnp.bfloat16)],
-        dkv, after=(give,))
+        far_first(dkv), after=(give,))
     grads = over_fsdp([kv_grad] * fsdp, far)
     if teams == 1:
         share = (span // devices, columns)
@@ -442,13 +450,13 @@
         sums = call(
             pair_kernel, [sds(share, f32)] + [sds(share)] * (KV_HEADS - 1), [],
             (own_sums, swapped(send_sums, "ctx", 1)), after=dq[2:3])
-        (weight_grads,) = call(own_total_kernel, [sds(share, f32)], [], along_heads(sums))
+        (weight_grads,) = call(own_total_kernel, [sds(share, f32)], [], far_first(along_heads(sums)))
     else:
         formed = call(functools.partial(weight_kernel, fsdp), [sds((span, columns))], [], (*hid, *grads))
         dq = along_heads(call(pair_kernel, [sds(wide)] * KV_HEADS, [], (keep, give), after=formed))
         sums = lax.all_to_all(formed[0].reshape(devices, span // devices, columns), "ctx", 0, 0, tiled=True)
         (weight_grads,) = call(total_kernel, [sds((span // devices, columns), f32)], [], (sums,))
-    (query_grads,) = call(query_kernel, [sds((rows, Q_HEADS * HEAD_DIM))], [], dq, after=formed)
+    (query_grads,) = call(query_kernel, [sds((rows, Q_HEADS * HEAD_DIM))], [], far_first(dq), after=formed)
     (input_grads,) = call(
         functools.partial(input_kernel, fsdp), [sds((rows, model))], [], (kv_grad, *w_parts), after=formed)
     return query_grads[None], input_grads[None], weight_grads

time: 74.1 us -> 72.8 us (0.982)
  starting transfers between devices: 34.6 us -> 30.9 us
  waiting for transfers between devices: 25.7 us -> 28.7 us
    ppermute x30, starting transfers between devices: 34.6 us -> 30.9 us  [swapped(): return lax.ppermute(array, axis, [(i, i ^ bits) for i in range(size)])]
    ppermute x30, waiting for transfers between devices: 25.7 us -> 28.7 us  [swapped(): return lax.ppermute(array, axis, [(i, i ^ bits) for i in range(size)])]
  transfers between devices with their start and end apart: 30 -> 30, of which waited for: 13 -> 12; matrix products, arithmetic and copies ran while one was open for 0% -> 0% of each run, Pallas kernels for 7% -> 7%
where the time goes in v2:
time: 72.8 us; the launch traced here: 73.2 us
  starting transfers between devices  30.9 us (42%)
  waiting for transfers between devices  28.7 us (39%)
  Pallas kernels  12.7 us (17%)
  between operations  0.81 us (1%)
    ppermute x30, starting transfers between devices, swapped(): return lax.ppermute(array, axis, [(i, i ^ bits) for i in range(size)])  30.9 us
    ppermute x30, waiting for transfers between devices, swapped(): return lax.ppermute(array, axis, [(i, i ^ bits) for i in range(size)])  28.7 us
    pallas_call x10, Pallas kernels, call(): pl.pallas_call(body, out_shape=out_shape, in_specs=specs, out_specs=[VMEM...  12.7 us
  transfers between devices with their start and end apart: 30, of which 12 were waited for; matrix products, arithmetic and copies ran while one was open for 0% of the time, Pallas kernels for 7%

profile of v2, /device:TPU:0, one launch (start us, length us, event | category | flops | bytes accessed | tf_op | source)
XLA Modules:
  0.0 73.2 jit_solution(13579805595338496196)
XLA Ops:
  0.6 3.0 %collective-permute-start.8 = (bf16[512,512]{1,0:T(8,128)(2,1)}, bf16[512,512]{1,0:T(8,128)(2,1)S(1)}, u32[]{:S(2)}, u32[]{:S(2)}) collective-permute-start(bf16[512,512]{1,0:T(8,128)(2,1)} %refs_1_.3), channel_id=1, source_target_pairs={{0,16},{8,24},{16,0},{24,8},{1,17},{9,25},{17,1},{25,9},{2,18},{10... | collective-permute-start | bytes 1572872 | tf_op jit(solution)/shard_map/ppermute | solution.py:38
  3.7 2.2 %shard_map.94 = (bf16[144,512]{1,0:T(8,128)(2,1)}, bf16[144,512]{1,0:T(8,128)(2,1)}, bf16[144,512]{1,0:T(8,128)(2,1)}, bf16[144,512]{1,0:T(8,128)(2,1)}) custom-call(bf16[128,1024]{1,0:T(8,128)(2,1)} %bitcast.14, bf16[128,1024]{1,0:T(8,128)(2,1)} %bitcast.15, bf16[128,1024]{1,0:T(8,128)(2,1)} %bitcast.16, f32[16,128]{1,0:T(8,128)} %bitcast.18), custom_call_target="tpu_custom_call" | custom-call | tf_op jit(solution)/shard_map/pallas_call | solution.py:49
  5.9 1.6 %collective-permute-start = (bf16[144,512]{1,0:T(8,128)(2,1)}, bf16[144,512]{1,0:T(8,128)(2,1)S(1)}, u32[]{:S(2)}, u32[]{:S(2)}) collective-permute-start(bf16[144,512]{1,0:T(8,128)(2,1)} %get-tuple-element.31), channel_id=1, source_target_pairs={{0,2},{1,3},{2,0},{3,1},{4,6},{5,7},{6,4},{7,5},{8,10},{9,11},{10,... | collective-permute-start | bytes 442376 | tf_op jit(solution)/shard_map/ppermute | solution.py:38
  7.5 2.6 %collective-permute-start.1 = (bf16[144,512]{1,0:T(8,128)(2,1)}, bf16[144,512]{1,0:T(8,128)(2,1)S(1)}, u32[]{:S(2)}, u32[]{:S(2)}) collective-permute-start(bf16[144,512]{1,0:T(8,128)(2,1)} %get-tuple-element.32), channel_id=1, source_target_pairs={{0,4},{1,5},{2,6},{3,7},{4,0},{5,1},{6,2},{7,3},{8,12},{9,13},{10,... | collective-permute-start | bytes 442376 | tf_op jit(solution)/shard_map/ppermute | solution.py:38
  10.4 1.5 %collective-permute-start.3 = (bf16[144,512]{1,0:T(8,128)(2,1)}, bf16[144,512]{1,0:T(8,128)(2,1)S(1)}, u32[]{:S(2)}, u32[]{:S(2)}) collective-permute-start(bf16[144,512]{1,0:T(8,128)(2,1)} %get-tuple-element.30.refs_2_), channel_id=1, source_target_pairs={{0,1},{1,0},{2,3},{3,2},{4,5},{5,4},{6,7},{7,6},{8,9},{9,8},{10,11... | collective-permute-start | bytes 442376 | tf_op jit(solution)/shard_map/ppermute | solution.py:38
  11.9 1.5 %collective-permute-done.refs_3_ = bf16[144,512]{1,0:T(8,128)(2,1)S(1)} collective-permute-done((bf16[144,512]{1,0:T(8,128)(2,1)}, bf16[144,512]{1,0:T(8,128)(2,1)S(1)}, u32[]{:S(2)}, u32[]{:S(2)}) %collective-permute-start) | collective-permute-done | bytes 147488 | tf_op jit(solution)/shard_map/ppermute | solution.py:38
  13.3 1.5 %collective-permute-start.4 = (bf16[144,512]{1,0:T(8,128)(2,1)S(1)}, bf16[144,512]{1,0:T(8,128)(2,1)S(1)}, u32[]{:S(2)}, u32[]{:S(2)}) collective-permute-start(bf16[144,512]{1,0:T(8,128)(2,1)S(1)} %collective-permute-done.refs_3_), channel_id=1, source_target_pairs={{0,1},{1,0},{2,3},{3,2},{4,5},{5,4},{6,7},{7,6},{8,9},{9,8},{10,11... | collective-permute-start | bytes 442376 | tf_op jit(solution)/shard_map/ppermute | solution.py:38
  14.8 6.8 %collective-permute-done.1.refs_1_.refs_4_ = bf16[144,512]{1,0:T(8,128)(2,1)S(1)} collective-permute-done((bf16[144,512]{1,0:T(8,128)(2,1)}, bf16[144,512]{1,0:T(8,128)(2,1)S(1)}, u32[]{:S(2)}, u32[]{:S(2)}) %collective-permute-start.1) | collective-permute-done | bytes 147488 | tf_op jit(solution)/shard_map/ppermute | solution.py:38
  22.2 1.5 %collective-permute-start.5 = (bf16[144,512]{1,0:T(8,128)(2,1)S(1)}, bf16[144,512]{1,0:T(8,128)(2,1)S(1)}, u32[]{:S(2)}, u32[]{:S(2)}) collective-permute-start(bf16[144,512]{1,0:T(8,128)(2,1)S(1)} %collective-permute-done.1.refs_1_.refs_4_), channel_id=1, source_target_pairs={{0,1},{1,0},{2,3},{3,2},{4,5},{5,4},{6,7},{7,6},{8,9},{9,8},{10,11... | collective-permute-start | bytes 442376 | tf_op jit(solution)/shard_map/ppermute | solution.py:38
  24.8 2.8 %collective-permute-start.10 = (bf16[128,128]{1,0:T(8,128)(2,1)S(1)}, bf16[128,128]{1,0:T(8,128)(2,1)S(1)}, u32[]{:S(2)}, u32[]{:S(2)}) collective-permute-start(bf16[128,128]{1,0:T(8,128)(2,1)S(1)} %get-tuple-element.35), channel_id=1, source_target_pairs={{0,4},{1,5},{2,6},{3,7},{4,0},{5,1},{6,2},{7,3},{8,12},{9,13},{10,... | collective-permute-start | bytes 98312 | tf_op jit(solution)/shard_map/ppermute | solution.py:38
  27.6 1.3 %collective-permute-start.11 = (bf16[128,128]{1,0:T(8,128)(2,1)S(1)}, bf16[128,128]{1,0:T(8,128)(2,1)S(1)}, u32[]{:S(2)}, u32[]{:S(2)}) collective-permute-start(bf16[128,128]{1,0:T(8,128)(2,1)S(1)} %get-tuple-element.36), channel_id=1, source_target_pairs={{0,6},{1,7},{2,4},{3,5},{4,2},{5,3},{6,0},{7,1},{8,14},{9,15},{10,... | collective-permute-start | bytes 98312 | tf_op jit(solution)/shard_map/ppermute | solution.py:38
  29.0 2.3 %collective-permute-done.6.refs_9_ = bf16[144,512]{1,0:T(8,128)(2,1)S(1)} collective-permute-done((bf16[144,512]{1,0:T(8,128)(2,1)S(1)}, bf16[144,512]{1,0:T(8,128)(2,1)S(1)}, u32[]{:S(2)}, u32[]{:S(2)}) %collective-permute-start.6) | collective-permute-done | bytes 147488 | tf_op jit(solution)/shard_map/ppermute | solution.py:38
  31.2 2.1 %collective-permute-done.11.refs_12_ = bf16[128,128]{1,0:T(8,128)(2,1)S(1)} collective-permute-done((bf16[128,128]{1,0:T(8,128)(2,1)S(1)}, bf16[128,128]{1,0:T(8,128)(2,1)S(1)}, u32[]{:S(2)}, u32[]{:S(2)}) %collective-permute-start.11) | collective-permute-done | bytes 32800 | tf_op jit(solution)/shard_map/ppermute | solution.py:38
  33.4 6.2 %shard_map.97 = (bf16[128,128]{1,0:T(8,128)(2,1)S(1)}, bf16[128,128]{1,0:T(8,128)(2,1)S(1)}, bf16[128,128]{1,0:T(8,128)(2,1)S(1)}, bf16[128,128]{1,0:T(8,128)(2,...) custom-call(s32[1,8]{1,0:T(1,128)S(1)} %copy-done.3, ...), custom_call_target="tpu_custom_call" | custom-call | tf_op jit(solution)/shard_map/pallas_call | solution.py:49
  39.6 2.2 %collective-permute-start.15 = (bf16[2,128,512]{2,1,0:T(8,128)(2,1)S(1)}, bf16[2,128,512]{2,1,0:T(8,128)(2,1)S(1)}, u32[]{:S(2)}, u32[]{:S(2)}) collective-permute-start(bf16[2,128,512]{2,1,0:T(8,128)(2,1)S(1)} %get-tuple-element.42), channel_id=1, source_target_pairs={{0,16},{8,24},{16,0},{24,8},{1,17},{9,25},{17,1},{25,9},{2,18},{10... | collective-permute-start | bytes 786440 | tf_op jit(solution)/shard_map/ppermute | solution.py:38
  41.8 1.0 %collective-permute-start.17 = (bf16[128,128]{1,0:T(8,128)(2,1)S(1)}, bf16[128,128]{1,0:T(8,128)(2,1)S(1)}, u32[]{:S(2)}, u32[]{:S(2)}) collective-permute-start(bf16[128,128]{1,0:T(8,128)(2,1)S(1)} %get-tuple-element.44), channel_id=1, source_target_pairs={{0,4},{1,5},{2,6},{3,7},{4,0},{5,1},{6,2},{7,3},{8,12},{9,13},{10,... | collective-permute-start | bytes 98312 | tf_op jit(solution)/shard_map/ppermute | solution.py:38
  42.8 1.4 %collective-permute-start.18 = (bf16[128,128]{1,0:T(8,128)(2,1)S(1)}, bf16[128,128]{1,0:T(8,128)(2,1)S(1)}, u32[]{:S(2)}, u32[]{:S(2)}) collective-permute-start(bf16[128,128]{1,0:T(8,128)(2,1)S(1)} %get-tuple-element.45), channel_id=1, source_target_pairs={{0,6},{1,7},{2,4},{3,5},{4,2},{5,3},{6,0},{7,1},{8,14},{9,15},{10,... | collective-permute-start | bytes 98312 | tf_op jit(solution)/shard_map/ppermute | solution.py:38
  44.2 1.1 %collective-permute-start.19 = (bf16[128,128]{1,0:T(8,128)(2,1)S(1)}, bf16[128,128]{1,0:T(8,128)(2,1)S(1)}, u32[]{:S(2)}, u32[]{:S(2)}) collective-permute-start(bf16[128,128]{1,0:T(8,128)(2,1)S(1)} %get-tuple-element.46), channel_id=1, source_target_pairs={{0,2},{1,3},{2,0},{3,1},{4,6},{5,7},{6,4},{7,5},{8,10},{9,11},{10,... | collective-permute-start | bytes 98312 | tf_op jit(solution)/shard_map/ppermute | solution.py:38
  45.3 1.3 %collective-permute-done.17.refs_1_ = bf16[128,128]{1,0:T(8,128)(2,1)S(1)} collective-permute-done((bf16[128,128]{1,0:T(8,128)(2,1)S(1)}, bf16[128,128]{1,0:T(8,128)(2,1)S(1)}, u32[]{:S(2)}, u32[]{:S(2)}) %collective-permute-start.17) | collective-permute-done | bytes 32800 | tf_op jit(solution)/shard_map/ppermute | solution.py:38
  46.6 1.9 %collective-permute-done.18.refs_2_ = bf16[128,128]{1,0:T(8,128)(2,1)S(1)} collective-permute-done((bf16[128,128]{1,0:T(8,128)(2,1)S(1)}, bf16[128,128]{1,0:T(8,128)(2,1)S(1)}, u32[]{:S(2)}, u32[]{:S(2)}) %collective-permute-start.18) | collective-permute-done | bytes 32800 | tf_op jit(solution)/shard_map/ppermute | solution.py:38
  49.4 4.3 %collective-permute-done.21.refs_6_ = bf16[128,512]{1,0:T(8,128)(2,1)S(1)} collective-permute-done((bf16[128,512]{1,0:T(8,128)(2,1)S(1)}, bf16[128,512]{1,0:T(8,128)(2,1)S(1)}, u32[]{:S(2)}, u32[]{:S(2)}) %collective-permute-start.21) | collective-permute-done | bytes 131104 | tf_op jit(solution)/shard_map/ppermute | solution.py:38
  53.7 1.3 %collective-permute-done.22.refs_7_ = bf16[128,512]{1,0:T(8,128)(2,1)S(1)} collective-permute-done((bf16[128,512]{1,0:T(8,128)(2,1)S(1)}, bf16[128,512]{1,0:T(8,128)(2,1)S(1)}, u32[]{:S(2)}, u32[]{:S(2)}) %collective-permute-start.22) | collective-permute-done | bytes 131104 | tf_op jit(solution)/shard_map/ppermute | solution.py:38
  55.8 1.3 %collective-permute-start.23 = (bf16[128,256]{1,0:T(8,128)(2,1)S(1)}, bf16[128,256]{1,0:T(8,128)(2,1)S(1)}, u32[]{:S(2)}, u32[]{:S(2)}) collective-permute-start(bf16[128,256]{1,0:T(8,128)(2,1)S(1)} %get-tuple-element.49), channel_id=1, source_target_pairs={{0,4},{1,5},{2,6},{3,7},{4,0},{5,1},{6,2},{7,3},{8,12},{9,13},{10,... | collective-permute-start | bytes 196616 | tf_op jit(solution)/shard_map/ppermute | solution.py:38
  57.1 1.8 %collective-permute-start.24 = (bf16[128,256]{1,0:T(8,128)(2,1)S(1)}, bf16[128,256]{1,0:T(8,128)(2,1)S(1)}, u32[]{:S(2)}, u32[]{:S(2)}) collective-permute-start(bf16[128,256]{1,0:T(8,128)(2,1)S(1)} %get-tuple-element.50), channel_id=1, source_target_pairs={{0,6},{1,7},{2,4},{3,5},{4,2},{5,3},{6,0},{7,1},{8,14},{9,15},{10,... | collective-permute-start | bytes 196616 | tf_op jit(solution)/shard_map/ppermute | solution.py:38
  59.3 4.6 %collective-permute-done.23.refs_1_.refs_2_ = bf16[128,256]{1,0:T(8,128)(2,1)S(1)} collective-permute-done((bf16[128,256]{1,0:T(8,128)(2,1)S(1)}, bf16[128,256]{1,0:T(8,128)(2,1)S(1)}, u32[]{:S(2)}, u32[]{:S(2)}) %collective-permute-start.23) | collective-permute-done | bytes 65568 | tf_op jit(solution)/shard_map/ppermute | solution.py:38
  64.0 1.3 %collective-permute-start.27 = (bf16[64,512]{1,0:T(8,128)(2,1)S(1)}, bf16[64,512]{1,0:T(8,128)(2,1)S(1)}, u32[]{:S(2)}, u32[]{:S(2)}) collective-permute-start(bf16[64,512]{1,0:T(8,128)(2,1)S(1)} %get-tuple-element.54), channel_id=1, source_target_pairs={{0,4},{1,5},{2,6},{3,7},{4,0},{5,1},{6,2},{7,3},{8,12},{9,13},{10,... | collective-permute-start | bytes 196616 | tf_op jit(solution)/shard_map/ppermute | solution.py:38
  65.3 1.8 %collective-permute-start.28 = (bf16[64,512]{1,0:T(8,128)(2,1)S(1)}, bf16[64,512]{1,0:T(8,128)(2,1)S(1)}, u32[]{:S(2)}, u32[]{:S(2)}) collective-permute-start(bf16[64,512]{1,0:T(8,128)(2,1)S(1)} %get-tuple-element.55), channel_id=1, source_target_pairs={{0,6},{1,7},{2,4},{3,5},{4,2},{5,3},{6,0},{7,1},{8,14},{9,15},{10,... | collective-permute-start | bytes 196616 | tf_op jit(solution)/shard_map/ppermute | solution.py:38
  67.6 1.6 %shard_map.102 = bf16[128,2048]{1,0:T(8,128)(2,1)} custom-call(bf16[128,512]{1,0:T(8,128)(2,1)S(1)} %shard_map.98.refs_4_.refs_0_, bf16[512,512]{1,0:T(8,128)(2,1)S(1)} %copy-done, bf16[512,512]{1,0:T(8,128)(2,1)S(1)} %collective-permute-done.7.refs_2_, bf16[512,512]{1,0:T(8,128)(2,1)S(1)} %shard_map.95.refs_3_, ...), custom_call_target="tpu_custom_call" | custom-call | tf_op jit(solution)/shard_map/pallas_call | solution.py:49
  69.2 0.7 %shard_map.101 = bf16[128,1024]{1,0:T(8,128)(2,1)} custom-call(bf16[128,256]{1,0:T(8,128)(2,1)S(1)} %get-tuple-element.48.refs_0_, bf16[128,256]{1,0:T(8,128)(2,1)S(1)} %collective-permute-done.23.refs_1_.refs_2_, bf16[128,256]{1,0:T(8,128)(2,1)S(1)} %collective-permute-done.24.refs_2_, bf16[128,256]{1,0:T(8,128)(2,1)S(1)} %collective-permute-done.25.refs_3_, ...), custom_call_target="tpu_custom_call" | custom-call | tf_op jit(solution)/shard_map/pallas_call | solution.py:49
  69.9 2.0 %collective-permute-done.27.refs_1_ = bf16[64,512]{1,0:T(8,128)(2,1)S(1)} collective-permute-done((bf16[64,512]{1,0:T(8,128)(2,1)S(1)}, bf16[64,512]{1,0:T(8,128)(2,1)S(1)}, u32[]{:S(2)}, u32[]{:S(2)}) %collective-permute-start.27) | collective-permute-done | bytes 65568 | tf_op jit(solution)/shard_map/ppermute | solution.py:38
  71.9 0.6 collective-permute-done.29.refs_3_
  72.5 0.7 shard_map.104
  (48 shorter events, 4.6 us)
Async XLA Ops:
  0.6 21.0 %copy-start = (bf16[512,512]{1,0:T(8,128)(2,1)S(1)}, bf16[512,512]{1,0:T(8,128)(2,1)}, u32[]{:S(2)}) copy-start(bf16[512,512]{1,0:T(8,128)(2,1)} %refs_1_.3) | copy-start | bytes 1572868
  0.6 21.0 %collective-permute-start.8 = (bf16[512,512]{1,0:T(8,128)(2,1)}, bf16[512,512]{1,0:T(8,128)(2,1)S(1)}, u32[]{:S(2)}, u32[]{:S(2)}) collective-permute-start(bf16[512,512]{1,0:T(8,128)(2,1)} %refs_1_.3), channel_id=1, source_target_pairs={{0,16},{8,24},{16,0},{24,8},{1,17},{9,25},{17,1},{25,9},{2,18},{10... | collective-permute-start | bytes 1572872 | tf_op jit(solution)/shard_map/ppermute | solution.py:38
  5.9 7.4 %collective-permute-start = (bf16[144,512]{1,0:T(8,128)(2,1)}, bf16[144,512]{1,0:T(8,128)(2,1)S(1)}, u32[]{:S(2)}, u32[]{:S(2)}) collective-permute-start(bf16[144,512]{1,0:T(8,128)(2,1)} %get-tuple-element.31), channel_id=1, source_target_pairs={{0,2},{1,3},{2,0},{3,1},{4,6},{5,7},{6,4},{7,5},{8,10},{9,11},{10,... | collective-permute-start | bytes 442376 | tf_op jit(solution)/shard_map/ppermute | solution.py:38
  7.5 14.1 %collective-permute-start.1 = (bf16[144,512]{1,0:T(8,128)(2,1)}, bf16[144,512]{1,0:T(8,128)(2,1)S(1)}, u32[]{:S(2)}, u32[]{:S(2)}) collective-permute-start(bf16[144,512]{1,0:T(8,128)(2,1)} %get-tuple-element.32), channel_id=1, source_target_pairs={{0,4},{1,5},{2,6},{3,7},{4,0},{5,1},{6,2},{7,3},{8,12},{9,13},{10,... | collective-permute-start | bytes 442376 | tf_op jit(solution)/shard_map/ppermute | solution.py:38
  10.1 11.5 %collective-permute-start.2 = (bf16[144,512]{1,0:T(8,128)(2,1)}, bf16[144,512]{1,0:T(8,128)(2,1)S(1)}, u32[]{:S(2)}, u32[]{:S(2)}) collective-permute-start(bf16[144,512]{1,0:T(8,128)(2,1)} %get-tuple-element.33), channel_id=1, source_target_pairs={{0,6},{1,7},{2,4},{3,5},{4,2},{5,3},{6,0},{7,1},{8,14},{9,15},{10,... | collective-permute-start | bytes 442376 | tf_op jit(solution)/shard_map/ppermute | solution.py:38
  10.4 13.9 %copy-start.1 = (bf16[1,128,2048]{2,1,0:T(8,128)(2,1)S(1)}, bf16[1,128,2048]{2,1,0:T(8,128)(2,1)}, u32[]{:S(2)}) copy-start(bf16[1,128,2048]{2,1,0:T(8,128)(2,1)} %param.7) | copy-start | bytes 1572868
  10.4 11.3 %collective-permute-start.3 = (bf16[144,512]{1,0:T(8,128)(2,1)}, bf16[144,512]{1,0:T(8,128)(2,1)S(1)}, u32[]{:S(2)}, u32[]{:S(2)}) collective-permute-start(bf16[144,512]{1,0:T(8,128)(2,1)} %get-tuple-element.30.refs_2_), channel_id=1, source_target_pairs={{0,1},{1,0},{2,3},{3,2},{4,5},{5,4},{6,7},{7,6},{8,9},{9,8},{10,11... | collective-permute-start | bytes 442376 | tf_op jit(solution)/shard_map/ppermute | solution.py:38
  13.3 8.3 %collective-permute-start.4 = (bf16[144,512]{1,0:T(8,128)(2,1)S(1)}, bf16[144,512]{1,0:T(8,128)(2,1)S(1)}, u32[]{:S(2)}, u32[]{:S(2)}) collective-permute-start(bf16[144,512]{1,0:T(8,128)(2,1)S(1)} %collective-permute-done.refs_3_), channel_id=1, source_target_pairs={{0,1},{1,0},{2,3},{3,2},{4,5},{5,4},{6,7},{7,6},{8,9},{9,8},{10,11... | collective-permute-start | bytes 442376 | tf_op jit(solution)/shard_map/ppermute | solution.py:38
  21.6 2.6 %collective-permute-start.7 = (bf16[512,512]{1,0:T(8,128)(2,1)S(1)}, bf16[512,512]{1,0:T(8,128)(2,1)S(1)}, u32[]{:S(2)}, u32[]{:S(2)}) collective-permute-start(bf16[512,512]{1,0:T(8,128)(2,1)S(1)} %copy-done), channel_id=1, source_target_pairs={{0,8},{8,0},{16,24},{24,16},{1,9},{9,1},{17,25},{25,17},{2,10},{10... | collective-permute-start | bytes 1572872 | tf_op jit(solution)/shard_map/ppermute | solution.py:38
  21.7 2.6 %collective-permute-start.9 = (bf16[512,512]{1,0:T(8,128)(2,1)S(1)}, bf16[512,512]{1,0:T(8,128)(2,1)S(1)}, u32[]{:S(2)}, u32[]{:S(2)}) collective-permute-start(bf16[512,512]{1,0:T(8,128)(2,1)S(1)} %shard_map.95.refs_3_), channel_id=1, source_target_pairs={{0,8},{8,0},{16,24},{24,16},{1,9},{9,1},{17,25},{25,17},{2,10},{10... | collective-permute-start | bytes 1572872 | tf_op jit(solution)/shard_map/ppermute | solution.py:38
  22.2 6.7 %collective-permute-start.5 = (bf16[144,512]{1,0:T(8,128)(2,1)S(1)}, bf16[144,512]{1,0:T(8,128)(2,1)S(1)}, u32[]{:S(2)}, u32[]{:S(2)}) collective-permute-start(bf16[144,512]{1,0:T(8,128)(2,1)S(1)} %collective-permute-done.1.refs_1_.refs_4_), channel_id=1, source_target_pairs={{0,1},{1,0},{2,3},{3,2},{4,5},{5,4},{6,7},{7,6},{8,9},{9,8},{10,11... | collective-permute-start | bytes 442376 | tf_op jit(solution)/shard_map/ppermute | solution.py:38
  23.7 7.5 %collective-permute-start.6 = (bf16[144,512]{1,0:T(8,128)(2,1)S(1)}, bf16[144,512]{1,0:T(8,128)(2,1)S(1)}, u32[]{:S(2)}, u32[]{:S(2)}) collective-permute-start(bf16[144,512]{1,0:T(8,128)(2,1)S(1)} %collective-permute-done.2.refs_2_.refs_5_), channel_id=1, source_target_pairs={{0,1},{1,0},{2,3},{3,2},{4,5},{5,4},{6,7},{7,6},{8,9},{9,8},{10,11... | collective-permute-start | bytes 442376 | tf_op jit(solution)/shard_map/ppermute | solution.py:38
  24.8 6.4 %collective-permute-start.10 = (bf16[128,128]{1,0:T(8,128)(2,1)S(1)}, bf16[128,128]{1,0:T(8,128)(2,1)S(1)}, u32[]{:S(2)}, u32[]{:S(2)}) collective-permute-start(bf16[128,128]{1,0:T(8,128)(2,1)S(1)} %get-tuple-element.35), channel_id=1, source_target_pairs={{0,4},{1,5},{2,6},{3,7},{4,0},{5,1},{6,2},{7,3},{8,12},{9,13},{10,... | collective-permute-start | bytes 98312 | tf_op jit(solution)/shard_map/ppermute | solution.py:38
  27.6 5.7 %collective-permute-start.11 = (bf16[128,128]{1,0:T(8,128)(2,1)S(1)}, bf16[128,128]{1,0:T(8,128)(2,1)S(1)}, u32[]{:S(2)}, u32[]{:S(2)}) collective-permute-start(bf16[128,128]{1,0:T(8,128)(2,1)S(1)} %get-tuple-element.36), channel_id=1, source_target_pairs={{0,6},{1,7},{2,4},{3,5},{4,2},{5,3},{6,0},{7,1},{8,14},{9,15},{10,... | collective-permute-start | bytes 98312 | tf_op jit(solution)/shard_map/ppermute | solution.py:38
  29.0 4.4 %collective-permute-start.12 = (bf16[128,128]{1,0:T(8,128)(2,1)S(1)}, bf16[128,128]{1,0:T(8,128)(2,1)S(1)}, u32[]{:S(2)}, u32[]{:S(2)}) collective-permute-start(bf16[128,128]{1,0:T(8,128)(2,1)S(1)} %get-tuple-element.37), channel_id=1, source_target_pairs={{0,2},{1,3},{2,0},{3,1},{4,6},{5,7},{6,4},{7,5},{8,10},{9,11},{10,... | collective-permute-start | bytes 98312 | tf_op jit(solution)/shard_map/ppermute | solution.py:38
  39.6 9.0 %collective-permute-start.13 = (bf16[4,128,256]{2,1,0:T(8,128)(2,1)S(1)}, bf16[4,128,256]{2,1,0:T(8,128)(2,1)S(1)}, u32[]{:S(2)}, u32[]{:S(2)}) collective-permute-start(bf16[4,128,256]{2,1,0:T(8,128)(2,1)S(1)} %get-tuple-element.39), channel_id=1, source_target_pairs={{0,1},{1,0},{2,3},{3,2},{4,5},{5,4},{6,7},{7,6},{8,9},{9,8},{10,11... | collective-permute-start | bytes 786440 | tf_op jit(solution)/shard_map/ppermute | solution.py:38
  39.6 9.2 %collective-permute-start.15 = (bf16[2,128,512]{2,1,0:T(8,128)(2,1)S(1)}, bf16[2,128,512]{2,1,0:T(8,128)(2,1)S(1)}, u32[]{:S(2)}, u32[]{:S(2)}) collective-permute-start(bf16[2,128,512]{2,1,0:T(8,128)(2,1)S(1)} %get-tuple-element.42), channel_id=1, source_target_pairs={{0,16},{8,24},{16,0},{24,8},{1,17},{9,25},{17,1},{25,9},{2,18},{10... | collective-permute-start | bytes 786440 | tf_op jit(solution)/shard_map/ppermute | solution.py:38
  41.8 4.8 %collective-permute-start.17 = (bf16[128,128]{1,0:T(8,128)(2,1)S(1)}, bf16[128,128]{1,0:T(8,128)(2,1)S(1)}, u32[]{:S(2)}, u32[]{:S(2)}) collective-permute-start(bf16[128,128]{1,0:T(8,128)(2,1)S(1)} %get-tuple-element.44), channel_id=1, source_target_pairs={{0,4},{1,5},{2,6},{3,7},{4,0},{5,1},{6,2},{7,3},{8,12},{9,13},{10,... | collective-permute-start | bytes 98312 | tf_op jit(solution)/shard_map/ppermute | solution.py:38
  42.8 5.7 %collective-permute-start.18 = (bf16[128,128]{1,0:T(8,128)(2,1)S(1)}, bf16[128,128]{1,0:T(8,128)(2,1)S(1)}, u32[]{:S(2)}, u32[]{:S(2)}) collective-permute-start(bf16[128,128]{1,0:T(8,128)(2,1)S(1)} %get-tuple-element.45), channel_id=1, source_target_pairs={{0,6},{1,7},{2,4},{3,5},{4,2},{5,3},{6,0},{7,1},{8,14},{9,15},{10,... | collective-permute-start | bytes 98312 | tf_op jit(solution)/shard_map/ppermute | solution.py:38
  44.2 4.4 %collective-permute-start.19 = (bf16[128,128]{1,0:T(8,128)(2,1)S(1)}, bf16[128,128]{1,0:T(8,128)(2,1)S(1)}, u32[]{:S(2)}, u32[]{:S(2)}) collective-permute-start(bf16[128,128]{1,0:T(8,128)(2,1)S(1)} %get-tuple-element.46), channel_id=1, source_target_pairs={{0,2},{1,3},{2,0},{3,1},{4,6},{5,7},{6,4},{7,5},{8,10},{9,11},{10,... | collective-permute-start | bytes 98312 | tf_op jit(solution)/shard_map/ppermute | solution.py:38
  46.6 7.1 %collective-permute-start.14 = (bf16[128,512]{1,0:T(8,128)(2,1)S(1)}, bf16[128,512]{1,0:T(8,128)(2,1)S(1)}, u32[]{:S(2)}, u32[]{:S(2)}) collective-permute-start(bf16[128,512]{1,0:T(8,128)(2,1)S(1)} %get-tuple-element.41), channel_id=1, source_target_pairs={{0,8},{8,0},{16,24},{24,16},{1,9},{9,1},{17,25},{25,17},{2,10},{10... | collective-permute-start | bytes 393224 | tf_op jit(solution)/shard_map/ppermute | solution.py:38
  48.6 5.0 %collective-permute-start.21 = (bf16[128,512]{1,0:T(8,128)(2,1)S(1)}, bf16[128,512]{1,0:T(8,128)(2,1)S(1)}, u32[]{:S(2)}, u32[]{:S(2)}) collective-permute-start(bf16[128,512]{1,0:T(8,128)(2,1)S(1)} %shard_map.98.refs_4_.refs_0_), channel_id=1, source_target_pairs={{0,16},{8,24},{16,0},{24,8},{1,17},{9,25},{17,1},{25,9},{2,18},{10... | collective-permute-start | bytes 393224 | tf_op jit(solution)/shard_map/ppermute | solution.py:38
  48.7 5.0 %collective-permute-start.20 = (bf16[128,512]{1,0:T(8,128)(2,1)S(1)}, bf16[128,512]{1,0:T(8,128)(2,1)S(1)}, u32[]{:S(2)}, u32[]{:S(2)}) collective-permute-start(bf16[128,512]{1,0:T(8,128)(2,1)S(1)} %shard_map.98.refs_4_.refs_0_), channel_id=1, source_target_pairs={{0,8},{8,0},{16,24},{24,16},{1,9},{9,1},{17,25},{25,17},{2,10},{10... | collective-permute-start | bytes 393224 | tf_op jit(solution)/shard_map/ppermute | solution.py:38
  48.8 4.9 %collective-permute-start.16 = (bf16[128,512]{1,0:T(8,128)(2,1)S(1)}, bf16[128,512]{1,0:T(8,128)(2,1)S(1)}, u32[]{:S(2)}, u32[]{:S(2)}) collective-permute-start(bf16[128,512]{1,0:T(8,128)(2,1)S(1)} %get-tuple-element.57), channel_id=1, source_target_pairs={{0,8},{8,0},{16,24},{24,16},{1,9},{9,1},{17,25},{25,17},{2,10},{10... | collective-permute-start | bytes 393224 | tf_op jit(solution)/shard_map/ppermute | solution.py:38
  53.7 1.3 %collective-permute-start.22 = (bf16[128,512]{1,0:T(8,128)(2,1)S(1)}, bf16[128,512]{1,0:T(8,128)(2,1)S(1)}, u32[]{:S(2)}, u32[]{:S(2)}) collective-permute-start(bf16[128,512]{1,0:T(8,128)(2,1)S(1)} %collective-permute-done.21.refs_6_), channel_id=1, source_target_pairs={{0,8},{8,0},{16,24},{24,16},{1,9},{9,1},{17,25},{25,17},{2,10},{10... | collective-permute-start | bytes 393224 | tf_op jit(solution)/shard_map/ppermute | solution.py:38
  55.6 8.4 %collective-permute-start.26 = (bf16[4,64,512]{2,1,0:T(8,128)(2,1)S(1)}, bf16[4,64,512]{2,1,0:T(8,128)(2,1)S(1)}, u32[]{:S(2)}, u32[]{:S(2)}) collective-permute-start(bf16[4,64,512]{2,1,0:T(8,128)(2,1)S(1)} %get-tuple-element.52), channel_id=1, source_target_pairs={{0,1},{1,0},{2,3},{3,2},{4,5},{5,4},{6,7},{7,6},{8,9},{9,8},{10,11... | collective-permute-start | bytes 786440 | tf_op jit(solution)/shard_map/ppermute | solution.py:38
  55.8 8.1 %collective-permute-start.23 = (bf16[128,256]{1,0:T(8,128)(2,1)S(1)}, bf16[128,256]{1,0:T(8,128)(2,1)S(1)}, u32[]{:S(2)}, u32[]{:S(2)}) collective-permute-start(bf16[128,256]{1,0:T(8,128)(2,1)S(1)} %get-tuple-element.49), channel_id=1, source_target_pairs={{0,4},{1,5},{2,6},{3,7},{4,0},{5,1},{6,2},{7,3},{8,12},{9,13},{10,... | collective-permute-start | bytes 196616 | tf_op jit(solution)/shard_map/ppermute | solution.py:38
  57.1 12.1 %collective-permute-start.24 = (bf16[128,256]{1,0:T(8,128)(2,1)S(1)}, bf16[128,256]{1,0:T(8,128)(2,1)S(1)}, u32[]{:S(2)}, u32[]{:S(2)}) collective-permute-start(bf16[128,256]{1,0:T(8,128)(2,1)S(1)} %get-tuple-element.50), channel_id=1, source_target_pairs={{0,6},{1,7},{2,4},{3,5},{4,2},{5,3},{6,0},{7,1},{8,14},{9,15},{10,... | collective-permute-start | bytes 196616 | tf_op jit(solution)/shard_map/ppermute | solution.py:38
  58.9 10.3 %collective-permute-start.25 = (bf16[128,256]{1,0:T(8,128)(2,1)S(1)}, bf16[128,256]{1,0:T(8,128)(2,1)S(1)}, u32[]{:S(2)}, u32[]{:S(2)}) collective-permute-start(bf16[128,256]{1,0:T(8,128)(2,1)S(1)} %get-tuple-element.51), channel_id=1, source_target_pairs={{0,2},{1,3},{2,0},{3,1},{4,6},{5,7},{6,4},{7,5},{8,10},{9,11},{10,... | collective-permute-start | bytes 196616 | tf_op jit(solution)/shard_map/ppermute | solution.py:38
  64.0 7.9 %collective-permute-start.27 = (bf16[64,512]{1,0:T(8,128)(2,1)S(1)}, bf16[64,512]{1,0:T(8,128)(2,1)S(1)}, u32[]{:S(2)}, u32[]{:S(2)}) collective-permute-start(bf16[64,512]{1,0:T(8,128)(2,1)S(1)} %get-tuple-element.54), channel_id=1, source_target_pairs={{0,4},{1,5},{2,6},{3,7},{4,0},{5,1},{6,2},{7,3},{8,12},{9,13},{10,... | collective-permute-start | bytes 196616 | tf_op jit(solution)/shard_map/ppermute | solution.py:38
  65.3 6.6 %collective-permute-start.28 = (bf16[64,512]{1,0:T(8,128)(2,1)S(1)}, bf16[64,512]{1,0:T(8,128)(2,1)S(1)}, u32[]{:S(2)}, u32[]{:S(2)}) collective-permute-start(bf16[64,512]{1,0:T(8,128)(2,1)S(1)} %get-tuple-element.55), channel_id=1, source_target_pairs={{0,6},{1,7},{2,4},{3,5},{4,2},{5,3},{6,0},{7,1},{8,14},{9,15},{10,... | collective-permute-start | bytes 196616 | tf_op jit(solution)/shard_map/ppermute | solution.py:38
  67.2 5.3 %collective-permute-start.29 = (bf16[64,512]{1,0:T(8,128)(2,1)S(1)}, bf16[64,512]{1,0:T(8,128)(2,1)S(1)}, u32[]{:S(2)}, u32[]{:S(2)}) collective-permute-start(bf16[64,512]{1,0:T(8,128)(2,1)S(1)} %get-tuple-element.56), channel_id=1, source_target_pairs={{0,2},{1,3},{2,0},{3,1},{4,6},{5,7},{6,4},{7,5},{8,10},{9,11},{10,... | collective-permute-start | bytes 196616 | tf_op jit(solution)/shard_map/ppermute | solution.py:38
  (2 other events, 13.4 us)

commit v3 on v2

--- a/solution.py
+++ b/solution.py
@@ -233,7 +233,7 @@
     head, side = head_side()
     near = [order_ref[0, 2 * jnp.bitwise_xor(head, m) + side] for m in range(KV_HEADS)]
     far = [order_ref[0, 2 * jnp.bitwise_xor(head, m) + 1 - side] for m in range(KV_HEADS)]
-    for place, ref in zip(near + far, qd_refs):
+    for place, ref in zip(near + far, by_head(qd_refs[:KV_HEADS]) + list(qd_refs[KV_HEADS:])):
         for pair in range(PAIRS):
             q_all[pair, place] = ref[0:rows, pair * PAIR:(pair + 1) * PAIR]
             go_all[pair, place] = ref[0:rows, GROUP + pair * PAIR:GROUP + (pair + 1) * PAIR]
@@ -402,7 +402,7 @@
         (queries[0], grad_out[0], attn_out[0], log_sums[0]), hbm=4)
     qd = along_heads(qd)
     turned = [swapped(one, "ctx", 1) for one in qd[:2]]
-    w_far = held(swapped(w_kv, "fsdp", far), (*far_first(qd[:KV_HEADS])[1:], *turned))
+    w_far = held(swapped(w_kv, "fsdp", far), (*far_first(qd[:KV_HEADS])[1:], turned[0]))
     w_parts = over_fsdp([w_kv] * far + [w_far] * (fsdp - far), far // 2)
 
     kv = call(
@@ -420,7 +420,7 @@
             [pltpu.VMEM((PAIRS, TEAM) + block, jnp.bfloat16)] * 2 + [pltpu.VMEM((TEAM, 2 * GROUPS, rows), f32)]
             + [pltpu.VMEM((TEAM, 2 * rows, PAIR), jnp.bfloat16)] * 2
             + [pltpu.VMEM((PAIRS, TEAM) + block, f32), pltpu.VMEM((TEAM,) + block, f32), cut_sems],
-            (block_order, inputs, *qd, *far_first(kv)), smem=1, hbm=1)
+            (block_order, inputs, *far_first(qd[:KV_HEADS]), *qd[KV_HEADS:], *far_first(kv)), smem=1, hbm=1)
         dkv, (keep, give, *hid, hid_far) = outs[:KV_HEADS], outs[KV_HEADS:]
     else:
         alike = [[t * TEAM + i for t in range(teams)] for i in range(TEAM)]
@@ -449,7 +449,7 @@
         dq = along_heads(call(pair_kernel, [sds(wide)] * KV_HEADS, [], (keep, give), after=formed))
         sums = call(
             pair_kernel, [sds(share, f32)] + [sds(share)] * (KV_HEADS - 1), [],
-            (own_sums, swapped(send_sums, "ctx", 1)), after=dq[2:3])
+            (own_sums, swapped(send_sums, "ctx", 1)), after=dq[1:2])
         (weight_grads,) = call(own_total_kernel, [sds(share, f32)], [], far_first(along_heads(sums)))
     else:
         formed = call(functools.partial(weight_kernel, fsdp), [sds((span, columns))], [], (*hid, *grads))

time: 72.8 us -> 74.3 us (1.021); the launches traced: 73.2 us -> 73.7 us
  starting transfers between devices: 30.9 us -> 33.2 us
  waiting for transfers between devices: 28.7 us -> 26.8 us
    ppermute x30, starting transfers between devices: 30.9 us -> 33.2 us  [swapped(): return lax.ppermute(array, axis, [(i, i ^ bits) for i in range(size)])]
    ppermute x30, waiting for transfers between devices: 28.7 us -> 26.8 us  [swapped(): return lax.ppermute(array, axis, [(i, i ^ bits) for i in range(size)])]
  transfers between devices with their start and end apart: 30 -> 30, of which waited for: 12 -> 13; matrix products, arithmetic and copies ran while one was open for 0% -> 0% of each run, Pallas kernels for 7% -> 7%
where the time goes in v3:
time: 74.3 us; the launch traced here: 73.7 us
  starting transfers between devices  33.2 us (45%)
  waiting for transfers between devices  26.8 us (36%)
  Pallas kernels  12.8 us (17%)
  between operations  0.77 us (1%)
    ppermute x30, starting transfers between devices, swapped(): return lax.ppermute(array, axis, [(i, i ^ bits) for i in range(size)])  33.2 us
    ppermute x30, waiting for transfers between devices, swapped(): return lax.ppermute(array, axis, [(i, i ^ bits) for i in range(size)])  26.8 us
    pallas_call x10, Pallas kernels, call(): pl.pallas_call(body, out_shape=out_shape, in_specs=specs, out_specs=[VMEM...  12.8 us
  transfers between devices with their start and end apart: 30, of which 13 were waited for; matrix products, arithmetic and copies ran while one was open for 0% of the time, Pallas kernels for 7%

profile of v3, /device:TPU:0, one launch (start us, length us, event | category | flops | bytes accessed | tf_op | source)
XLA Modules:
  0.0 73.7 jit_solution(18302216014823755176)
XLA Ops:
  0.6 3.0 %collective-permute-start.8 = (bf16[512,512]{1,0:T(8,128)(2,1)}, bf16[512,512]{1,0:T(8,128)(2,1)S(1)}, u32[]{:S(2)}, u32[]{:S(2)}) collective-permute-start(bf16[512,512]{1,0:T(8,128)(2,1)} %refs_1_.3), channel_id=1, source_target_pairs={{0,16},{8,24},{16,0},{24,8},{1,17},{9,25},{17,1},{25,9},{2,18},{10... | collective-permute-start | bytes 1572872 | tf_op jit(solution)/shard_map/ppermute | solution.py:38
  3.7 2.2 %shard_map.94 = (bf16[144,512]{1,0:T(8,128)(2,1)}, bf16[144,512]{1,0:T(8,128)(2,1)}, bf16[144,512]{1,0:T(8,128)(2,1)}, bf16[144,512]{1,0:T(8,128)(2,1)}) custom-call(bf16[128,1024]{1,0:T(8,128)(2,1)} %bitcast.14, bf16[128,1024]{1,0:T(8,128)(2,1)} %bitcast.15, bf16[128,1024]{1,0:T(8,128)(2,1)} %bitcast.16, f32[16,128]{1,0:T(8,128)} %bitcast.18), custom_call_target="tpu_custom_call" | custom-call | tf_op jit(solution)/shard_map/pallas_call | solution.py:49
  5.9 2.7 %collective-permute-start = (bf16[144,512]{1,0:T(8,128)(2,1)}, bf16[144,512]{1,0:T(8,128)(2,1)S(1)}, u32[]{:S(2)}, u32[]{:S(2)}) collective-permute-start(bf16[144,512]{1,0:T(8,128)(2,1)} %get-tuple-element.31), channel_id=1, source_target_pairs={{0,4},{1,5},{2,6},{3,7},{4,0},{5,1},{6,2},{7,3},{8,12},{9,13},{10,... | collective-permute-start | bytes 442376 | tf_op jit(solution)/shard_map/ppermute | solution.py:38
  8.6 1.3 %collective-permute-start.1 = (bf16[144,512]{1,0:T(8,128)(2,1)}, bf16[144,512]{1,0:T(8,128)(2,1)S(1)}, u32[]{:S(2)}, u32[]{:S(2)}) collective-permute-start(bf16[144,512]{1,0:T(8,128)(2,1)} %get-tuple-element.32), channel_id=1, source_target_pairs={{0,6},{1,7},{2,4},{3,5},{4,2},{5,3},{6,0},{7,1},{8,14},{9,15},{10,... | collective-permute-start | bytes 442376 | tf_op jit(solution)/shard_map/ppermute | solution.py:38
  10.1 1.5 %collective-permute-start.3 = (bf16[144,512]{1,0:T(8,128)(2,1)}, bf16[144,512]{1,0:T(8,128)(2,1)S(1)}, u32[]{:S(2)}, u32[]{:S(2)}) collective-permute-start(bf16[144,512]{1,0:T(8,128)(2,1)} %get-tuple-element.30.refs_2_), channel_id=1, source_target_pairs={{0,1},{1,0},{2,3},{3,2},{4,5},{5,4},{6,7},{7,6},{8,9},{9,8},{10,11... | collective-permute-start | bytes 442376 | tf_op jit(solution)/shard_map/ppermute | solution.py:38
  11.6 8.2 %collective-permute-done.refs_1_.refs_3_ = bf16[144,512]{1,0:T(8,128)(2,1)S(1)} collective-permute-done((bf16[144,512]{1,0:T(8,128)(2,1)}, bf16[144,512]{1,0:T(8,128)(2,1)S(1)}, u32[]{:S(2)}, u32[]{:S(2)}) %collective-permute-start) | collective-permute-done | bytes 147488 | tf_op jit(solution)/shard_map/ppermute | solution.py:38
  20.5 1.5 %collective-permute-start.5 = (bf16[144,512]{1,0:T(8,128)(2,1)S(1)}, bf16[144,512]{1,0:T(8,128)(2,1)S(1)}, u32[]{:S(2)}, u32[]{:S(2)}) collective-permute-start(bf16[144,512]{1,0:T(8,128)(2,1)S(1)} %collective-permute-done.refs_1_.refs_3_), channel_id=1, source_target_pairs={{0,1},{1,0},{2,3},{3,2},{4,5},{5,4},{6,7},{7,6},{8,9},{9,8},{10,11... | collective-permute-start | bytes 442376 | tf_op jit(solution)/shard_map/ppermute | solution.py:38
  22.5 1.5 %collective-permute-start.4 = (bf16[144,512]{1,0:T(8,128)(2,1)S(1)}, bf16[144,512]{1,0:T(8,128)(2,1)S(1)}, u32[]{:S(2)}, u32[]{:S(2)}) collective-permute-start(bf16[144,512]{1,0:T(8,128)(2,1)S(1)} %collective-permute-done.2.refs_3_.refs_5_), channel_id=1, source_target_pairs={{0,1},{1,0},{2,3},{3,2},{4,5},{5,4},{6,7},{7,6},{8,9},{9,8},{10,11... | collective-permute-start | bytes 442376 | tf_op jit(solution)/shard_map/ppermute | solution.py:38
  24.0 0.6 shard_map.96
  24.6 4.2 %collective-permute-start.10 = (bf16[128,128]{1,0:T(8,128)(2,1)S(1)}, bf16[128,128]{1,0:T(8,128)(2,1)S(1)}, u32[]{:S(2)}, u32[]{:S(2)}) collective-permute-start(bf16[128,128]{1,0:T(8,128)(2,1)S(1)} %get-tuple-element.35), channel_id=1, source_target_pairs={{0,4},{1,5},{2,6},{3,7},{4,0},{5,1},{6,2},{7,3},{8,12},{9,13},{10,... | collective-permute-start | bytes 98312 | tf_op jit(solution)/shard_map/ppermute | solution.py:38
  29.5 0.8 %collective-permute-done.6.refs_9_ = bf16[144,512]{1,0:T(8,128)(2,1)S(1)} collective-permute-done((bf16[144,512]{1,0:T(8,128)(2,1)S(1)}, bf16[144,512]{1,0:T(8,128)(2,1)S(1)}, u32[]{:S(2)}, u32[]{:S(2)}) %collective-permute-start.6) | collective-permute-done | bytes 147488 | tf_op jit(solution)/shard_map/ppermute | solution.py:38
  30.3 2.4 %collective-permute-done.4.refs_7_ = bf16[144,512]{1,0:T(8,128)(2,1)S(1)} collective-permute-done((bf16[144,512]{1,0:T(8,128)(2,1)S(1)}, bf16[144,512]{1,0:T(8,128)(2,1)S(1)}, u32[]{:S(2)}, u32[]{:S(2)}) %collective-permute-start.4) | collective-permute-done | bytes 147488 | tf_op jit(solution)/shard_map/ppermute | solution.py:38
  32.8 1.8 %collective-permute-done.11.refs_12_ = bf16[128,128]{1,0:T(8,128)(2,1)S(1)} collective-permute-done((bf16[128,128]{1,0:T(8,128)(2,1)S(1)}, bf16[128,128]{1,0:T(8,128)(2,1)S(1)}, u32[]{:S(2)}, u32[]{:S(2)}) %collective-permute-start.11) | collective-permute-done | bytes 32800 | tf_op jit(solution)/shard_map/ppermute | solution.py:38
  34.6 6.3 %shard_map.97 = (bf16[128,128]{1,0:T(8,128)(2,1)S(1)}, bf16[128,128]{1,0:T(8,128)(2,1)S(1)}, bf16[128,128]{1,0:T(8,128)(2,1)S(1)}, bf16[128,128]{1,0:T(8,128)(2,...) custom-call(s32[1,8]{1,0:T(1,128)S(1)} %copy-done.3, ...), custom_call_target="tpu_custom_call" | custom-call | tf_op jit(solution)/shard_map/pallas_call | solution.py:49
  41.1 3.1 %collective-permute-start.17 = (bf16[128,128]{1,0:T(8,128)(2,1)S(1)}, bf16[128,128]{1,0:T(8,128)(2,1)S(1)}, u32[]{:S(2)}, u32[]{:S(2)}) collective-permute-start(bf16[128,128]{1,0:T(8,128)(2,1)S(1)} %get-tuple-element.44), channel_id=1, source_target_pairs={{0,4},{1,5},{2,6},{3,7},{4,0},{5,1},{6,2},{7,3},{8,12},{9,13},{10,... | collective-permute-start | bytes 98312 | tf_op jit(solution)/shard_map/ppermute | solution.py:38
  44.7 1.3 %collective-permute-done.17.refs_1_ = bf16[128,128]{1,0:T(8,128)(2,1)S(1)} collective-permute-done((bf16[128,128]{1,0:T(8,128)(2,1)S(1)}, bf16[128,128]{1,0:T(8,128)(2,1)S(1)}, u32[]{:S(2)}, u32[]{:S(2)}) %collective-permute-start.17) | collective-permute-done | bytes 32800 | tf_op jit(solution)/shard_map/ppermute | solution.py:38
  46.1 3.8 %collective-permute-done.18.refs_2_ = bf16[128,128]{1,0:T(8,128)(2,1)S(1)} collective-permute-done((bf16[128,128]{1,0:T(8,128)(2,1)S(1)}, bf16[128,128]{1,0:T(8,128)(2,1)S(1)}, u32[]{:S(2)}, u32[]{:S(2)}) %collective-permute-start.18) | collective-permute-done | bytes 32800 | tf_op jit(solution)/shard_map/ppermute | solution.py:38
  50.0 1.6 %collective-permute-start.21 = (bf16[128,512]{1,0:T(8,128)(2,1)S(1)}, bf16[128,512]{1,0:T(8,128)(2,1)S(1)}, u32[]{:S(2)}, u32[]{:S(2)}) collective-permute-start(bf16[128,512]{1,0:T(8,128)(2,1)S(1)} %shard_map.98.refs_4_.refs_0_), channel_id=1, source_target_pairs={{0,16},{8,24},{16,0},{24,8},{1,17},{9,25},{17,1},{25,9},{2,18},{10... | collective-permute-start | bytes 393224 | tf_op jit(solution)/shard_map/ppermute | solution.py:38
  51.6 0.6 collective-permute-start.16
  52.2 2.9 %collective-permute-done.21.refs_6_ = bf16[128,512]{1,0:T(8,128)(2,1)S(1)} collective-permute-done((bf16[128,512]{1,0:T(8,128)(2,1)S(1)}, bf16[128,512]{1,0:T(8,128)(2,1)S(1)}, u32[]{:S(2)}, u32[]{:S(2)}) %collective-permute-start.21) | collective-permute-done | bytes 131104 | tf_op jit(solution)/shard_map/ppermute | solution.py:38
  55.1 1.3 %collective-permute-done.22.refs_7_ = bf16[128,512]{1,0:T(8,128)(2,1)S(1)} collective-permute-done((bf16[128,512]{1,0:T(8,128)(2,1)S(1)}, bf16[128,512]{1,0:T(8,128)(2,1)S(1)}, u32[]{:S(2)}, u32[]{:S(2)}) %collective-permute-start.22) | collective-permute-done | bytes 131104 | tf_op jit(solution)/shard_map/ppermute | solution.py:38
  56.9 1.6 %collective-permute-start.26 = (bf16[4,64,512]{2,1,0:T(8,128)(2,1)S(1)}, bf16[4,64,512]{2,1,0:T(8,128)(2,1)S(1)}, u32[]{:S(2)}, u32[]{:S(2)}) collective-permute-start(bf16[4,64,512]{2,1,0:T(8,128)(2,1)S(1)} %get-tuple-element.52), channel_id=1, source_target_pairs={{0,1},{1,0},{2,3},{3,2},{4,5},{5,4},{6,7},{7,6},{8,9},{9,8},{10,11... | collective-permute-start | bytes 786440 | tf_op jit(solution)/shard_map/ppermute | solution.py:38
  58.7 2.6 %collective-permute-start.23 = (bf16[128,256]{1,0:T(8,128)(2,1)S(1)}, bf16[128,256]{1,0:T(8,128)(2,1)S(1)}, u32[]{:S(2)}, u32[]{:S(2)}) collective-permute-start(bf16[128,256]{1,0:T(8,128)(2,1)S(1)} %get-tuple-element.49), channel_id=1, source_target_pairs={{0,4},{1,5},{2,6},{3,7},{4,0},{5,1},{6,2},{7,3},{8,12},{9,13},{10,... | collective-permute-start | bytes 196616 | tf_op jit(solution)/shard_map/ppermute | solution.py:38
  61.3 1.8 %collective-permute-start.24 = (bf16[128,256]{1,0:T(8,128)(2,1)S(1)}, bf16[128,256]{1,0:T(8,128)(2,1)S(1)}, u32[]{:S(2)}, u32[]{:S(2)}) collective-permute-start(bf16[128,256]{1,0:T(8,128)(2,1)S(1)} %get-tuple-element.50), channel_id=1, source_target_pairs={{0,6},{1,7},{2,4},{3,5},{4,2},{5,3},{6,0},{7,1},{8,14},{9,15},{10,... | collective-permute-start | bytes 196616 | tf_op jit(solution)/shard_map/ppermute | solution.py:38
  63.6 1.8 %collective-permute-done.26.refs_1_ = bf16[4,64,512]{2,1,0:T(8,128)(2,1)S(1)} collective-permute-done((bf16[4,64,512]{2,1,0:T(8,128)(2,1)S(1)}, bf16[4,64,512]{2,1,0:T(8,128)(2,1)S(1)}, u32[]{:S(2)}, u32[]{:S(2)}) %collective-permute-start.26) | collective-permute-done | bytes 262176 | tf_op jit(solution)/shard_map/ppermute | solution.py:38
  65.4 1.0 %collective-permute-start.27 = (bf16[64,512]{1,0:T(8,128)(2,1)S(1)}, bf16[64,512]{1,0:T(8,128)(2,1)S(1)}, u32[]{:S(2)}, u32[]{:S(2)}) collective-permute-start(bf16[64,512]{1,0:T(8,128)(2,1)S(1)} %get-tuple-element.54), channel_id=1, source_target_pairs={{0,4},{1,5},{2,6},{3,7},{4,0},{5,1},{6,2},{7,3},{8,12},{9,13},{10,... | collective-permute-start | bytes 196616 | tf_op jit(solution)/shard_map/ppermute | solution.py:38
  66.4 1.2 %collective-permute-start.28 = (bf16[64,512]{1,0:T(8,128)(2,1)S(1)}, bf16[64,512]{1,0:T(8,128)(2,1)S(1)}, u32[]{:S(2)}, u32[]{:S(2)}) collective-permute-start(bf16[64,512]{1,0:T(8,128)(2,1)S(1)} %get-tuple-element.55), channel_id=1, source_target_pairs={{0,6},{1,7},{2,4},{3,5},{4,2},{5,3},{6,0},{7,1},{8,14},{9,15},{10,... | collective-permute-start | bytes 196616 | tf_op jit(solution)/shard_map/ppermute | solution.py:38
  67.6 1.4 %collective-permute-start.29 = (bf16[64,512]{1,0:T(8,128)(2,1)S(1)}, bf16[64,512]{1,0:T(8,128)(2,1)S(1)}, u32[]{:S(2)}, u32[]{:S(2)}) collective-permute-start(bf16[64,512]{1,0:T(8,128)(2,1)S(1)} %get-tuple-element.56), channel_id=1, source_target_pairs={{0,2},{1,3},{2,0},{3,1},{4,6},{5,7},{6,4},{7,5},{8,10},{9,11},{10,... | collective-permute-start | bytes 196616 | tf_op jit(solution)/shard_map/ppermute | solution.py:38
  69.0 1.6 %shard_map.102 = bf16[128,2048]{1,0:T(8,128)(2,1)} custom-call(bf16[128,512]{1,0:T(8,128)(2,1)S(1)} %shard_map.98.refs_4_.refs_0_, bf16[512,512]{1,0:T(8,128)(2,1)S(1)} %copy-done, bf16[512,512]{1,0:T(8,128)(2,1)S(1)} %collective-permute-done.7.refs_2_, bf16[512,512]{1,0:T(8,128)(2,1)S(1)} %shard_map.95.refs_3_, ...), custom_call_target="tpu_custom_call" | custom-call | tf_op jit(solution)/shard_map/pallas_call | solution.py:49
  70.6 0.7 %shard_map.101 = bf16[128,1024]{1,0:T(8,128)(2,1)} custom-call(bf16[128,256]{1,0:T(8,128)(2,1)S(1)} %get-tuple-element.48.refs_0_, bf16[128,256]{1,0:T(8,128)(2,1)S(1)} %collective-permute-done.23.refs_1_, bf16[128,256]{1,0:T(8,128)(2,1)S(1)} %collective-permute-done.24.refs_2_, bf16[128,256]{1,0:T(8,128)(2,1)S(1)} %collective-permute-done.25.refs_3_.refs_2_, ...), custom_call_target="tpu_custom_call" | custom-call | tf_op jit(solution)/shard_map/pallas_call | solution.py:49
  71.3 1.4 %collective-permute-done.27.refs_1_ = bf16[64,512]{1,0:T(8,128)(2,1)S(1)} collective-permute-done((bf16[64,512]{1,0:T(8,128)(2,1)S(1)}, bf16[64,512]{1,0:T(8,128)(2,1)S(1)}, u32[]{:S(2)}, u32[]{:S(2)}) %collective-permute-start.27) | collective-permute-done | bytes 65568 | tf_op jit(solution)/shard_map/ppermute | solution.py:38
  73.0 0.7 shard_map.104
  (48 shorter events, 4.5 us)
Async XLA Ops:
  0.6 19.2 %copy-start = (bf16[512,512]{1,0:T(8,128)(2,1)S(1)}, bf16[512,512]{1,0:T(8,128)(2,1)}, u32[]{:S(2)}) copy-start(bf16[512,512]{1,0:T(8,128)(2,1)} %refs_1_.3) | copy-start | bytes 1572868
  0.6 19.5 %collective-permute-start.8 = (bf16[512,512]{1,0:T(8,128)(2,1)}, bf16[512,512]{1,0:T(8,128)(2,1)S(1)}, u32[]{:S(2)}, u32[]{:S(2)}) collective-permute-start(bf16[512,512]{1,0:T(8,128)(2,1)} %refs_1_.3), channel_id=1, source_target_pairs={{0,16},{8,24},{16,0},{24,8},{1,17},{9,25},{17,1},{25,9},{2,18},{10... | collective-permute-start | bytes 1572872 | tf_op jit(solution)/shard_map/ppermute | solution.py:38
  5.9 14.0 %collective-permute-start = (bf16[144,512]{1,0:T(8,128)(2,1)}, bf16[144,512]{1,0:T(8,128)(2,1)S(1)}, u32[]{:S(2)}, u32[]{:S(2)}) collective-permute-start(bf16[144,512]{1,0:T(8,128)(2,1)} %get-tuple-element.31), channel_id=1, source_target_pairs={{0,4},{1,5},{2,6},{3,7},{4,0},{5,1},{6,2},{7,3},{8,12},{9,13},{10,... | collective-permute-start | bytes 442376 | tf_op jit(solution)/shard_map/ppermute | solution.py:38
  8.6 11.3 %collective-permute-start.1 = (bf16[144,512]{1,0:T(8,128)(2,1)}, bf16[144,512]{1,0:T(8,128)(2,1)S(1)}, u32[]{:S(2)}, u32[]{:S(2)}) collective-permute-start(bf16[144,512]{1,0:T(8,128)(2,1)} %get-tuple-element.32), channel_id=1, source_target_pairs={{0,6},{1,7},{2,4},{3,5},{4,2},{5,3},{6,0},{7,1},{8,14},{9,15},{10,... | collective-permute-start | bytes 442376 | tf_op jit(solution)/shard_map/ppermute | solution.py:38
  9.9 10.2 %collective-permute-start.2 = (bf16[144,512]{1,0:T(8,128)(2,1)}, bf16[144,512]{1,0:T(8,128)(2,1)S(1)}, u32[]{:S(2)}, u32[]{:S(2)}) collective-permute-start(bf16[144,512]{1,0:T(8,128)(2,1)} %get-tuple-element.33), channel_id=1, source_target_pairs={{0,2},{1,3},{2,0},{3,1},{4,6},{5,7},{6,4},{7,5},{8,10},{9,11},{10,... | collective-permute-start | bytes 442376 | tf_op jit(solution)/shard_map/ppermute | solution.py:38
  10.1 13.9 %copy-start.1 = (bf16[1,128,2048]{2,1,0:T(8,128)(2,1)S(1)}, bf16[1,128,2048]{2,1,0:T(8,128)(2,1)}, u32[]{:S(2)}) copy-start(bf16[1,128,2048]{2,1,0:T(8,128)(2,1)} %param.7) | copy-start | bytes 1572868
  10.1 10.0 %collective-permute-start.3 = (bf16[144,512]{1,0:T(8,128)(2,1)}, bf16[144,512]{1,0:T(8,128)(2,1)S(1)}, u32[]{:S(2)}, u32[]{:S(2)}) collective-permute-start(bf16[144,512]{1,0:T(8,128)(2,1)} %get-tuple-element.30.refs_2_), channel_id=1, source_target_pairs={{0,1},{1,0},{2,3},{3,2},{4,5},{5,4},{6,7},{7,6},{8,9},{9,8},{10,11... | collective-permute-start | bytes 442376 | tf_op jit(solution)/shard_map/ppermute | solution.py:38
  19.9 4.1 %collective-permute-start.7 = (bf16[512,512]{1,0:T(8,128)(2,1)S(1)}, bf16[512,512]{1,0:T(8,128)(2,1)S(1)}, u32[]{:S(2)}, u32[]{:S(2)}) collective-permute-start(bf16[512,512]{1,0:T(8,128)(2,1)S(1)} %copy-done), channel_id=1, source_target_pairs={{0,8},{8,0},{16,24},{24,16},{1,9},{9,1},{17,25},{25,17},{2,10},{10... | collective-permute-start | bytes 1572872 | tf_op jit(solution)/shard_map/ppermute | solution.py:38
  20.1 3.9 %collective-permute-start.9 = (bf16[512,512]{1,0:T(8,128)(2,1)S(1)}, bf16[512,512]{1,0:T(8,128)(2,1)S(1)}, u32[]{:S(2)}, u32[]{:S(2)}) collective-permute-start(bf16[512,512]{1,0:T(8,128)(2,1)S(1)} %shard_map.95.refs_3_), channel_id=1, source_target_pairs={{0,8},{8,0},{16,24},{24,16},{1,9},{9,1},{17,25},{25,17},{2,10},{10... | collective-permute-start | bytes 1572872 | tf_op jit(solution)/shard_map/ppermute | solution.py:38
  20.5 8.9 %collective-permute-start.5 = (bf16[144,512]{1,0:T(8,128)(2,1)S(1)}, bf16[144,512]{1,0:T(8,128)(2,1)S(1)}, u32[]{:S(2)}, u32[]{:S(2)}) collective-permute-start(bf16[144,512]{1,0:T(8,128)(2,1)S(1)} %collective-permute-done.refs_1_.refs_3_), channel_id=1, source_target_pairs={{0,1},{1,0},{2,3},{3,2},{4,5},{5,4},{6,7},{7,6},{8,9},{9,8},{10,11... | collective-permute-start | bytes 442376 | tf_op jit(solution)/shard_map/ppermute | solution.py:38
  22.0 8.4 %collective-permute-start.6 = (bf16[144,512]{1,0:T(8,128)(2,1)S(1)}, bf16[144,512]{1,0:T(8,128)(2,1)S(1)}, u32[]{:S(2)}, u32[]{:S(2)}) collective-permute-start(bf16[144,512]{1,0:T(8,128)(2,1)S(1)} %collective-permute-done.1.refs_2_.refs_4_), channel_id=1, source_target_pairs={{0,1},{1,0},{2,3},{3,2},{4,5},{5,4},{6,7},{7,6},{8,9},{9,8},{10,11... | collective-permute-start | bytes 442376 | tf_op jit(solution)/shard_map/ppermute | solution.py:38
  22.5 10.2 %collective-permute-start.4 = (bf16[144,512]{1,0:T(8,128)(2,1)S(1)}, bf16[144,512]{1,0:T(8,128)(2,1)S(1)}, u32[]{:S(2)}, u32[]{:S(2)}) collective-permute-start(bf16[144,512]{1,0:T(8,128)(2,1)S(1)} %collective-permute-done.2.refs_3_.refs_5_), channel_id=1, source_target_pairs={{0,1},{1,0},{2,3},{3,2},{4,5},{5,4},{6,7},{7,6},{8,9},{9,8},{10,11... | collective-permute-start | bytes 442376 | tf_op jit(solution)/shard_map/ppermute | solution.py:38
  24.6 8.2 %collective-permute-start.10 = (bf16[128,128]{1,0:T(8,128)(2,1)S(1)}, bf16[128,128]{1,0:T(8,128)(2,1)S(1)}, u32[]{:S(2)}, u32[]{:S(2)}) collective-permute-start(bf16[128,128]{1,0:T(8,128)(2,1)S(1)} %get-tuple-element.35), channel_id=1, source_target_pairs={{0,4},{1,5},{2,6},{3,7},{4,0},{5,1},{6,2},{7,3},{8,12},{9,13},{10,... | collective-permute-start | bytes 98312 | tf_op jit(solution)/shard_map/ppermute | solution.py:38
  28.8 5.7 %collective-permute-start.11 = (bf16[128,128]{1,0:T(8,128)(2,1)S(1)}, bf16[128,128]{1,0:T(8,128)(2,1)S(1)}, u32[]{:S(2)}, u32[]{:S(2)}) collective-permute-start(bf16[128,128]{1,0:T(8,128)(2,1)S(1)} %get-tuple-element.36), channel_id=1, source_target_pairs={{0,6},{1,7},{2,4},{3,5},{4,2},{5,3},{6,0},{7,1},{8,14},{9,15},{10,... | collective-permute-start | bytes 98312 | tf_op jit(solution)/shard_map/ppermute | solution.py:38
  29.4 5.2 %collective-permute-start.12 = (bf16[128,128]{1,0:T(8,128)(2,1)S(1)}, bf16[128,128]{1,0:T(8,128)(2,1)S(1)}, u32[]{:S(2)}, u32[]{:S(2)}) collective-permute-start(bf16[128,128]{1,0:T(8,128)(2,1)S(1)} %get-tuple-element.37), channel_id=1, source_target_pairs={{0,2},{1,3},{2,0},{3,1},{4,6},{5,7},{6,4},{7,5},{8,10},{9,11},{10,... | collective-permute-start | bytes 98312 | tf_op jit(solution)/shard_map/ppermute | solution.py:38
  40.8 9.1 %collective-permute-start.13 = (bf16[4,128,256]{2,1,0:T(8,128)(2,1)S(1)}, bf16[4,128,256]{2,1,0:T(8,128)(2,1)S(1)}, u32[]{:S(2)}, u32[]{:S(2)}) collective-permute-start(bf16[4,128,256]{2,1,0:T(8,128)(2,1)S(1)} %get-tuple-element.39), channel_id=1, source_target_pairs={{0,1},{1,0},{2,3},{3,2},{4,5},{5,4},{6,7},{7,6},{8,9},{9,8},{10,11... | collective-permute-start | bytes 786440 | tf_op jit(solution)/shard_map/ppermute | solution.py:38
  40.9 10.7 %collective-permute-start.15 = (bf16[2,128,512]{2,1,0:T(8,128)(2,1)S(1)}, bf16[2,128,512]{2,1,0:T(8,128)(2,1)S(1)}, u32[]{:S(2)}, u32[]{:S(2)}) collective-permute-start(bf16[2,128,512]{2,1,0:T(8,128)(2,1)S(1)} %get-tuple-element.42), channel_id=1, source_target_pairs={{0,16},{8,24},{16,0},{24,8},{1,17},{9,25},{17,1},{25,9},{2,18},{10... | collective-permute-start | bytes 786440 | tf_op jit(solution)/shard_map/ppermute | solution.py:38
  41.1 4.9 %collective-permute-start.17 = (bf16[128,128]{1,0:T(8,128)(2,1)S(1)}, bf16[128,128]{1,0:T(8,128)(2,1)S(1)}, u32[]{:S(2)}, u32[]{:S(2)}) collective-permute-start(bf16[128,128]{1,0:T(8,128)(2,1)S(1)} %get-tuple-element.44), channel_id=1, source_target_pairs={{0,4},{1,5},{2,6},{3,7},{4,0},{5,1},{6,2},{7,3},{8,12},{9,13},{10,... | collective-permute-start | bytes 98312 | tf_op jit(solution)/shard_map/ppermute | solution.py:38
  44.2 5.7 %collective-permute-start.18 = (bf16[128,128]{1,0:T(8,128)(2,1)S(1)}, bf16[128,128]{1,0:T(8,128)(2,1)S(1)}, u32[]{:S(2)}, u32[]{:S(2)}) collective-permute-start(bf16[128,128]{1,0:T(8,128)(2,1)S(1)} %get-tuple-element.45), channel_id=1, source_target_pairs={{0,6},{1,7},{2,4},{3,5},{4,2},{5,3},{6,0},{7,1},{8,14},{9,15},{10,... | collective-permute-start | bytes 98312 | tf_op jit(solution)/shard_map/ppermute | solution.py:38
  44.7 5.2 %collective-permute-start.19 = (bf16[128,128]{1,0:T(8,128)(2,1)S(1)}, bf16[128,128]{1,0:T(8,128)(2,1)S(1)}, u32[]{:S(2)}, u32[]{:S(2)}) collective-permute-start(bf16[128,128]{1,0:T(8,128)(2,1)S(1)} %get-tuple-element.46), channel_id=1, source_target_pairs={{0,2},{1,3},{2,0},{3,1},{4,6},{5,7},{6,4},{7,5},{8,10},{9,11},{10,... | collective-permute-start | bytes 98312 | tf_op jit(solution)/shard_map/ppermute | solution.py:38
  46.1 9.0 %collective-permute-start.14 = (bf16[128,512]{1,0:T(8,128)(2,1)S(1)}, bf16[128,512]{1,0:T(8,128)(2,1)S(1)}, u32[]{:S(2)}, u32[]{:S(2)}) collective-permute-start(bf16[128,512]{1,0:T(8,128)(2,1)S(1)} %get-tuple-element.41), channel_id=1, source_target_pairs={{0,8},{8,0},{16,24},{24,16},{1,9},{9,1},{17,25},{25,17},{2,10},{10... | collective-permute-start | bytes 393224 | tf_op jit(solution)/shard_map/ppermute | solution.py:38
  50.0 5.0 %collective-permute-start.21 = (bf16[128,512]{1,0:T(8,128)(2,1)S(1)}, bf16[128,512]{1,0:T(8,128)(2,1)S(1)}, u32[]{:S(2)}, u32[]{:S(2)}) collective-permute-start(bf16[128,512]{1,0:T(8,128)(2,1)S(1)} %shard_map.98.refs_4_.refs_0_), channel_id=1, source_target_pairs={{0,16},{8,24},{16,0},{24,8},{1,17},{9,25},{17,1},{25,9},{2,18},{10... | collective-permute-start | bytes 393224 | tf_op jit(solution)/shard_map/ppermute | solution.py:38
  51.6 3.5 %collective-permute-start.20 = (bf16[128,512]{1,0:T(8,128)(2,1)S(1)}, bf16[128,512]{1,0:T(8,128)(2,1)S(1)}, u32[]{:S(2)}, u32[]{:S(2)}) collective-permute-start(bf16[128,512]{1,0:T(8,128)(2,1)S(1)} %shard_map.98.refs_4_.refs_0_), channel_id=1, source_target_pairs={{0,8},{8,0},{16,24},{24,16},{1,9},{9,1},{17,25},{25,17},{2,10},{10... | collective-permute-start | bytes 393224 | tf_op jit(solution)/shard_map/ppermute | solution.py:38
  51.6 3.5 %collective-permute-start.16 = (bf16[128,512]{1,0:T(8,128)(2,1)S(1)}, bf16[128,512]{1,0:T(8,128)(2,1)S(1)}, u32[]{:S(2)}, u32[]{:S(2)}) collective-permute-start(bf16[128,512]{1,0:T(8,128)(2,1)S(1)} %get-tuple-element.57), channel_id=1, source_target_pairs={{0,8},{8,0},{16,24},{24,16},{1,9},{9,1},{17,25},{25,17},{2,10},{10... | collective-permute-start | bytes 393224 | tf_op jit(solution)/shard_map/ppermute | solution.py:38
  55.0 1.3 %collective-permute-start.22 = (bf16[128,512]{1,0:T(8,128)(2,1)S(1)}, bf16[128,512]{1,0:T(8,128)(2,1)S(1)}, u32[]{:S(2)}, u32[]{:S(2)}) collective-permute-start(bf16[128,512]{1,0:T(8,128)(2,1)S(1)} %collective-permute-done.21.refs_6_), channel_id=1, source_target_pairs={{0,8},{8,0},{16,24},{24,16},{1,9},{9,1},{17,25},{25,17},{2,10},{10... | collective-permute-start | bytes 393224 | tf_op jit(solution)/shard_map/ppermute | solution.py:38
  56.9 8.4 %collective-permute-start.26 = (bf16[4,64,512]{2,1,0:T(8,128)(2,1)S(1)}, bf16[4,64,512]{2,1,0:T(8,128)(2,1)S(1)}, u32[]{:S(2)}, u32[]{:S(2)}) collective-permute-start(bf16[4,64,512]{2,1,0:T(8,128)(2,1)S(1)} %get-tuple-element.52), channel_id=1, source_target_pairs={{0,1},{1,0},{2,3},{3,2},{4,5},{5,4},{6,7},{7,6},{8,9},{9,8},{10,11... | collective-permute-start | bytes 786440 | tf_op jit(solution)/shard_map/ppermute | solution.py:38
  58.6 5.0 %collective-permute-start.25 = (bf16[128,256]{1,0:T(8,128)(2,1)S(1)}, bf16[128,256]{1,0:T(8,128)(2,1)S(1)}, u32[]{:S(2)}, u32[]{:S(2)}) collective-permute-start(bf16[128,256]{1,0:T(8,128)(2,1)S(1)} %get-tuple-element.51), channel_id=1, source_target_pairs={{0,2},{1,3},{2,0},{3,1},{4,6},{5,7},{6,4},{7,5},{8,10},{9,11},{10,... | collective-permute-start | bytes 196616 | tf_op jit(solution)/shard_map/ppermute | solution.py:38
  58.7 11.9 %collective-permute-start.23 = (bf16[128,256]{1,0:T(8,128)(2,1)S(1)}, bf16[128,256]{1,0:T(8,128)(2,1)S(1)}, u32[]{:S(2)}, u32[]{:S(2)}) collective-permute-start(bf16[128,256]{1,0:T(8,128)(2,1)S(1)} %get-tuple-element.49), channel_id=1, source_target_pairs={{0,4},{1,5},{2,6},{3,7},{4,0},{5,1},{6,2},{7,3},{8,12},{9,13},{10,... | collective-permute-start | bytes 196616 | tf_op jit(solution)/shard_map/ppermute | solution.py:38
  61.3 9.3 %collective-permute-start.24 = (bf16[128,256]{1,0:T(8,128)(2,1)S(1)}, bf16[128,256]{1,0:T(8,128)(2,1)S(1)}, u32[]{:S(2)}, u32[]{:S(2)}) collective-permute-start(bf16[128,256]{1,0:T(8,128)(2,1)S(1)} %get-tuple-element.50), channel_id=1, source_target_pairs={{0,6},{1,7},{2,4},{3,5},{4,2},{5,3},{6,0},{7,1},{8,14},{9,15},{10,... | collective-permute-start | bytes 196616 | tf_op jit(solution)/shard_map/ppermute | solution.py:38
  65.4 7.3 %collective-permute-start.27 = (bf16[64,512]{1,0:T(8,128)(2,1)S(1)}, bf16[64,512]{1,0:T(8,128)(2,1)S(1)}, u32[]{:S(2)}, u32[]{:S(2)}) collective-permute-start(bf16[64,512]{1,0:T(8,128)(2,1)S(1)} %get-tuple-element.54), channel_id=1, source_target_pairs={{0,4},{1,5},{2,6},{3,7},{4,0},{5,1},{6,2},{7,3},{8,12},{9,13},{10,... | collective-permute-start | bytes 196616 | tf_op jit(solution)/shard_map/ppermute | solution.py:38
  66.4 6.3 %collective-permute-start.28 = (bf16[64,512]{1,0:T(8,128)(2,1)S(1)}, bf16[64,512]{1,0:T(8,128)(2,1)S(1)}, u32[]{:S(2)}, u32[]{:S(2)}) collective-permute-start(bf16[64,512]{1,0:T(8,128)(2,1)S(1)} %get-tuple-element.55), channel_id=1, source_target_pairs={{0,6},{1,7},{2,4},{3,5},{4,2},{5,3},{6,0},{7,1},{8,14},{9,15},{10,... | collective-permute-start | bytes 196616 | tf_op jit(solution)/shard_map/ppermute | solution.py:38
  67.6 5.4 %collective-permute-start.29 = (bf16[64,512]{1,0:T(8,128)(2,1)S(1)}, bf16[64,512]{1,0:T(8,128)(2,1)S(1)}, u32[]{:S(2)}, u32[]{:S(2)}) collective-permute-start(bf16[64,512]{1,0:T(8,128)(2,1)S(1)} %get-tuple-element.56), channel_id=1, source_target_pairs={{0,2},{1,3},{2,0},{3,1},{4,6},{5,7},{6,4},{7,5},{8,10},{9,11},{10,... | collective-permute-start | bytes 196616 | tf_op jit(solution)/shard_map/ppermute | solution.py:38
  (2 other events, 15.7 us)

commit v4 on v3

--- a/solution.py
+++ b/solution.py
@@ -315,8 +315,8 @@
 
 
 def pair_kernel(keep_ref, got_ref, *out_refs):
-    for m in range(KV_HEADS):
-        out_refs[m][...] = (keep_ref[m] + got_ref[m].astype(jnp.float32)).astype(out_refs[m].dtype)
+    for m, ref in enumerate(out_refs):
+        ref[...] = (keep_ref[m] + got_ref[m].astype(jnp.float32)).astype(ref.dtype)
 
 
 def query_kernel(*rest):
@@ -347,20 +347,21 @@
 
 
 def sides_kernel(fsdp, *rest):
-    keep_ref, send_ref, parts = rest[2 * fsdp:]
+    keep_refs, send_refs, parts = rest[2 * fsdp:2 * fsdp + 2], rest[2 * fsdp + 2:2 * fsdp + 4], rest[-1]
     head, side = head_side()
     parts[...] = weight_sums(fsdp, rest).reshape(parts.shape)
     for m in range(KV_HEADS):
         to = 2 * jnp.bitwise_xor(head, m)
-        keep_ref[m] = parts[to + side]
-        send_ref[m] = parts[to + 1 - side].astype(jnp.bfloat16)
-
-
-def own_total_kernel(own_ref, *rest):
+        keep_refs[m // 2][m % 2] = parts[to + side]
+        send_refs[m // 2][m % 2] = parts[to + 1 - side].astype(jnp.bfloat16)
+
+
+def own_total_kernel(*rest):
+    part_refs, own_ref, out_ref = rest[:-2], rest[-2], rest[-1]
     total = own_ref[...]
-    for ref in rest[:-1]:
+    for ref in part_refs:
         total = total + ref[...].astype(jnp.float32)
-    rest[-1][...] = total
+    out_ref[...] = total
 
 
 def total_kernel(part_ref, out_ref):
@@ -402,7 +403,7 @@
         (queries[0], grad_out[0], attn_out[0], log_sums[0]), hbm=4)
     qd = along_heads(qd)
     turned = [swapped(one, "ctx", 1) for one in qd[:2]]
-    w_far = held(swapped(w_kv, "fsdp", far), (*far_first(qd[:KV_HEADS])[1:], turned[0]))
+    w_far = held(swapped(w_kv, "fsdp", far), (*far_first(qd[:KV_HEADS])[1:], *turned))
     w_parts = over_fsdp([w_kv] * far + [w_far] * (fsdp - far), far // 2)
 
     kv = call(
@@ -442,15 +443,17 @@
     grads = over_fsdp([kv_grad] * fsdp, far)
     if teams == 1:
         share = (span // devices, columns)
-        own_sums, send_sums = call(
-            functools.partial(sides_kernel, fsdp), [sds((KV_HEADS,) + share, f32), sds((KV_HEADS,) + share)],
+        two = (2,) + share
+        near_sums, far_sums, near_send, far_send = call(
+            functools.partial(sides_kernel, fsdp), [sds(two, f32)] * 2 + [sds(two)] * 2,
             [pltpu.VMEM((devices,) + share, f32)], (*hid, *grads))
-        formed = (own_sums,)
+        formed = (near_sums,)
         dq = along_heads(call(pair_kernel, [sds(wide)] * KV_HEADS, [], (keep, give), after=formed))
-        sums = call(
-            pair_kernel, [sds(share, f32)] + [sds(share)] * (KV_HEADS - 1), [],
-            (own_sums, swapped(send_sums, "ctx", 1)), after=dq[1:2])
-        (weight_grads,) = call(own_total_kernel, [sds(share, f32)], [], far_first(along_heads(sums)))
+        far_sums = call(pair_kernel, [sds(share)] * 2, [], (far_sums, swapped(far_send, "ctx", 1)))
+        near_sums = call(
+            pair_kernel, [sds(share, f32), sds(share)], [], (near_sums, swapped(near_send, "ctx", 1)), after=dq[1:2])
+        own_sums, *sums = far_first(along_heads([*near_sums, *far_sums]))
+        (weight_grads,) = call(own_total_kernel, [sds(share, f32)], [], (*sums, own_sums))
     else:
         formed = call(functools.partial(weight_kernel, fsdp), [sds((span, columns))], [], (*hid, *grads))
         dq = along_heads(call(pair_kernel, [sds(wide)] * KV_HEADS, [], (keep, give), after=formed))

time: 74.3 us -> 72.1 us (0.970)
  waiting for transfers between devices: 26.8 us -> 24.5 us
    ppermute x30 -> x31, waiting for transfers between devices: 26.8 us -> 24.5 us  [swapped(): return lax.ppermute(array, axis, [(i, i ^ bits) for i in range(size)])]
    ppermute x30 -> x31, starting transfers between devices: 33.2 us -> 33.7 us  [swapped(): return lax.ppermute(array, axis, [(i, i ^ bits) for i in range(size)])]
    pallas_call x10 -> x11, Pallas kernels: 12.8 us -> 12.6 us  [call(): pl.pallas_call(body, out_shape=out_shape, in_specs=specs, out_specs=[VMEM...]
  transfers between devices with their start and end apart: 30 -> 31, of which waited for: 13 -> 10; matrix products, arithmetic and copies ran while one was open for 0% -> 0% of each run, Pallas kernels for 7% -> 7%
where the time goes in v4:
time: 72.1 us; the launch traced here: 71.7 us
  starting transfers between devices  33.7 us (47%)
  waiting for transfers between devices  24.5 us (34%)
  Pallas kernels  12.6 us (17%)
  between operations  0.78 us (1%)
    ppermute x31, starting transfers between devices, swapped(): return lax.ppermute(array, axis, [(i, i ^ bits) for i in range(size)])  33.7 us
    ppermute x31, waiting for transfers between devices, swapped(): return lax.ppermute(array, axis, [(i, i ^ bits) for i in range(size)])  24.5 us
    pallas_call x11, Pallas kernels, call(): pl.pallas_call(body, out_shape=out_shape, in_specs=specs, out_specs=[VMEM...  12.6 us
  transfers between devices with their start and end apart: 31, of which 10 were waited for; matrix products, arithmetic and copies ran while one was open for 0% of the time, Pallas kernels for 7%

profile of v4, /device:TPU:0, one launch (start us, length us, event | category | flops | bytes accessed | tf_op | source)
XLA Modules:
  0.0 71.7 jit_solution(8733920215886442442)
XLA Ops:
  0.6 3.0 %collective-permute-start.8 = (bf16[512,512]{1,0:T(8,128)(2,1)}, bf16[512,512]{1,0:T(8,128)(2,1)S(1)}, u32[]{:S(2)}, u32[]{:S(2)}) collective-permute-start(bf16[512,512]{1,0:T(8,128)(2,1)} %refs_1_.3), channel_id=1, source_target_pairs={{0,16},{8,24},{16,0},{24,8},{1,17},{9,25},{17,1},{25,9},{2,18},{10... | collective-permute-start | bytes 1572872 | tf_op jit(solution)/shard_map/ppermute | solution.py:38
  3.7 2.2 %shard_map.94 = (bf16[144,512]{1,0:T(8,128)(2,1)}, bf16[144,512]{1,0:T(8,128)(2,1)}, bf16[144,512]{1,0:T(8,128)(2,1)}, bf16[144,512]{1,0:T(8,128)(2,1)}) custom-call(bf16[128,1024]{1,0:T(8,128)(2,1)} %bitcast.14, bf16[128,1024]{1,0:T(8,128)(2,1)} %bitcast.15, bf16[128,1024]{1,0:T(8,128)(2,1)} %bitcast.16, f32[16,128]{1,0:T(8,128)} %bitcast.18), custom_call_target="tpu_custom_call" | custom-call | tf_op jit(solution)/shard_map/pallas_call | solution.py:49
  5.9 1.6 %collective-permute-start.2 = (bf16[144,512]{1,0:T(8,128)(2,1)}, bf16[144,512]{1,0:T(8,128)(2,1)S(1)}, u32[]{:S(2)}, u32[]{:S(2)}) collective-permute-start(bf16[144,512]{1,0:T(8,128)(2,1)} %get-tuple-element.35), channel_id=1, source_target_pairs={{0,2},{1,3},{2,0},{3,1},{4,6},{5,7},{6,4},{7,5},{8,10},{9,11},{10,... | collective-permute-start | bytes 442376 | tf_op jit(solution)/shard_map/ppermute | solution.py:38
  7.5 2.6 %collective-permute-start = (bf16[144,512]{1,0:T(8,128)(2,1)}, bf16[144,512]{1,0:T(8,128)(2,1)S(1)}, u32[]{:S(2)}, u32[]{:S(2)}) collective-permute-start(bf16[144,512]{1,0:T(8,128)(2,1)} %get-tuple-element.33), channel_id=1, source_target_pairs={{0,4},{1,5},{2,6},{3,7},{4,0},{5,1},{6,2},{7,3},{8,12},{9,13},{10,... | collective-permute-start | bytes 442376 | tf_op jit(solution)/shard_map/ppermute | solution.py:38
  10.4 1.5 %collective-permute-start.3 = (bf16[144,512]{1,0:T(8,128)(2,1)}, bf16[144,512]{1,0:T(8,128)(2,1)S(1)}, u32[]{:S(2)}, u32[]{:S(2)}) collective-permute-start(bf16[144,512]{1,0:T(8,128)(2,1)} %get-tuple-element.32.refs_2_), channel_id=1, source_target_pairs={{0,1},{1,0},{2,3},{3,2},{4,5},{5,4},{6,7},{7,6},{8,9},{9,8},{10,11... | collective-permute-start | bytes 442376 | tf_op jit(solution)/shard_map/ppermute | solution.py:38
  11.9 1.5 %collective-permute-done.2.refs_3_.refs_5_ = bf16[144,512]{1,0:T(8,128)(2,1)S(1)} collective-permute-done((bf16[144,512]{1,0:T(8,128)(2,1)}, bf16[144,512]{1,0:T(8,128)(2,1)S(1)}, u32[]{:S(2)}, u32[]{:S(2)}) %collective-permute-start.2) | collective-permute-done | bytes 147488 | tf_op jit(solution)/shard_map/ppermute | solution.py:38
  13.3 1.5 %collective-permute-start.4 = (bf16[144,512]{1,0:T(8,128)(2,1)S(1)}, bf16[144,512]{1,0:T(8,128)(2,1)S(1)}, u32[]{:S(2)}, u32[]{:S(2)}) collective-permute-start(bf16[144,512]{1,0:T(8,128)(2,1)S(1)} %collective-permute-done.2.refs_3_.refs_5_), channel_id=1, source_target_pairs={{0,1},{1,0},{2,3},{3,2},{4,5},{5,4},{6,7},{7,6},{8,9},{9,8},{10,11... | collective-permute-start | bytes 442376 | tf_op jit(solution)/shard_map/ppermute | solution.py:38
  14.8 6.8 %collective-permute-done.refs_1_.refs_3_ = bf16[144,512]{1,0:T(8,128)(2,1)S(1)} collective-permute-done((bf16[144,512]{1,0:T(8,128)(2,1)}, bf16[144,512]{1,0:T(8,128)(2,1)S(1)}, u32[]{:S(2)}, u32[]{:S(2)}) %collective-permute-start) | collective-permute-done | bytes 147488 | tf_op jit(solution)/shard_map/ppermute | solution.py:38
  22.2 1.5 %collective-permute-start.5 = (bf16[144,512]{1,0:T(8,128)(2,1)S(1)}, bf16[144,512]{1,0:T(8,128)(2,1)S(1)}, u32[]{:S(2)}, u32[]{:S(2)}) collective-permute-start(bf16[144,512]{1,0:T(8,128)(2,1)S(1)} %collective-permute-done.refs_1_.refs_3_), channel_id=1, source_target_pairs={{0,1},{1,0},{2,3},{3,2},{4,5},{5,4},{6,7},{7,6},{8,9},{9,8},{10,11... | collective-permute-start | bytes 442376 | tf_op jit(solution)/shard_map/ppermute | solution.py:38
  24.8 2.8 %collective-permute-start.10 = (bf16[128,128]{1,0:T(8,128)(2,1)S(1)}, bf16[128,128]{1,0:T(8,128)(2,1)S(1)}, u32[]{:S(2)}, u32[]{:S(2)}) collective-permute-start(bf16[128,128]{1,0:T(8,128)(2,1)S(1)} %get-tuple-element.37), channel_id=1, source_target_pairs={{0,4},{1,5},{2,6},{3,7},{4,0},{5,1},{6,2},{7,3},{8,12},{9,13},{10,... | collective-permute-start | bytes 98312 | tf_op jit(solution)/shard_map/ppermute | solution.py:38
  27.6 1.3 %collective-permute-start.11 = (bf16[128,128]{1,0:T(8,128)(2,1)S(1)}, bf16[128,128]{1,0:T(8,128)(2,1)S(1)}, u32[]{:S(2)}, u32[]{:S(2)}) collective-permute-start(bf16[128,128]{1,0:T(8,128)(2,1)S(1)} %get-tuple-element.38), channel_id=1, source_target_pairs={{0,6},{1,7},{2,4},{3,5},{4,2},{5,3},{6,0},{7,1},{8,14},{9,15},{10,... | collective-permute-start | bytes 98312 | tf_op jit(solution)/shard_map/ppermute | solution.py:38
  29.0 2.3 %collective-permute-done.6.refs_9_ = bf16[144,512]{1,0:T(8,128)(2,1)S(1)} collective-permute-done((bf16[144,512]{1,0:T(8,128)(2,1)S(1)}, bf16[144,512]{1,0:T(8,128)(2,1)S(1)}, u32[]{:S(2)}, u32[]{:S(2)}) %collective-permute-start.6) | collective-permute-done | bytes 147488 | tf_op jit(solution)/shard_map/ppermute | solution.py:38
  31.2 2.1 %collective-permute-done.11.refs_12_ = bf16[128,128]{1,0:T(8,128)(2,1)S(1)} collective-permute-done((bf16[128,128]{1,0:T(8,128)(2,1)S(1)}, bf16[128,128]{1,0:T(8,128)(2,1)S(1)}, u32[]{:S(2)}, u32[]{:S(2)}) %collective-permute-start.11) | collective-permute-done | bytes 32800 | tf_op jit(solution)/shard_map/ppermute | solution.py:38
  33.4 6.1 %shard_map.97 = (bf16[128,128]{1,0:T(8,128)(2,1)S(1)}, bf16[128,128]{1,0:T(8,128)(2,1)S(1)}, bf16[128,128]{1,0:T(8,128)(2,1)S(1)}, bf16[128,128]{1,0:T(8,128)(2,...) custom-call(s32[1,8]{1,0:T(1,128)S(1)} %copy-done.3, ...), custom_call_target="tpu_custom_call" | custom-call | tf_op jit(solution)/shard_map/pallas_call | solution.py:49
  39.6 1.3 %collective-permute-start.15 = (bf16[2,128,512]{2,1,0:T(8,128)(2,1)S(1)}, bf16[2,128,512]{2,1,0:T(8,128)(2,1)S(1)}, u32[]{:S(2)}, u32[]{:S(2)}) collective-permute-start(bf16[2,128,512]{2,1,0:T(8,128)(2,1)S(1)} %get-tuple-element.44), channel_id=1, source_target_pairs={{0,16},{8,24},{16,0},{24,8},{1,17},{9,25},{17,1},{25,9},{2,18},{10... | collective-permute-start | bytes 786440 | tf_op jit(solution)/shard_map/ppermute | solution.py:38
  40.9 1.0 %collective-permute-start.17 = (bf16[128,128]{1,0:T(8,128)(2,1)S(1)}, bf16[128,128]{1,0:T(8,128)(2,1)S(1)}, u32[]{:S(2)}, u32[]{:S(2)}) collective-permute-start(bf16[128,128]{1,0:T(8,128)(2,1)S(1)} %get-tuple-element.46), channel_id=1, source_target_pairs={{0,4},{1,5},{2,6},{3,7},{4,0},{5,1},{6,2},{7,3},{8,12},{9,13},{10,... | collective-permute-start | bytes 98312 | tf_op jit(solution)/shard_map/ppermute | solution.py:38
  41.9 1.3 %collective-permute-start.18 = (bf16[128,128]{1,0:T(8,128)(2,1)S(1)}, bf16[128,128]{1,0:T(8,128)(2,1)S(1)}, u32[]{:S(2)}, u32[]{:S(2)}) collective-permute-start(bf16[128,128]{1,0:T(8,128)(2,1)S(1)} %get-tuple-element.47), channel_id=1, source_target_pairs={{0,6},{1,7},{2,4},{3,5},{4,2},{5,3},{6,0},{7,1},{8,14},{9,15},{10,... | collective-permute-start | bytes 98312 | tf_op jit(solution)/shard_map/ppermute | solution.py:38
  43.2 1.1 %collective-permute-start.19 = (bf16[128,128]{1,0:T(8,128)(2,1)S(1)}, bf16[128,128]{1,0:T(8,128)(2,1)S(1)}, u32[]{:S(2)}, u32[]{:S(2)}) collective-permute-start(bf16[128,128]{1,0:T(8,128)(2,1)S(1)} %get-tuple-element.48), channel_id=1, source_target_pairs={{0,2},{1,3},{2,0},{3,1},{4,6},{5,7},{6,4},{7,5},{8,10},{9,11},{10,... | collective-permute-start | bytes 98312 | tf_op jit(solution)/shard_map/ppermute | solution.py:38
  44.4 1.7 %collective-permute-done.17.refs_1_ = bf16[128,128]{1,0:T(8,128)(2,1)S(1)} collective-permute-done((bf16[128,128]{1,0:T(8,128)(2,1)S(1)}, bf16[128,128]{1,0:T(8,128)(2,1)S(1)}, u32[]{:S(2)}, u32[]{:S(2)}) %collective-permute-start.17) | collective-permute-done | bytes 32800 | tf_op jit(solution)/shard_map/ppermute | solution.py:38
  46.0 1.5 %collective-permute-done.18.refs_2_ = bf16[128,128]{1,0:T(8,128)(2,1)S(1)} collective-permute-done((bf16[128,128]{1,0:T(8,128)(2,1)S(1)}, bf16[128,128]{1,0:T(8,128)(2,1)S(1)}, u32[]{:S(2)}, u32[]{:S(2)}) %collective-permute-start.18) | collective-permute-done | bytes 32800 | tf_op jit(solution)/shard_map/ppermute | solution.py:38
  47.7 0.8 %collective-permute-start.21 = (bf16[128,512]{1,0:T(8,128)(2,1)S(1)}, bf16[128,512]{1,0:T(8,128)(2,1)S(1)}, u32[]{:S(2)}, u32[]{:S(2)}) collective-permute-start(bf16[128,512]{1,0:T(8,128)(2,1)S(1)} %shard_map.98.refs_4_.refs_0_), channel_id=1, source_target_pairs={{0,16},{8,24},{16,0},{24,8},{1,17},{9,25},{17,1},{25,9},{2,18},{10... | collective-permute-start | bytes 393224 | tf_op jit(solution)/shard_map/ppermute | solution.py:38
  49.2 3.6 %collective-permute-done.21.refs_6_ = bf16[128,512]{1,0:T(8,128)(2,1)S(1)} collective-permute-done((bf16[128,512]{1,0:T(8,128)(2,1)S(1)}, bf16[128,512]{1,0:T(8,128)(2,1)S(1)}, u32[]{:S(2)}, u32[]{:S(2)}) %collective-permute-start.21) | collective-permute-done | bytes 131104 | tf_op jit(solution)/shard_map/ppermute | solution.py:38
  52.8 1.3 %collective-permute-done.22.refs_7_ = bf16[128,512]{1,0:T(8,128)(2,1)S(1)} collective-permute-done((bf16[128,512]{1,0:T(8,128)(2,1)S(1)}, bf16[128,512]{1,0:T(8,128)(2,1)S(1)}, u32[]{:S(2)}, u32[]{:S(2)}) %collective-permute-start.22) | collective-permute-done | bytes 131104 | tf_op jit(solution)/shard_map/ppermute | solution.py:38
  55.4 1.4 %collective-permute-start.29 = (bf16[2,64,512]{2,1,0:T(8,128)(2,1)S(1)}, bf16[2,64,512]{2,1,0:T(8,128)(2,1)S(1)}, u32[]{:S(2)}, u32[]{:S(2)}) collective-permute-start(bf16[2,64,512]{2,1,0:T(8,128)(2,1)S(1)} %get-tuple-element.58), channel_id=1, source_target_pairs={{0,1},{1,0},{2,3},{3,2},{4,5},{5,4},{6,7},{7,6},{8,9},{9,8},{10,11... | collective-permute-start | bytes 393224 | tf_op jit(solution)/shard_map/ppermute | solution.py:38
  56.8 0.8 %collective-permute-start.25 = (bf16[128,256]{1,0:T(8,128)(2,1)S(1)}, bf16[128,256]{1,0:T(8,128)(2,1)S(1)}, u32[]{:S(2)}, u32[]{:S(2)}) collective-permute-start(bf16[128,256]{1,0:T(8,128)(2,1)S(1)} %get-tuple-element.53), channel_id=1, source_target_pairs={{0,2},{1,3},{2,0},{3,1},{4,6},{5,7},{6,4},{7,5},{8,10},{9,11},{10,... | collective-permute-start | bytes 196616 | tf_op jit(solution)/shard_map/ppermute | solution.py:38
  57.5 1.9 %collective-permute-start.23 = (bf16[128,256]{1,0:T(8,128)(2,1)S(1)}, bf16[128,256]{1,0:T(8,128)(2,1)S(1)}, u32[]{:S(2)}, u32[]{:S(2)}) collective-permute-start(bf16[128,256]{1,0:T(8,128)(2,1)S(1)} %get-tuple-element.51), channel_id=1, source_target_pairs={{0,4},{1,5},{2,6},{3,7},{4,0},{5,1},{6,2},{7,3},{8,12},{9,13},{10,... | collective-permute-start | bytes 196616 | tf_op jit(solution)/shard_map/ppermute | solution.py:38
  59.4 1.8 %collective-permute-start.24 = (bf16[128,256]{1,0:T(8,128)(2,1)S(1)}, bf16[128,256]{1,0:T(8,128)(2,1)S(1)}, u32[]{:S(2)}, u32[]{:S(2)}) collective-permute-start(bf16[128,256]{1,0:T(8,128)(2,1)S(1)} %get-tuple-element.52), channel_id=1, source_target_pairs={{0,6},{1,7},{2,4},{3,5},{4,2},{5,3},{6,0},{7,1},{8,14},{9,15},{10,... | collective-permute-start | bytes 196616 | tf_op jit(solution)/shard_map/ppermute | solution.py:38
  61.3 1.1 %collective-permute-start.27 = (bf16[64,512]{1,0:T(8,128)(2,1)S(1)}, bf16[64,512]{1,0:T(8,128)(2,1)S(1)}, u32[]{:S(2)}, u32[]{:S(2)}) collective-permute-start(bf16[64,512]{1,0:T(8,128)(2,1)S(1)} %get-tuple-element.56), channel_id=1, source_target_pairs={{0,4},{1,5},{2,6},{3,7},{4,0},{5,1},{6,2},{7,3},{8,12},{9,13},{10,... | collective-permute-start | bytes 196616 | tf_op jit(solution)/shard_map/ppermute | solution.py:38
  62.4 1.8 %collective-permute-start.28 = (bf16[64,512]{1,0:T(8,128)(2,1)S(1)}, bf16[64,512]{1,0:T(8,128)(2,1)S(1)}, u32[]{:S(2)}, u32[]{:S(2)}) collective-permute-start(bf16[64,512]{1,0:T(8,128)(2,1)S(1)} %get-tuple-element.57), channel_id=1, source_target_pairs={{0,6},{1,7},{2,4},{3,5},{4,2},{5,3},{6,0},{7,1},{8,14},{9,15},{10,... | collective-permute-start | bytes 196616 | tf_op jit(solution)/shard_map/ppermute | solution.py:38
  64.9 1.6 %shard_map.102 = bf16[128,2048]{1,0:T(8,128)(2,1)} custom-call(bf16[128,512]{1,0:T(8,128)(2,1)S(1)} %shard_map.98.refs_4_.refs_0_, bf16[512,512]{1,0:T(8,128)(2,1)S(1)} %copy-done.1, bf16[512,512]{1,0:T(8,128)(2,1)S(1)} %collective-permute-done.7.refs_2_, bf16[512,512]{1,0:T(8,128)(2,1)S(1)} %shard_map.95.refs_3_, ...), custom_call_target="tpu_custom_call" | custom-call | tf_op jit(solution)/shard_map/pallas_call | solution.py:49
  66.5 2.1 %collective-permute-done.23.refs_1_ = bf16[128,256]{1,0:T(8,128)(2,1)S(1)} collective-permute-done((bf16[128,256]{1,0:T(8,128)(2,1)S(1)}, bf16[128,256]{1,0:T(8,128)(2,1)S(1)}, u32[]{:S(2)}, u32[]{:S(2)}) %collective-permute-start.23) | collective-permute-done | bytes 65568 | tf_op jit(solution)/shard_map/ppermute | solution.py:38
  69.3 1.6 %collective-permute-done.27.refs_0_ = bf16[64,512]{1,0:T(8,128)(2,1)S(1)} collective-permute-done((bf16[64,512]{1,0:T(8,128)(2,1)S(1)}, bf16[64,512]{1,0:T(8,128)(2,1)S(1)}, u32[]{:S(2)}, u32[]{:S(2)}) %collective-permute-start.27) | collective-permute-done | bytes 65568 | tf_op jit(solution)/shard_map/ppermute | solution.py:38
  (51 shorter events, 6.3 us)
Async XLA Ops:
  0.6 21.0 %copy-start.1 = (bf16[512,512]{1,0:T(8,128)(2,1)S(1)}, bf16[512,512]{1,0:T(8,128)(2,1)}, u32[]{:S(2)}) copy-start(bf16[512,512]{1,0:T(8,128)(2,1)} %refs_1_.3) | copy-start | bytes 1572868
  0.6 21.0 %collective-permute-start.8 = (bf16[512,512]{1,0:T(8,128)(2,1)}, bf16[512,512]{1,0:T(8,128)(2,1)S(1)}, u32[]{:S(2)}, u32[]{:S(2)}) collective-permute-start(bf16[512,512]{1,0:T(8,128)(2,1)} %refs_1_.3), channel_id=1, source_target_pairs={{0,16},{8,24},{16,0},{24,8},{1,17},{9,25},{17,1},{25,9},{2,18},{10... | collective-permute-start | bytes 1572872 | tf_op jit(solution)/shard_map/ppermute | solution.py:38
  5.9 7.4 %collective-permute-start.2 = (bf16[144,512]{1,0:T(8,128)(2,1)}, bf16[144,512]{1,0:T(8,128)(2,1)S(1)}, u32[]{:S(2)}, u32[]{:S(2)}) collective-permute-start(bf16[144,512]{1,0:T(8,128)(2,1)} %get-tuple-element.35), channel_id=1, source_target_pairs={{0,2},{1,3},{2,0},{3,1},{4,6},{5,7},{6,4},{7,5},{8,10},{9,11},{10,... | collective-permute-start | bytes 442376 | tf_op jit(solution)/shard_map/ppermute | solution.py:38
  7.5 14.1 %collective-permute-start = (bf16[144,512]{1,0:T(8,128)(2,1)}, bf16[144,512]{1,0:T(8,128)(2,1)S(1)}, u32[]{:S(2)}, u32[]{:S(2)}) collective-permute-start(bf16[144,512]{1,0:T(8,128)(2,1)} %get-tuple-element.33), channel_id=1, source_target_pairs={{0,4},{1,5},{2,6},{3,7},{4,0},{5,1},{6,2},{7,3},{8,12},{9,13},{10,... | collective-permute-start | bytes 442376 | tf_op jit(solution)/shard_map/ppermute | solution.py:38
  10.1 11.5 %collective-permute-start.1 = (bf16[144,512]{1,0:T(8,128)(2,1)}, bf16[144,512]{1,0:T(8,128)(2,1)S(1)}, u32[]{:S(2)}, u32[]{:S(2)}) collective-permute-start(bf16[144,512]{1,0:T(8,128)(2,1)} %get-tuple-element.34), channel_id=1, source_target_pairs={{0,6},{1,7},{2,4},{3,5},{4,2},{5,3},{6,0},{7,1},{8,14},{9,15},{10,... | collective-permute-start | bytes 442376 | tf_op jit(solution)/shard_map/ppermute | solution.py:38
  10.4 11.3 %collective-permute-start.3 = (bf16[144,512]{1,0:T(8,128)(2,1)}, bf16[144,512]{1,0:T(8,128)(2,1)S(1)}, u32[]{:S(2)}, u32[]{:S(2)}) collective-permute-start(bf16[144,512]{1,0:T(8,128)(2,1)} %get-tuple-element.32.refs_2_), channel_id=1, source_target_pairs={{0,1},{1,0},{2,3},{3,2},{4,5},{5,4},{6,7},{7,6},{8,9},{9,8},{10,11... | collective-permute-start | bytes 442376 | tf_op jit(solution)/shard_map/ppermute | solution.py:38
  13.3 8.3 %collective-permute-start.4 = (bf16[144,512]{1,0:T(8,128)(2,1)S(1)}, bf16[144,512]{1,0:T(8,128)(2,1)S(1)}, u32[]{:S(2)}, u32[]{:S(2)}) collective-permute-start(bf16[144,512]{1,0:T(8,128)(2,1)S(1)} %collective-permute-done.2.refs_3_.refs_5_), channel_id=1, source_target_pairs={{0,1},{1,0},{2,3},{3,2},{4,5},{5,4},{6,7},{7,6},{8,9},{9,8},{10,11... | collective-permute-start | bytes 442376 | tf_op jit(solution)/shard_map/ppermute | solution.py:38
  21.6 2.6 %collective-permute-start.7 = (bf16[512,512]{1,0:T(8,128)(2,1)S(1)}, bf16[512,512]{1,0:T(8,128)(2,1)S(1)}, u32[]{:S(2)}, u32[]{:S(2)}) collective-permute-start(bf16[512,512]{1,0:T(8,128)(2,1)S(1)} %copy-done.1), channel_id=1, source_target_pairs={{0,8},{8,0},{16,24},{24,16},{1,9},{9,1},{17,25},{25,17},{2,10},{10... | collective-permute-start | bytes 1572872 | tf_op jit(solution)/shard_map/ppermute | solution.py:38
  21.7 2.6 %collective-permute-start.9 = (bf16[512,512]{1,0:T(8,128)(2,1)S(1)}, bf16[512,512]{1,0:T(8,128)(2,1)S(1)}, u32[]{:S(2)}, u32[]{:S(2)}) collective-permute-start(bf16[512,512]{1,0:T(8,128)(2,1)S(1)} %shard_map.95.refs_3_), channel_id=1, source_target_pairs={{0,8},{8,0},{16,24},{24,16},{1,9},{9,1},{17,25},{25,17},{2,10},{10... | collective-permute-start | bytes 1572872 | tf_op jit(solution)/shard_map/ppermute | solution.py:38
  22.2 6.7 %collective-permute-start.5 = (bf16[144,512]{1,0:T(8,128)(2,1)S(1)}, bf16[144,512]{1,0:T(8,128)(2,1)S(1)}, u32[]{:S(2)}, u32[]{:S(2)}) collective-permute-start(bf16[144,512]{1,0:T(8,128)(2,1)S(1)} %collective-permute-done.refs_1_.refs_3_), channel_id=1, source_target_pairs={{0,1},{1,0},{2,3},{3,2},{4,5},{5,4},{6,7},{7,6},{8,9},{9,8},{10,11... | collective-permute-start | bytes 442376 | tf_op jit(solution)/shard_map/ppermute | solution.py:38
  23.7 7.5 %collective-permute-start.6 = (bf16[144,512]{1,0:T(8,128)(2,1)S(1)}, bf16[144,512]{1,0:T(8,128)(2,1)S(1)}, u32[]{:S(2)}, u32[]{:S(2)}) collective-permute-start(bf16[144,512]{1,0:T(8,128)(2,1)S(1)} %collective-permute-done.1.refs_2_.refs_4_), channel_id=1, source_target_pairs={{0,1},{1,0},{2,3},{3,2},{4,5},{5,4},{6,7},{7,6},{8,9},{9,8},{10,11... | collective-permute-start | bytes 442376 | tf_op jit(solution)/shard_map/ppermute | solution.py:38
  24.8 6.4 %collective-permute-start.10 = (bf16[128,128]{1,0:T(8,128)(2,1)S(1)}, bf16[128,128]{1,0:T(8,128)(2,1)S(1)}, u32[]{:S(2)}, u32[]{:S(2)}) collective-permute-start(bf16[128,128]{1,0:T(8,128)(2,1)S(1)} %get-tuple-element.37), channel_id=1, source_target_pairs={{0,4},{1,5},{2,6},{3,7},{4,0},{5,1},{6,2},{7,3},{8,12},{9,13},{10,... | collective-permute-start | bytes 98312 | tf_op jit(solution)/shard_map/ppermute | solution.py:38
  27.6 5.7 %collective-permute-start.11 = (bf16[128,128]{1,0:T(8,128)(2,1)S(1)}, bf16[128,128]{1,0:T(8,128)(2,1)S(1)}, u32[]{:S(2)}, u32[]{:S(2)}) collective-permute-start(bf16[128,128]{1,0:T(8,128)(2,1)S(1)} %get-tuple-element.38), channel_id=1, source_target_pairs={{0,6},{1,7},{2,4},{3,5},{4,2},{5,3},{6,0},{7,1},{8,14},{9,15},{10,... | collective-permute-start | bytes 98312 | tf_op jit(solution)/shard_map/ppermute | solution.py:38
  29.0 4.4 %collective-permute-start.12 = (bf16[128,128]{1,0:T(8,128)(2,1)S(1)}, bf16[128,128]{1,0:T(8,128)(2,1)S(1)}, u32[]{:S(2)}, u32[]{:S(2)}) collective-permute-start(bf16[128,128]{1,0:T(8,128)(2,1)S(1)} %get-tuple-element.39), channel_id=1, source_target_pairs={{0,2},{1,3},{2,0},{3,1},{4,6},{5,7},{6,4},{7,5},{8,10},{9,11},{10,... | collective-permute-start | bytes 98312 | tf_op jit(solution)/shard_map/ppermute | solution.py:38
  39.4 8.1 %collective-permute-start.13 = (bf16[4,128,256]{2,1,0:T(8,128)(2,1)S(1)}, bf16[4,128,256]{2,1,0:T(8,128)(2,1)S(1)}, u32[]{:S(2)}, u32[]{:S(2)}) collective-permute-start(bf16[4,128,256]{2,1,0:T(8,128)(2,1)S(1)} %get-tuple-element.41), channel_id=1, source_target_pairs={{0,1},{1,0},{2,3},{3,2},{4,5},{5,4},{6,7},{7,6},{8,9},{9,8},{10,11... | collective-permute-start | bytes 786440 | tf_op jit(solution)/shard_map/ppermute | solution.py:38
  39.6 8.9 %collective-permute-start.15 = (bf16[2,128,512]{2,1,0:T(8,128)(2,1)S(1)}, bf16[2,128,512]{2,1,0:T(8,128)(2,1)S(1)}, u32[]{:S(2)}, u32[]{:S(2)}) collective-permute-start(bf16[2,128,512]{2,1,0:T(8,128)(2,1)S(1)} %get-tuple-element.44), channel_id=1, source_target_pairs={{0,16},{8,24},{16,0},{24,8},{1,17},{9,25},{17,1},{25,9},{2,18},{10... | collective-permute-start | bytes 786440 | tf_op jit(solution)/shard_map/ppermute | solution.py:38
  40.9 5.2 %collective-permute-start.17 = (bf16[128,128]{1,0:T(8,128)(2,1)S(1)}, bf16[128,128]{1,0:T(8,128)(2,1)S(1)}, u32[]{:S(2)}, u32[]{:S(2)}) collective-permute-start(bf16[128,128]{1,0:T(8,128)(2,1)S(1)} %get-tuple-element.46), channel_id=1, source_target_pairs={{0,4},{1,5},{2,6},{3,7},{4,0},{5,1},{6,2},{7,3},{8,12},{9,13},{10,... | collective-permute-start | bytes 98312 | tf_op jit(solution)/shard_map/ppermute | solution.py:38
  41.9 5.7 %collective-permute-start.18 = (bf16[128,128]{1,0:T(8,128)(2,1)S(1)}, bf16[128,128]{1,0:T(8,128)(2,1)S(1)}, u32[]{:S(2)}, u32[]{:S(2)}) collective-permute-start(bf16[128,128]{1,0:T(8,128)(2,1)S(1)} %get-tuple-element.47), channel_id=1, source_target_pairs={{0,6},{1,7},{2,4},{3,5},{4,2},{5,3},{6,0},{7,1},{8,14},{9,15},{10,... | collective-permute-start | bytes 98312 | tf_op jit(solution)/shard_map/ppermute | solution.py:38
  43.2 4.4 %collective-permute-start.19 = (bf16[128,128]{1,0:T(8,128)(2,1)S(1)}, bf16[128,128]{1,0:T(8,128)(2,1)S(1)}, u32[]{:S(2)}, u32[]{:S(2)}) collective-permute-start(bf16[128,128]{1,0:T(8,128)(2,1)S(1)} %get-tuple-element.48), channel_id=1, source_target_pairs={{0,2},{1,3},{2,0},{3,1},{4,6},{5,7},{6,4},{7,5},{8,10},{9,11},{10,... | collective-permute-start | bytes 98312 | tf_op jit(solution)/shard_map/ppermute | solution.py:38
  46.0 6.7 %collective-permute-start.14 = (bf16[128,512]{1,0:T(8,128)(2,1)S(1)}, bf16[128,512]{1,0:T(8,128)(2,1)S(1)}, u32[]{:S(2)}, u32[]{:S(2)}) collective-permute-start(bf16[128,512]{1,0:T(8,128)(2,1)S(1)} %get-tuple-element.43), channel_id=1, source_target_pairs={{0,8},{8,0},{16,24},{24,16},{1,9},{9,1},{17,25},{25,17},{2,10},{10... | collective-permute-start | bytes 393224 | tf_op jit(solution)/shard_map/ppermute | solution.py:38
  47.7 5.0 %collective-permute-start.21 = (bf16[128,512]{1,0:T(8,128)(2,1)S(1)}, bf16[128,512]{1,0:T(8,128)(2,1)S(1)}, u32[]{:S(2)}, u32[]{:S(2)}) collective-permute-start(bf16[128,512]{1,0:T(8,128)(2,1)S(1)} %shard_map.98.refs_4_.refs_0_), channel_id=1, source_target_pairs={{0,16},{8,24},{16,0},{24,8},{1,17},{9,25},{17,1},{25,9},{2,18},{10... | collective-permute-start | bytes 393224 | tf_op jit(solution)/shard_map/ppermute | solution.py:38
  48.5 4.2 %collective-permute-start.20 = (bf16[128,512]{1,0:T(8,128)(2,1)S(1)}, bf16[128,512]{1,0:T(8,128)(2,1)S(1)}, u32[]{:S(2)}, u32[]{:S(2)}) collective-permute-start(bf16[128,512]{1,0:T(8,128)(2,1)S(1)} %shard_map.98.refs_4_.refs_0_), channel_id=1, source_target_pairs={{0,8},{8,0},{16,24},{24,16},{1,9},{9,1},{17,25},{25,17},{2,10},{10... | collective-permute-start | bytes 393224 | tf_op jit(solution)/shard_map/ppermute | solution.py:38
  48.6 4.2 %collective-permute-start.16 = (bf16[128,512]{1,0:T(8,128)(2,1)S(1)}, bf16[128,512]{1,0:T(8,128)(2,1)S(1)}, u32[]{:S(2)}, u32[]{:S(2)}) collective-permute-start(bf16[128,512]{1,0:T(8,128)(2,1)S(1)} %get-tuple-element.61), channel_id=1, source_target_pairs={{0,8},{8,0},{16,24},{24,16},{1,9},{9,1},{17,25},{25,17},{2,10},{10... | collective-permute-start | bytes 393224 | tf_op jit(solution)/shard_map/ppermute | solution.py:38
  52.7 1.3 %collective-permute-start.22 = (bf16[128,512]{1,0:T(8,128)(2,1)S(1)}, bf16[128,512]{1,0:T(8,128)(2,1)S(1)}, u32[]{:S(2)}, u32[]{:S(2)}) collective-permute-start(bf16[128,512]{1,0:T(8,128)(2,1)S(1)} %collective-permute-done.21.refs_6_), channel_id=1, source_target_pairs={{0,8},{8,0},{16,24},{24,16},{1,9},{9,1},{17,25},{25,17},{2,10},{10... | collective-permute-start | bytes 393224 | tf_op jit(solution)/shard_map/ppermute | solution.py:38
  54.6 6.6 %collective-permute-start.26 = (bf16[2,64,512]{2,1,0:T(8,128)(2,1)S(1)}, bf16[2,64,512]{2,1,0:T(8,128)(2,1)S(1)}, u32[]{:S(2)}, u32[]{:S(2)}) collective-permute-start(bf16[2,64,512]{2,1,0:T(8,128)(2,1)S(1)} %get-tuple-element.55), channel_id=1, source_target_pairs={{0,1},{1,0},{2,3},{3,2},{4,5},{5,4},{6,7},{7,6},{8,9},{9,8},{10,11... | collective-permute-start | bytes 393224 | tf_op jit(solution)/shard_map/ppermute | solution.py:38
  55.4 8.8 %collective-permute-start.29 = (bf16[2,64,512]{2,1,0:T(8,128)(2,1)S(1)}, bf16[2,64,512]{2,1,0:T(8,128)(2,1)S(1)}, u32[]{:S(2)}, u32[]{:S(2)}) collective-permute-start(bf16[2,64,512]{2,1,0:T(8,128)(2,1)S(1)} %get-tuple-element.58), channel_id=1, source_target_pairs={{0,1},{1,0},{2,3},{3,2},{4,5},{5,4},{6,7},{7,6},{8,9},{9,8},{10,11... | collective-permute-start | bytes 393224 | tf_op jit(solution)/shard_map/ppermute | solution.py:38
  56.8 5.6 %collective-permute-start.25 = (bf16[128,256]{1,0:T(8,128)(2,1)S(1)}, bf16[128,256]{1,0:T(8,128)(2,1)S(1)}, u32[]{:S(2)}, u32[]{:S(2)}) collective-permute-start(bf16[128,256]{1,0:T(8,128)(2,1)S(1)} %get-tuple-element.53), channel_id=1, source_target_pairs={{0,2},{1,3},{2,0},{3,1},{4,6},{5,7},{6,4},{7,5},{8,10},{9,11},{10,... | collective-permute-start | bytes 196616 | tf_op jit(solution)/shard_map/ppermute | solution.py:38
  57.5 11.1 %collective-permute-start.23 = (bf16[128,256]{1,0:T(8,128)(2,1)S(1)}, bf16[128,256]{1,0:T(8,128)(2,1)S(1)}, u32[]{:S(2)}, u32[]{:S(2)}) collective-permute-start(bf16[128,256]{1,0:T(8,128)(2,1)S(1)} %get-tuple-element.51), channel_id=1, source_target_pairs={{0,4},{1,5},{2,6},{3,7},{4,0},{5,1},{6,2},{7,3},{8,12},{9,13},{10,... | collective-permute-start | bytes 196616 | tf_op jit(solution)/shard_map/ppermute | solution.py:38
  59.4 9.2 %collective-permute-start.24 = (bf16[128,256]{1,0:T(8,128)(2,1)S(1)}, bf16[128,256]{1,0:T(8,128)(2,1)S(1)}, u32[]{:S(2)}, u32[]{:S(2)}) collective-permute-start(bf16[128,256]{1,0:T(8,128)(2,1)S(1)} %get-tuple-element.52), channel_id=1, source_target_pairs={{0,6},{1,7},{2,4},{3,5},{4,2},{5,3},{6,0},{7,1},{8,14},{9,15},{10,... | collective-permute-start | bytes 196616 | tf_op jit(solution)/shard_map/ppermute | solution.py:38
  61.3 9.7 %collective-permute-start.27 = (bf16[64,512]{1,0:T(8,128)(2,1)S(1)}, bf16[64,512]{1,0:T(8,128)(2,1)S(1)}, u32[]{:S(2)}, u32[]{:S(2)}) collective-permute-start(bf16[64,512]{1,0:T(8,128)(2,1)S(1)} %get-tuple-element.56), channel_id=1, source_target_pairs={{0,4},{1,5},{2,6},{3,7},{4,0},{5,1},{6,2},{7,3},{8,12},{9,13},{10,... | collective-permute-start | bytes 196616 | tf_op jit(solution)/shard_map/ppermute | solution.py:38
  62.4 8.6 %collective-permute-start.28 = (bf16[64,512]{1,0:T(8,128)(2,1)S(1)}, bf16[64,512]{1,0:T(8,128)(2,1)S(1)}, u32[]{:S(2)}, u32[]{:S(2)}) collective-permute-start(bf16[64,512]{1,0:T(8,128)(2,1)S(1)} %get-tuple-element.57), channel_id=1, source_target_pairs={{0,6},{1,7},{2,4},{3,5},{4,2},{5,3},{6,0},{7,1},{8,14},{9,15},{10,... | collective-permute-start | bytes 196616 | tf_op jit(solution)/shard_map/ppermute | solution.py:38
  64.2 6.8 %collective-permute-start.30 = (bf16[64,512]{1,0:T(8,128)(2,1)S(1)}, bf16[64,512]{1,0:T(8,128)(2,1)S(1)}, u32[]{:S(2)}, u32[]{:S(2)}) collective-permute-start(bf16[64,512]{1,0:T(8,128)(2,1)S(1)} %get-tuple-element.59), channel_id=1, source_target_pairs={{0,2},{1,3},{2,0},{3,1},{4,6},{5,7},{6,4},{7,5},{8,10},{9,11},{10,... | collective-permute-start | bytes 196616 | tf_op jit(solution)/shard_map/ppermute | solution.py:38
  (3 other events, 27.4 us)

commit v5 on v4

--- a/solution.py
+++ b/solution.py
@@ -304,14 +304,15 @@
     send_ref[...] = dq_all[KV_HEADS:].astype(jnp.bfloat16)
 
 
-def owner_kernel(*rest):
-    dkv_refs, out_ref, parts = rest[:KV_HEADS], rest[KV_HEADS], rest[KV_HEADS + 1]
+def owner_kernel(keep_ref, got_ref, *rest):
+    dkv_refs, out_ref, dq_refs, parts = rest[:KV_HEADS], rest[KV_HEADS], rest[KV_HEADS + 1:-1], rest[-1]
     head, _ = head_side()
     for m, ref in enumerate(by_head(dkv_refs)):
         parts[jnp.bitwise_xor(head, m)] = ref[...]
     keys = [parts[g, :, :HEAD_DIM] for g in range(KV_HEADS)]
     values = [parts[g, :, HEAD_DIM:] for g in range(KV_HEADS)]
     out_ref[...] = jnp.concatenate(keys + values, axis=1)
+    pair_kernel(keep_ref, got_ref, *dq_refs)
 
 
 def pair_kernel(keep_ref, got_ref, *out_refs):
@@ -437,10 +438,12 @@
     hid = over_fsdp(hid + [hid_far[m] for m in range(fsdp - far)], far // 2)
     dkv = along_heads(dkv)
     give = swapped(give, "ctx", 1)
-    (kv_grad,) = call(
-        owner_kernel, [sds((rows, columns))], [pltpu.VMEM((KV_HEADS,) + block, jnp.bfloat16)],
-        far_first(dkv), after=(give,))
-    grads = over_fsdp([kv_grad] * fsdp, far)
+    kv_grad, *dq = call(
+        owner_kernel, [sds((rows, columns))] + [sds(wide)] * KV_HEADS,
+        [pltpu.VMEM((KV_HEADS,) + block, jnp.bfloat16)], (keep, give, *far_first(dkv)))
+    dq = along_heads(dq)
+    grad_far = held(swapped(kv_grad, "fsdp", far), dq[2:3])
+    grads = over_fsdp([kv_grad] * far + [grad_far] * (fsdp - far), far // 2)
     if teams == 1:
         share = (span // devices, columns)
         two = (2,) + share
@@ -448,15 +451,13 @@
             functools.partial(sides_kernel, fsdp), [sds(two, f32)] * 2 + [sds(two)] * 2,
             [pltpu.VMEM((devices,) + share, f32)], (*hid, *grads))
         formed = (near_sums,)
-        dq = along_heads(call(pair_kernel, [sds(wide)] * KV_HEADS, [], (keep, give), after=formed))
         far_sums = call(pair_kernel, [sds(share)] * 2, [], (far_sums, swapped(far_send, "ctx", 1)))
         near_sums = call(
-            pair_kernel, [sds(share, f32), sds(share)], [], (near_sums, swapped(near_send, "ctx", 1)), after=dq[1:2])
+            pair_kernel, [sds(share, f32), sds(share)], [], (near_sums, swapped(near_send, "ctx", 1)))
         own_sums, *sums = far_first(along_heads([*near_sums, *far_sums]))
         (weight_grads,) = call(own_total_kernel, [sds(share, f32)], [], (*sums, own_sums))
     else:
         formed = call(functools.partial(weight_kernel, fsdp), [sds((span, columns))], [], (*hid, *grads))
-        dq = along_heads(call(pair_kernel, [sds(wide)] * KV_HEADS, [], (keep, give), after=formed))
         sums = lax.all_to_all(formed[0].reshape(devices, span // devices, columns), "ctx", 0, 0, tiled=True)
         (weight_grads,) = call(total_kernel, [sds((span // devices, columns), f32)], [], (sums,))
     (query_grads,) = call(query_kernel, [sds((rows, Q_HEADS * HEAD_DIM))], [], far_first(dq), after=formed)

time: 72.1 us -> 72.9 us (1.011); the launches traced: 71.7 us -> 73.3 us
  starting transfers between devices: 33.7 us -> 35.5 us
  Pallas kernels: 12.6 us -> 10.9 us
  waiting for transfers between devices: 24.5 us -> 26.1 us
    ppermute x31, starting transfers between devices: 33.7 us -> 35.5 us  [swapped(): return lax.ppermute(array, axis, [(i, i ^ bits) for i in range(size)])]
    pallas_call x11 -> x10, Pallas kernels: 12.6 us -> 10.9 us  [call(): pl.pallas_call(body, out_shape=out_shape, in_specs=specs, out_specs=[VMEM...]
    ppermute x31, waiting for transfers between devices: 24.5 us -> 26.1 us  [swapped(): return lax.ppermute(array, axis, [(i, i ^ bits) for i in range(size)])]
  transfers between devices with their start and end apart: 31 -> 31, of which waited for: 10 -> 11; matrix products, arithmetic and copies ran while one was open for 0% -> 0% of each run, Pallas kernels for 7% -> 7%
where the time goes in v5:
time: 72.9 us; the launch traced here: 73.3 us
  starting transfers between devices  35.5 us (49%)
  waiting for transfers between devices  26.1 us (36%)
  Pallas kernels  10.9 us (15%)
  between operations  0.78 us (1%)
    ppermute x31, starting transfers between devices, swapped(): return lax.ppermute(array, axis, [(i, i ^ bits) for i in range(size)])  35.5 us
    ppermute x31, waiting for transfers between devices, swapped(): return lax.ppermute(array, axis, [(i, i ^ bits) for i in range(size)])  26.1 us
    pallas_call x10, Pallas kernels, call(): pl.pallas_call(body, out_shape=out_shape, in_specs=specs, out_specs=[VMEM...  10.9 us
  transfers between devices with their start and end apart: 31, of which 11 were waited for; matrix products, arithmetic and copies ran while one was open for 0% of the time, Pallas kernels for 7%

profile of v5, /device:TPU:0, one launch (start us, length us, event | category | flops | bytes accessed | tf_op | source)
XLA Modules:
  0.0 73.3 jit_solution(7769252490586093692)
XLA Ops:
  0.6 3.0 %collective-permute-start.8 = (bf16[512,512]{1,0:T(8,128)(2,1)}, bf16[512,512]{1,0:T(8,128)(2,1)S(1)}, u32[]{:S(2)}, u32[]{:S(2)}) collective-permute-start(bf16[512,512]{1,0:T(8,128)(2,1)} %refs_1_.3), channel_id=1, source_target_pairs={{0,16},{8,24},{16,0},{24,8},{1,17},{9,25},{17,1},{25,9},{2,18},{10... | collective-permute-start | bytes 1572872 | tf_op jit(solution)/shard_map/ppermute | solution.py:38
  3.7 2.2 %shard_map.94 = (bf16[144,512]{1,0:T(8,128)(2,1)}, bf16[144,512]{1,0:T(8,128)(2,1)}, bf16[144,512]{1,0:T(8,128)(2,1)}, bf16[144,512]{1,0:T(8,128)(2,1)}) custom-call(bf16[128,1024]{1,0:T(8,128)(2,1)} %bitcast.14, bf16[128,1024]{1,0:T(8,128)(2,1)} %bitcast.15, bf16[128,1024]{1,0:T(8,128)(2,1)} %bitcast.16, f32[16,128]{1,0:T(8,128)} %bitcast.18), custom_call_target="tpu_custom_call" | custom-call | tf_op jit(solution)/shard_map/pallas_call | solution.py:49
  5.9 1.6 %collective-permute-start.2 = (bf16[144,512]{1,0:T(8,128)(2,1)}, bf16[144,512]{1,0:T(8,128)(2,1)S(1)}, u32[]{:S(2)}, u32[]{:S(2)}) collective-permute-start(bf16[144,512]{1,0:T(8,128)(2,1)} %get-tuple-element.36), channel_id=1, source_target_pairs={{0,2},{1,3},{2,0},{3,1},{4,6},{5,7},{6,4},{7,5},{8,10},{9,11},{10,... | collective-permute-start | bytes 442376 | tf_op jit(solution)/shard_map/ppermute | solution.py:38
  7.5 2.6 %collective-permute-start = (bf16[144,512]{1,0:T(8,128)(2,1)}, bf16[144,512]{1,0:T(8,128)(2,1)S(1)}, u32[]{:S(2)}, u32[]{:S(2)}) collective-permute-start(bf16[144,512]{1,0:T(8,128)(2,1)} %get-tuple-element.34), channel_id=1, source_target_pairs={{0,4},{1,5},{2,6},{3,7},{4,0},{5,1},{6,2},{7,3},{8,12},{9,13},{10,... | collective-permute-start | bytes 442376 | tf_op jit(solution)/shard_map/ppermute | solution.py:38
  10.4 1.5 %collective-permute-start.3 = (bf16[144,512]{1,0:T(8,128)(2,1)}, bf16[144,512]{1,0:T(8,128)(2,1)S(1)}, u32[]{:S(2)}, u32[]{:S(2)}) collective-permute-start(bf16[144,512]{1,0:T(8,128)(2,1)} %get-tuple-element.33.refs_2_), channel_id=1, source_target_pairs={{0,1},{1,0},{2,3},{3,2},{4,5},{5,4},{6,7},{7,6},{8,9},{9,8},{10,11... | collective-permute-start | bytes 442376 | tf_op jit(solution)/shard_map/ppermute | solution.py:38
  11.9 1.5 %collective-permute-done.2.refs_3_.refs_5_ = bf16[144,512]{1,0:T(8,128)(2,1)S(1)} collective-permute-done((bf16[144,512]{1,0:T(8,128)(2,1)}, bf16[144,512]{1,0:T(8,128)(2,1)S(1)}, u32[]{:S(2)}, u32[]{:S(2)}) %collective-permute-start.2) | collective-permute-done | bytes 147488 | tf_op jit(solution)/shard_map/ppermute | solution.py:38
  13.3 1.5 %collective-permute-start.4 = (bf16[144,512]{1,0:T(8,128)(2,1)S(1)}, bf16[144,512]{1,0:T(8,128)(2,1)S(1)}, u32[]{:S(2)}, u32[]{:S(2)}) collective-permute-start(bf16[144,512]{1,0:T(8,128)(2,1)S(1)} %collective-permute-done.2.refs_3_.refs_5_), channel_id=1, source_target_pairs={{0,1},{1,0},{2,3},{3,2},{4,5},{5,4},{6,7},{7,6},{8,9},{9,8},{10,11... | collective-permute-start | bytes 442376 | tf_op jit(solution)/shard_map/ppermute | solution.py:38
  14.8 6.8 %collective-permute-done.refs_1_.refs_3_ = bf16[144,512]{1,0:T(8,128)(2,1)S(1)} collective-permute-done((bf16[144,512]{1,0:T(8,128)(2,1)}, bf16[144,512]{1,0:T(8,128)(2,1)S(1)}, u32[]{:S(2)}, u32[]{:S(2)}) %collective-permute-start) | collective-permute-done | bytes 147488 | tf_op jit(solution)/shard_map/ppermute | solution.py:38
  22.2 1.5 %collective-permute-start.5 = (bf16[144,512]{1,0:T(8,128)(2,1)S(1)}, bf16[144,512]{1,0:T(8,128)(2,1)S(1)}, u32[]{:S(2)}, u32[]{:S(2)}) collective-permute-start(bf16[144,512]{1,0:T(8,128)(2,1)S(1)} %collective-permute-done.refs_1_.refs_3_), channel_id=1, source_target_pairs={{0,1},{1,0},{2,3},{3,2},{4,5},{5,4},{6,7},{7,6},{8,9},{9,8},{10,11... | collective-permute-start | bytes 442376 | tf_op jit(solution)/shard_map/ppermute | solution.py:38
  24.8 2.8 %collective-permute-start.10 = (bf16[128,128]{1,0:T(8,128)(2,1)S(1)}, bf16[128,128]{1,0:T(8,128)(2,1)S(1)}, u32[]{:S(2)}, u32[]{:S(2)}) collective-permute-start(bf16[128,128]{1,0:T(8,128)(2,1)S(1)} %get-tuple-element.38), channel_id=1, source_target_pairs={{0,4},{1,5},{2,6},{3,7},{4,0},{5,1},{6,2},{7,3},{8,12},{9,13},{10,... | collective-permute-start | bytes 98312 | tf_op jit(solution)/shard_map/ppermute | solution.py:38
  27.6 1.3 %collective-permute-start.11 = (bf16[128,128]{1,0:T(8,128)(2,1)S(1)}, bf16[128,128]{1,0:T(8,128)(2,1)S(1)}, u32[]{:S(2)}, u32[]{:S(2)}) collective-permute-start(bf16[128,128]{1,0:T(8,128)(2,1)S(1)} %get-tuple-element.39), channel_id=1, source_target_pairs={{0,6},{1,7},{2,4},{3,5},{4,2},{5,3},{6,0},{7,1},{8,14},{9,15},{10,... | collective-permute-start | bytes 98312 | tf_op jit(solution)/shard_map/ppermute | solution.py:38
  29.0 2.3 %collective-permute-done.6.refs_9_ = bf16[144,512]{1,0:T(8,128)(2,1)S(1)} collective-permute-done((bf16[144,512]{1,0:T(8,128)(2,1)S(1)}, bf16[144,512]{1,0:T(8,128)(2,1)S(1)}, u32[]{:S(2)}, u32[]{:S(2)}) %collective-permute-start.6) | collective-permute-done | bytes 147488 | tf_op jit(solution)/shard_map/ppermute | solution.py:38
  31.2 2.1 %collective-permute-done.11.refs_12_ = bf16[128,128]{1,0:T(8,128)(2,1)S(1)} collective-permute-done((bf16[128,128]{1,0:T(8,128)(2,1)S(1)}, bf16[128,128]{1,0:T(8,128)(2,1)S(1)}, u32[]{:S(2)}, u32[]{:S(2)}) %collective-permute-start.11) | collective-permute-done | bytes 32800 | tf_op jit(solution)/shard_map/ppermute | solution.py:38
  33.4 4.4 %shard_map.97 = (bf16[128,128]{1,0:T(8,128)(2,1)S(1)}, bf16[128,128]{1,0:T(8,128)(2,1)S(1)}, bf16[128,128]{1,0:T(8,128)(2,1)S(1)}, bf16[128,128]{1,0:T(8,128)(2,...) custom-call(s32[1,8]{1,0:T(1,128)S(1)} %copy-done.3, ...), custom_call_target="tpu_custom_call" | custom-call | tf_op jit(solution)/shard_map/pallas_call | solution.py:49
  37.8 3.4 %collective-permute-start.13 = (bf16[4,128,256]{2,1,0:T(8,128)(2,1)S(1)}, bf16[4,128,256]{2,1,0:T(8,128)(2,1)S(1)}, u32[]{:S(2)}, u32[]{:S(2)}) collective-permute-start(bf16[4,128,256]{2,1,0:T(8,128)(2,1)S(1)} %get-tuple-element.42), channel_id=1, source_target_pairs={{0,1},{1,0},{2,3},{3,2},{4,5},{5,4},{6,7},{7,6},{8,9},{9,8},{10,11... | collective-permute-start | bytes 786440 | tf_op jit(solution)/shard_map/ppermute | solution.py:38
  41.7 1.0 %collective-permute-start.14 = (bf16[128,128]{1,0:T(8,128)(2,1)S(1)}, bf16[128,128]{1,0:T(8,128)(2,1)S(1)}, u32[]{:S(2)}, u32[]{:S(2)}) collective-permute-start(bf16[128,128]{1,0:T(8,128)(2,1)S(1)} %get-tuple-element.44), channel_id=1, source_target_pairs={{0,4},{1,5},{2,6},{3,7},{4,0},{5,1},{6,2},{7,3},{8,12},{9,13},{10,... | collective-permute-start | bytes 98312 | tf_op jit(solution)/shard_map/ppermute | solution.py:38
  42.7 1.4 %collective-permute-start.15 = (bf16[128,128]{1,0:T(8,128)(2,1)S(1)}, bf16[128,128]{1,0:T(8,128)(2,1)S(1)}, u32[]{:S(2)}, u32[]{:S(2)}) collective-permute-start(bf16[128,128]{1,0:T(8,128)(2,1)S(1)} %get-tuple-element.45), channel_id=1, source_target_pairs={{0,6},{1,7},{2,4},{3,5},{4,2},{5,3},{6,0},{7,1},{8,14},{9,15},{10,... | collective-permute-start | bytes 98312 | tf_op jit(solution)/shard_map/ppermute | solution.py:38
  44.0 1.1 %collective-permute-start.16 = (bf16[128,128]{1,0:T(8,128)(2,1)S(1)}, bf16[128,128]{1,0:T(8,128)(2,1)S(1)}, u32[]{:S(2)}, u32[]{:S(2)}) collective-permute-start(bf16[128,128]{1,0:T(8,128)(2,1)S(1)} %get-tuple-element.46), channel_id=1, source_target_pairs={{0,2},{1,3},{2,0},{3,1},{4,6},{5,7},{6,4},{7,5},{8,10},{9,11},{10,... | collective-permute-start | bytes 98312 | tf_op jit(solution)/shard_map/ppermute | solution.py:38
  45.2 1.3 %collective-permute-done.14.refs_3_ = bf16[128,128]{1,0:T(8,128)(2,1)S(1)} collective-permute-done((bf16[128,128]{1,0:T(8,128)(2,1)S(1)}, bf16[128,128]{1,0:T(8,128)(2,1)S(1)}, u32[]{:S(2)}, u32[]{:S(2)}) %collective-permute-start.14) | collective-permute-done | bytes 32800 | tf_op jit(solution)/shard_map/ppermute | solution.py:38
  46.5 1.9 %collective-permute-done.15.refs_4_ = bf16[128,128]{1,0:T(8,128)(2,1)S(1)} collective-permute-done((bf16[128,128]{1,0:T(8,128)(2,1)S(1)}, bf16[128,128]{1,0:T(8,128)(2,1)S(1)}, u32[]{:S(2)}, u32[]{:S(2)}) %collective-permute-start.15) | collective-permute-done | bytes 32800 | tf_op jit(solution)/shard_map/ppermute | solution.py:38
  48.5 1.7 %collective-permute-start.24 = (bf16[128,512]{1,0:T(8,128)(2,1)S(1)}, bf16[128,512]{1,0:T(8,128)(2,1)S(1)}, u32[]{:S(2)}, u32[]{:S(2)}) collective-permute-start(bf16[128,512]{1,0:T(8,128)(2,1)S(1)} %get-tuple-element.54.refs_4_.refs_0_), channel_id=1, source_target_pairs={{0,16},{8,24},{16,0},{24,8},{1,17},{9,25},{17,1},{25,9},{2,18},{10... | collective-permute-start | bytes 393224 | tf_op jit(solution)/shard_map/ppermute | solution.py:38
  50.2 1.2 %collective-permute-start.17 = (bf16[128,256]{1,0:T(8,128)(2,1)S(1)}, bf16[128,256]{1,0:T(8,128)(2,1)S(1)}, u32[]{:S(2)}, u32[]{:S(2)}) collective-permute-start(bf16[128,256]{1,0:T(8,128)(2,1)S(1)} %get-tuple-element.48), channel_id=1, source_target_pairs={{0,4},{1,5},{2,6},{3,7},{4,0},{5,1},{6,2},{7,3},{8,12},{9,13},{10,... | collective-permute-start | bytes 196616 | tf_op jit(solution)/shard_map/ppermute | solution.py:38
  51.7 5.3 %collective-permute-done.17.refs_1_ = bf16[128,256]{1,0:T(8,128)(2,1)S(1)} collective-permute-done((bf16[128,256]{1,0:T(8,128)(2,1)S(1)}, bf16[128,256]{1,0:T(8,128)(2,1)S(1)}, u32[]{:S(2)}, u32[]{:S(2)}) %collective-permute-start.17) | collective-permute-done | bytes 65568 | tf_op jit(solution)/shard_map/ppermute | solution.py:38
  57.0 1.3 %collective-permute-done.25.refs_7_ = bf16[128,512]{1,0:T(8,128)(2,1)S(1)} collective-permute-done((bf16[128,512]{1,0:T(8,128)(2,1)S(1)}, bf16[128,512]{1,0:T(8,128)(2,1)S(1)}, u32[]{:S(2)}, u32[]{:S(2)}) %collective-permute-start.25) | collective-permute-done | bytes 131104 | tf_op jit(solution)/shard_map/ppermute | solution.py:38
  59.0 1.9 %collective-permute-start.29 = (bf16[2,64,512]{2,1,0:T(8,128)(2,1)S(1)}, bf16[2,64,512]{2,1,0:T(8,128)(2,1)S(1)}, u32[]{:S(2)}, u32[]{:S(2)}) collective-permute-start(bf16[2,64,512]{2,1,0:T(8,128)(2,1)S(1)} %get-tuple-element.60), channel_id=1, source_target_pairs={{0,1},{1,0},{2,3},{3,2},{4,5},{5,4},{6,7},{7,6},{8,9},{9,8},{10,11... | collective-permute-start | bytes 393224 | tf_op jit(solution)/shard_map/ppermute | solution.py:38
  61.0 2.0 %collective-permute-start.18 = (bf16[128,256]{1,0:T(8,128)(2,1)S(1)}, bf16[128,256]{1,0:T(8,128)(2,1)S(1)}, u32[]{:S(2)}, u32[]{:S(2)}) collective-permute-start(bf16[128,256]{1,0:T(8,128)(2,1)S(1)} %get-tuple-element.49), channel_id=1, source_target_pairs={{0,6},{1,7},{2,4},{3,5},{4,2},{5,3},{6,0},{7,1},{8,14},{9,15},{10,... | collective-permute-start | bytes 196616 | tf_op jit(solution)/shard_map/ppermute | solution.py:38
  63.0 2.3 %collective-permute-done.26.refs_1_ = bf16[2,64,512]{2,1,0:T(8,128)(2,1)S(1)} collective-permute-done((bf16[2,64,512]{2,1,0:T(8,128)(2,1)S(1)}, bf16[2,64,512]{2,1,0:T(8,128)(2,1)S(1)}, u32[]{:S(2)}, u32[]{:S(2)}) %collective-permute-start.26) | collective-permute-done | bytes 131104 | tf_op jit(solution)/shard_map/ppermute | solution.py:38
  65.5 2.0 %collective-permute-start.28 = (bf16[64,512]{1,0:T(8,128)(2,1)S(1)}, bf16[64,512]{1,0:T(8,128)(2,1)S(1)}, u32[]{:S(2)}, u32[]{:S(2)}) collective-permute-start(bf16[64,512]{1,0:T(8,128)(2,1)S(1)} %get-tuple-element.59), channel_id=1, source_target_pairs={{0,6},{1,7},{2,4},{3,5},{4,2},{5,3},{6,0},{7,1},{8,14},{9,15},{10,... | collective-permute-start | bytes 196616 | tf_op jit(solution)/shard_map/ppermute | solution.py:38
  67.5 1.5 %collective-permute-start.30 = (bf16[64,512]{1,0:T(8,128)(2,1)S(1)}, bf16[64,512]{1,0:T(8,128)(2,1)S(1)}, u32[]{:S(2)}, u32[]{:S(2)}) collective-permute-start(bf16[64,512]{1,0:T(8,128)(2,1)S(1)} %get-tuple-element.61), channel_id=1, source_target_pairs={{0,2},{1,3},{2,0},{3,1},{4,6},{5,7},{6,4},{7,5},{8,10},{9,11},{10,... | collective-permute-start | bytes 196616 | tf_op jit(solution)/shard_map/ppermute | solution.py:38
  69.0 1.6 %shard_map.102 = bf16[128,2048]{1,0:T(8,128)(2,1)} custom-call(bf16[128,512]{1,0:T(8,128)(2,1)S(1)} %get-tuple-element.54.refs_4_.refs_0_, bf16[512,512]{1,0:T(8,128)(2,1)S(1)} %copy-done.1, bf16[512,512]{1,0:T(8,128)(2,1)S(1)} %collective-permute-done.7.refs_2_, bf16[512,512]{1,0:T(8,128)(2,1)S(1)} %shard_map.95.refs_3_, ...), custom_call_target="tpu_custom_call" | custom-call | tf_op jit(solution)/shard_map/pallas_call | solution.py:49
  70.6 0.7 %shard_map.101 = bf16[128,1024]{1,0:T(8,128)(2,1)} custom-call(bf16[128,256]{1,0:T(8,128)(2,1)S(1)} %get-tuple-element.47.refs_0_, bf16[128,256]{1,0:T(8,128)(2,1)S(1)} %collective-permute-done.17.refs_1_, bf16[128,256]{1,0:T(8,128)(2,1)S(1)} %collective-permute-done.18.refs_2_, bf16[128,256]{1,0:T(8,128)(2,1)S(1)} %collective-permute-done.19.refs_3_, ...), custom_call_target="tpu_custom_call" | custom-call | tf_op jit(solution)/shard_map/pallas_call | solution.py:49
  71.3 0.8 %collective-permute-done.27.refs_0_ = bf16[64,512]{1,0:T(8,128)(2,1)S(1)} collective-permute-done((bf16[64,512]{1,0:T(8,128)(2,1)S(1)}, bf16[64,512]{1,0:T(8,128)(2,1)S(1)}, u32[]{:S(2)}, u32[]{:S(2)}) %collective-permute-start.27) | collective-permute-done | bytes 65568 | tf_op jit(solution)/shard_map/ppermute | solution.py:38
  (51 shorter events, 4.9 us)
Async XLA Ops:
  0.6 21.0 %copy-start.1 = (bf16[512,512]{1,0:T(8,128)(2,1)S(1)}, bf16[512,512]{1,0:T(8,128)(2,1)}, u32[]{:S(2)}) copy-start(bf16[512,512]{1,0:T(8,128)(2,1)} %refs_1_.3) | copy-start | bytes 1572868
  0.6 21.0 %collective-permute-start.8 = (bf16[512,512]{1,0:T(8,128)(2,1)}, bf16[512,512]{1,0:T(8,128)(2,1)S(1)}, u32[]{:S(2)}, u32[]{:S(2)}) collective-permute-start(bf16[512,512]{1,0:T(8,128)(2,1)} %refs_1_.3), channel_id=1, source_target_pairs={{0,16},{8,24},{16,0},{24,8},{1,17},{9,25},{17,1},{25,9},{2,18},{10... | collective-permute-start | bytes 1572872 | tf_op jit(solution)/shard_map/ppermute | solution.py:38
  5.9 7.4 %collective-permute-start.2 = (bf16[144,512]{1,0:T(8,128)(2,1)}, bf16[144,512]{1,0:T(8,128)(2,1)S(1)}, u32[]{:S(2)}, u32[]{:S(2)}) collective-permute-start(bf16[144,512]{1,0:T(8,128)(2,1)} %get-tuple-element.36), channel_id=1, source_target_pairs={{0,2},{1,3},{2,0},{3,1},{4,6},{5,7},{6,4},{7,5},{8,10},{9,11},{10,... | collective-permute-start | bytes 442376 | tf_op jit(solution)/shard_map/ppermute | solution.py:38
  7.5 14.1 %collective-permute-start = (bf16[144,512]{1,0:T(8,128)(2,1)}, bf16[144,512]{1,0:T(8,128)(2,1)S(1)}, u32[]{:S(2)}, u32[]{:S(2)}) collective-permute-start(bf16[144,512]{1,0:T(8,128)(2,1)} %get-tuple-element.34), channel_id=1, source_target_pairs={{0,4},{1,5},{2,6},{3,7},{4,0},{5,1},{6,2},{7,3},{8,12},{9,13},{10,... | collective-permute-start | bytes 442376 | tf_op jit(solution)/shard_map/ppermute | solution.py:38
  10.1 11.5 %collective-permute-start.1 = (bf16[144,512]{1,0:T(8,128)(2,1)}, bf16[144,512]{1,0:T(8,128)(2,1)S(1)}, u32[]{:S(2)}, u32[]{:S(2)}) collective-permute-start(bf16[144,512]{1,0:T(8,128)(2,1)} %get-tuple-element.35), channel_id=1, source_target_pairs={{0,6},{1,7},{2,4},{3,5},{4,2},{5,3},{6,0},{7,1},{8,14},{9,15},{10,... | collective-permute-start | bytes 442376 | tf_op jit(solution)/shard_map/ppermute | solution.py:38
  10.4 11.3 %collective-permute-start.3 = (bf16[144,512]{1,0:T(8,128)(2,1)}, bf16[144,512]{1,0:T(8,128)(2,1)S(1)}, u32[]{:S(2)}, u32[]{:S(2)}) collective-permute-start(bf16[144,512]{1,0:T(8,128)(2,1)} %get-tuple-element.33.refs_2_), channel_id=1, source_target_pairs={{0,1},{1,0},{2,3},{3,2},{4,5},{5,4},{6,7},{7,6},{8,9},{9,8},{10,11... | collective-permute-start | bytes 442376 | tf_op jit(solution)/shard_map/ppermute | solution.py:38
  13.3 8.3 %collective-permute-start.4 = (bf16[144,512]{1,0:T(8,128)(2,1)S(1)}, bf16[144,512]{1,0:T(8,128)(2,1)S(1)}, u32[]{:S(2)}, u32[]{:S(2)}) collective-permute-start(bf16[144,512]{1,0:T(8,128)(2,1)S(1)} %collective-permute-done.2.refs_3_.refs_5_), channel_id=1, source_target_pairs={{0,1},{1,0},{2,3},{3,2},{4,5},{5,4},{6,7},{7,6},{8,9},{9,8},{10,11... | collective-permute-start | bytes 442376 | tf_op jit(solution)/shard_map/ppermute | solution.py:38
  21.6 2.6 %collective-permute-start.7 = (bf16[512,512]{1,0:T(8,128)(2,1)S(1)}, bf16[512,512]{1,0:T(8,128)(2,1)S(1)}, u32[]{:S(2)}, u32[]{:S(2)}) collective-permute-start(bf16[512,512]{1,0:T(8,128)(2,1)S(1)} %copy-done.1), channel_id=1, source_target_pairs={{0,8},{8,0},{16,24},{24,16},{1,9},{9,1},{17,25},{25,17},{2,10},{10... | collective-permute-start | bytes 1572872 | tf_op jit(solution)/shard_map/ppermute | solution.py:38
  21.7 2.6 %collective-permute-start.9 = (bf16[512,512]{1,0:T(8,128)(2,1)S(1)}, bf16[512,512]{1,0:T(8,128)(2,1)S(1)}, u32[]{:S(2)}, u32[]{:S(2)}) collective-permute-start(bf16[512,512]{1,0:T(8,128)(2,1)S(1)} %shard_map.95.refs_3_), channel_id=1, source_target_pairs={{0,8},{8,0},{16,24},{24,16},{1,9},{9,1},{17,25},{25,17},{2,10},{10... | collective-permute-start | bytes 1572872 | tf_op jit(solution)/shard_map/ppermute | solution.py:38
  22.2 6.7 %collective-permute-start.5 = (bf16[144,512]{1,0:T(8,128)(2,1)S(1)}, bf16[144,512]{1,0:T(8,128)(2,1)S(1)}, u32[]{:S(2)}, u32[]{:S(2)}) collective-permute-start(bf16[144,512]{1,0:T(8,128)(2,1)S(1)} %collective-permute-done.refs_1_.refs_3_), channel_id=1, source_target_pairs={{0,1},{1,0},{2,3},{3,2},{4,5},{5,4},{6,7},{7,6},{8,9},{9,8},{10,11... | collective-permute-start | bytes 442376 | tf_op jit(solution)/shard_map/ppermute | solution.py:38
  23.7 7.5 %collective-permute-start.6 = (bf16[144,512]{1,0:T(8,128)(2,1)S(1)}, bf16[144,512]{1,0:T(8,128)(2,1)S(1)}, u32[]{:S(2)}, u32[]{:S(2)}) collective-permute-start(bf16[144,512]{1,0:T(8,128)(2,1)S(1)} %collective-permute-done.1.refs_2_.refs_4_), channel_id=1, source_target_pairs={{0,1},{1,0},{2,3},{3,2},{4,5},{5,4},{6,7},{7,6},{8,9},{9,8},{10,11... | collective-permute-start | bytes 442376 | tf_op jit(solution)/shard_map/ppermute | solution.py:38
  24.8 6.4 %collective-permute-start.10 = (bf16[128,128]{1,0:T(8,128)(2,1)S(1)}, bf16[128,128]{1,0:T(8,128)(2,1)S(1)}, u32[]{:S(2)}, u32[]{:S(2)}) collective-permute-start(bf16[128,128]{1,0:T(8,128)(2,1)S(1)} %get-tuple-element.38), channel_id=1, source_target_pairs={{0,4},{1,5},{2,6},{3,7},{4,0},{5,1},{6,2},{7,3},{8,12},{9,13},{10,... | collective-permute-start | bytes 98312 | tf_op jit(solution)/shard_map/ppermute | solution.py:38
  27.6 5.7 %collective-permute-start.11 = (bf16[128,128]{1,0:T(8,128)(2,1)S(1)}, bf16[128,128]{1,0:T(8,128)(2,1)S(1)}, u32[]{:S(2)}, u32[]{:S(2)}) collective-permute-start(bf16[128,128]{1,0:T(8,128)(2,1)S(1)} %get-tuple-element.39), channel_id=1, source_target_pairs={{0,6},{1,7},{2,4},{3,5},{4,2},{5,3},{6,0},{7,1},{8,14},{9,15},{10,... | collective-permute-start | bytes 98312 | tf_op jit(solution)/shard_map/ppermute | solution.py:38
  29.0 4.4 %collective-permute-start.12 = (bf16[128,128]{1,0:T(8,128)(2,1)S(1)}, bf16[128,128]{1,0:T(8,128)(2,1)S(1)}, u32[]{:S(2)}, u32[]{:S(2)}) collective-permute-start(bf16[128,128]{1,0:T(8,128)(2,1)S(1)} %get-tuple-element.40), channel_id=1, source_target_pairs={{0,2},{1,3},{2,0},{3,1},{4,6},{5,7},{6,4},{7,5},{8,10},{9,11},{10,... | collective-permute-start | bytes 98312 | tf_op jit(solution)/shard_map/ppermute | solution.py:38
  37.8 10.6 %collective-permute-start.13 = (bf16[4,128,256]{2,1,0:T(8,128)(2,1)S(1)}, bf16[4,128,256]{2,1,0:T(8,128)(2,1)S(1)}, u32[]{:S(2)}, u32[]{:S(2)}) collective-permute-start(bf16[4,128,256]{2,1,0:T(8,128)(2,1)S(1)} %get-tuple-element.42), channel_id=1, source_target_pairs={{0,1},{1,0},{2,3},{3,2},{4,5},{5,4},{6,7},{7,6},{8,9},{9,8},{10,11... | collective-permute-start | bytes 786440 | tf_op jit(solution)/shard_map/ppermute | solution.py:38
  41.2 10.2 %collective-permute-start.21 = (bf16[2,128,512]{2,1,0:T(8,128)(2,1)S(1)}, bf16[2,128,512]{2,1,0:T(8,128)(2,1)S(1)}, u32[]{:S(2)}, u32[]{:S(2)}) collective-permute-start(bf16[2,128,512]{2,1,0:T(8,128)(2,1)S(1)} %get-tuple-element.53), channel_id=1, source_target_pairs={{0,16},{8,24},{16,0},{24,8},{1,17},{9,25},{17,1},{25,9},{2,18},{10... | collective-permute-start | bytes 786440 | tf_op jit(solution)/shard_map/ppermute | solution.py:38
  41.7 4.8 %collective-permute-start.14 = (bf16[128,128]{1,0:T(8,128)(2,1)S(1)}, bf16[128,128]{1,0:T(8,128)(2,1)S(1)}, u32[]{:S(2)}, u32[]{:S(2)}) collective-permute-start(bf16[128,128]{1,0:T(8,128)(2,1)S(1)} %get-tuple-element.44), channel_id=1, source_target_pairs={{0,4},{1,5},{2,6},{3,7},{4,0},{5,1},{6,2},{7,3},{8,12},{9,13},{10,... | collective-permute-start | bytes 98312 | tf_op jit(solution)/shard_map/ppermute | solution.py:38
  42.7 5.7 %collective-permute-start.15 = (bf16[128,128]{1,0:T(8,128)(2,1)S(1)}, bf16[128,128]{1,0:T(8,128)(2,1)S(1)}, u32[]{:S(2)}, u32[]{:S(2)}) collective-permute-start(bf16[128,128]{1,0:T(8,128)(2,1)S(1)} %get-tuple-element.45), channel_id=1, source_target_pairs={{0,6},{1,7},{2,4},{3,5},{4,2},{5,3},{6,0},{7,1},{8,14},{9,15},{10,... | collective-permute-start | bytes 98312 | tf_op jit(solution)/shard_map/ppermute | solution.py:38
  44.0 4.4 %collective-permute-start.16 = (bf16[128,128]{1,0:T(8,128)(2,1)S(1)}, bf16[128,128]{1,0:T(8,128)(2,1)S(1)}, u32[]{:S(2)}, u32[]{:S(2)}) collective-permute-start(bf16[128,128]{1,0:T(8,128)(2,1)S(1)} %get-tuple-element.46), channel_id=1, source_target_pairs={{0,2},{1,3},{2,0},{3,1},{4,6},{5,7},{6,4},{7,5},{8,10},{9,11},{10,... | collective-permute-start | bytes 98312 | tf_op jit(solution)/shard_map/ppermute | solution.py:38
  46.5 10.5 %collective-permute-start.20 = (bf16[128,512]{1,0:T(8,128)(2,1)S(1)}, bf16[128,512]{1,0:T(8,128)(2,1)S(1)}, u32[]{:S(2)}, u32[]{:S(2)}) collective-permute-start(bf16[128,512]{1,0:T(8,128)(2,1)S(1)} %get-tuple-element.52), channel_id=1, source_target_pairs={{0,8},{8,0},{16,24},{24,16},{1,9},{9,1},{17,25},{25,17},{2,10},{10... | collective-permute-start | bytes 393224 | tf_op jit(solution)/shard_map/ppermute | solution.py:38
  48.5 8.5 %collective-permute-start.24 = (bf16[128,512]{1,0:T(8,128)(2,1)S(1)}, bf16[128,512]{1,0:T(8,128)(2,1)S(1)}, u32[]{:S(2)}, u32[]{:S(2)}) collective-permute-start(bf16[128,512]{1,0:T(8,128)(2,1)S(1)} %get-tuple-element.54.refs_4_.refs_0_), channel_id=1, source_target_pairs={{0,16},{8,24},{16,0},{24,8},{1,17},{9,25},{17,1},{25,9},{2,18},{10... | collective-permute-start | bytes 393224 | tf_op jit(solution)/shard_map/ppermute | solution.py:38
  50.2 6.8 %collective-permute-start.23 = (bf16[128,512]{1,0:T(8,128)(2,1)S(1)}, bf16[128,512]{1,0:T(8,128)(2,1)S(1)}, u32[]{:S(2)}, u32[]{:S(2)}) collective-permute-start(bf16[128,512]{1,0:T(8,128)(2,1)S(1)} %get-tuple-element.54.refs_4_.refs_0_), channel_id=1, source_target_pairs={{0,8},{8,0},{16,24},{24,16},{1,9},{9,1},{17,25},{25,17},{2,10},{10... | collective-permute-start | bytes 393224 | tf_op jit(solution)/shard_map/ppermute | solution.py:38
  50.2 6.8 %collective-permute-start.17 = (bf16[128,256]{1,0:T(8,128)(2,1)S(1)}, bf16[128,256]{1,0:T(8,128)(2,1)S(1)}, u32[]{:S(2)}, u32[]{:S(2)}) collective-permute-start(bf16[128,256]{1,0:T(8,128)(2,1)S(1)} %get-tuple-element.48), channel_id=1, source_target_pairs={{0,4},{1,5},{2,6},{3,7},{4,0},{5,1},{6,2},{7,3},{8,12},{9,13},{10,... | collective-permute-start | bytes 196616 | tf_op jit(solution)/shard_map/ppermute | solution.py:38
  51.5 5.6 %collective-permute-start.22 = (bf16[128,512]{1,0:T(8,128)(2,1)S(1)}, bf16[128,512]{1,0:T(8,128)(2,1)S(1)}, u32[]{:S(2)}, u32[]{:S(2)}) collective-permute-start(bf16[128,512]{1,0:T(8,128)(2,1)S(1)} %get-tuple-element.63), channel_id=1, source_target_pairs={{0,8},{8,0},{16,24},{24,16},{1,9},{9,1},{17,25},{25,17},{2,10},{10... | collective-permute-start | bytes 393224 | tf_op jit(solution)/shard_map/ppermute | solution.py:38
  57.0 1.3 %collective-permute-start.25 = (bf16[128,512]{1,0:T(8,128)(2,1)S(1)}, bf16[128,512]{1,0:T(8,128)(2,1)S(1)}, u32[]{:S(2)}, u32[]{:S(2)}) collective-permute-start(bf16[128,512]{1,0:T(8,128)(2,1)S(1)} %shard_map.99.refs_6_), channel_id=1, source_target_pairs={{0,8},{8,0},{16,24},{24,16},{1,9},{9,1},{17,25},{25,17},{2,10},{10... | collective-permute-start | bytes 393224 | tf_op jit(solution)/shard_map/ppermute | solution.py:38
  58.9 6.4 %collective-permute-start.26 = (bf16[2,64,512]{2,1,0:T(8,128)(2,1)S(1)}, bf16[2,64,512]{2,1,0:T(8,128)(2,1)S(1)}, u32[]{:S(2)}, u32[]{:S(2)}) collective-permute-start(bf16[2,64,512]{2,1,0:T(8,128)(2,1)S(1)} %get-tuple-element.57), channel_id=1, source_target_pairs={{0,1},{1,0},{2,3},{3,2},{4,5},{5,4},{6,7},{7,6},{8,9},{9,8},{10,11... | collective-permute-start | bytes 393224 | tf_op jit(solution)/shard_map/ppermute | solution.py:38
  59.0 8.5 %collective-permute-start.29 = (bf16[2,64,512]{2,1,0:T(8,128)(2,1)S(1)}, bf16[2,64,512]{2,1,0:T(8,128)(2,1)S(1)}, u32[]{:S(2)}, u32[]{:S(2)}) collective-permute-start(bf16[2,64,512]{2,1,0:T(8,128)(2,1)S(1)} %get-tuple-element.60), channel_id=1, source_target_pairs={{0,1},{1,0},{2,3},{3,2},{4,5},{5,4},{6,7},{7,6},{8,9},{9,8},{10,11... | collective-permute-start | bytes 393224 | tf_op jit(solution)/shard_map/ppermute | solution.py:38
  61.0 9.6 %collective-permute-start.18 = (bf16[128,256]{1,0:T(8,128)(2,1)S(1)}, bf16[128,256]{1,0:T(8,128)(2,1)S(1)}, u32[]{:S(2)}, u32[]{:S(2)}) collective-permute-start(bf16[128,256]{1,0:T(8,128)(2,1)S(1)} %get-tuple-element.49), channel_id=1, source_target_pairs={{0,6},{1,7},{2,4},{3,5},{4,2},{5,3},{6,0},{7,1},{8,14},{9,15},{10,... | collective-permute-start | bytes 196616 | tf_op jit(solution)/shard_map/ppermute | solution.py:38
  63.0 7.6 %collective-permute-start.19 = (bf16[128,256]{1,0:T(8,128)(2,1)S(1)}, bf16[128,256]{1,0:T(8,128)(2,1)S(1)}, u32[]{:S(2)}, u32[]{:S(2)}) collective-permute-start(bf16[128,256]{1,0:T(8,128)(2,1)S(1)} %get-tuple-element.50), channel_id=1, source_target_pairs={{0,2},{1,3},{2,0},{3,1},{4,6},{5,7},{6,4},{7,5},{8,10},{9,11},{10,... | collective-permute-start | bytes 196616 | tf_op jit(solution)/shard_map/ppermute | solution.py:38
  65.3 6.8 %collective-permute-start.27 = (bf16[64,512]{1,0:T(8,128)(2,1)S(1)}, bf16[64,512]{1,0:T(8,128)(2,1)S(1)}, u32[]{:S(2)}, u32[]{:S(2)}) collective-permute-start(bf16[64,512]{1,0:T(8,128)(2,1)S(1)} %get-tuple-element.58), channel_id=1, source_target_pairs={{0,4},{1,5},{2,6},{3,7},{4,0},{5,1},{6,2},{7,3},{8,12},{9,13},{10,... | collective-permute-start | bytes 196616 | tf_op jit(solution)/shard_map/ppermute | solution.py:38
  65.5 6.7 %collective-permute-start.28 = (bf16[64,512]{1,0:T(8,128)(2,1)S(1)}, bf16[64,512]{1,0:T(8,128)(2,1)S(1)}, u32[]{:S(2)}, u32[]{:S(2)}) collective-permute-start(bf16[64,512]{1,0:T(8,128)(2,1)S(1)} %get-tuple-element.59), channel_id=1, source_target_pairs={{0,6},{1,7},{2,4},{3,5},{4,2},{5,3},{6,0},{7,1},{8,14},{9,15},{10,... | collective-permute-start | bytes 196616 | tf_op jit(solution)/shard_map/ppermute | solution.py:38
  67.5 5.1 %collective-permute-start.30 = (bf16[64,512]{1,0:T(8,128)(2,1)S(1)}, bf16[64,512]{1,0:T(8,128)(2,1)S(1)}, u32[]{:S(2)}, u32[]{:S(2)}) collective-permute-start(bf16[64,512]{1,0:T(8,128)(2,1)S(1)} %get-tuple-element.61), channel_id=1, source_target_pairs={{0,2},{1,3},{2,0},{3,1},{4,6},{5,7},{6,4},{7,5},{8,10},{9,11},{10,... | collective-permute-start | bytes 196616 | tf_op jit(solution)/shard_map/ppermute | solution.py:38
  (3 other events, 27.4 us)

commit v6 on v4

--- a/solution.py
+++ b/solution.py
@@ -180,28 +180,29 @@
     return keys.astype(jnp.bfloat16), values.astype(jnp.bfloat16)
 
 
-def tile(keys, values, query, grad, stats, mask):
-    size, edge = keys.shape[0] // 2, mask.shape[1]
-    pairs = len(stats)
-    width = query.shape[0] // pairs
-    scores = matmul(keys, query, NT)
-    prob_grad = matmul(values, grad, NT)
-    lows, grads = [], []
-    for head in range(2):
-        part = slice(head * size, (head + 1) * size)
-        lse = jnp.concatenate([lines[head] for lines in stats], axis=1)
-        delta = jnp.concatenate([lines[2 + head] for lines in stats], axis=1)
-        probs = jnp.exp(scores[part] - lse)
-        pieces = []
-        for first in range(0, pairs * width, width):
-            pieces.append(jnp.where(mask, probs[:, first:first + edge], 0.0))
-            if edge < width:
-                pieces.append(probs[:, first + edge:first + width])
-        probs = jnp.concatenate(pieces, axis=1)
-        lows.append(probs.astype(jnp.bfloat16))
-        grads.append((probs * (prob_grad[part] - delta)).astype(jnp.bfloat16))
-    low, score_grad = jnp.concatenate(lows, axis=0), jnp.concatenate(grads, axis=0)
-    return matmul(score_grad, query), matmul(low, grad), matmul(score_grad, keys, TN)
+def tile(keys, values, query, grad, stats, mask, rooms):
+    size = mask.shape[0]
+    width = query.shape[0]
+    of_pair = width // len(stats)
+    scores, prob_grad, low, score_grad = (room.at[:, 0:width] for room in rooms)
+    scores[...] = matmul(keys, query, NT)
+    prob_grad[...] = matmul(values, grad, NT)
+    for first in range(0, width, size):
+        pair, start = first // of_pair, first % of_pair
+        for head in range(2):
+            part = (slice(head * size, (head + 1) * size), slice(first, first + size))
+            lse, delta = (stats[pair][i][:, start:start + size] for i in (head, 2 + head))
+            probs = jnp.exp(scores[part] - lse)
+            if start == 0:
+                probs = jnp.where(mask, probs, 0.0)
+            low[part] = probs.astype(jnp.bfloat16)
+            score_grad[part] = (probs * (prob_grad[part] - delta)).astype(jnp.bfloat16)
+    left = score_grad[...]
+    return matmul(left, query), matmul(low[...], grad), matmul(left, keys, TN)
+
+
+def rooms_for(rows, width):
+    return [pltpu.VMEM((2 * rows, width), kind) for kind in (jnp.float32, jnp.float32, jnp.bfloat16, jnp.bfloat16)]
 
 
 def folded(key_sum, value_sum):
@@ -227,7 +228,7 @@
     qd_refs, kv_refs, rest = rest[:TEAM], rest[TEAM:TEAM + KV_HEADS], rest[TEAM + KV_HEADS:]
     dkv_refs, keep_ref, send_ref, rest = rest[:KV_HEADS], rest[KV_HEADS], rest[KV_HEADS + 1], rest[KV_HEADS + 2:]
     near_refs, far_ref, rest = rest[:near_parts], rest[near_parts], rest[near_parts + 1:]
-    q_all, go_all, stat_all, key_all, value_all, dq_all, dkv_all, sems = rest
+    q_all, go_all, stat_all, key_all, value_all, dq_all, dkv_all, sems, *rooms = rest
     moves = hidden_moves(hid_ref, near_refs, far_ref, sems)
     rows = kv_refs[0].shape[0]
     head, side = head_side()
@@ -253,7 +254,8 @@
             query = q_all[:, block:].reshape(PAIRS * count * rows, PAIR)
             grad = go_all[:, block:].reshape(PAIRS * count * rows, PAIR)
             key_sum, value_sum, query_part = tile(
-                key_all[block], value_all[block], query, grad, [pair_stats(stats, pair) for pair in range(PAIRS)], mask)
+                key_all[block], value_all[block], query, grad, [pair_stats(stats, pair) for pair in range(PAIRS)], mask,
+                rooms)
             dq_all[:, block:] += query_part.reshape(PAIRS, count, rows, PAIR)
             dkv_all[block] = folded(key_sum, value_sum)
 
@@ -267,7 +269,7 @@
         copy.wait()
 
 
-def teams_kernel(order_ref, qd_ref, kv_ref, dkv_ref, keep_ref, send_ref, dq_all):
+def teams_kernel(order_ref, qd_ref, kv_ref, dkv_ref, keep_ref, send_ref, dq_all, *rooms):
     rows = kv_ref.shape[1]
     head, side = head_side()
     base = lax.axis_index("ctx") // TEAM * TEAM
@@ -296,7 +298,7 @@
                     first = pair * PAIR
                     key_part, value_part, query_part = tile(
                         keys, values, one[0:rows, first:first + PAIR], one[0:rows, GROUP + first:GROUP + first + PAIR],
-                        [pair_stats(stats, pair)], mask)
+                        [pair_stats(stats, pair)], mask, rooms)
                     dq_all[at, :, first:first + PAIR] += query_part
                     dkv_ref[block] += folded(key_part, value_part)
 
@@ -420,7 +422,8 @@
             functools.partial(sequence_kernel, far), [sds(block)] * KV_HEADS + [sds(half, f32), sds(half)] + cut,
             [pltpu.VMEM((PAIRS, TEAM) + block, jnp.bfloat16)] * 2 + [pltpu.VMEM((TEAM, 2 * GROUPS, rows), f32)]
             + [pltpu.VMEM((TEAM, 2 * rows, PAIR), jnp.bfloat16)] * 2
-            + [pltpu.VMEM((PAIRS, TEAM) + block, f32), pltpu.VMEM((TEAM,) + block, f32), cut_sems],
+            + [pltpu.VMEM((PAIRS, TEAM) + block, f32), pltpu.VMEM((TEAM,) + block, f32), cut_sems]
+            + rooms_for(rows, PAIRS * TEAM * rows),
             (block_order, inputs, *far_first(qd[:KV_HEADS]), *qd[KV_HEADS:], *far_first(kv)), smem=1, hbm=1)
         dkv, (keep, give, *hid, hid_far) = outs[:KV_HEADS], outs[KV_HEADS:]
     else:
@@ -428,7 +431,7 @@
         kv = lax.all_gather(jnp.stack(kv), "ctx", axis_index_groups=alike, axis=0, tiled=True)
         dkv, keep, give = call(
             teams_kernel, [sds((teams * KV_HEADS,) + block, f32), sds(half, f32), sds(half)],
-            [pltpu.VMEM((TEAM,) + wide, f32)], (block_order, jnp.stack(qd), kv), smem=1)
+            [pltpu.VMEM((TEAM,) + wide, f32)] + rooms_for(rows, rows), (block_order, jnp.stack(qd), kv), smem=1)
         dkv = lax.psum_scatter(dkv, "ctx", axis_index_groups=alike, scatter_dimension=0, tiled=True)
         dkv = [dkv[m].astype(jnp.bfloat16) for m in range(KV_HEADS)]
         *hid, hid_far = call(hidden_kernel, cut, [cut_sems], (inputs,), hbm=1)

time: 72.1 us -> 72.2 us (level)
  transfers between devices with their start and end apart: 31 -> 31, of which waited for: 10 -> 11; matrix products, arithmetic and copies ran while one was open for 0% -> 0% of each run, Pallas kernels for 7% -> 7%
where the time goes in v6:
time: 72.2 us; the launch traced here: 72 us
  starting transfers between devices  34 us (47%)
  waiting for transfers between devices  24.4 us (34%)
  Pallas kernels  12.7 us (18%)
  between operations  0.78 us (1%)
    ppermute x31, starting transfers between devices, swapped(): return lax.ppermute(array, axis, [(i, i ^ bits) for i in range(size)])  34 us
    ppermute x31, waiting for transfers between devices, swapped(): return lax.ppermute(array, axis, [(i, i ^ bits) for i in range(size)])  24.4 us
    pallas_call x11, Pallas kernels, call(): pl.pallas_call(body, out_shape=out_shape, in_specs=specs, out_specs=[VMEM...  12.7 us
  transfers between devices with their start and end apart: 31, of which 11 were waited for; matrix products, arithmetic and copies ran while one was open for 0% of the time, Pallas kernels for 7%

profile of v6, /device:TPU:0, one launch (start us, length us, event | category | flops | bytes accessed | tf_op | source)
XLA Modules:
  0.0 72.0 jit_solution(15465464672223819352)
XLA Ops:
  0.6 3.0 %collective-permute-start.8 = (bf16[512,512]{1,0:T(8,128)(2,1)}, bf16[512,512]{1,0:T(8,128)(2,1)S(1)}, u32[]{:S(2)}, u32[]{:S(2)}) collective-permute-start(bf16[512,512]{1,0:T(8,128)(2,1)} %refs_1_.3), channel_id=1, source_target_pairs={{0,16},{8,24},{16,0},{24,8},{1,17},{9,25},{17,1},{25,9},{2,18},{10... | collective-permute-start | bytes 1572872 | tf_op jit(solution)/shard_map/ppermute | solution.py:38
  3.7 2.2 %shard_map.94 = (bf16[144,512]{1,0:T(8,128)(2,1)}, bf16[144,512]{1,0:T(8,128)(2,1)}, bf16[144,512]{1,0:T(8,128)(2,1)}, bf16[144,512]{1,0:T(8,128)(2,1)}) custom-call(bf16[128,1024]{1,0:T(8,128)(2,1)} %bitcast.14, bf16[128,1024]{1,0:T(8,128)(2,1)} %bitcast.15, bf16[128,1024]{1,0:T(8,128)(2,1)} %bitcast.16, f32[16,128]{1,0:T(8,128)} %bitcast.18), custom_call_target="tpu_custom_call" | custom-call | tf_op jit(solution)/shard_map/pallas_call | solution.py:49
  5.9 1.6 %collective-permute-start.2 = (bf16[144,512]{1,0:T(8,128)(2,1)}, bf16[144,512]{1,0:T(8,128)(2,1)S(1)}, u32[]{:S(2)}, u32[]{:S(2)}) collective-permute-start(bf16[144,512]{1,0:T(8,128)(2,1)} %get-tuple-element.35), channel_id=1, source_target_pairs={{0,2},{1,3},{2,0},{3,1},{4,6},{5,7},{6,4},{7,5},{8,10},{9,11},{10,... | collective-permute-start | bytes 442376 | tf_op jit(solution)/shard_map/ppermute | solution.py:38
  7.5 2.6 %collective-permute-start = (bf16[144,512]{1,0:T(8,128)(2,1)}, bf16[144,512]{1,0:T(8,128)(2,1)S(1)}, u32[]{:S(2)}, u32[]{:S(2)}) collective-permute-start(bf16[144,512]{1,0:T(8,128)(2,1)} %get-tuple-element.33), channel_id=1, source_target_pairs={{0,4},{1,5},{2,6},{3,7},{4,0},{5,1},{6,2},{7,3},{8,12},{9,13},{10,... | collective-permute-start | bytes 442376 | tf_op jit(solution)/shard_map/ppermute | solution.py:38
  10.4 1.5 %collective-permute-start.3 = (bf16[144,512]{1,0:T(8,128)(2,1)}, bf16[144,512]{1,0:T(8,128)(2,1)S(1)}, u32[]{:S(2)}, u32[]{:S(2)}) collective-permute-start(bf16[144,512]{1,0:T(8,128)(2,1)} %get-tuple-element.32.refs_2_), channel_id=1, source_target_pairs={{0,1},{1,0},{2,3},{3,2},{4,5},{5,4},{6,7},{7,6},{8,9},{9,8},{10,11... | collective-permute-start | bytes 442376 | tf_op jit(solution)/shard_map/ppermute | solution.py:38
  11.9 1.5 %collective-permute-done.2.refs_3_.refs_5_ = bf16[144,512]{1,0:T(8,128)(2,1)S(1)} collective-permute-done((bf16[144,512]{1,0:T(8,128)(2,1)}, bf16[144,512]{1,0:T(8,128)(2,1)S(1)}, u32[]{:S(2)}, u32[]{:S(2)}) %collective-permute-start.2) | collective-permute-done | bytes 147488 | tf_op jit(solution)/shard_map/ppermute | solution.py:38
  13.3 1.5 %collective-permute-start.4 = (bf16[144,512]{1,0:T(8,128)(2,1)S(1)}, bf16[144,512]{1,0:T(8,128)(2,1)S(1)}, u32[]{:S(2)}, u32[]{:S(2)}) collective-permute-start(bf16[144,512]{1,0:T(8,128)(2,1)S(1)} %collective-permute-done.2.refs_3_.refs_5_), channel_id=1, source_target_pairs={{0,1},{1,0},{2,3},{3,2},{4,5},{5,4},{6,7},{7,6},{8,9},{9,8},{10,11... | collective-permute-start | bytes 442376 | tf_op jit(solution)/shard_map/ppermute | solution.py:38
  14.8 6.8 %collective-permute-done.refs_1_.refs_3_ = bf16[144,512]{1,0:T(8,128)(2,1)S(1)} collective-permute-done((bf16[144,512]{1,0:T(8,128)(2,1)}, bf16[144,512]{1,0:T(8,128)(2,1)S(1)}, u32[]{:S(2)}, u32[]{:S(2)}) %collective-permute-start) | collective-permute-done | bytes 147488 | tf_op jit(solution)/shard_map/ppermute | solution.py:38
  22.2 1.5 %collective-permute-start.5 = (bf16[144,512]{1,0:T(8,128)(2,1)S(1)}, bf16[144,512]{1,0:T(8,128)(2,1)S(1)}, u32[]{:S(2)}, u32[]{:S(2)}) collective-permute-start(bf16[144,512]{1,0:T(8,128)(2,1)S(1)} %collective-permute-done.refs_1_.refs_3_), channel_id=1, source_target_pairs={{0,1},{1,0},{2,3},{3,2},{4,5},{5,4},{6,7},{7,6},{8,9},{9,8},{10,11... | collective-permute-start | bytes 442376 | tf_op jit(solution)/shard_map/ppermute | solution.py:38
  24.8 2.8 %collective-permute-start.10 = (bf16[128,128]{1,0:T(8,128)(2,1)S(1)}, bf16[128,128]{1,0:T(8,128)(2,1)S(1)}, u32[]{:S(2)}, u32[]{:S(2)}) collective-permute-start(bf16[128,128]{1,0:T(8,128)(2,1)S(1)} %get-tuple-element.37), channel_id=1, source_target_pairs={{0,4},{1,5},{2,6},{3,7},{4,0},{5,1},{6,2},{7,3},{8,12},{9,13},{10,... | collective-permute-start | bytes 98312 | tf_op jit(solution)/shard_map/ppermute | solution.py:38
  27.6 1.3 %collective-permute-start.11 = (bf16[128,128]{1,0:T(8,128)(2,1)S(1)}, bf16[128,128]{1,0:T(8,128)(2,1)S(1)}, u32[]{:S(2)}, u32[]{:S(2)}) collective-permute-start(bf16[128,128]{1,0:T(8,128)(2,1)S(1)} %get-tuple-element.38), channel_id=1, source_target_pairs={{0,6},{1,7},{2,4},{3,5},{4,2},{5,3},{6,0},{7,1},{8,14},{9,15},{10,... | collective-permute-start | bytes 98312 | tf_op jit(solution)/shard_map/ppermute | solution.py:38
  29.0 2.3 %collective-permute-done.6.refs_9_ = bf16[144,512]{1,0:T(8,128)(2,1)S(1)} collective-permute-done((bf16[144,512]{1,0:T(8,128)(2,1)S(1)}, bf16[144,512]{1,0:T(8,128)(2,1)S(1)}, u32[]{:S(2)}, u32[]{:S(2)}) %collective-permute-start.6) | collective-permute-done | bytes 147488 | tf_op jit(solution)/shard_map/ppermute | solution.py:38
  31.2 2.1 %collective-permute-done.11.refs_12_ = bf16[128,128]{1,0:T(8,128)(2,1)S(1)} collective-permute-done((bf16[128,128]{1,0:T(8,128)(2,1)S(1)}, bf16[128,128]{1,0:T(8,128)(2,1)S(1)}, u32[]{:S(2)}, u32[]{:S(2)}) %collective-permute-start.11) | collective-permute-done | bytes 32800 | tf_op jit(solution)/shard_map/ppermute | solution.py:38
  33.4 6.2 %shard_map.97 = (bf16[128,128]{1,0:T(8,128)(2,1)S(1)}, bf16[128,128]{1,0:T(8,128)(2,1)S(1)}, bf16[128,128]{1,0:T(8,128)(2,1)S(1)}, bf16[128,128]{1,0:T(8,128)(2,...) custom-call(s32[1,8]{1,0:T(1,128)S(1)} %copy-done.3, ...), custom_call_target="tpu_custom_call" | custom-call | tf_op jit(solution)/shard_map/pallas_call | solution.py:49
  40.2 0.9 %collective-permute-start.15 = (bf16[2,128,512]{2,1,0:T(8,128)(2,1)S(1)}, bf16[2,128,512]{2,1,0:T(8,128)(2,1)S(1)}, u32[]{:S(2)}, u32[]{:S(2)}) collective-permute-start(bf16[2,128,512]{2,1,0:T(8,128)(2,1)S(1)} %get-tuple-element.44), channel_id=1, source_target_pairs={{0,16},{8,24},{16,0},{24,8},{1,17},{9,25},{17,1},{25,9},{2,18},{10... | collective-permute-start | bytes 786440 | tf_op jit(solution)/shard_map/ppermute | solution.py:38
  41.2 1.0 %collective-permute-start.17 = (bf16[128,128]{1,0:T(8,128)(2,1)S(1)}, bf16[128,128]{1,0:T(8,128)(2,1)S(1)}, u32[]{:S(2)}, u32[]{:S(2)}) collective-permute-start(bf16[128,128]{1,0:T(8,128)(2,1)S(1)} %get-tuple-element.46), channel_id=1, source_target_pairs={{0,4},{1,5},{2,6},{3,7},{4,0},{5,1},{6,2},{7,3},{8,12},{9,13},{10,... | collective-permute-start | bytes 98312 | tf_op jit(solution)/shard_map/ppermute | solution.py:38
  42.1 1.4 %collective-permute-start.18 = (bf16[128,128]{1,0:T(8,128)(2,1)S(1)}, bf16[128,128]{1,0:T(8,128)(2,1)S(1)}, u32[]{:S(2)}, u32[]{:S(2)}) collective-permute-start(bf16[128,128]{1,0:T(8,128)(2,1)S(1)} %get-tuple-element.47), channel_id=1, source_target_pairs={{0,6},{1,7},{2,4},{3,5},{4,2},{5,3},{6,0},{7,1},{8,14},{9,15},{10,... | collective-permute-start | bytes 98312 | tf_op jit(solution)/shard_map/ppermute | solution.py:38
  43.5 1.1 %collective-permute-start.19 = (bf16[128,128]{1,0:T(8,128)(2,1)S(1)}, bf16[128,128]{1,0:T(8,128)(2,1)S(1)}, u32[]{:S(2)}, u32[]{:S(2)}) collective-permute-start(bf16[128,128]{1,0:T(8,128)(2,1)S(1)} %get-tuple-element.48), channel_id=1, source_target_pairs={{0,2},{1,3},{2,0},{3,1},{4,6},{5,7},{6,4},{7,5},{8,10},{9,11},{10,... | collective-permute-start | bytes 98312 | tf_op jit(solution)/shard_map/ppermute | solution.py:38
  44.6 1.4 %collective-permute-done.17.refs_1_ = bf16[128,128]{1,0:T(8,128)(2,1)S(1)} collective-permute-done((bf16[128,128]{1,0:T(8,128)(2,1)S(1)}, bf16[128,128]{1,0:T(8,128)(2,1)S(1)}, u32[]{:S(2)}, u32[]{:S(2)}) %collective-permute-start.17) | collective-permute-done | bytes 32800 | tf_op jit(solution)/shard_map/ppermute | solution.py:38
  46.1 1.9 %collective-permute-done.18.refs_2_ = bf16[128,128]{1,0:T(8,128)(2,1)S(1)} collective-permute-done((bf16[128,128]{1,0:T(8,128)(2,1)S(1)}, bf16[128,128]{1,0:T(8,128)(2,1)S(1)}, u32[]{:S(2)}, u32[]{:S(2)}) %collective-permute-start.18) | collective-permute-done | bytes 32800 | tf_op jit(solution)/shard_map/ppermute | solution.py:38
  48.2 1.0 %collective-permute-start.21 = (bf16[128,512]{1,0:T(8,128)(2,1)S(1)}, bf16[128,512]{1,0:T(8,128)(2,1)S(1)}, u32[]{:S(2)}, u32[]{:S(2)}) collective-permute-start(bf16[128,512]{1,0:T(8,128)(2,1)S(1)} %shard_map.98.refs_4_.refs_0_), channel_id=1, source_target_pairs={{0,16},{8,24},{16,0},{24,8},{1,17},{9,25},{17,1},{25,9},{2,18},{10... | collective-permute-start | bytes 393224 | tf_op jit(solution)/shard_map/ppermute | solution.py:38
  49.8 3.4 %collective-permute-done.21.refs_6_ = bf16[128,512]{1,0:T(8,128)(2,1)S(1)} collective-permute-done((bf16[128,512]{1,0:T(8,128)(2,1)S(1)}, bf16[128,512]{1,0:T(8,128)(2,1)S(1)}, u32[]{:S(2)}, u32[]{:S(2)}) %collective-permute-start.21) | collective-permute-done | bytes 131104 | tf_op jit(solution)/shard_map/ppermute | solution.py:38
  53.2 1.3 %collective-permute-done.22.refs_7_ = bf16[128,512]{1,0:T(8,128)(2,1)S(1)} collective-permute-done((bf16[128,512]{1,0:T(8,128)(2,1)S(1)}, bf16[128,512]{1,0:T(8,128)(2,1)S(1)}, u32[]{:S(2)}, u32[]{:S(2)}) %collective-permute-start.22) | collective-permute-done | bytes 131104 | tf_op jit(solution)/shard_map/ppermute | solution.py:38
  55.5 1.6 %collective-permute-start.29 = (bf16[2,64,512]{2,1,0:T(8,128)(2,1)S(1)}, bf16[2,64,512]{2,1,0:T(8,128)(2,1)S(1)}, u32[]{:S(2)}, u32[]{:S(2)}) collective-permute-start(bf16[2,64,512]{2,1,0:T(8,128)(2,1)S(1)} %get-tuple-element.58), channel_id=1, source_target_pairs={{0,1},{1,0},{2,3},{3,2},{4,5},{5,4},{6,7},{7,6},{8,9},{9,8},{10,11... | collective-permute-start | bytes 393224 | tf_op jit(solution)/shard_map/ppermute | solution.py:38
  57.8 1.9 %collective-permute-start.23 = (bf16[128,256]{1,0:T(8,128)(2,1)S(1)}, bf16[128,256]{1,0:T(8,128)(2,1)S(1)}, u32[]{:S(2)}, u32[]{:S(2)}) collective-permute-start(bf16[128,256]{1,0:T(8,128)(2,1)S(1)} %get-tuple-element.51), channel_id=1, source_target_pairs={{0,4},{1,5},{2,6},{3,7},{4,0},{5,1},{6,2},{7,3},{8,12},{9,13},{10,... | collective-permute-start | bytes 196616 | tf_op jit(solution)/shard_map/ppermute | solution.py:38
  59.7 2.0 %collective-permute-start.24 = (bf16[128,256]{1,0:T(8,128)(2,1)S(1)}, bf16[128,256]{1,0:T(8,128)(2,1)S(1)}, u32[]{:S(2)}, u32[]{:S(2)}) collective-permute-start(bf16[128,256]{1,0:T(8,128)(2,1)S(1)} %get-tuple-element.52), channel_id=1, source_target_pairs={{0,6},{1,7},{2,4},{3,5},{4,2},{5,3},{6,0},{7,1},{8,14},{9,15},{10,... | collective-permute-start | bytes 196616 | tf_op jit(solution)/shard_map/ppermute | solution.py:38
  61.7 0.9 %collective-permute-start.27 = (bf16[64,512]{1,0:T(8,128)(2,1)S(1)}, bf16[64,512]{1,0:T(8,128)(2,1)S(1)}, u32[]{:S(2)}, u32[]{:S(2)}) collective-permute-start(bf16[64,512]{1,0:T(8,128)(2,1)S(1)} %get-tuple-element.56), channel_id=1, source_target_pairs={{0,4},{1,5},{2,6},{3,7},{4,0},{5,1},{6,2},{7,3},{8,12},{9,13},{10,... | collective-permute-start | bytes 196616 | tf_op jit(solution)/shard_map/ppermute | solution.py:38
  62.7 1.8 %collective-permute-start.28 = (bf16[64,512]{1,0:T(8,128)(2,1)S(1)}, bf16[64,512]{1,0:T(8,128)(2,1)S(1)}, u32[]{:S(2)}, u32[]{:S(2)}) collective-permute-start(bf16[64,512]{1,0:T(8,128)(2,1)S(1)} %get-tuple-element.57), channel_id=1, source_target_pairs={{0,6},{1,7},{2,4},{3,5},{4,2},{5,3},{6,0},{7,1},{8,14},{9,15},{10,... | collective-permute-start | bytes 196616 | tf_op jit(solution)/shard_map/ppermute | solution.py:38
  64.5 0.9 %collective-permute-start.30 = (bf16[64,512]{1,0:T(8,128)(2,1)S(1)}, bf16[64,512]{1,0:T(8,128)(2,1)S(1)}, u32[]{:S(2)}, u32[]{:S(2)}) collective-permute-start(bf16[64,512]{1,0:T(8,128)(2,1)S(1)} %get-tuple-element.59), channel_id=1, source_target_pairs={{0,2},{1,3},{2,0},{3,1},{4,6},{5,7},{6,4},{7,5},{8,10},{9,11},{10,... | collective-permute-start | bytes 196616 | tf_op jit(solution)/shard_map/ppermute | solution.py:38
  65.4 1.6 %shard_map.102 = bf16[128,2048]{1,0:T(8,128)(2,1)} custom-call(bf16[128,512]{1,0:T(8,128)(2,1)S(1)} %shard_map.98.refs_4_.refs_0_, bf16[512,512]{1,0:T(8,128)(2,1)S(1)} %copy-done.1, bf16[512,512]{1,0:T(8,128)(2,1)S(1)} %collective-permute-done.7.refs_2_, bf16[512,512]{1,0:T(8,128)(2,1)S(1)} %shard_map.95.refs_3_, ...), custom_call_target="tpu_custom_call" | custom-call | tf_op jit(solution)/shard_map/pallas_call | solution.py:49
  67.0 2.0 %collective-permute-done.23.refs_1_ = bf16[128,256]{1,0:T(8,128)(2,1)S(1)} collective-permute-done((bf16[128,256]{1,0:T(8,128)(2,1)S(1)}, bf16[128,256]{1,0:T(8,128)(2,1)S(1)}, u32[]{:S(2)}, u32[]{:S(2)}) %collective-permute-start.23) | collective-permute-done | bytes 65568 | tf_op jit(solution)/shard_map/ppermute | solution.py:38
  69.7 1.6 %collective-permute-done.27.refs_0_ = bf16[64,512]{1,0:T(8,128)(2,1)S(1)} collective-permute-done((bf16[64,512]{1,0:T(8,128)(2,1)S(1)}, bf16[64,512]{1,0:T(8,128)(2,1)S(1)}, u32[]{:S(2)}, u32[]{:S(2)}) %collective-permute-start.27) | collective-permute-done | bytes 65568 | tf_op jit(solution)/shard_map/ppermute | solution.py:38
  (51 shorter events, 6.5 us)
Async XLA Ops:
  0.6 21.0 %copy-start.1 = (bf16[512,512]{1,0:T(8,128)(2,1)S(1)}, bf16[512,512]{1,0:T(8,128)(2,1)}, u32[]{:S(2)}) copy-start(bf16[512,512]{1,0:T(8,128)(2,1)} %refs_1_.3) | copy-start | bytes 1572868
  0.6 21.0 %collective-permute-start.8 = (bf16[512,512]{1,0:T(8,128)(2,1)}, bf16[512,512]{1,0:T(8,128)(2,1)S(1)}, u32[]{:S(2)}, u32[]{:S(2)}) collective-permute-start(bf16[512,512]{1,0:T(8,128)(2,1)} %refs_1_.3), channel_id=1, source_target_pairs={{0,16},{8,24},{16,0},{24,8},{1,17},{9,25},{17,1},{25,9},{2,18},{10... | collective-permute-start | bytes 1572872 | tf_op jit(solution)/shard_map/ppermute | solution.py:38
  5.9 7.4 %collective-permute-start.2 = (bf16[144,512]{1,0:T(8,128)(2,1)}, bf16[144,512]{1,0:T(8,128)(2,1)S(1)}, u32[]{:S(2)}, u32[]{:S(2)}) collective-permute-start(bf16[144,512]{1,0:T(8,128)(2,1)} %get-tuple-element.35), channel_id=1, source_target_pairs={{0,2},{1,3},{2,0},{3,1},{4,6},{5,7},{6,4},{7,5},{8,10},{9,11},{10,... | collective-permute-start | bytes 442376 | tf_op jit(solution)/shard_map/ppermute | solution.py:38
  7.5 14.1 %collective-permute-start = (bf16[144,512]{1,0:T(8,128)(2,1)}, bf16[144,512]{1,0:T(8,128)(2,1)S(1)}, u32[]{:S(2)}, u32[]{:S(2)}) collective-permute-start(bf16[144,512]{1,0:T(8,128)(2,1)} %get-tuple-element.33), channel_id=1, source_target_pairs={{0,4},{1,5},{2,6},{3,7},{4,0},{5,1},{6,2},{7,3},{8,12},{9,13},{10,... | collective-permute-start | bytes 442376 | tf_op jit(solution)/shard_map/ppermute | solution.py:38
  10.1 11.5 %collective-permute-start.1 = (bf16[144,512]{1,0:T(8,128)(2,1)}, bf16[144,512]{1,0:T(8,128)(2,1)S(1)}, u32[]{:S(2)}, u32[]{:S(2)}) collective-permute-start(bf16[144,512]{1,0:T(8,128)(2,1)} %get-tuple-element.34), channel_id=1, source_target_pairs={{0,6},{1,7},{2,4},{3,5},{4,2},{5,3},{6,0},{7,1},{8,14},{9,15},{10,... | collective-permute-start | bytes 442376 | tf_op jit(solution)/shard_map/ppermute | solution.py:38
  10.4 11.3 %collective-permute-start.3 = (bf16[144,512]{1,0:T(8,128)(2,1)}, bf16[144,512]{1,0:T(8,128)(2,1)S(1)}, u32[]{:S(2)}, u32[]{:S(2)}) collective-permute-start(bf16[144,512]{1,0:T(8,128)(2,1)} %get-tuple-element.32.refs_2_), channel_id=1, source_target_pairs={{0,1},{1,0},{2,3},{3,2},{4,5},{5,4},{6,7},{7,6},{8,9},{9,8},{10,11... | collective-permute-start | bytes 442376 | tf_op jit(solution)/shard_map/ppermute | solution.py:38
  13.3 8.3 %collective-permute-start.4 = (bf16[144,512]{1,0:T(8,128)(2,1)S(1)}, bf16[144,512]{1,0:T(8,128)(2,1)S(1)}, u32[]{:S(2)}, u32[]{:S(2)}) collective-permute-start(bf16[144,512]{1,0:T(8,128)(2,1)S(1)} %collective-permute-done.2.refs_3_.refs_5_), channel_id=1, source_target_pairs={{0,1},{1,0},{2,3},{3,2},{4,5},{5,4},{6,7},{7,6},{8,9},{9,8},{10,11... | collective-permute-start | bytes 442376 | tf_op jit(solution)/shard_map/ppermute | solution.py:38
  21.6 2.6 %collective-permute-start.7 = (bf16[512,512]{1,0:T(8,128)(2,1)S(1)}, bf16[512,512]{1,0:T(8,128)(2,1)S(1)}, u32[]{:S(2)}, u32[]{:S(2)}) collective-permute-start(bf16[512,512]{1,0:T(8,128)(2,1)S(1)} %copy-done.1), channel_id=1, source_target_pairs={{0,8},{8,0},{16,24},{24,16},{1,9},{9,1},{17,25},{25,17},{2,10},{10... | collective-permute-start | bytes 1572872 | tf_op jit(solution)/shard_map/ppermute | solution.py:38
  21.7 2.6 %collective-permute-start.9 = (bf16[512,512]{1,0:T(8,128)(2,1)S(1)}, bf16[512,512]{1,0:T(8,128)(2,1)S(1)}, u32[]{:S(2)}, u32[]{:S(2)}) collective-permute-start(bf16[512,512]{1,0:T(8,128)(2,1)S(1)} %shard_map.95.refs_3_), channel_id=1, source_target_pairs={{0,8},{8,0},{16,24},{24,16},{1,9},{9,1},{17,25},{25,17},{2,10},{10... | collective-permute-start | bytes 1572872 | tf_op jit(solution)/shard_map/ppermute | solution.py:38
  22.2 6.7 %collective-permute-start.5 = (bf16[144,512]{1,0:T(8,128)(2,1)S(1)}, bf16[144,512]{1,0:T(8,128)(2,1)S(1)}, u32[]{:S(2)}, u32[]{:S(2)}) collective-permute-start(bf16[144,512]{1,0:T(8,128)(2,1)S(1)} %collective-permute-done.refs_1_.refs_3_), channel_id=1, source_target_pairs={{0,1},{1,0},{2,3},{3,2},{4,5},{5,4},{6,7},{7,6},{8,9},{9,8},{10,11... | collective-permute-start | bytes 442376 | tf_op jit(solution)/shard_map/ppermute | solution.py:38
  23.7 7.5 %collective-permute-start.6 = (bf16[144,512]{1,0:T(8,128)(2,1)S(1)}, bf16[144,512]{1,0:T(8,128)(2,1)S(1)}, u32[]{:S(2)}, u32[]{:S(2)}) collective-permute-start(bf16[144,512]{1,0:T(8,128)(2,1)S(1)} %collective-permute-done.1.refs_2_.refs_4_), channel_id=1, source_target_pairs={{0,1},{1,0},{2,3},{3,2},{4,5},{5,4},{6,7},{7,6},{8,9},{9,8},{10,11... | collective-permute-start | bytes 442376 | tf_op jit(solution)/shard_map/ppermute | solution.py:38
  24.8 6.4 %collective-permute-start.10 = (bf16[128,128]{1,0:T(8,128)(2,1)S(1)}, bf16[128,128]{1,0:T(8,128)(2,1)S(1)}, u32[]{:S(2)}, u32[]{:S(2)}) collective-permute-start(bf16[128,128]{1,0:T(8,128)(2,1)S(1)} %get-tuple-element.37), channel_id=1, source_target_pairs={{0,4},{1,5},{2,6},{3,7},{4,0},{5,1},{6,2},{7,3},{8,12},{9,13},{10,... | collective-permute-start | bytes 98312 | tf_op jit(solution)/shard_map/ppermute | solution.py:38
  27.6 5.7 %collective-permute-start.11 = (bf16[128,128]{1,0:T(8,128)(2,1)S(1)}, bf16[128,128]{1,0:T(8,128)(2,1)S(1)}, u32[]{:S(2)}, u32[]{:S(2)}) collective-permute-start(bf16[128,128]{1,0:T(8,128)(2,1)S(1)} %get-tuple-element.38), channel_id=1, source_target_pairs={{0,6},{1,7},{2,4},{3,5},{4,2},{5,3},{6,0},{7,1},{8,14},{9,15},{10,... | collective-permute-start | bytes 98312 | tf_op jit(solution)/shard_map/ppermute | solution.py:38
  29.0 4.4 %collective-permute-start.12 = (bf16[128,128]{1,0:T(8,128)(2,1)S(1)}, bf16[128,128]{1,0:T(8,128)(2,1)S(1)}, u32[]{:S(2)}, u32[]{:S(2)}) collective-permute-start(bf16[128,128]{1,0:T(8,128)(2,1)S(1)} %get-tuple-element.39), channel_id=1, source_target_pairs={{0,2},{1,3},{2,0},{3,1},{4,6},{5,7},{6,4},{7,5},{8,10},{9,11},{10,... | collective-permute-start | bytes 98312 | tf_op jit(solution)/shard_map/ppermute | solution.py:38
  39.5 8.5 %collective-permute-start.13 = (bf16[4,128,256]{2,1,0:T(8,128)(2,1)S(1)}, bf16[4,128,256]{2,1,0:T(8,128)(2,1)S(1)}, u32[]{:S(2)}, u32[]{:S(2)}) collective-permute-start(bf16[4,128,256]{2,1,0:T(8,128)(2,1)S(1)} %get-tuple-element.41), channel_id=1, source_target_pairs={{0,1},{1,0},{2,3},{3,2},{4,5},{5,4},{6,7},{7,6},{8,9},{9,8},{10,11... | collective-permute-start | bytes 786440 | tf_op jit(solution)/shard_map/ppermute | solution.py:38
  40.2 8.9 %collective-permute-start.15 = (bf16[2,128,512]{2,1,0:T(8,128)(2,1)S(1)}, bf16[2,128,512]{2,1,0:T(8,128)(2,1)S(1)}, u32[]{:S(2)}, u32[]{:S(2)}) collective-permute-start(bf16[2,128,512]{2,1,0:T(8,128)(2,1)S(1)} %get-tuple-element.44), channel_id=1, source_target_pairs={{0,16},{8,24},{16,0},{24,8},{1,17},{9,25},{17,1},{25,9},{2,18},{10... | collective-permute-start | bytes 786440 | tf_op jit(solution)/shard_map/ppermute | solution.py:38
  41.2 4.9 %collective-permute-start.17 = (bf16[128,128]{1,0:T(8,128)(2,1)S(1)}, bf16[128,128]{1,0:T(8,128)(2,1)S(1)}, u32[]{:S(2)}, u32[]{:S(2)}) collective-permute-start(bf16[128,128]{1,0:T(8,128)(2,1)S(1)} %get-tuple-element.46), channel_id=1, source_target_pairs={{0,4},{1,5},{2,6},{3,7},{4,0},{5,1},{6,2},{7,3},{8,12},{9,13},{10,... | collective-permute-start | bytes 98312 | tf_op jit(solution)/shard_map/ppermute | solution.py:38
  42.1 5.8 %collective-permute-start.18 = (bf16[128,128]{1,0:T(8,128)(2,1)S(1)}, bf16[128,128]{1,0:T(8,128)(2,1)S(1)}, u32[]{:S(2)}, u32[]{:S(2)}) collective-permute-start(bf16[128,128]{1,0:T(8,128)(2,1)S(1)} %get-tuple-element.47), channel_id=1, source_target_pairs={{0,6},{1,7},{2,4},{3,5},{4,2},{5,3},{6,0},{7,1},{8,14},{9,15},{10,... | collective-permute-start | bytes 98312 | tf_op jit(solution)/shard_map/ppermute | solution.py:38
  43.5 4.5 %collective-permute-start.19 = (bf16[128,128]{1,0:T(8,128)(2,1)S(1)}, bf16[128,128]{1,0:T(8,128)(2,1)S(1)}, u32[]{:S(2)}, u32[]{:S(2)}) collective-permute-start(bf16[128,128]{1,0:T(8,128)(2,1)S(1)} %get-tuple-element.48), channel_id=1, source_target_pairs={{0,2},{1,3},{2,0},{3,1},{4,6},{5,7},{6,4},{7,5},{8,10},{9,11},{10,... | collective-permute-start | bytes 98312 | tf_op jit(solution)/shard_map/ppermute | solution.py:38
  46.1 7.1 %collective-permute-start.14 = (bf16[128,512]{1,0:T(8,128)(2,1)S(1)}, bf16[128,512]{1,0:T(8,128)(2,1)S(1)}, u32[]{:S(2)}, u32[]{:S(2)}) collective-permute-start(bf16[128,512]{1,0:T(8,128)(2,1)S(1)} %get-tuple-element.43), channel_id=1, source_target_pairs={{0,8},{8,0},{16,24},{24,16},{1,9},{9,1},{17,25},{25,17},{2,10},{10... | collective-permute-start | bytes 393224 | tf_op jit(solution)/shard_map/ppermute | solution.py:38
  48.2 5.0 %collective-permute-start.21 = (bf16[128,512]{1,0:T(8,128)(2,1)S(1)}, bf16[128,512]{1,0:T(8,128)(2,1)S(1)}, u32[]{:S(2)}, u32[]{:S(2)}) collective-permute-start(bf16[128,512]{1,0:T(8,128)(2,1)S(1)} %shard_map.98.refs_4_.refs_0_), channel_id=1, source_target_pairs={{0,16},{8,24},{16,0},{24,8},{1,17},{9,25},{17,1},{25,9},{2,18},{10... | collective-permute-start | bytes 393224 | tf_op jit(solution)/shard_map/ppermute | solution.py:38
  49.2 4.1 %collective-permute-start.20 = (bf16[128,512]{1,0:T(8,128)(2,1)S(1)}, bf16[128,512]{1,0:T(8,128)(2,1)S(1)}, u32[]{:S(2)}, u32[]{:S(2)}) collective-permute-start(bf16[128,512]{1,0:T(8,128)(2,1)S(1)} %shard_map.98.refs_4_.refs_0_), channel_id=1, source_target_pairs={{0,8},{8,0},{16,24},{24,16},{1,9},{9,1},{17,25},{25,17},{2,10},{10... | collective-permute-start | bytes 393224 | tf_op jit(solution)/shard_map/ppermute | solution.py:38
  49.2 4.0 %collective-permute-start.16 = (bf16[128,512]{1,0:T(8,128)(2,1)S(1)}, bf16[128,512]{1,0:T(8,128)(2,1)S(1)}, u32[]{:S(2)}, u32[]{:S(2)}) collective-permute-start(bf16[128,512]{1,0:T(8,128)(2,1)S(1)} %get-tuple-element.61), channel_id=1, source_target_pairs={{0,8},{8,0},{16,24},{24,16},{1,9},{9,1},{17,25},{25,17},{2,10},{10... | collective-permute-start | bytes 393224 | tf_op jit(solution)/shard_map/ppermute | solution.py:38
  53.2 1.3 %collective-permute-start.22 = (bf16[128,512]{1,0:T(8,128)(2,1)S(1)}, bf16[128,512]{1,0:T(8,128)(2,1)S(1)}, u32[]{:S(2)}, u32[]{:S(2)}) collective-permute-start(bf16[128,512]{1,0:T(8,128)(2,1)S(1)} %collective-permute-done.21.refs_6_), channel_id=1, source_target_pairs={{0,8},{8,0},{16,24},{24,16},{1,9},{9,1},{17,25},{25,17},{2,10},{10... | collective-permute-start | bytes 393224 | tf_op jit(solution)/shard_map/ppermute | solution.py:38
  55.1 6.6 %collective-permute-start.26 = (bf16[2,64,512]{2,1,0:T(8,128)(2,1)S(1)}, bf16[2,64,512]{2,1,0:T(8,128)(2,1)S(1)}, u32[]{:S(2)}, u32[]{:S(2)}) collective-permute-start(bf16[2,64,512]{2,1,0:T(8,128)(2,1)S(1)} %get-tuple-element.55), channel_id=1, source_target_pairs={{0,1},{1,0},{2,3},{3,2},{4,5},{5,4},{6,7},{7,6},{8,9},{9,8},{10,11... | collective-permute-start | bytes 393224 | tf_op jit(solution)/shard_map/ppermute | solution.py:38
  55.5 8.9 %collective-permute-start.29 = (bf16[2,64,512]{2,1,0:T(8,128)(2,1)S(1)}, bf16[2,64,512]{2,1,0:T(8,128)(2,1)S(1)}, u32[]{:S(2)}, u32[]{:S(2)}) collective-permute-start(bf16[2,64,512]{2,1,0:T(8,128)(2,1)S(1)} %get-tuple-element.58), channel_id=1, source_target_pairs={{0,1},{1,0},{2,3},{3,2},{4,5},{5,4},{6,7},{7,6},{8,9},{9,8},{10,11... | collective-permute-start | bytes 393224 | tf_op jit(solution)/shard_map/ppermute | solution.py:38
  57.2 5.4 %collective-permute-start.25 = (bf16[128,256]{1,0:T(8,128)(2,1)S(1)}, bf16[128,256]{1,0:T(8,128)(2,1)S(1)}, u32[]{:S(2)}, u32[]{:S(2)}) collective-permute-start(bf16[128,256]{1,0:T(8,128)(2,1)S(1)} %get-tuple-element.53), channel_id=1, source_target_pairs={{0,2},{1,3},{2,0},{3,1},{4,6},{5,7},{6,4},{7,5},{8,10},{9,11},{10,... | collective-permute-start | bytes 196616 | tf_op jit(solution)/shard_map/ppermute | solution.py:38
  57.8 11.1 %collective-permute-start.23 = (bf16[128,256]{1,0:T(8,128)(2,1)S(1)}, bf16[128,256]{1,0:T(8,128)(2,1)S(1)}, u32[]{:S(2)}, u32[]{:S(2)}) collective-permute-start(bf16[128,256]{1,0:T(8,128)(2,1)S(1)} %get-tuple-element.51), channel_id=1, source_target_pairs={{0,4},{1,5},{2,6},{3,7},{4,0},{5,1},{6,2},{7,3},{8,12},{9,13},{10,... | collective-permute-start | bytes 196616 | tf_op jit(solution)/shard_map/ppermute | solution.py:38
  59.7 9.2 %collective-permute-start.24 = (bf16[128,256]{1,0:T(8,128)(2,1)S(1)}, bf16[128,256]{1,0:T(8,128)(2,1)S(1)}, u32[]{:S(2)}, u32[]{:S(2)}) collective-permute-start(bf16[128,256]{1,0:T(8,128)(2,1)S(1)} %get-tuple-element.52), channel_id=1, source_target_pairs={{0,6},{1,7},{2,4},{3,5},{4,2},{5,3},{6,0},{7,1},{8,14},{9,15},{10,... | collective-permute-start | bytes 196616 | tf_op jit(solution)/shard_map/ppermute | solution.py:38
  61.7 9.6 %collective-permute-start.27 = (bf16[64,512]{1,0:T(8,128)(2,1)S(1)}, bf16[64,512]{1,0:T(8,128)(2,1)S(1)}, u32[]{:S(2)}, u32[]{:S(2)}) collective-permute-start(bf16[64,512]{1,0:T(8,128)(2,1)S(1)} %get-tuple-element.56), channel_id=1, source_target_pairs={{0,4},{1,5},{2,6},{3,7},{4,0},{5,1},{6,2},{7,3},{8,12},{9,13},{10,... | collective-permute-start | bytes 196616 | tf_op jit(solution)/shard_map/ppermute | solution.py:38
  62.7 8.6 %collective-permute-start.28 = (bf16[64,512]{1,0:T(8,128)(2,1)S(1)}, bf16[64,512]{1,0:T(8,128)(2,1)S(1)}, u32[]{:S(2)}, u32[]{:S(2)}) collective-permute-start(bf16[64,512]{1,0:T(8,128)(2,1)S(1)} %get-tuple-element.57), channel_id=1, source_target_pairs={{0,6},{1,7},{2,4},{3,5},{4,2},{5,3},{6,0},{7,1},{8,14},{9,15},{10,... | collective-permute-start | bytes 196616 | tf_op jit(solution)/shard_map/ppermute | solution.py:38
  64.5 6.8 %collective-permute-start.30 = (bf16[64,512]{1,0:T(8,128)(2,1)S(1)}, bf16[64,512]{1,0:T(8,128)(2,1)S(1)}, u32[]{:S(2)}, u32[]{:S(2)}) collective-permute-start(bf16[64,512]{1,0:T(8,128)(2,1)S(1)} %get-tuple-element.59), channel_id=1, source_target_pairs={{0,2},{1,3},{2,0},{3,1},{4,6},{5,7},{6,4},{7,5},{8,10},{9,11},{10,... | collective-permute-start | bytes 196616 | tf_op jit(solution)/shard_map/ppermute | solution.py:38
  (3 other events, 27.4 us)

commit v7 on v4

--- a/solution.py
+++ b/solution.py
@@ -99,12 +99,9 @@
     head, _ = head_side()
     loads = [pltpu.make_async_copy(ref, to, sems.at[i])
              for i, (ref, to) in enumerate(((go_ref, grad), (ao_ref, output), (lse_ref, lse)))]
-    moves = []
-    for m in range(KV_HEADS):
-        columns = pl.ds(pl.multiple_of(jnp.bitwise_xor(head, m) * GROUP, GROUP), GROUP)
-        for i, ref in enumerate((q_ref, go_ref)):
-            moves.append(pltpu.make_async_copy(
-                ref.at[:, columns], out_refs[m].at[0:rows, i * GROUP:(i + 1) * GROUP], sems.at[3 + 2 * m + i]))
+    columns = [pl.ds(pl.multiple_of(jnp.bitwise_xor(head, m) * GROUP, GROUP), GROUP) for m in range(KV_HEADS)]
+    moves = [pltpu.make_async_copy(q_ref.at[:, columns[m]], out_refs[m].at[0:rows, 0:GROUP], sems.at[3 + m])
+             for m in range(KV_HEADS)]
     for copy in loads + moves:
         copy.start()
     for copy in loads:
@@ -120,6 +117,7 @@
         stat[g] = jnp.concatenate([lse[part, :], delta[part, :]], axis=0)
     zero = jnp.zeros((2 * GROUPS, rows), jnp.float32)
     for m in range(KV_HEADS):
+        out_refs[m][0:rows, GROUP:] = grad[:, columns[m]]
         lines = [*split(stat[jnp.bitwise_xor(head, m)]), zero]
         for i, one in enumerate(lines):
             full = jnp.concatenate([one, zero], axis=0).astype(jnp.bfloat16)
@@ -399,7 +397,7 @@
         pieces_kernel, [sds((rows + 16, 2 * GROUP))] * KV_HEADS,
         [pltpu.VMEM((rows, Q_HEADS * HEAD_DIM), jnp.bfloat16)] * 2
         + [pltpu.VMEM((Q_HEADS, rows), f32), pltpu.VMEM((KV_HEADS, 2 * GROUPS, rows), f32),
-           pltpu.SemaphoreType.DMA((3 + 2 * KV_HEADS,))],
+           pltpu.SemaphoreType.DMA((3 + KV_HEADS,))],
         (queries[0], grad_out[0], attn_out[0], log_sums[0]), hbm=4)
     qd = along_heads(qd)
     turned = [swapped(one, "ctx", 1) for one in qd[:2]]

time: 72.1 us -> 72.2 us (level)
  starting transfers between devices: 33.7 us -> 35.9 us
  Pallas kernels: 12.6 us -> 11.5 us
  waiting for transfers between devices: 24.5 us -> 23.6 us
    ppermute x31, starting transfers between devices: 33.7 us -> 35.9 us  [swapped(): return lax.ppermute(array, axis, [(i, i ^ bits) for i in range(size)])]
    pallas_call x11, Pallas kernels: 12.6 us -> 11.5 us  [call(): pl.pallas_call(body, out_shape=out_shape, in_specs=specs, out_specs=[VMEM...]
    ppermute x31, waiting for transfers between devices: 24.5 us -> 23.6 us  [swapped(): return lax.ppermute(array, axis, [(i, i ^ bits) for i in range(size)])]
where the time goes in v7:
time: 72.2 us; the launch traced here: 71.8 us
  starting transfers between devices  35.9 us (50%)
  waiting for transfers between devices  23.6 us (33%)
  Pallas kernels  11.5 us (16%)
  between operations  0.78 us (1%)
    ppermute x31, starting transfers between devices, swapped(): return lax.ppermute(array, axis, [(i, i ^ bits) for i in range(size)])  35.9 us
    ppermute x31, waiting for transfers between devices, swapped(): return lax.ppermute(array, axis, [(i, i ^ bits) for i in range(size)])  23.6 us
    pallas_call x11, Pallas kernels, call(): pl.pallas_call(body, out_shape=out_shape, in_specs=specs, out_specs=[VMEM...  11.5 us
  transfers between devices with their start and end apart: 31, of which 10 were waited for; matrix products, arithmetic and copies ran while one was open for 0% of the time, Pallas kernels for 7%

profile of v7, /device:TPU:0, one launch (start us, length us, event | category | flops | bytes accessed | tf_op | source)
XLA Modules:
  0.0 71.8 jit_solution(16876466979629502217)
XLA Ops:
  0.6 3.0 %collective-permute-start.8 = (bf16[512,512]{1,0:T(8,128)(2,1)}, bf16[512,512]{1,0:T(8,128)(2,1)S(1)}, u32[]{:S(2)}, u32[]{:S(2)}) collective-permute-start(bf16[512,512]{1,0:T(8,128)(2,1)} %refs_1_.3), channel_id=1, source_target_pairs={{0,16},{8,24},{16,0},{24,8},{1,17},{9,25},{17,1},{25,9},{2,18},{10... | collective-permute-start | bytes 1572872 | tf_op jit(solution)/shard_map/ppermute | solution.py:38
  3.7 2.2 %shard_map.94 = (bf16[144,512]{1,0:T(8,128)(2,1)}, bf16[144,512]{1,0:T(8,128)(2,1)}, bf16[144,512]{1,0:T(8,128)(2,1)}, bf16[144,512]{1,0:T(8,128)(2,1)}) custom-call(bf16[128,1024]{1,0:T(8,128)(2,1)} %bitcast.14, bf16[128,1024]{1,0:T(8,128)(2,1)} %bitcast.15, bf16[128,1024]{1,0:T(8,128)(2,1)} %bitcast.16, f32[16,128]{1,0:T(8,128)} %bitcast.18), custom_call_target="tpu_custom_call" | custom-call | tf_op jit(solution)/shard_map/pallas_call | solution.py:49
  5.9 1.6 %collective-permute-start.2 = (bf16[144,512]{1,0:T(8,128)(2,1)}, bf16[144,512]{1,0:T(8,128)(2,1)S(1)}, u32[]{:S(2)}, u32[]{:S(2)}) collective-permute-start(bf16[144,512]{1,0:T(8,128)(2,1)} %get-tuple-element.35), channel_id=1, source_target_pairs={{0,2},{1,3},{2,0},{3,1},{4,6},{5,7},{6,4},{7,5},{8,10},{9,11},{10,... | collective-permute-start | bytes 442376 | tf_op jit(solution)/shard_map/ppermute | solution.py:38
  7.5 2.6 %collective-permute-start = (bf16[144,512]{1,0:T(8,128)(2,1)}, bf16[144,512]{1,0:T(8,128)(2,1)S(1)}, u32[]{:S(2)}, u32[]{:S(2)}) collective-permute-start(bf16[144,512]{1,0:T(8,128)(2,1)} %get-tuple-element.33), channel_id=1, source_target_pairs={{0,4},{1,5},{2,6},{3,7},{4,0},{5,1},{6,2},{7,3},{8,12},{9,13},{10,... | collective-permute-start | bytes 442376 | tf_op jit(solution)/shard_map/ppermute | solution.py:38
  10.3 1.5 %collective-permute-start.3 = (bf16[144,512]{1,0:T(8,128)(2,1)}, bf16[144,512]{1,0:T(8,128)(2,1)S(1)}, u32[]{:S(2)}, u32[]{:S(2)}) collective-permute-start(bf16[144,512]{1,0:T(8,128)(2,1)} %get-tuple-element.32.refs_2_), channel_id=1, source_target_pairs={{0,1},{1,0},{2,3},{3,2},{4,5},{5,4},{6,7},{7,6},{8,9},{9,8},{10,11... | collective-permute-start | bytes 442376 | tf_op jit(solution)/shard_map/ppermute | solution.py:38
  11.8 1.5 %collective-permute-done.2.refs_3_.refs_5_ = bf16[144,512]{1,0:T(8,128)(2,1)S(1)} collective-permute-done((bf16[144,512]{1,0:T(8,128)(2,1)}, bf16[144,512]{1,0:T(8,128)(2,1)S(1)}, u32[]{:S(2)}, u32[]{:S(2)}) %collective-permute-start.2) | collective-permute-done | bytes 147488 | tf_op jit(solution)/shard_map/ppermute | solution.py:38
  13.3 1.5 %collective-permute-start.4 = (bf16[144,512]{1,0:T(8,128)(2,1)S(1)}, bf16[144,512]{1,0:T(8,128)(2,1)S(1)}, u32[]{:S(2)}, u32[]{:S(2)}) collective-permute-start(bf16[144,512]{1,0:T(8,128)(2,1)S(1)} %collective-permute-done.2.refs_3_.refs_5_), channel_id=1, source_target_pairs={{0,1},{1,0},{2,3},{3,2},{4,5},{5,4},{6,7},{7,6},{8,9},{9,8},{10,11... | collective-permute-start | bytes 442376 | tf_op jit(solution)/shard_map/ppermute | solution.py:38
  14.8 6.8 %collective-permute-done.refs_1_.refs_3_ = bf16[144,512]{1,0:T(8,128)(2,1)S(1)} collective-permute-done((bf16[144,512]{1,0:T(8,128)(2,1)}, bf16[144,512]{1,0:T(8,128)(2,1)S(1)}, u32[]{:S(2)}, u32[]{:S(2)}) %collective-permute-start) | collective-permute-done | bytes 147488 | tf_op jit(solution)/shard_map/ppermute | solution.py:38
  22.2 1.5 %collective-permute-start.5 = (bf16[144,512]{1,0:T(8,128)(2,1)S(1)}, bf16[144,512]{1,0:T(8,128)(2,1)S(1)}, u32[]{:S(2)}, u32[]{:S(2)}) collective-permute-start(bf16[144,512]{1,0:T(8,128)(2,1)S(1)} %collective-permute-done.refs_1_.refs_3_), channel_id=1, source_target_pairs={{0,1},{1,0},{2,3},{3,2},{4,5},{5,4},{6,7},{7,6},{8,9},{9,8},{10,11... | collective-permute-start | bytes 442376 | tf_op jit(solution)/shard_map/ppermute | solution.py:38
  24.8 2.8 %collective-permute-start.10 = (bf16[128,128]{1,0:T(8,128)(2,1)S(1)}, bf16[128,128]{1,0:T(8,128)(2,1)S(1)}, u32[]{:S(2)}, u32[]{:S(2)}) collective-permute-start(bf16[128,128]{1,0:T(8,128)(2,1)S(1)} %get-tuple-element.37), channel_id=1, source_target_pairs={{0,4},{1,5},{2,6},{3,7},{4,0},{5,1},{6,2},{7,3},{8,12},{9,13},{10,... | collective-permute-start | bytes 98312 | tf_op jit(solution)/shard_map/ppermute | solution.py:38
  27.6 1.3 %collective-permute-start.11 = (bf16[128,128]{1,0:T(8,128)(2,1)S(1)}, bf16[128,128]{1,0:T(8,128)(2,1)S(1)}, u32[]{:S(2)}, u32[]{:S(2)}) collective-permute-start(bf16[128,128]{1,0:T(8,128)(2,1)S(1)} %get-tuple-element.38), channel_id=1, source_target_pairs={{0,6},{1,7},{2,4},{3,5},{4,2},{5,3},{6,0},{7,1},{8,14},{9,15},{10,... | collective-permute-start | bytes 98312 | tf_op jit(solution)/shard_map/ppermute | solution.py:38
  29.0 2.3 %collective-permute-done.6.refs_9_ = bf16[144,512]{1,0:T(8,128)(2,1)S(1)} collective-permute-done((bf16[144,512]{1,0:T(8,128)(2,1)S(1)}, bf16[144,512]{1,0:T(8,128)(2,1)S(1)}, u32[]{:S(2)}, u32[]{:S(2)}) %collective-permute-start.6) | collective-permute-done | bytes 147488 | tf_op jit(solution)/shard_map/ppermute | solution.py:38
  31.2 2.1 %collective-permute-done.11.refs_12_ = bf16[128,128]{1,0:T(8,128)(2,1)S(1)} collective-permute-done((bf16[128,128]{1,0:T(8,128)(2,1)S(1)}, bf16[128,128]{1,0:T(8,128)(2,1)S(1)}, u32[]{:S(2)}, u32[]{:S(2)}) %collective-permute-start.11) | collective-permute-done | bytes 32800 | tf_op jit(solution)/shard_map/ppermute | solution.py:38
  33.3 5.0 %shard_map.97 = (bf16[128,128]{1,0:T(8,128)(2,1)S(1)}, bf16[128,128]{1,0:T(8,128)(2,1)S(1)}, bf16[128,128]{1,0:T(8,128)(2,1)S(1)}, bf16[128,128]{1,0:T(8,128)(2,...) custom-call(s32[1,8]{1,0:T(1,128)S(1)} %copy-done.3, ...), custom_call_target="tpu_custom_call" | custom-call | tf_op jit(solution)/shard_map/pallas_call | solution.py:49
  38.3 2.4 %collective-permute-start.13 = (bf16[4,128,256]{2,1,0:T(8,128)(2,1)S(1)}, bf16[4,128,256]{2,1,0:T(8,128)(2,1)S(1)}, u32[]{:S(2)}, u32[]{:S(2)}) collective-permute-start(bf16[4,128,256]{2,1,0:T(8,128)(2,1)S(1)} %get-tuple-element.41), channel_id=1, source_target_pairs={{0,1},{1,0},{2,3},{3,2},{4,5},{5,4},{6,7},{7,6},{8,9},{9,8},{10,11... | collective-permute-start | bytes 786440 | tf_op jit(solution)/shard_map/ppermute | solution.py:38
  41.0 1.0 %collective-permute-start.17 = (bf16[128,128]{1,0:T(8,128)(2,1)S(1)}, bf16[128,128]{1,0:T(8,128)(2,1)S(1)}, u32[]{:S(2)}, u32[]{:S(2)}) collective-permute-start(bf16[128,128]{1,0:T(8,128)(2,1)S(1)} %get-tuple-element.46), channel_id=1, source_target_pairs={{0,4},{1,5},{2,6},{3,7},{4,0},{5,1},{6,2},{7,3},{8,12},{9,13},{10,... | collective-permute-start | bytes 98312 | tf_op jit(solution)/shard_map/ppermute | solution.py:38
  42.0 1.4 %collective-permute-start.18 = (bf16[128,128]{1,0:T(8,128)(2,1)S(1)}, bf16[128,128]{1,0:T(8,128)(2,1)S(1)}, u32[]{:S(2)}, u32[]{:S(2)}) collective-permute-start(bf16[128,128]{1,0:T(8,128)(2,1)S(1)} %get-tuple-element.47), channel_id=1, source_target_pairs={{0,6},{1,7},{2,4},{3,5},{4,2},{5,3},{6,0},{7,1},{8,14},{9,15},{10,... | collective-permute-start | bytes 98312 | tf_op jit(solution)/shard_map/ppermute | solution.py:38
  43.3 1.1 %collective-permute-start.19 = (bf16[128,128]{1,0:T(8,128)(2,1)S(1)}, bf16[128,128]{1,0:T(8,128)(2,1)S(1)}, u32[]{:S(2)}, u32[]{:S(2)}) collective-permute-start(bf16[128,128]{1,0:T(8,128)(2,1)S(1)} %get-tuple-element.48), channel_id=1, source_target_pairs={{0,2},{1,3},{2,0},{3,1},{4,6},{5,7},{6,4},{7,5},{8,10},{9,11},{10,... | collective-permute-start | bytes 98312 | tf_op jit(solution)/shard_map/ppermute | solution.py:38
  44.5 1.5 %collective-permute-done.17.refs_1_ = bf16[128,128]{1,0:T(8,128)(2,1)S(1)} collective-permute-done((bf16[128,128]{1,0:T(8,128)(2,1)S(1)}, bf16[128,128]{1,0:T(8,128)(2,1)S(1)}, u32[]{:S(2)}, u32[]{:S(2)}) %collective-permute-start.17) | collective-permute-done | bytes 32800 | tf_op jit(solution)/shard_map/ppermute | solution.py:38
  45.9 1.8 %collective-permute-done.18.refs_2_ = bf16[128,128]{1,0:T(8,128)(2,1)S(1)} collective-permute-done((bf16[128,128]{1,0:T(8,128)(2,1)S(1)}, bf16[128,128]{1,0:T(8,128)(2,1)S(1)}, u32[]{:S(2)}, u32[]{:S(2)}) %collective-permute-start.18) | collective-permute-done | bytes 32800 | tf_op jit(solution)/shard_map/ppermute | solution.py:38
  47.8 1.8 %collective-permute-start.21 = (bf16[128,512]{1,0:T(8,128)(2,1)S(1)}, bf16[128,512]{1,0:T(8,128)(2,1)S(1)}, u32[]{:S(2)}, u32[]{:S(2)}) collective-permute-start(bf16[128,512]{1,0:T(8,128)(2,1)S(1)} %shard_map.98.refs_4_.refs_0_), channel_id=1, source_target_pairs={{0,16},{8,24},{16,0},{24,8},{1,17},{9,25},{17,1},{25,9},{2,18},{10... | collective-permute-start | bytes 393224 | tf_op jit(solution)/shard_map/ppermute | solution.py:38
  50.2 2.6 %collective-permute-done.21.refs_6_ = bf16[128,512]{1,0:T(8,128)(2,1)S(1)} collective-permute-done((bf16[128,512]{1,0:T(8,128)(2,1)S(1)}, bf16[128,512]{1,0:T(8,128)(2,1)S(1)}, u32[]{:S(2)}, u32[]{:S(2)}) %collective-permute-start.21) | collective-permute-done | bytes 131104 | tf_op jit(solution)/shard_map/ppermute | solution.py:38
  52.9 1.3 %collective-permute-done.22.refs_7_ = bf16[128,512]{1,0:T(8,128)(2,1)S(1)} collective-permute-done((bf16[128,512]{1,0:T(8,128)(2,1)S(1)}, bf16[128,512]{1,0:T(8,128)(2,1)S(1)}, u32[]{:S(2)}, u32[]{:S(2)}) %collective-permute-start.22) | collective-permute-done | bytes 131104 | tf_op jit(solution)/shard_map/ppermute | solution.py:38
  55.0 1.9 %collective-permute-start.29 = (bf16[2,64,512]{2,1,0:T(8,128)(2,1)S(1)}, bf16[2,64,512]{2,1,0:T(8,128)(2,1)S(1)}, u32[]{:S(2)}, u32[]{:S(2)}) collective-permute-start(bf16[2,64,512]{2,1,0:T(8,128)(2,1)S(1)} %get-tuple-element.58), channel_id=1, source_target_pairs={{0,1},{1,0},{2,3},{3,2},{4,5},{5,4},{6,7},{7,6},{8,9},{9,8},{10,11... | collective-permute-start | bytes 393224 | tf_op jit(solution)/shard_map/ppermute | solution.py:38
  56.9 0.8 %collective-permute-start.25 = (bf16[128,256]{1,0:T(8,128)(2,1)S(1)}, bf16[128,256]{1,0:T(8,128)(2,1)S(1)}, u32[]{:S(2)}, u32[]{:S(2)}) collective-permute-start(bf16[128,256]{1,0:T(8,128)(2,1)S(1)} %get-tuple-element.53), channel_id=1, source_target_pairs={{0,2},{1,3},{2,0},{3,1},{4,6},{5,7},{6,4},{7,5},{8,10},{9,11},{10,... | collective-permute-start | bytes 196616 | tf_op jit(solution)/shard_map/ppermute | solution.py:38
  57.6 1.9 %collective-permute-start.23 = (bf16[128,256]{1,0:T(8,128)(2,1)S(1)}, bf16[128,256]{1,0:T(8,128)(2,1)S(1)}, u32[]{:S(2)}, u32[]{:S(2)}) collective-permute-start(bf16[128,256]{1,0:T(8,128)(2,1)S(1)} %get-tuple-element.51), channel_id=1, source_target_pairs={{0,4},{1,5},{2,6},{3,7},{4,0},{5,1},{6,2},{7,3},{8,12},{9,13},{10,... | collective-permute-start | bytes 196616 | tf_op jit(solution)/shard_map/ppermute | solution.py:38
  59.5 1.8 %collective-permute-start.24 = (bf16[128,256]{1,0:T(8,128)(2,1)S(1)}, bf16[128,256]{1,0:T(8,128)(2,1)S(1)}, u32[]{:S(2)}, u32[]{:S(2)}) collective-permute-start(bf16[128,256]{1,0:T(8,128)(2,1)S(1)} %get-tuple-element.52), channel_id=1, source_target_pairs={{0,6},{1,7},{2,4},{3,5},{4,2},{5,3},{6,0},{7,1},{8,14},{9,15},{10,... | collective-permute-start | bytes 196616 | tf_op jit(solution)/shard_map/ppermute | solution.py:38
  61.4 1.1 %collective-permute-start.27 = (bf16[64,512]{1,0:T(8,128)(2,1)S(1)}, bf16[64,512]{1,0:T(8,128)(2,1)S(1)}, u32[]{:S(2)}, u32[]{:S(2)}) collective-permute-start(bf16[64,512]{1,0:T(8,128)(2,1)S(1)} %get-tuple-element.56), channel_id=1, source_target_pairs={{0,4},{1,5},{2,6},{3,7},{4,0},{5,1},{6,2},{7,3},{8,12},{9,13},{10,... | collective-permute-start | bytes 196616 | tf_op jit(solution)/shard_map/ppermute | solution.py:38
  62.5 1.8 %collective-permute-start.28 = (bf16[64,512]{1,0:T(8,128)(2,1)S(1)}, bf16[64,512]{1,0:T(8,128)(2,1)S(1)}, u32[]{:S(2)}, u32[]{:S(2)}) collective-permute-start(bf16[64,512]{1,0:T(8,128)(2,1)S(1)} %get-tuple-element.57), channel_id=1, source_target_pairs={{0,6},{1,7},{2,4},{3,5},{4,2},{5,3},{6,0},{7,1},{8,14},{9,15},{10,... | collective-permute-start | bytes 196616 | tf_op jit(solution)/shard_map/ppermute | solution.py:38
  65.0 1.6 %shard_map.102 = bf16[128,2048]{1,0:T(8,128)(2,1)} custom-call(bf16[128,512]{1,0:T(8,128)(2,1)S(1)} %shard_map.98.refs_4_.refs_0_, bf16[512,512]{1,0:T(8,128)(2,1)S(1)} %copy-done.1, bf16[512,512]{1,0:T(8,128)(2,1)S(1)} %collective-permute-done.7.refs_2_, bf16[512,512]{1,0:T(8,128)(2,1)S(1)} %shard_map.95.refs_3_, ...), custom_call_target="tpu_custom_call" | custom-call | tf_op jit(solution)/shard_map/pallas_call | solution.py:49
  66.6 2.1 %collective-permute-done.23.refs_1_ = bf16[128,256]{1,0:T(8,128)(2,1)S(1)} collective-permute-done((bf16[128,256]{1,0:T(8,128)(2,1)S(1)}, bf16[128,256]{1,0:T(8,128)(2,1)S(1)}, u32[]{:S(2)}, u32[]{:S(2)}) %collective-permute-start.23) | collective-permute-done | bytes 65568 | tf_op jit(solution)/shard_map/ppermute | solution.py:38
  69.4 1.6 %collective-permute-done.27.refs_0_ = bf16[64,512]{1,0:T(8,128)(2,1)S(1)} collective-permute-done((bf16[64,512]{1,0:T(8,128)(2,1)S(1)}, bf16[64,512]{1,0:T(8,128)(2,1)S(1)}, u32[]{:S(2)}, u32[]{:S(2)}) %collective-permute-start.27) | collective-permute-done | bytes 65568 | tf_op jit(solution)/shard_map/ppermute | solution.py:38
  (51 shorter events, 6.0 us)
Async XLA Ops:
  0.6 21.0 %copy-start.1 = (bf16[512,512]{1,0:T(8,128)(2,1)S(1)}, bf16[512,512]{1,0:T(8,128)(2,1)}, u32[]{:S(2)}) copy-start(bf16[512,512]{1,0:T(8,128)(2,1)} %refs_1_.3) | copy-start | bytes 1572868
  0.6 21.0 %collective-permute-start.8 = (bf16[512,512]{1,0:T(8,128)(2,1)}, bf16[512,512]{1,0:T(8,128)(2,1)S(1)}, u32[]{:S(2)}, u32[]{:S(2)}) collective-permute-start(bf16[512,512]{1,0:T(8,128)(2,1)} %refs_1_.3), channel_id=1, source_target_pairs={{0,16},{8,24},{16,0},{24,8},{1,17},{9,25},{17,1},{25,9},{2,18},{10... | collective-permute-start | bytes 1572872 | tf_op jit(solution)/shard_map/ppermute | solution.py:38
  5.9 7.4 %collective-permute-start.2 = (bf16[144,512]{1,0:T(8,128)(2,1)}, bf16[144,512]{1,0:T(8,128)(2,1)S(1)}, u32[]{:S(2)}, u32[]{:S(2)}) collective-permute-start(bf16[144,512]{1,0:T(8,128)(2,1)} %get-tuple-element.35), channel_id=1, source_target_pairs={{0,2},{1,3},{2,0},{3,1},{4,6},{5,7},{6,4},{7,5},{8,10},{9,11},{10,... | collective-permute-start | bytes 442376 | tf_op jit(solution)/shard_map/ppermute | solution.py:38
  7.5 14.1 %collective-permute-start = (bf16[144,512]{1,0:T(8,128)(2,1)}, bf16[144,512]{1,0:T(8,128)(2,1)S(1)}, u32[]{:S(2)}, u32[]{:S(2)}) collective-permute-start(bf16[144,512]{1,0:T(8,128)(2,1)} %get-tuple-element.33), channel_id=1, source_target_pairs={{0,4},{1,5},{2,6},{3,7},{4,0},{5,1},{6,2},{7,3},{8,12},{9,13},{10,... | collective-permute-start | bytes 442376 | tf_op jit(solution)/shard_map/ppermute | solution.py:38
  10.1 11.5 %collective-permute-start.1 = (bf16[144,512]{1,0:T(8,128)(2,1)}, bf16[144,512]{1,0:T(8,128)(2,1)S(1)}, u32[]{:S(2)}, u32[]{:S(2)}) collective-permute-start(bf16[144,512]{1,0:T(8,128)(2,1)} %get-tuple-element.34), channel_id=1, source_target_pairs={{0,6},{1,7},{2,4},{3,5},{4,2},{5,3},{6,0},{7,1},{8,14},{9,15},{10,... | collective-permute-start | bytes 442376 | tf_op jit(solution)/shard_map/ppermute | solution.py:38
  10.3 11.3 %collective-permute-start.3 = (bf16[144,512]{1,0:T(8,128)(2,1)}, bf16[144,512]{1,0:T(8,128)(2,1)S(1)}, u32[]{:S(2)}, u32[]{:S(2)}) collective-permute-start(bf16[144,512]{1,0:T(8,128)(2,1)} %get-tuple-element.32.refs_2_), channel_id=1, source_target_pairs={{0,1},{1,0},{2,3},{3,2},{4,5},{5,4},{6,7},{7,6},{8,9},{9,8},{10,11... | collective-permute-start | bytes 442376 | tf_op jit(solution)/shard_map/ppermute | solution.py:38
  13.3 8.3 %collective-permute-start.4 = (bf16[144,512]{1,0:T(8,128)(2,1)S(1)}, bf16[144,512]{1,0:T(8,128)(2,1)S(1)}, u32[]{:S(2)}, u32[]{:S(2)}) collective-permute-start(bf16[144,512]{1,0:T(8,128)(2,1)S(1)} %collective-permute-done.2.refs_3_.refs_5_), channel_id=1, source_target_pairs={{0,1},{1,0},{2,3},{3,2},{4,5},{5,4},{6,7},{7,6},{8,9},{9,8},{10,11... | collective-permute-start | bytes 442376 | tf_op jit(solution)/shard_map/ppermute | solution.py:38
  21.6 2.6 %collective-permute-start.7 = (bf16[512,512]{1,0:T(8,128)(2,1)S(1)}, bf16[512,512]{1,0:T(8,128)(2,1)S(1)}, u32[]{:S(2)}, u32[]{:S(2)}) collective-permute-start(bf16[512,512]{1,0:T(8,128)(2,1)S(1)} %copy-done.1), channel_id=1, source_target_pairs={{0,8},{8,0},{16,24},{24,16},{1,9},{9,1},{17,25},{25,17},{2,10},{10... | collective-permute-start | bytes 1572872 | tf_op jit(solution)/shard_map/ppermute | solution.py:38
  21.7 2.6 %collective-permute-start.9 = (bf16[512,512]{1,0:T(8,128)(2,1)S(1)}, bf16[512,512]{1,0:T(8,128)(2,1)S(1)}, u32[]{:S(2)}, u32[]{:S(2)}) collective-permute-start(bf16[512,512]{1,0:T(8,128)(2,1)S(1)} %shard_map.95.refs_3_), channel_id=1, source_target_pairs={{0,8},{8,0},{16,24},{24,16},{1,9},{9,1},{17,25},{25,17},{2,10},{10... | collective-permute-start | bytes 1572872 | tf_op jit(solution)/shard_map/ppermute | solution.py:38
  22.2 6.7 %collective-permute-start.5 = (bf16[144,512]{1,0:T(8,128)(2,1)S(1)}, bf16[144,512]{1,0:T(8,128)(2,1)S(1)}, u32[]{:S(2)}, u32[]{:S(2)}) collective-permute-start(bf16[144,512]{1,0:T(8,128)(2,1)S(1)} %collective-permute-done.refs_1_.refs_3_), channel_id=1, source_target_pairs={{0,1},{1,0},{2,3},{3,2},{4,5},{5,4},{6,7},{7,6},{8,9},{9,8},{10,11... | collective-permute-start | bytes 442376 | tf_op jit(solution)/shard_map/ppermute | solution.py:38
  23.7 7.5 %collective-permute-start.6 = (bf16[144,512]{1,0:T(8,128)(2,1)S(1)}, bf16[144,512]{1,0:T(8,128)(2,1)S(1)}, u32[]{:S(2)}, u32[]{:S(2)}) collective-permute-start(bf16[144,512]{1,0:T(8,128)(2,1)S(1)} %collective-permute-done.1.refs_2_.refs_4_), channel_id=1, source_target_pairs={{0,1},{1,0},{2,3},{3,2},{4,5},{5,4},{6,7},{7,6},{8,9},{9,8},{10,11... | collective-permute-start | bytes 442376 | tf_op jit(solution)/shard_map/ppermute | solution.py:38
  24.8 6.4 %collective-permute-start.10 = (bf16[128,128]{1,0:T(8,128)(2,1)S(1)}, bf16[128,128]{1,0:T(8,128)(2,1)S(1)}, u32[]{:S(2)}, u32[]{:S(2)}) collective-permute-start(bf16[128,128]{1,0:T(8,128)(2,1)S(1)} %get-tuple-element.37), channel_id=1, source_target_pairs={{0,4},{1,5},{2,6},{3,7},{4,0},{5,1},{6,2},{7,3},{8,12},{9,13},{10,... | collective-permute-start | bytes 98312 | tf_op jit(solution)/shard_map/ppermute | solution.py:38
  27.6 5.7 %collective-permute-start.11 = (bf16[128,128]{1,0:T(8,128)(2,1)S(1)}, bf16[128,128]{1,0:T(8,128)(2,1)S(1)}, u32[]{:S(2)}, u32[]{:S(2)}) collective-permute-start(bf16[128,128]{1,0:T(8,128)(2,1)S(1)} %get-tuple-element.38), channel_id=1, source_target_pairs={{0,6},{1,7},{2,4},{3,5},{4,2},{5,3},{6,0},{7,1},{8,14},{9,15},{10,... | collective-permute-start | bytes 98312 | tf_op jit(solution)/shard_map/ppermute | solution.py:38
  29.0 4.4 %collective-permute-start.12 = (bf16[128,128]{1,0:T(8,128)(2,1)S(1)}, bf16[128,128]{1,0:T(8,128)(2,1)S(1)}, u32[]{:S(2)}, u32[]{:S(2)}) collective-permute-start(bf16[128,128]{1,0:T(8,128)(2,1)S(1)} %get-tuple-element.39), channel_id=1, source_target_pairs={{0,2},{1,3},{2,0},{3,1},{4,6},{5,7},{6,4},{7,5},{8,10},{9,11},{10,... | collective-permute-start | bytes 98312 | tf_op jit(solution)/shard_map/ppermute | solution.py:38
  38.3 9.4 %collective-permute-start.13 = (bf16[4,128,256]{2,1,0:T(8,128)(2,1)S(1)}, bf16[4,128,256]{2,1,0:T(8,128)(2,1)S(1)}, u32[]{:S(2)}, u32[]{:S(2)}) collective-permute-start(bf16[4,128,256]{2,1,0:T(8,128)(2,1)S(1)} %get-tuple-element.41), channel_id=1, source_target_pairs={{0,1},{1,0},{2,3},{3,2},{4,5},{5,4},{6,7},{7,6},{8,9},{9,8},{10,11... | collective-permute-start | bytes 786440 | tf_op jit(solution)/shard_map/ppermute | solution.py:38
  40.7 8.9 %collective-permute-start.15 = (bf16[2,128,512]{2,1,0:T(8,128)(2,1)S(1)}, bf16[2,128,512]{2,1,0:T(8,128)(2,1)S(1)}, u32[]{:S(2)}, u32[]{:S(2)}) collective-permute-start(bf16[2,128,512]{2,1,0:T(8,128)(2,1)S(1)} %get-tuple-element.44), channel_id=1, source_target_pairs={{0,16},{8,24},{16,0},{24,8},{1,17},{9,25},{17,1},{25,9},{2,18},{10... | collective-permute-start | bytes 786440 | tf_op jit(solution)/shard_map/ppermute | solution.py:38
  41.0 4.9 %collective-permute-start.17 = (bf16[128,128]{1,0:T(8,128)(2,1)S(1)}, bf16[128,128]{1,0:T(8,128)(2,1)S(1)}, u32[]{:S(2)}, u32[]{:S(2)}) collective-permute-start(bf16[128,128]{1,0:T(8,128)(2,1)S(1)} %get-tuple-element.46), channel_id=1, source_target_pairs={{0,4},{1,5},{2,6},{3,7},{4,0},{5,1},{6,2},{7,3},{8,12},{9,13},{10,... | collective-permute-start | bytes 98312 | tf_op jit(solution)/shard_map/ppermute | solution.py:38
  42.0 5.7 %collective-permute-start.18 = (bf16[128,128]{1,0:T(8,128)(2,1)S(1)}, bf16[128,128]{1,0:T(8,128)(2,1)S(1)}, u32[]{:S(2)}, u32[]{:S(2)}) collective-permute-start(bf16[128,128]{1,0:T(8,128)(2,1)S(1)} %get-tuple-element.47), channel_id=1, source_target_pairs={{0,6},{1,7},{2,4},{3,5},{4,2},{5,3},{6,0},{7,1},{8,14},{9,15},{10,... | collective-permute-start | bytes 98312 | tf_op jit(solution)/shard_map/ppermute | solution.py:38
  43.3 4.4 %collective-permute-start.19 = (bf16[128,128]{1,0:T(8,128)(2,1)S(1)}, bf16[128,128]{1,0:T(8,128)(2,1)S(1)}, u32[]{:S(2)}, u32[]{:S(2)}) collective-permute-start(bf16[128,128]{1,0:T(8,128)(2,1)S(1)} %get-tuple-element.48), channel_id=1, source_target_pairs={{0,2},{1,3},{2,0},{3,1},{4,6},{5,7},{6,4},{7,5},{8,10},{9,11},{10,... | collective-permute-start | bytes 98312 | tf_op jit(solution)/shard_map/ppermute | solution.py:38
  45.9 6.9 %collective-permute-start.14 = (bf16[128,512]{1,0:T(8,128)(2,1)S(1)}, bf16[128,512]{1,0:T(8,128)(2,1)S(1)}, u32[]{:S(2)}, u32[]{:S(2)}) collective-permute-start(bf16[128,512]{1,0:T(8,128)(2,1)S(1)} %get-tuple-element.43), channel_id=1, source_target_pairs={{0,8},{8,0},{16,24},{24,16},{1,9},{9,1},{17,25},{25,17},{2,10},{10... | collective-permute-start | bytes 393224 | tf_op jit(solution)/shard_map/ppermute | solution.py:38
  47.8 5.0 %collective-permute-start.21 = (bf16[128,512]{1,0:T(8,128)(2,1)S(1)}, bf16[128,512]{1,0:T(8,128)(2,1)S(1)}, u32[]{:S(2)}, u32[]{:S(2)}) collective-permute-start(bf16[128,512]{1,0:T(8,128)(2,1)S(1)} %shard_map.98.refs_4_.refs_0_), channel_id=1, source_target_pairs={{0,16},{8,24},{16,0},{24,8},{1,17},{9,25},{17,1},{25,9},{2,18},{10... | collective-permute-start | bytes 393224 | tf_op jit(solution)/shard_map/ppermute | solution.py:38
  49.6 3.2 %collective-permute-start.20 = (bf16[128,512]{1,0:T(8,128)(2,1)S(1)}, bf16[128,512]{1,0:T(8,128)(2,1)S(1)}, u32[]{:S(2)}, u32[]{:S(2)}) collective-permute-start(bf16[128,512]{1,0:T(8,128)(2,1)S(1)} %shard_map.98.refs_4_.refs_0_), channel_id=1, source_target_pairs={{0,8},{8,0},{16,24},{24,16},{1,9},{9,1},{17,25},{25,17},{2,10},{10... | collective-permute-start | bytes 393224 | tf_op jit(solution)/shard_map/ppermute | solution.py:38
  49.6 3.2 %collective-permute-start.16 = (bf16[128,512]{1,0:T(8,128)(2,1)S(1)}, bf16[128,512]{1,0:T(8,128)(2,1)S(1)}, u32[]{:S(2)}, u32[]{:S(2)}) collective-permute-start(bf16[128,512]{1,0:T(8,128)(2,1)S(1)} %get-tuple-element.61), channel_id=1, source_target_pairs={{0,8},{8,0},{16,24},{24,16},{1,9},{9,1},{17,25},{25,17},{2,10},{10... | collective-permute-start | bytes 393224 | tf_op jit(solution)/shard_map/ppermute | solution.py:38
  52.8 1.3 %collective-permute-start.22 = (bf16[128,512]{1,0:T(8,128)(2,1)S(1)}, bf16[128,512]{1,0:T(8,128)(2,1)S(1)}, u32[]{:S(2)}, u32[]{:S(2)}) collective-permute-start(bf16[128,512]{1,0:T(8,128)(2,1)S(1)} %collective-permute-done.21.refs_6_), channel_id=1, source_target_pairs={{0,8},{8,0},{16,24},{24,16},{1,9},{9,1},{17,25},{25,17},{2,10},{10... | collective-permute-start | bytes 393224 | tf_op jit(solution)/shard_map/ppermute | solution.py:38
  54.7 6.6 %collective-permute-start.26 = (bf16[2,64,512]{2,1,0:T(8,128)(2,1)S(1)}, bf16[2,64,512]{2,1,0:T(8,128)(2,1)S(1)}, u32[]{:S(2)}, u32[]{:S(2)}) collective-permute-start(bf16[2,64,512]{2,1,0:T(8,128)(2,1)S(1)} %get-tuple-element.55), channel_id=1, source_target_pairs={{0,1},{1,0},{2,3},{3,2},{4,5},{5,4},{6,7},{7,6},{8,9},{9,8},{10,11... | collective-permute-start | bytes 393224 | tf_op jit(solution)/shard_map/ppermute | solution.py:38
  55.0 9.3 %collective-permute-start.29 = (bf16[2,64,512]{2,1,0:T(8,128)(2,1)S(1)}, bf16[2,64,512]{2,1,0:T(8,128)(2,1)S(1)}, u32[]{:S(2)}, u32[]{:S(2)}) collective-permute-start(bf16[2,64,512]{2,1,0:T(8,128)(2,1)S(1)} %get-tuple-element.58), channel_id=1, source_target_pairs={{0,1},{1,0},{2,3},{3,2},{4,5},{5,4},{6,7},{7,6},{8,9},{9,8},{10,11... | collective-permute-start | bytes 393224 | tf_op jit(solution)/shard_map/ppermute | solution.py:38
  56.9 5.6 %collective-permute-start.25 = (bf16[128,256]{1,0:T(8,128)(2,1)S(1)}, bf16[128,256]{1,0:T(8,128)(2,1)S(1)}, u32[]{:S(2)}, u32[]{:S(2)}) collective-permute-start(bf16[128,256]{1,0:T(8,128)(2,1)S(1)} %get-tuple-element.53), channel_id=1, source_target_pairs={{0,2},{1,3},{2,0},{3,1},{4,6},{5,7},{6,4},{7,5},{8,10},{9,11},{10,... | collective-permute-start | bytes 196616 | tf_op jit(solution)/shard_map/ppermute | solution.py:38
  57.6 11.1 %collective-permute-start.23 = (bf16[128,256]{1,0:T(8,128)(2,1)S(1)}, bf16[128,256]{1,0:T(8,128)(2,1)S(1)}, u32[]{:S(2)}, u32[]{:S(2)}) collective-permute-start(bf16[128,256]{1,0:T(8,128)(2,1)S(1)} %get-tuple-element.51), channel_id=1, source_target_pairs={{0,4},{1,5},{2,6},{3,7},{4,0},{5,1},{6,2},{7,3},{8,12},{9,13},{10,... | collective-permute-start | bytes 196616 | tf_op jit(solution)/shard_map/ppermute | solution.py:38
  59.5 9.2 %collective-permute-start.24 = (bf16[128,256]{1,0:T(8,128)(2,1)S(1)}, bf16[128,256]{1,0:T(8,128)(2,1)S(1)}, u32[]{:S(2)}, u32[]{:S(2)}) collective-permute-start(bf16[128,256]{1,0:T(8,128)(2,1)S(1)} %get-tuple-element.52), channel_id=1, source_target_pairs={{0,6},{1,7},{2,4},{3,5},{4,2},{5,3},{6,0},{7,1},{8,14},{9,15},{10,... | collective-permute-start | bytes 196616 | tf_op jit(solution)/shard_map/ppermute | solution.py:38
  61.4 9.7 %collective-permute-start.27 = (bf16[64,512]{1,0:T(8,128)(2,1)S(1)}, bf16[64,512]{1,0:T(8,128)(2,1)S(1)}, u32[]{:S(2)}, u32[]{:S(2)}) collective-permute-start(bf16[64,512]{1,0:T(8,128)(2,1)S(1)} %get-tuple-element.56), channel_id=1, source_target_pairs={{0,4},{1,5},{2,6},{3,7},{4,0},{5,1},{6,2},{7,3},{8,12},{9,13},{10,... | collective-permute-start | bytes 196616 | tf_op jit(solution)/shard_map/ppermute | solution.py:38
  62.5 8.6 %collective-permute-start.28 = (bf16[64,512]{1,0:T(8,128)(2,1)S(1)}, bf16[64,512]{1,0:T(8,128)(2,1)S(1)}, u32[]{:S(2)}, u32[]{:S(2)}) collective-permute-start(bf16[64,512]{1,0:T(8,128)(2,1)S(1)} %get-tuple-element.57), channel_id=1, source_target_pairs={{0,6},{1,7},{2,4},{3,5},{4,2},{5,3},{6,0},{7,1},{8,14},{9,15},{10,... | collective-permute-start | bytes 196616 | tf_op jit(solution)/shard_map/ppermute | solution.py:38
  64.3 6.8 %collective-permute-start.30 = (bf16[64,512]{1,0:T(8,128)(2,1)S(1)}, bf16[64,512]{1,0:T(8,128)(2,1)S(1)}, u32[]{:S(2)}, u32[]{:S(2)}) collective-permute-start(bf16[64,512]{1,0:T(8,128)(2,1)S(1)} %get-tuple-element.59), channel_id=1, source_target_pairs={{0,2},{1,3},{2,0},{3,1},{4,6},{5,7},{6,4},{7,5},{8,10},{9,11},{10,... | collective-permute-start | bytes 196616 | tf_op jit(solution)/shard_map/ppermute | solution.py:38
  (3 other events, 27.4 us)

commit v8 on v7

--- a/solution.py
+++ b/solution.py
@@ -449,7 +449,7 @@
         dq = along_heads(call(pair_kernel, [sds(wide)] * KV_HEADS, [], (keep, give), after=formed))
         far_sums = call(pair_kernel, [sds(share)] * 2, [], (far_sums, swapped(far_send, "ctx", 1)))
         near_sums = call(
-            pair_kernel, [sds(share, f32), sds(share)], [], (near_sums, swapped(near_send, "ctx", 1)), after=dq[1:2])
+            pair_kernel, [sds(share, f32), sds(share)], [], (near_sums, swapped(near_send, "ctx", 1)), after=dq[2:3])
         own_sums, *sums = far_first(along_heads([*near_sums, *far_sums]))
         (weight_grads,) = call(own_total_kernel, [sds(share, f32)], [], (*sums, own_sums))
     else:

time: 72.2 us -> 73 us (1.011)
  waiting for transfers between devices: 23.6 us -> 25.8 us
  starting transfers between devices: 35.9 us -> 34.3 us
    ppermute x31, waiting for transfers between devices: 23.6 us -> 25.8 us  [swapped(): return lax.ppermute(array, axis, [(i, i ^ bits) for i in range(size)])]
    ppermute x31, starting transfers between devices: 35.9 us -> 34.3 us  [swapped(): return lax.ppermute(array, axis, [(i, i ^ bits) for i in range(size)])]
  transfers between devices with their start and end apart: 31 -> 31, of which waited for: 10 -> 12; matrix products, arithmetic and copies ran while one was open for 0% -> 0% of each run, Pallas kernels for 7% -> 7%
where the time goes in v8:
time: 73 us; the launch traced here: 72.7 us
  starting transfers between devices  34.3 us (47%)
  waiting for transfers between devices  25.8 us (35%)
  Pallas kernels  11.9 us (16%)
  between operations  0.79 us (1%)
    ppermute x31, starting transfers between devices, swapped(): return lax.ppermute(array, axis, [(i, i ^ bits) for i in range(size)])  34.3 us
    ppermute x31, waiting for transfers between devices, swapped(): return lax.ppermute(array, axis, [(i, i ^ bits) for i in range(size)])  25.8 us
    pallas_call x11, Pallas kernels, call(): pl.pallas_call(body, out_shape=out_shape, in_specs=specs, out_specs=[VMEM...  11.8 us
  transfers between devices with their start and end apart: 31, of which 12 were waited for; matrix products, arithmetic and copies ran while one was open for 0% of the time, Pallas kernels for 7%

profile of v8, /device:TPU:0, one launch (start us, length us, event | category | flops | bytes accessed | tf_op | source)
XLA Modules:
  0.0 72.7 jit_solution(1201104746328536396)
XLA Ops:
  0.6 3.0 %collective-permute-start.8 = (bf16[512,512]{1,0:T(8,128)(2,1)}, bf16[512,512]{1,0:T(8,128)(2,1)S(1)}, u32[]{:S(2)}, u32[]{:S(2)}) collective-permute-start(bf16[512,512]{1,0:T(8,128)(2,1)} %refs_1_.3), channel_id=1, source_target_pairs={{0,16},{8,24},{16,0},{24,8},{1,17},{9,25},{17,1},{25,9},{2,18},{10... | collective-permute-start | bytes 1572872 | tf_op jit(solution)/shard_map/ppermute | solution.py:38
  3.7 2.2 %shard_map.94 = (bf16[144,512]{1,0:T(8,128)(2,1)}, bf16[144,512]{1,0:T(8,128)(2,1)}, bf16[144,512]{1,0:T(8,128)(2,1)}, bf16[144,512]{1,0:T(8,128)(2,1)}) custom-call(bf16[128,1024]{1,0:T(8,128)(2,1)} %bitcast.14, bf16[128,1024]{1,0:T(8,128)(2,1)} %bitcast.15, bf16[128,1024]{1,0:T(8,128)(2,1)} %bitcast.16, f32[16,128]{1,0:T(8,128)} %bitcast.18), custom_call_target="tpu_custom_call" | custom-call | tf_op jit(solution)/shard_map/pallas_call | solution.py:49
  5.9 1.6 %collective-permute-start.2 = (bf16[144,512]{1,0:T(8,128)(2,1)}, bf16[144,512]{1,0:T(8,128)(2,1)S(1)}, u32[]{:S(2)}, u32[]{:S(2)}) collective-permute-start(bf16[144,512]{1,0:T(8,128)(2,1)} %get-tuple-element.35), channel_id=1, source_target_pairs={{0,2},{1,3},{2,0},{3,1},{4,6},{5,7},{6,4},{7,5},{8,10},{9,11},{10,... | collective-permute-start | bytes 442376 | tf_op jit(solution)/shard_map/ppermute | solution.py:38
  7.5 2.6 %collective-permute-start = (bf16[144,512]{1,0:T(8,128)(2,1)}, bf16[144,512]{1,0:T(8,128)(2,1)S(1)}, u32[]{:S(2)}, u32[]{:S(2)}) collective-permute-start(bf16[144,512]{1,0:T(8,128)(2,1)} %get-tuple-element.33), channel_id=1, source_target_pairs={{0,4},{1,5},{2,6},{3,7},{4,0},{5,1},{6,2},{7,3},{8,12},{9,13},{10,... | collective-permute-start | bytes 442376 | tf_op jit(solution)/shard_map/ppermute | solution.py:38
  10.3 1.5 %collective-permute-start.3 = (bf16[144,512]{1,0:T(8,128)(2,1)}, bf16[144,512]{1,0:T(8,128)(2,1)S(1)}, u32[]{:S(2)}, u32[]{:S(2)}) collective-permute-start(bf16[144,512]{1,0:T(8,128)(2,1)} %get-tuple-element.32.refs_2_), channel_id=1, source_target_pairs={{0,1},{1,0},{2,3},{3,2},{4,5},{5,4},{6,7},{7,6},{8,9},{9,8},{10,11... | collective-permute-start | bytes 442376 | tf_op jit(solution)/shard_map/ppermute | solution.py:38
  11.8 1.5 %collective-permute-done.2.refs_3_.refs_5_ = bf16[144,512]{1,0:T(8,128)(2,1)S(1)} collective-permute-done((bf16[144,512]{1,0:T(8,128)(2,1)}, bf16[144,512]{1,0:T(8,128)(2,1)S(1)}, u32[]{:S(2)}, u32[]{:S(2)}) %collective-permute-start.2) | collective-permute-done | bytes 147488 | tf_op jit(solution)/shard_map/ppermute | solution.py:38
  13.3 1.5 %collective-permute-start.4 = (bf16[144,512]{1,0:T(8,128)(2,1)S(1)}, bf16[144,512]{1,0:T(8,128)(2,1)S(1)}, u32[]{:S(2)}, u32[]{:S(2)}) collective-permute-start(bf16[144,512]{1,0:T(8,128)(2,1)S(1)} %collective-permute-done.2.refs_3_.refs_5_), channel_id=1, source_target_pairs={{0,1},{1,0},{2,3},{3,2},{4,5},{5,4},{6,7},{7,6},{8,9},{9,8},{10,11... | collective-permute-start | bytes 442376 | tf_op jit(solution)/shard_map/ppermute | solution.py:38
  14.8 6.8 %collective-permute-done.refs_1_.refs_3_ = bf16[144,512]{1,0:T(8,128)(2,1)S(1)} collective-permute-done((bf16[144,512]{1,0:T(8,128)(2,1)}, bf16[144,512]{1,0:T(8,128)(2,1)S(1)}, u32[]{:S(2)}, u32[]{:S(2)}) %collective-permute-start) | collective-permute-done | bytes 147488 | tf_op jit(solution)/shard_map/ppermute | solution.py:38
  22.2 1.5 %collective-permute-start.5 = (bf16[144,512]{1,0:T(8,128)(2,1)S(1)}, bf16[144,512]{1,0:T(8,128)(2,1)S(1)}, u32[]{:S(2)}, u32[]{:S(2)}) collective-permute-start(bf16[144,512]{1,0:T(8,128)(2,1)S(1)} %collective-permute-done.refs_1_.refs_3_), channel_id=1, source_target_pairs={{0,1},{1,0},{2,3},{3,2},{4,5},{5,4},{6,7},{7,6},{8,9},{9,8},{10,11... | collective-permute-start | bytes 442376 | tf_op jit(solution)/shard_map/ppermute | solution.py:38
  24.8 2.8 %collective-permute-start.10 = (bf16[128,128]{1,0:T(8,128)(2,1)S(1)}, bf16[128,128]{1,0:T(8,128)(2,1)S(1)}, u32[]{:S(2)}, u32[]{:S(2)}) collective-permute-start(bf16[128,128]{1,0:T(8,128)(2,1)S(1)} %get-tuple-element.37), channel_id=1, source_target_pairs={{0,4},{1,5},{2,6},{3,7},{4,0},{5,1},{6,2},{7,3},{8,12},{9,13},{10,... | collective-permute-start | bytes 98312 | tf_op jit(solution)/shard_map/ppermute | solution.py:38
  27.6 1.3 %collective-permute-start.11 = (bf16[128,128]{1,0:T(8,128)(2,1)S(1)}, bf16[128,128]{1,0:T(8,128)(2,1)S(1)}, u32[]{:S(2)}, u32[]{:S(2)}) collective-permute-start(bf16[128,128]{1,0:T(8,128)(2,1)S(1)} %get-tuple-element.38), channel_id=1, source_target_pairs={{0,6},{1,7},{2,4},{3,5},{4,2},{5,3},{6,0},{7,1},{8,14},{9,15},{10,... | collective-permute-start | bytes 98312 | tf_op jit(solution)/shard_map/ppermute | solution.py:38
  29.0 2.3 %collective-permute-done.6.refs_9_ = bf16[144,512]{1,0:T(8,128)(2,1)S(1)} collective-permute-done((bf16[144,512]{1,0:T(8,128)(2,1)S(1)}, bf16[144,512]{1,0:T(8,128)(2,1)S(1)}, u32[]{:S(2)}, u32[]{:S(2)}) %collective-permute-start.6) | collective-permute-done | bytes 147488 | tf_op jit(solution)/shard_map/ppermute | solution.py:38
  31.2 2.1 %collective-permute-done.11.refs_12_ = bf16[128,128]{1,0:T(8,128)(2,1)S(1)} collective-permute-done((bf16[128,128]{1,0:T(8,128)(2,1)S(1)}, bf16[128,128]{1,0:T(8,128)(2,1)S(1)}, u32[]{:S(2)}, u32[]{:S(2)}) %collective-permute-start.11) | collective-permute-done | bytes 32800 | tf_op jit(solution)/shard_map/ppermute | solution.py:38
  33.3 5.3 %shard_map.97 = (bf16[128,128]{1,0:T(8,128)(2,1)S(1)}, bf16[128,128]{1,0:T(8,128)(2,1)S(1)}, bf16[128,128]{1,0:T(8,128)(2,1)S(1)}, bf16[128,128]{1,0:T(8,128)(2,...) custom-call(s32[1,8]{1,0:T(1,128)S(1)} %copy-done.3, ...), custom_call_target="tpu_custom_call" | custom-call | tf_op jit(solution)/shard_map/pallas_call | solution.py:49
  38.7 1.7 %collective-permute-start.13 = (bf16[4,128,256]{2,1,0:T(8,128)(2,1)S(1)}, bf16[4,128,256]{2,1,0:T(8,128)(2,1)S(1)}, u32[]{:S(2)}, u32[]{:S(2)}) collective-permute-start(bf16[4,128,256]{2,1,0:T(8,128)(2,1)S(1)} %get-tuple-element.41), channel_id=1, source_target_pairs={{0,1},{1,0},{2,3},{3,2},{4,5},{5,4},{6,7},{7,6},{8,9},{9,8},{10,11... | collective-permute-start | bytes 786440 | tf_op jit(solution)/shard_map/ppermute | solution.py:38
  40.5 1.0 %collective-permute-start.17 = (bf16[128,128]{1,0:T(8,128)(2,1)S(1)}, bf16[128,128]{1,0:T(8,128)(2,1)S(1)}, u32[]{:S(2)}, u32[]{:S(2)}) collective-permute-start(bf16[128,128]{1,0:T(8,128)(2,1)S(1)} %get-tuple-element.46), channel_id=1, source_target_pairs={{0,4},{1,5},{2,6},{3,7},{4,0},{5,1},{6,2},{7,3},{8,12},{9,13},{10,... | collective-permute-start | bytes 98312 | tf_op jit(solution)/shard_map/ppermute | solution.py:38
  41.5 1.4 %collective-permute-start.18 = (bf16[128,128]{1,0:T(8,128)(2,1)S(1)}, bf16[128,128]{1,0:T(8,128)(2,1)S(1)}, u32[]{:S(2)}, u32[]{:S(2)}) collective-permute-start(bf16[128,128]{1,0:T(8,128)(2,1)S(1)} %get-tuple-element.47), channel_id=1, source_target_pairs={{0,6},{1,7},{2,4},{3,5},{4,2},{5,3},{6,0},{7,1},{8,14},{9,15},{10,... | collective-permute-start | bytes 98312 | tf_op jit(solution)/shard_map/ppermute | solution.py:38
  42.9 1.1 %collective-permute-start.19 = (bf16[128,128]{1,0:T(8,128)(2,1)S(1)}, bf16[128,128]{1,0:T(8,128)(2,1)S(1)}, u32[]{:S(2)}, u32[]{:S(2)}) collective-permute-start(bf16[128,128]{1,0:T(8,128)(2,1)S(1)} %get-tuple-element.48), channel_id=1, source_target_pairs={{0,2},{1,3},{2,0},{3,1},{4,6},{5,7},{6,4},{7,5},{8,10},{9,11},{10,... | collective-permute-start | bytes 98312 | tf_op jit(solution)/shard_map/ppermute | solution.py:38
  44.0 1.5 %collective-permute-done.17.refs_1_ = bf16[128,128]{1,0:T(8,128)(2,1)S(1)} collective-permute-done((bf16[128,128]{1,0:T(8,128)(2,1)S(1)}, bf16[128,128]{1,0:T(8,128)(2,1)S(1)}, u32[]{:S(2)}, u32[]{:S(2)}) %collective-permute-start.17) | collective-permute-done | bytes 32800 | tf_op jit(solution)/shard_map/ppermute | solution.py:38
  45.6 1.7 %collective-permute-done.18.refs_2_ = bf16[128,128]{1,0:T(8,128)(2,1)S(1)} collective-permute-done((bf16[128,128]{1,0:T(8,128)(2,1)S(1)}, bf16[128,128]{1,0:T(8,128)(2,1)S(1)}, u32[]{:S(2)}, u32[]{:S(2)}) %collective-permute-start.18) | collective-permute-done | bytes 32800 | tf_op jit(solution)/shard_map/ppermute | solution.py:38
  47.4 1.9 %collective-permute-start.21 = (bf16[128,512]{1,0:T(8,128)(2,1)S(1)}, bf16[128,512]{1,0:T(8,128)(2,1)S(1)}, u32[]{:S(2)}, u32[]{:S(2)}) collective-permute-start(bf16[128,512]{1,0:T(8,128)(2,1)S(1)} %shard_map.98.refs_4_.refs_0_), channel_id=1, source_target_pairs={{0,16},{8,24},{16,0},{24,8},{1,17},{9,25},{17,1},{25,9},{2,18},{10... | collective-permute-start | bytes 393224 | tf_op jit(solution)/shard_map/ppermute | solution.py:38
  49.9 2.5 %collective-permute-done.21.refs_6_ = bf16[128,512]{1,0:T(8,128)(2,1)S(1)} collective-permute-done((bf16[128,512]{1,0:T(8,128)(2,1)S(1)}, bf16[128,512]{1,0:T(8,128)(2,1)S(1)}, u32[]{:S(2)}, u32[]{:S(2)}) %collective-permute-start.21) | collective-permute-done | bytes 131104 | tf_op jit(solution)/shard_map/ppermute | solution.py:38
  52.5 1.3 %collective-permute-done.22.refs_7_ = bf16[128,512]{1,0:T(8,128)(2,1)S(1)} collective-permute-done((bf16[128,512]{1,0:T(8,128)(2,1)S(1)}, bf16[128,512]{1,0:T(8,128)(2,1)S(1)}, u32[]{:S(2)}, u32[]{:S(2)}) %collective-permute-start.22) | collective-permute-done | bytes 131104 | tf_op jit(solution)/shard_map/ppermute | solution.py:38
  54.3 1.1 %collective-permute-start.26 = (bf16[2,64,512]{2,1,0:T(8,128)(2,1)S(1)}, bf16[2,64,512]{2,1,0:T(8,128)(2,1)S(1)}, u32[]{:S(2)}, u32[]{:S(2)}) collective-permute-start(bf16[2,64,512]{2,1,0:T(8,128)(2,1)S(1)} %get-tuple-element.55), channel_id=1, source_target_pairs={{0,1},{1,0},{2,3},{3,2},{4,5},{5,4},{6,7},{7,6},{8,9},{9,8},{10,11... | collective-permute-start | bytes 393224 | tf_op jit(solution)/shard_map/ppermute | solution.py:38
  55.4 1.0 %collective-permute-start.29 = (bf16[2,64,512]{2,1,0:T(8,128)(2,1)S(1)}, bf16[2,64,512]{2,1,0:T(8,128)(2,1)S(1)}, u32[]{:S(2)}, u32[]{:S(2)}) collective-permute-start(bf16[2,64,512]{2,1,0:T(8,128)(2,1)S(1)} %get-tuple-element.58), channel_id=1, source_target_pairs={{0,1},{1,0},{2,3},{3,2},{4,5},{5,4},{6,7},{7,6},{8,9},{9,8},{10,11... | collective-permute-start | bytes 393224 | tf_op jit(solution)/shard_map/ppermute | solution.py:38
  56.5 1.3 %collective-permute-start.23 = (bf16[128,256]{1,0:T(8,128)(2,1)S(1)}, bf16[128,256]{1,0:T(8,128)(2,1)S(1)}, u32[]{:S(2)}, u32[]{:S(2)}) collective-permute-start(bf16[128,256]{1,0:T(8,128)(2,1)S(1)} %get-tuple-element.51), channel_id=1, source_target_pairs={{0,4},{1,5},{2,6},{3,7},{4,0},{5,1},{6,2},{7,3},{8,12},{9,13},{10,... | collective-permute-start | bytes 196616 | tf_op jit(solution)/shard_map/ppermute | solution.py:38
  57.8 1.8 %collective-permute-start.24 = (bf16[128,256]{1,0:T(8,128)(2,1)S(1)}, bf16[128,256]{1,0:T(8,128)(2,1)S(1)}, u32[]{:S(2)}, u32[]{:S(2)}) collective-permute-start(bf16[128,256]{1,0:T(8,128)(2,1)S(1)} %get-tuple-element.52), channel_id=1, source_target_pairs={{0,6},{1,7},{2,4},{3,5},{4,2},{5,3},{6,0},{7,1},{8,14},{9,15},{10,... | collective-permute-start | bytes 196616 | tf_op jit(solution)/shard_map/ppermute | solution.py:38
  60.7 1.5 %collective-permute-start.27 = (bf16[64,512]{1,0:T(8,128)(2,1)S(1)}, bf16[64,512]{1,0:T(8,128)(2,1)S(1)}, u32[]{:S(2)}, u32[]{:S(2)}) collective-permute-start(bf16[64,512]{1,0:T(8,128)(2,1)S(1)} %get-tuple-element.56), channel_id=1, source_target_pairs={{0,4},{1,5},{2,6},{3,7},{4,0},{5,1},{6,2},{7,3},{8,12},{9,13},{10,... | collective-permute-start | bytes 196616 | tf_op jit(solution)/shard_map/ppermute | solution.py:38
  62.3 3.0 %collective-permute-done.23.refs_1_.refs_2_ = bf16[128,256]{1,0:T(8,128)(2,1)S(1)} collective-permute-done((bf16[128,256]{1,0:T(8,128)(2,1)S(1)}, bf16[128,256]{1,0:T(8,128)(2,1)S(1)}, u32[]{:S(2)}, u32[]{:S(2)}) %collective-permute-start.23) | collective-permute-done | bytes 65568 | tf_op jit(solution)/shard_map/ppermute | solution.py:38
  65.2 2.0 %collective-permute-start.28 = (bf16[64,512]{1,0:T(8,128)(2,1)S(1)}, bf16[64,512]{1,0:T(8,128)(2,1)S(1)}, u32[]{:S(2)}, u32[]{:S(2)}) collective-permute-start(bf16[64,512]{1,0:T(8,128)(2,1)S(1)} %get-tuple-element.57), channel_id=1, source_target_pairs={{0,6},{1,7},{2,4},{3,5},{4,2},{5,3},{6,0},{7,1},{8,14},{9,15},{10,... | collective-permute-start | bytes 196616 | tf_op jit(solution)/shard_map/ppermute | solution.py:38
  67.4 1.6 %shard_map.102 = bf16[128,2048]{1,0:T(8,128)(2,1)} custom-call(bf16[128,512]{1,0:T(8,128)(2,1)S(1)} %shard_map.98.refs_4_.refs_0_, bf16[512,512]{1,0:T(8,128)(2,1)S(1)} %copy-done.1, bf16[512,512]{1,0:T(8,128)(2,1)S(1)} %collective-permute-done.7.refs_2_, bf16[512,512]{1,0:T(8,128)(2,1)S(1)} %shard_map.95.refs_3_, ...), custom_call_target="tpu_custom_call" | custom-call | tf_op jit(solution)/shard_map/pallas_call | solution.py:49
  69.7 1.6 %collective-permute-done.28.refs_1_ = bf16[64,512]{1,0:T(8,128)(2,1)S(1)} collective-permute-done((bf16[64,512]{1,0:T(8,128)(2,1)S(1)}, bf16[64,512]{1,0:T(8,128)(2,1)S(1)}, u32[]{:S(2)}, u32[]{:S(2)}) %collective-permute-start.28) | collective-permute-done | bytes 65568 | tf_op jit(solution)/shard_map/ppermute | solution.py:38
  (51 shorter events, 6.8 us)
Async XLA Ops:
  0.6 21.0 %copy-start.1 = (bf16[512,512]{1,0:T(8,128)(2,1)S(1)}, bf16[512,512]{1,0:T(8,128)(2,1)}, u32[]{:S(2)}) copy-start(bf16[512,512]{1,0:T(8,128)(2,1)} %refs_1_.3) | copy-start | bytes 1572868
  0.6 21.0 %collective-permute-start.8 = (bf16[512,512]{1,0:T(8,128)(2,1)}, bf16[512,512]{1,0:T(8,128)(2,1)S(1)}, u32[]{:S(2)}, u32[]{:S(2)}) collective-permute-start(bf16[512,512]{1,0:T(8,128)(2,1)} %refs_1_.3), channel_id=1, source_target_pairs={{0,16},{8,24},{16,0},{24,8},{1,17},{9,25},{17,1},{25,9},{2,18},{10... | collective-permute-start | bytes 1572872 | tf_op jit(solution)/shard_map/ppermute | solution.py:38
  5.9 7.4 %collective-permute-start.2 = (bf16[144,512]{1,0:T(8,128)(2,1)}, bf16[144,512]{1,0:T(8,128)(2,1)S(1)}, u32[]{:S(2)}, u32[]{:S(2)}) collective-permute-start(bf16[144,512]{1,0:T(8,128)(2,1)} %get-tuple-element.35), channel_id=1, source_target_pairs={{0,2},{1,3},{2,0},{3,1},{4,6},{5,7},{6,4},{7,5},{8,10},{9,11},{10,... | collective-permute-start | bytes 442376 | tf_op jit(solution)/shard_map/ppermute | solution.py:38
  7.5 14.1 %collective-permute-start = (bf16[144,512]{1,0:T(8,128)(2,1)}, bf16[144,512]{1,0:T(8,128)(2,1)S(1)}, u32[]{:S(2)}, u32[]{:S(2)}) collective-permute-start(bf16[144,512]{1,0:T(8,128)(2,1)} %get-tuple-element.33), channel_id=1, source_target_pairs={{0,4},{1,5},{2,6},{3,7},{4,0},{5,1},{6,2},{7,3},{8,12},{9,13},{10,... | collective-permute-start | bytes 442376 | tf_op jit(solution)/shard_map/ppermute | solution.py:38
  10.1 11.5 %collective-permute-start.1 = (bf16[144,512]{1,0:T(8,128)(2,1)}, bf16[144,512]{1,0:T(8,128)(2,1)S(1)}, u32[]{:S(2)}, u32[]{:S(2)}) collective-permute-start(bf16[144,512]{1,0:T(8,128)(2,1)} %get-tuple-element.34), channel_id=1, source_target_pairs={{0,6},{1,7},{2,4},{3,5},{4,2},{5,3},{6,0},{7,1},{8,14},{9,15},{10,... | collective-permute-start | bytes 442376 | tf_op jit(solution)/shard_map/ppermute | solution.py:38
  10.3 11.3 %collective-permute-start.3 = (bf16[144,512]{1,0:T(8,128)(2,1)}, bf16[144,512]{1,0:T(8,128)(2,1)S(1)}, u32[]{:S(2)}, u32[]{:S(2)}) collective-permute-start(bf16[144,512]{1,0:T(8,128)(2,1)} %get-tuple-element.32.refs_2_), channel_id=1, source_target_pairs={{0,1},{1,0},{2,3},{3,2},{4,5},{5,4},{6,7},{7,6},{8,9},{9,8},{10,11... | collective-permute-start | bytes 442376 | tf_op jit(solution)/shard_map/ppermute | solution.py:38
  13.3 8.3 %collective-permute-start.4 = (bf16[144,512]{1,0:T(8,128)(2,1)S(1)}, bf16[144,512]{1,0:T(8,128)(2,1)S(1)}, u32[]{:S(2)}, u32[]{:S(2)}) collective-permute-start(bf16[144,512]{1,0:T(8,128)(2,1)S(1)} %collective-permute-done.2.refs_3_.refs_5_), channel_id=1, source_target_pairs={{0,1},{1,0},{2,3},{3,2},{4,5},{5,4},{6,7},{7,6},{8,9},{9,8},{10,11... | collective-permute-start | bytes 442376 | tf_op jit(solution)/shard_map/ppermute | solution.py:38
  21.6 2.6 %collective-permute-start.7 = (bf16[512,512]{1,0:T(8,128)(2,1)S(1)}, bf16[512,512]{1,0:T(8,128)(2,1)S(1)}, u32[]{:S(2)}, u32[]{:S(2)}) collective-permute-start(bf16[512,512]{1,0:T(8,128)(2,1)S(1)} %copy-done.1), channel_id=1, source_target_pairs={{0,8},{8,0},{16,24},{24,16},{1,9},{9,1},{17,25},{25,17},{2,10},{10... | collective-permute-start | bytes 1572872 | tf_op jit(solution)/shard_map/ppermute | solution.py:38
  21.7 2.6 %collective-permute-start.9 = (bf16[512,512]{1,0:T(8,128)(2,1)S(1)}, bf16[512,512]{1,0:T(8,128)(2,1)S(1)}, u32[]{:S(2)}, u32[]{:S(2)}) collective-permute-start(bf16[512,512]{1,0:T(8,128)(2,1)S(1)} %shard_map.95.refs_3_), channel_id=1, source_target_pairs={{0,8},{8,0},{16,24},{24,16},{1,9},{9,1},{17,25},{25,17},{2,10},{10... | collective-permute-start | bytes 1572872 | tf_op jit(solution)/shard_map/ppermute | solution.py:38
  22.2 6.7 %collective-permute-start.5 = (bf16[144,512]{1,0:T(8,128)(2,1)S(1)}, bf16[144,512]{1,0:T(8,128)(2,1)S(1)}, u32[]{:S(2)}, u32[]{:S(2)}) collective-permute-start(bf16[144,512]{1,0:T(8,128)(2,1)S(1)} %collective-permute-done.refs_1_.refs_3_), channel_id=1, source_target_pairs={{0,1},{1,0},{2,3},{3,2},{4,5},{5,4},{6,7},{7,6},{8,9},{9,8},{10,11... | collective-permute-start | bytes 442376 | tf_op jit(solution)/shard_map/ppermute | solution.py:38
  23.7 7.5 %collective-permute-start.6 = (bf16[144,512]{1,0:T(8,128)(2,1)S(1)}, bf16[144,512]{1,0:T(8,128)(2,1)S(1)}, u32[]{:S(2)}, u32[]{:S(2)}) collective-permute-start(bf16[144,512]{1,0:T(8,128)(2,1)S(1)} %collective-permute-done.1.refs_2_.refs_4_), channel_id=1, source_target_pairs={{0,1},{1,0},{2,3},{3,2},{4,5},{5,4},{6,7},{7,6},{8,9},{9,8},{10,11... | collective-permute-start | bytes 442376 | tf_op jit(solution)/shard_map/ppermute | solution.py:38
  24.8 6.4 %collective-permute-start.10 = (bf16[128,128]{1,0:T(8,128)(2,1)S(1)}, bf16[128,128]{1,0:T(8,128)(2,1)S(1)}, u32[]{:S(2)}, u32[]{:S(2)}) collective-permute-start(bf16[128,128]{1,0:T(8,128)(2,1)S(1)} %get-tuple-element.37), channel_id=1, source_target_pairs={{0,4},{1,5},{2,6},{3,7},{4,0},{5,1},{6,2},{7,3},{8,12},{9,13},{10,... | collective-permute-start | bytes 98312 | tf_op jit(solution)/shard_map/ppermute | solution.py:38
  27.6 5.7 %collective-permute-start.11 = (bf16[128,128]{1,0:T(8,128)(2,1)S(1)}, bf16[128,128]{1,0:T(8,128)(2,1)S(1)}, u32[]{:S(2)}, u32[]{:S(2)}) collective-permute-start(bf16[128,128]{1,0:T(8,128)(2,1)S(1)} %get-tuple-element.38), channel_id=1, source_target_pairs={{0,6},{1,7},{2,4},{3,5},{4,2},{5,3},{6,0},{7,1},{8,14},{9,15},{10,... | collective-permute-start | bytes 98312 | tf_op jit(solution)/shard_map/ppermute | solution.py:38
  29.0 4.4 %collective-permute-start.12 = (bf16[128,128]{1,0:T(8,128)(2,1)S(1)}, bf16[128,128]{1,0:T(8,128)(2,1)S(1)}, u32[]{:S(2)}, u32[]{:S(2)}) collective-permute-start(bf16[128,128]{1,0:T(8,128)(2,1)S(1)} %get-tuple-element.39), channel_id=1, source_target_pairs={{0,2},{1,3},{2,0},{3,1},{4,6},{5,7},{6,4},{7,5},{8,10},{9,11},{10,... | collective-permute-start | bytes 98312 | tf_op jit(solution)/shard_map/ppermute | solution.py:38
  38.7 8.6 %collective-permute-start.13 = (bf16[4,128,256]{2,1,0:T(8,128)(2,1)S(1)}, bf16[4,128,256]{2,1,0:T(8,128)(2,1)S(1)}, u32[]{:S(2)}, u32[]{:S(2)}) collective-permute-start(bf16[4,128,256]{2,1,0:T(8,128)(2,1)S(1)} %get-tuple-element.41), channel_id=1, source_target_pairs={{0,1},{1,0},{2,3},{3,2},{4,5},{5,4},{6,7},{7,6},{8,9},{9,8},{10,11... | collective-permute-start | bytes 786440 | tf_op jit(solution)/shard_map/ppermute | solution.py:38
  40.4 8.9 %collective-permute-start.15 = (bf16[2,128,512]{2,1,0:T(8,128)(2,1)S(1)}, bf16[2,128,512]{2,1,0:T(8,128)(2,1)S(1)}, u32[]{:S(2)}, u32[]{:S(2)}) collective-permute-start(bf16[2,128,512]{2,1,0:T(8,128)(2,1)S(1)} %get-tuple-element.44), channel_id=1, source_target_pairs={{0,16},{8,24},{16,0},{24,8},{1,17},{9,25},{17,1},{25,9},{2,18},{10... | collective-permute-start | bytes 786440 | tf_op jit(solution)/shard_map/ppermute | solution.py:38
  40.5 5.0 %collective-permute-start.17 = (bf16[128,128]{1,0:T(8,128)(2,1)S(1)}, bf16[128,128]{1,0:T(8,128)(2,1)S(1)}, u32[]{:S(2)}, u32[]{:S(2)}) collective-permute-start(bf16[128,128]{1,0:T(8,128)(2,1)S(1)} %get-tuple-element.46), channel_id=1, source_target_pairs={{0,4},{1,5},{2,6},{3,7},{4,0},{5,1},{6,2},{7,3},{8,12},{9,13},{10,... | collective-permute-start | bytes 98312 | tf_op jit(solution)/shard_map/ppermute | solution.py:38
  41.5 5.7 %collective-permute-start.18 = (bf16[128,128]{1,0:T(8,128)(2,1)S(1)}, bf16[128,128]{1,0:T(8,128)(2,1)S(1)}, u32[]{:S(2)}, u32[]{:S(2)}) collective-permute-start(bf16[128,128]{1,0:T(8,128)(2,1)S(1)} %get-tuple-element.47), channel_id=1, source_target_pairs={{0,6},{1,7},{2,4},{3,5},{4,2},{5,3},{6,0},{7,1},{8,14},{9,15},{10,... | collective-permute-start | bytes 98312 | tf_op jit(solution)/shard_map/ppermute | solution.py:38
  42.9 4.4 %collective-permute-start.19 = (bf16[128,128]{1,0:T(8,128)(2,1)S(1)}, bf16[128,128]{1,0:T(8,128)(2,1)S(1)}, u32[]{:S(2)}, u32[]{:S(2)}) collective-permute-start(bf16[128,128]{1,0:T(8,128)(2,1)S(1)} %get-tuple-element.48), channel_id=1, source_target_pairs={{0,2},{1,3},{2,0},{3,1},{4,6},{5,7},{6,4},{7,5},{8,10},{9,11},{10,... | collective-permute-start | bytes 98312 | tf_op jit(solution)/shard_map/ppermute | solution.py:38
  45.6 6.9 %collective-permute-start.14 = (bf16[128,512]{1,0:T(8,128)(2,1)S(1)}, bf16[128,512]{1,0:T(8,128)(2,1)S(1)}, u32[]{:S(2)}, u32[]{:S(2)}) collective-permute-start(bf16[128,512]{1,0:T(8,128)(2,1)S(1)} %get-tuple-element.43), channel_id=1, source_target_pairs={{0,8},{8,0},{16,24},{24,16},{1,9},{9,1},{17,25},{25,17},{2,10},{10... | collective-permute-start | bytes 393224 | tf_op jit(solution)/shard_map/ppermute | solution.py:38
  47.4 5.0 %collective-permute-start.21 = (bf16[128,512]{1,0:T(8,128)(2,1)S(1)}, bf16[128,512]{1,0:T(8,128)(2,1)S(1)}, u32[]{:S(2)}, u32[]{:S(2)}) collective-permute-start(bf16[128,512]{1,0:T(8,128)(2,1)S(1)} %shard_map.98.refs_4_.refs_0_), channel_id=1, source_target_pairs={{0,16},{8,24},{16,0},{24,8},{1,17},{9,25},{17,1},{25,9},{2,18},{10... | collective-permute-start | bytes 393224 | tf_op jit(solution)/shard_map/ppermute | solution.py:38
  49.3 3.2 %collective-permute-start.20 = (bf16[128,512]{1,0:T(8,128)(2,1)S(1)}, bf16[128,512]{1,0:T(8,128)(2,1)S(1)}, u32[]{:S(2)}, u32[]{:S(2)}) collective-permute-start(bf16[128,512]{1,0:T(8,128)(2,1)S(1)} %shard_map.98.refs_4_.refs_0_), channel_id=1, source_target_pairs={{0,8},{8,0},{16,24},{24,16},{1,9},{9,1},{17,25},{25,17},{2,10},{10... | collective-permute-start | bytes 393224 | tf_op jit(solution)/shard_map/ppermute | solution.py:38
  49.3 3.1 %collective-permute-start.16 = (bf16[128,512]{1,0:T(8,128)(2,1)S(1)}, bf16[128,512]{1,0:T(8,128)(2,1)S(1)}, u32[]{:S(2)}, u32[]{:S(2)}) collective-permute-start(bf16[128,512]{1,0:T(8,128)(2,1)S(1)} %get-tuple-element.61), channel_id=1, source_target_pairs={{0,8},{8,0},{16,24},{24,16},{1,9},{9,1},{17,25},{25,17},{2,10},{10... | collective-permute-start | bytes 393224 | tf_op jit(solution)/shard_map/ppermute | solution.py:38
  52.4 1.3 %collective-permute-start.22 = (bf16[128,512]{1,0:T(8,128)(2,1)S(1)}, bf16[128,512]{1,0:T(8,128)(2,1)S(1)}, u32[]{:S(2)}, u32[]{:S(2)}) collective-permute-start(bf16[128,512]{1,0:T(8,128)(2,1)S(1)} %collective-permute-done.21.refs_6_), channel_id=1, source_target_pairs={{0,8},{8,0},{16,24},{24,16},{1,9},{9,1},{17,25},{25,17},{2,10},{10... | collective-permute-start | bytes 393224 | tf_op jit(solution)/shard_map/ppermute | solution.py:38
  54.3 6.4 %collective-permute-start.26 = (bf16[2,64,512]{2,1,0:T(8,128)(2,1)S(1)}, bf16[2,64,512]{2,1,0:T(8,128)(2,1)S(1)}, u32[]{:S(2)}, u32[]{:S(2)}) collective-permute-start(bf16[2,64,512]{2,1,0:T(8,128)(2,1)S(1)} %get-tuple-element.55), channel_id=1, source_target_pairs={{0,1},{1,0},{2,3},{3,2},{4,5},{5,4},{6,7},{7,6},{8,9},{9,8},{10,11... | collective-permute-start | bytes 393224 | tf_op jit(solution)/shard_map/ppermute | solution.py:38
  55.4 11.9 %collective-permute-start.29 = (bf16[2,64,512]{2,1,0:T(8,128)(2,1)S(1)}, bf16[2,64,512]{2,1,0:T(8,128)(2,1)S(1)}, u32[]{:S(2)}, u32[]{:S(2)}) collective-permute-start(bf16[2,64,512]{2,1,0:T(8,128)(2,1)S(1)} %get-tuple-element.58), channel_id=1, source_target_pairs={{0,1},{1,0},{2,3},{3,2},{4,5},{5,4},{6,7},{7,6},{8,9},{9,8},{10,11... | collective-permute-start | bytes 393224 | tf_op jit(solution)/shard_map/ppermute | solution.py:38
  56.5 8.8 %collective-permute-start.23 = (bf16[128,256]{1,0:T(8,128)(2,1)S(1)}, bf16[128,256]{1,0:T(8,128)(2,1)S(1)}, u32[]{:S(2)}, u32[]{:S(2)}) collective-permute-start(bf16[128,256]{1,0:T(8,128)(2,1)S(1)} %get-tuple-element.51), channel_id=1, source_target_pairs={{0,4},{1,5},{2,6},{3,7},{4,0},{5,1},{6,2},{7,3},{8,12},{9,13},{10,... | collective-permute-start | bytes 196616 | tf_op jit(solution)/shard_map/ppermute | solution.py:38
  57.8 11.2 %collective-permute-start.24 = (bf16[128,256]{1,0:T(8,128)(2,1)S(1)}, bf16[128,256]{1,0:T(8,128)(2,1)S(1)}, u32[]{:S(2)}, u32[]{:S(2)}) collective-permute-start(bf16[128,256]{1,0:T(8,128)(2,1)S(1)} %get-tuple-element.52), channel_id=1, source_target_pairs={{0,6},{1,7},{2,4},{3,5},{4,2},{5,3},{6,0},{7,1},{8,14},{9,15},{10,... | collective-permute-start | bytes 196616 | tf_op jit(solution)/shard_map/ppermute | solution.py:38
  59.6 9.4 %collective-permute-start.25 = (bf16[128,256]{1,0:T(8,128)(2,1)S(1)}, bf16[128,256]{1,0:T(8,128)(2,1)S(1)}, u32[]{:S(2)}, u32[]{:S(2)}) collective-permute-start(bf16[128,256]{1,0:T(8,128)(2,1)S(1)} %get-tuple-element.53), channel_id=1, source_target_pairs={{0,2},{1,3},{2,0},{3,1},{4,6},{5,7},{6,4},{7,5},{8,10},{9,11},{10,... | collective-permute-start | bytes 196616 | tf_op jit(solution)/shard_map/ppermute | solution.py:38
  60.7 9.0 %collective-permute-start.27 = (bf16[64,512]{1,0:T(8,128)(2,1)S(1)}, bf16[64,512]{1,0:T(8,128)(2,1)S(1)}, u32[]{:S(2)}, u32[]{:S(2)}) collective-permute-start(bf16[64,512]{1,0:T(8,128)(2,1)S(1)} %get-tuple-element.56), channel_id=1, source_target_pairs={{0,4},{1,5},{2,6},{3,7},{4,0},{5,1},{6,2},{7,3},{8,12},{9,13},{10,... | collective-permute-start | bytes 196616 | tf_op jit(solution)/shard_map/ppermute | solution.py:38
  65.2 6.1 %collective-permute-start.28 = (bf16[64,512]{1,0:T(8,128)(2,1)S(1)}, bf16[64,512]{1,0:T(8,128)(2,1)S(1)}, u32[]{:S(2)}, u32[]{:S(2)}) collective-permute-start(bf16[64,512]{1,0:T(8,128)(2,1)S(1)} %get-tuple-element.57), channel_id=1, source_target_pairs={{0,6},{1,7},{2,4},{3,5},{4,2},{5,3},{6,0},{7,1},{8,14},{9,15},{10,... | collective-permute-start | bytes 196616 | tf_op jit(solution)/shard_map/ppermute | solution.py:38
  67.3 4.7 %collective-permute-start.30 = (bf16[64,512]{1,0:T(8,128)(2,1)S(1)}, bf16[64,512]{1,0:T(8,128)(2,1)S(1)}, u32[]{:S(2)}, u32[]{:S(2)}) collective-permute-start(bf16[64,512]{1,0:T(8,128)(2,1)S(1)} %get-tuple-element.59), channel_id=1, source_target_pairs={{0,2},{1,3},{2,0},{3,1},{4,6},{5,7},{6,4},{7,5},{8,10},{9,11},{10,... | collective-permute-start | bytes 196616 | tf_op jit(solution)/shard_map/ppermute | solution.py:38
  (3 other events, 27.4 us)
